TPU v7x, 32 devices: a whole 2x2x4 slice. The times are simulated.
32 devices in a mesh: fields: 2 (over y), row: 4 (over z), col: 4 (over x, core).
Axes of the slice: x: 2, y: 2, z: 4, core: 2. Of those that a mesh axis runs over, the one named last changes fastest.
Arguments:
- root_inverse: bfloat16 [8192, 4096], P(('fields', 'row'), 'col'), parts along dimension 0, as said below
- child_inverse: bfloat16 [4096, 2048], P(('fields', 'row'), 'col'), parts along dimension 0, as said below
- panel: bfloat16 [8192, 2048], P(('fields', 'row'), 'col'), parts along dimension 0, may hold values from -0.09375 to 0.09375
- structure: int32 [64], P(('fields', 'row')), parts along dimension 0, may hold values 0 or 1
Outputs:
- sigma_root: bfloat16 [8192, 4096], P(('fields', 'row'), 'col'), parts along dimension 0
- sigma_cross: bfloat16 [8192, 2048], P(('fields', 'row'), 'col'), parts along dimension 0
- sigma_child: float32 [4096, 2048], P(('fields', 'row'), 'col'), parts along dimension 0
There are 2 independent parts, one for each index of `fields`. A program takes and returns all parts, laid end to end along the dimension named above; each array names one. Nothing has to cross between parts.
Inputs may be any that keep to these rules, and one draw needn't show every extreme that they name: `root_inverse`: lower triangular with a positive diagonal. `child_inverse`: lower triangular with a positive diagonal. 1 marks a block row of 128 root rows in the child's structure.
All inputs are finite; a program needn't handle non-finite values.
Results may differ from a plain program's by a relative error of at most 0.008.
Values may be sent and summed in bfloat16 or wider, within the bound.
No kernel may reach another device: no remote copies, remote signals or barrier semaphores. Data moves between devices by JAX's collectives and lax.ppermute only.
A program may use at most 128 MiB of HBM per device.

v0:
```python
import jax
import jax.numpy as jnp
from jax import lax
from jax.sharding import PartitionSpec as P

BLOCK = 128


def inner_dot(left_part, right_part):
    return lax.dot_general(
        left_part, right_part, (((0,), (0,)), ((), ())), preferred_element_type=jnp.float32
    )


def on_device(root_inverse, child_inverse, panel, structure):
    kept_rows = jnp.repeat(structure, BLOCK)[:, None] > 0
    panel_kept = jnp.where(kept_rows, panel, jnp.zeros_like(panel))
    root_full, child_rows, panel_full = (
        lax.all_gather(root_inverse, "col", axis=1, tiled=True),
        lax.all_gather(child_inverse, "col", axis=1, tiled=True),
        lax.all_gather(panel_kept, "col", axis=1, tiled=True),
    )
    left_part = root_full
    root_sum = lax.psum_scatter(
        inner_dot(left_part, root_inverse), "row", scatter_dimension=0, tiled=True
    )
    sigma_root = root_sum.astype(jnp.bfloat16)
    sigma_rows = lax.all_gather(sigma_root, "col", axis=1, tiled=True)
    left_part = sigma_rows
    cross_sum = jnp.dot(
        left_part,
        lax.all_gather(panel_kept, "row", axis=0, tiled=True),
        preferred_element_type=jnp.float32,
    )
    sigma_cross = jnp.where(kept_rows, -cross_sum, jnp.zeros_like(cross_sum)).astype(jnp.bfloat16)
    sigma_child = lax.psum_scatter(
        (inner_dot(child_rows, child_inverse) - inner_dot(panel_full, sigma_cross)).astype(
            jnp.bfloat16
        ),
        "row",
        scatter_dimension=0,
        tiled=True,
    ).astype(jnp.float32)
    return (sigma_root, sigma_cross, sigma_child)


def solution(mesh):
    return jax.shard_map(
        on_device,
        mesh=mesh,
        in_specs=(
            P(("fields", "row"), "col"),
            P(("fields", "row"), "col"),
            P(("fields", "row"), "col"),
            P(("fields", "row")),
        ),
        out_specs=(
            P(("fields", "row"), "col"),
            P(("fields", "row"), "col"),
            P(("fields", "row"), "col"),
        ),
        check_vma=False,
    )
```

profile of v0, /device:TPU:0, one launch (start us, length us, event | category | flops | bytes accessed | tf_op | source)
XLA Modules:
  0.0 629.1 jit_solution(1440417712852313874)
XLA Ops:
  7.2 0.0 all-gather.6.cloned.1.call-start
  7.2 0.7 all-gather.6.cloned.1.call-update
  7.9 0.0 reduce-scatter.3.cloned.1.call-start
  7.9 62.6 %all-gather.6.cloned.1.call-done = bf16[1024,4096]{1,0:T(8,128)(2,1)} async-done(((bf16[1024,1024]{1,0:T(8,128)(2,1)}), bf16[1024,4096]{1,0:T(8,128)(2,1)}) %all-gather.6.cloned.1.call-update) | async-done | bytes 8388624 | tf_op jit(solution)/shard_map/all_gather | solution.py:19
  70.6 16.1 %fusion = f32[4096,1024]{1,0:T(8,128)} fusion(bf16[1024,4096]{1,0:T(8,128)(2,1)} %all-gather.6.cloned.1.call-done, bf16[1024,1024]{1,0:T(8,128)(2,1)} %param.4), kind=kOutput, calls=%fused_computation.5 | convolution fusion | flops 8589934592 | bytes 27262976 | tf_op jit(solution)/shard_map/dot_general | solution.py:10
  86.7 0.0 copy-start.2
  86.7 0.0 copy-start.1
  86.7 0.0 reduce-scatter.3.cloned.1.call-update
  86.7 0.0 all-gather.10.cloned.1.call-start
  86.8 0.6 copy-done.2
  87.4 0.1 broadcast_bitcast_fusion
  87.4 0.5 copy-done.1
  88.0 1.2 broadcast_select_fusion
  89.1 0.0 all-gather.10.cloned.1.call-update
  89.2 0.0 all-gather.8.cloned.1.call-start
  89.2 278.0 %reduce-scatter.3.cloned.1.call-done = f32[1024,1024]{1,0:T(8,128)} async-done(((f32[4096,1024]{1,0:T(8,128)}), f32[1024,1024]{1,0:T(8,128)}) %reduce-scatter.3.cloned.1.call-update) | async-done | bytes 4194320 | tf_op jit(solution)/shard_map/reduce_scatter | solution.py:24
  367.2 3.8 convert_element_type.12
  371.0 0.0 all-gather.8.cloned.1.call-update
  371.1 0.0 all-gather.14.cloned.1.call-start
  371.1 0.5 all-gather.14.cloned.1.call-update
  371.6 0.0 all-gather.12.cloned.1.call-start
  371.7 0.5 all-gather.12.cloned.1.call-update
  372.2 0.0 reduce-scatter.5.cloned.1.call-start
  372.3 78.7 %all-gather.10.cloned.1.call-done = bf16[4096,512]{1,0:T(8,128)(2,1)} async-done(((bf16[1024,512]{1,0:T(8,128)(2,1)}), bf16[4096,512]{1,0:T(8,128)(2,1)}) %all-gather.10.cloned.1.call-update) | async-done | bytes 4194320 | tf_op jit(solution)/shard_map/all_gather | solution.py:32
  451.0 58.9 %all-gather.8.cloned.1.call-done = bf16[1024,4096]{1,0:T(8,128)(2,1)} async-done(((bf16[1024,1024]{1,0:T(8,128)(2,1)}), bf16[1024,4096]{1,0:T(8,128)(2,1)}) %all-gather.8.cloned.1.call-update) | async-done | bytes 8388624 | tf_op jit(solution)/shard_map/all_gather | solution.py:28
  509.9 9.0 %select_convert_fusion = bf16[1024,512]{1,0:T(8,128)(2,1)S(1)} fusion(bf16[1024,4096]{1,0:T(8,128)(2,1)} %all-gather.8.cloned.1.call-done, bf16[4096,512]{1,0:T(8,128)(2,1)} %all-gather.10.cloned.1.call-done, pred[1024]{0:T(1024)(128)(4,1)S(1)} %broadcast_bitcast_fusion), kind=kOutput, calls=%fused_computation.1 | convolution fusion | flops 4296540160 | bytes 13632512 | tf_op jit(solution)/shard_map/dot_general | solution.py:30
  518.9 0.0 copy-start.3
  518.9 0.0 copy-start
  519.0 27.5 %all-gather.14.cloned.1.call-done = bf16[1024,2048]{1,0:T(8,128)(2,1)} async-done(((bf16[1024,512]{1,0:T(8,128)(2,1)}), bf16[1024,2048]{1,0:T(8,128)(2,1)}) %all-gather.14.cloned.1.call-update) | async-done | bytes 4194320 | tf_op jit(solution)/shard_map/all_gather | solution.py:21
  546.5 6.5 %fusion.1 = f32[2048,512]{1,0:T(8,128)} fusion(bf16[1024,2048]{1,0:T(8,128)(2,1)} %all-gather.14.cloned.1.call-done, bf16[1024,512]{1,0:T(8,128)(2,1)S(1)} %select_convert_fusion), kind=kOutput, calls=%fused_computation.6 | convolution fusion | flops 2147483648 | bytes 9437184 | tf_op jit(solution)/shard_map/dot_general | solution.py:10
  553.0 0.0 copy-done.3
  553.0 17.6 %all-gather.12.cloned.1.call-done = bf16[512,2048]{1,0:T(8,128)(2,1)} async-done(((bf16[512,512]{1,0:T(8,128)(2,1)}), bf16[512,2048]{1,0:T(8,128)(2,1)}) %all-gather.12.cloned.1.call-update) | async-done | bytes 2097168 | tf_op jit(solution)/shard_map/all_gather | solution.py:20
  570.6 0.0 copy-done
  570.6 5.5 subtract_convert_fusion
  576.0 0.0 reduce-scatter.5.cloned.1.call-update
  576.1 44.0 %reduce-scatter.5.cloned.1.call-done = bf16[512,512]{1,0:T(8,128)(2,1)} async-done(((bf16[2048,512]{1,0:T(8,128)(2,1)}), bf16[512,512]{1,0:T(8,128)(2,1)}) %reduce-scatter.5.cloned.1.call-update) | async-done | bytes 524304 | tf_op jit(solution)/shard_map/reduce_scatter | solution.py:36
  620.1 2.1 convert_element_type.15
  (1 shorter events, 0.0 us)
Async XLA Ops:
  7.2 63.4 %all-gather.6.cloned.1.call-start = ((), (), s32[]{:S(2)}) async-start(), calls=%async_computation.2 | async-start | bytes 10485760 | tf_op jit(solution)/shard_map/all_gather | solution.py:19
  7.9 359.3 %reduce-scatter.3.cloned.1.call-start = ((), (), s32[]{:S(2)}) async-start(), calls=%async_computation.3 | async-start | bytes 20971520 | tf_op jit(solution)/shard_map/reduce_scatter | solution.py:24
  86.7 0.7 copy-start.2
  86.7 1.2 copy-start.1
  86.7 364.2 %all-gather.10.cloned.1.call-start = ((), (), s32[]{:S(2)}) async-start(), calls=%async_computation.5 | async-start | bytes 5242880 | tf_op jit(solution)/shard_map/all_gather | solution.py:32
  89.2 420.7 %all-gather.8.cloned.1.call-start = ((), (), s32[]{:S(2)}) async-start(), calls=%async_computation.4 | async-start | bytes 10485760 | tf_op jit(solution)/shard_map/all_gather | solution.py:28
  371.1 175.4 %all-gather.14.cloned.1.call-start = ((), (), s32[]{:S(2)}) async-start(), calls=%async_computation.7 | async-start | bytes 5242880 | tf_op jit(solution)/shard_map/all_gather | solution.py:21
  371.6 198.9 %all-gather.12.cloned.1.call-start = ((), (), s32[]{:S(2)}) async-start(), calls=%async_computation.6 | async-start | bytes 2621440 | tf_op jit(solution)/shard_map/all_gather | solution.py:20
  372.2 247.9 %reduce-scatter.5.cloned.1.call-start = ((), (), s32[]{:S(2)}) async-start(), calls=%async_computation.8 | async-start | bytes 2621440 | tf_op jit(solution)/shard_map/reduce_scatter | solution.py:36
  518.9 34.1 %copy-start.3 = (bf16[1024,512]{1,0:T(8,128)(2,1)}, bf16[1024,512]{1,0:T(8,128)(2,1)S(1)}, u32[]{:S(2)}) copy-start(bf16[1024,512]{1,0:T(8,128)(2,1)S(1)} %select_convert_fusion) | copy-start | bytes 3145732
  518.9 51.6 %copy-start = (bf16[512,512]{1,0:T(8,128)(2,1)S(1)}, bf16[512,512]{1,0:T(8,128)(2,1)}, u32[]{:S(2)}) copy-start(bf16[512,512]{1,0:T(8,128)(2,1)} %param.5) | copy-start | bytes 1572868
Sparse Core Ops, SparseCore 0:
  9.6 60.9 all-gather.5
  86.9 280.2 reduce-scatter.2
  369.4 81.4 all-gather.9
  453.0 56.8 all-gather.7
  511.9 34.4 all-gather.13
  547.9 22.5 all-gather.11
  576.2 43.8 reduce-scatter.4
where the time goes:
time: 629 us
  waiting for transfers between devices  569 us (90%)
  matrix products  37.2 us (6%)
  between operations  14.2 us (2%)
  other arithmetic  7.16 us (1%)
    reduce_scatter x1, waiting for transfers between devices, on_device(): lax.psum_scatter(inner_dot(left_part, root_inverse), 'row', scatter_dimen...  278 us
    all_gather x1, waiting for transfers between devices, on_device(): lax.all_gather(panel_kept, 'row', axis=0, tiled=True)  78.7 us
    all_gather x1, waiting for transfers between devices, on_device(): lax.all_gather(root_inverse, 'col', axis=1, tiled=True)  62.6 us
    all_gather x1, waiting for transfers between devices, on_device(): sigma_rows = lax.all_gather(sigma_root, 'col', axis=1, tiled=True)  58.9 us
    reduce_scatter x1, waiting for transfers between devices, on_device(): lax.psum_scatter((inner_dot(child_rows, child_inverse) - inner_dot(panel_...  44 us
    dot_general x3, matrix products, inner_dot(): lax.dot_general(left_part, right_part, (((0,), (0,)), ((), ())), preferre...  28.1 us
    all_gather x1, waiting for transfers between devices, on_device(): lax.all_gather(panel_kept, 'col', axis=1, tiled=True)  27.5 us
    all_gather x1, waiting for transfers between devices, on_device(): lax.all_gather(child_inverse, 'col', axis=1, tiled=True)  17.6 us
  transfers between devices with their start and end apart: 7, of which 7 were waited for; matrix products, arithmetic and copies ran while one was open for 3% of the time, Pallas kernels for 0%

commit v1 on v0

v1 whole, which is shorter than its diff:
```python
import jax
import jax.numpy as jnp
from jax import lax
from jax.sharding import PartitionSpec as P

BLOCK = 128
AXES = ("fields", "row", "col")
BF16 = jnp.bfloat16
F32 = jnp.float32


def inner_dot(left_part, right_part):
    return lax.dot_general(
        left_part, right_part, (((0,), (0,)), ((), ())), preferred_element_type=F32
    )


def mask_panel(panel, structure):
    kept_rows = jnp.repeat(structure, BLOCK)[:, None] > 0
    return kept_rows, jnp.where(kept_rows, panel, jnp.zeros_like(panel))


def gather_plan(root_inverse, child_inverse, panel, structure):
    kept_rows, panel_kept = mask_panel(panel, structure)
    root_full, child_rows, panel_full = (
        lax.all_gather(root_inverse, "col", axis=1, tiled=True),
        lax.all_gather(child_inverse, "col", axis=1, tiled=True),
        lax.all_gather(panel_kept, "col", axis=1, tiled=True),
    )
    root_sum = lax.psum_scatter(
        inner_dot(root_full, root_inverse), "row", scatter_dimension=0, tiled=True
    )
    sigma_root = root_sum.astype(BF16)
    sigma_rows = lax.all_gather(sigma_root, "col", axis=1, tiled=True)
    cross_sum = jnp.dot(
        sigma_rows,
        lax.all_gather(panel_kept, "row", axis=0, tiled=True),
        preferred_element_type=F32,
    )
    sigma_cross = jnp.where(kept_rows, -cross_sum, jnp.zeros_like(cross_sum)).astype(BF16)
    sigma_child = lax.psum_scatter(
        (inner_dot(child_rows, child_inverse) - inner_dot(panel_full, sigma_cross)).astype(BF16),
        "row",
        scatter_dimension=0,
        tiled=True,
    ).astype(F32)
    return (sigma_root, sigma_cross, sigma_child)


def square_plan(fields):
    n = 4

    def move(x, target):
        pairs = []
        for f in range(fields):
            for r in range(n):
                for c in range(n):
                    to = target(r, c)
                    if to is not None and 0 <= to[0] < n:
                        pairs.append(((f * n + r) * n + c, (f * n + to[0]) * n + to[1]))
        return lax.ppermute(x, AXES, pairs)

    def in_row(x, c, nonzero):
        own = x
        across = move(x, lambda r, c: (r, c ^ 2) if nonzero(r, c) else None)
        beside = move(x, lambda r, c: (r, c ^ 1) if nonzero(r, c) else None)
        both = move(across, lambda r, c: (r, c ^ 1) if nonzero(r, c ^ 2) else None)
        h, w = x.shape
        full = jnp.zeros((h, n * w), x.dtype)
        for m, part in enumerate((own, beside, across, both)):
            full = lax.dynamic_update_slice(full, part, (0, (c ^ m) * w))
        return full

    def on_device(root_inverse, child_inverse, panel, structure):
        r, c = lax.axis_index("row"), lax.axis_index("col")
        kept_rows, panel_kept = mask_panel(panel, structure)
        h, w = panel.shape
        lower = lambda r, c: c <= r

        panel_all = jnp.zeros((n * h, w), BF16)
        panels = [panel_kept] + [
            move(panel_kept, lambda r, c, s=s: (r + s, c)) for s in (1, 2, 3)
        ]
        for s in range(n):
            panel_all = lax.dynamic_update_slice(panel_all, panels[s], (((r - s) % n) * h, 0))
        root_row = in_row(root_inverse, c, lower)
        below = [root_inverse] + [
            move(
                root_inverse,
                lambda r, c, s=s: (r - s, c) if c <= r and not (r == s and c == 1) else None,
            )
            for s in (1, 2, 3)
        ]

        t = jnp.dot(root_row, panel_all, preferred_element_type=F32).astype(BF16)
        child_row = in_row(child_inverse, c, lower)
        t_row = in_row(t, c, lambda r, c: True)
        cross = inner_dot(root_row, t).astype(BF16)

        block = lambda x, i, size: lax.dynamic_slice_in_dim(x, i * size, size, 0)
        near = move(block(cross, r ^ 1, h), lambda r, c: (r ^ 1, c) if r % 2 else None)
        far = move(block(cross, r ^ 3, h), lambda r, c: (r ^ 1, c) if r >= 2 else None)
        onward = block(cross, r ^ 2, h) + far
        last = move(onward, lambda r, c: (r - 2, c))
        cross_sum = block(cross, r, h).astype(F32) + near.astype(F32) + last.astype(F32)
        sigma_cross = jnp.where(kept_rows, -cross_sum, jnp.zeros_like(cross_sum)).astype(BF16)

        child = (inner_dot(t_row, t) + inner_dot(child_row, child_inverse)).astype(BF16)
        near = move(block(child, r ^ 1, w), lambda r, c: (r ^ 1, c))
        far = move(block(child, r ^ 3, w), lambda r, c: (r ^ 1, c))
        last = move(block(child, r ^ 2, w) + far, lambda r, c: (r ^ 2, c))
        sigma_child = block(child, r, w).astype(F32) + near.astype(F32) + last.astype(F32)

        root_sum = inner_dot(lax.dynamic_slice_in_dim(root_row, r * h, h, 1), root_inverse)
        for s in (1, 2, 3):
            across = move(
                below[s], lambda r, c, s=s: (r, c ^ 2) if r == c and 2 <= r + s < n else None
            )
            have = jnp.where(c == r, below[s], across)
            beside = move(
                have, lambda r, c, s=s: (r, c ^ 1) if r in (c, c ^ 2) and r + s < n else None
            )
            left = jnp.where((c == r) | (c == (r ^ 2)), have, beside)
            root_sum = root_sum + inner_dot(left, below[s])
        sigma_root = root_sum.astype(BF16)
        mirror = move(sigma_root, lambda r, c: (0, 1) if (r, c) == (1, 0) else None)
        sigma_root = jnp.where((r == 0) & (c == 1), mirror.T, sigma_root)
        return (sigma_root, sigma_cross, sigma_child)

    return on_device


def solution(mesh):
    square = mesh.shape["row"] == 4 and mesh.shape["col"] == 4
    spec = P(("fields", "row"), "col")
    return jax.shard_map(
        square_plan(mesh.shape["fields"]) if square else gather_plan,
        mesh=mesh,
        in_specs=(spec, spec, spec, P(("fields", "row"))),
        out_specs=(spec, spec, spec),
        check_vma=False,
    )
```

time: 629 us -> 400 us (0.64)
  waiting for transfers between devices: 569 us -> 232 us
  starting transfers between devices: 0.28 us -> 76.1 us
  local copies, waits for them, and re-layouts: 1.17 us -> 30.6 us
  between operations: 14.2 us -> 1.08 us
  other arithmetic: 7.16 us -> 17.2 us
    reduce_scatter x2 -> x0, waiting for transfers between devices: 322 us -> none  [the longest x1 278 us: on_device(): lax.psum_scatter(inner_dot(left_part, root_inverse), 'row', scatter_dimen...]
    all_gather x5 -> x0, waiting for transfers between devices: 245 us -> none  [the longest x1 78.7 us: on_device(): lax.all_gather(panel_kept, 'row', axis=0, tiled=True)]
    ppermute x0 -> x28, waiting for transfers between devices: none -> 232 us  [move(): return lax.ppermute(x, AXES, pairs)]
    ppermute x0 -> x28, starting transfers between devices: none -> 76.1 us  [move(): return lax.ppermute(x, AXES, pairs)]
    dynamic_update_slice x0 -> x14, local copies, waits for them, and re-layouts: none -> 20.4 us  [the longest x11 13.6 us: in_row(): full = lax.dynamic_update_slice(full, part, (0, (c ^ m) * w))]
    dot_general x3 -> x7, matrix products: 28.1 us -> 34.4 us  [inner_dot(): lax.dot_general(left_part, right_part, (((0,), (0,)), ((), ())), preferre...]
  transfers between devices with their start and end apart: 7 -> 28, of which waited for: 7 -> 10; matrix products, arithmetic and copies ran while one was open for 3% -> 21% of each run, Pallas kernels for 0% -> 0%
where the time goes in v1:
time: 400 us; the launch traced here: 399 us
  waiting for transfers between devices  232 us (58%)
  starting transfers between devices  76.1 us (19%)
  matrix products  42 us (10%)
  local copies, waits for them, and re-layouts  30.6 us (8%)
  other arithmetic  17.2 us (4%)
    ppermute x28, waiting for transfers between devices, move(): return lax.ppermute(x, AXES, pairs)  232 us
    ppermute x28, starting transfers between devices, move(): return lax.ppermute(x, AXES, pairs)  76.1 us
    dot_general x7, matrix products, inner_dot(): lax.dot_general(left_part, right_part, (((0,), (0,)), ((), ())), preferre...  34.4 us
    dynamic_update_slice x11, local copies, waits for them, and re-layouts, in_row(): full = lax.dynamic_update_slice(full, part, (0, (c ^ m) * w))  13.6 us
  transfers between devices with their start and end apart: 28, of which 10 were waited for; matrix products, arithmetic and copies ran while one was open for 21% of the time, Pallas kernels for 0%

profile of v1, /device:TPU:0, one launch (start us, length us, event | category | flops | bytes accessed | tf_op | source)
XLA Modules:
  0.0 398.5 jit_solution(14618318793397289903)
XLA Ops:
  0.6 6.2 %collective-permute-start.1 = (bf16[1024,1024]{1,0:T(8,128)(2,1)}, bf16[1024,1024]{1,0:T(8,128)(2,1)}, u32[]{:S(2)}, u32[]{:S(2)}) collective-permute-start(bf16[1024,1024]{1,0:T(8,128)(2,1)} %param.4), channel_id=1, source_target_pairs={{0,2},{4,6},{5,7},{8,10},{9,11},{10,8},{12,14},{13,15},{14,12},{15... | collective-permute-start | bytes 6291464 | tf_op jit(solution)/shard_map/ppermute | solution.py:61
  6.8 1.3 collective-permute-start.22
  8.9 2.2 broadcast_in_dim.38
  11.1 1.3 constant_dynamic-update-slice_fusion.10
  12.4 5.0 %collective-permute-start.13 = (bf16[1024,512]{1,0:T(8,128)(2,1)S(1)}, bf16[1024,512]{1,0:T(8,128)(2,1)}, u32[]{:S(2)}, u32[]{:S(2)}) collective-permute-start(bf16[1024,512]{1,0:T(8,128)(2,1)S(1)} %get-tuple-element.4), channel_id=1, source_target_pairs={{0,4},{1,5},{2,6},{3,7},{4,8},{5,9},{6,10},{7,11},{8,12},{9,13},{1... | collective-permute-start | bytes 3145736 | tf_op jit(solution)/shard_map/ppermute | solution.py:61
  17.4 3.3 collective-permute-start.14
  20.7 2.3 collective-permute-start.15
  23.0 3.2 collective-permute-start.23
  26.2 8.6 %collective-permute-done.23 = bf16[512,512]{1,0:T(8,128)(2,1)} collective-permute-done((bf16[512,512]{1,0:T(8,128)(2,1)S(1)}, bf16[512,512]{1,0:T(8,128)(2,1)}, u32[]{:S(2)}, u32[]{:S(2)}) %collective-permute-start.23) | collective-permute-done | bytes 524320 | tf_op jit(solution)/shard_map/ppermute | solution.py:61
  34.8 2.7 collective-permute-start
  37.5 2.4 collective-permute-done.13
  39.9 1.3 collective-permute-start.3
  41.2 21.2 %collective-permute-done.14 = bf16[1024,512]{1,0:T(8,128)(2,1)} collective-permute-done((bf16[1024,512]{1,0:T(8,128)(2,1)S(1)}, bf16[1024,512]{1,0:T(8,128)(2,1)}, u32[]{:S(2)}, u32[]{:S(2)}) %collective-permute-start.14) | collective-permute-done | bytes 1048608 | tf_op jit(solution)/shard_map/ppermute | solution.py:61
  62.4 1.3 collective-permute-start.6
  63.7 20.8 %collective-permute-done.15 = bf16[1024,512]{1,0:T(8,128)(2,1)} collective-permute-done((bf16[1024,512]{1,0:T(8,128)(2,1)S(1)}, bf16[1024,512]{1,0:T(8,128)(2,1)}, u32[]{:S(2)}, u32[]{:S(2)}) %collective-permute-start.15) | collective-permute-done | bytes 1048608 | tf_op jit(solution)/shard_map/ppermute | solution.py:61
  84.5 1.3 collective-permute-start.9
  85.8 2.1 collective-permute-start.2
  88.2 1.0 broadcast_in_dim.35
  89.2 1.9 constant_dynamic-update-slice_fusion.14
  91.2 2.3 constant_dynamic-update-slice_fusion.9
  93.5 2.3 constant_dynamic-update-slice_fusion.8
  95.7 2.2 constant_dynamic-update-slice_fusion.7
  98.0 1.5 collective-permute-start.24
  100.2 104.6 %collective-permute-done.6 = bf16[1024,1024]{1,0:T(8,128)(2,1)} collective-permute-done((bf16[1024,1024]{1,0:T(8,128)(2,1)}, bf16[1024,1024]{1,0:T(8,128)(2,1)}, u32[]{:S(2)}, u32[]{:S(2)}) %collective-permute-start.6) | collective-permute-done | bytes 2097184 | tf_op jit(solution)/shard_map/ppermute | solution.py:61
  204.9 23.0 %collective-permute-start.7 = (bf16[1024,1024]{1,0:T(8,128)(2,1)}, bf16[1024,1024]{1,0:T(8,128)(2,1)S(1)}, u32[]{:S(2)}, u32[]{:S(2)}) collective-permute-start(bf16[1024,1024]{1,0:T(8,128)(2,1)} %collective-permute-done.6), channel_id=1, source_target_pairs={{0,2},{5,7},{16,18},{21,23}} | collective-permute-start | bytes 6291464 | tf_op jit(solution)/shard_map/ppermute | solution.py:61
  227.9 1.4 collective-permute-start.10
  229.3 1.9 constant_dynamic-update-slice_fusion.13
  231.2 1.9 constant_dynamic-update-slice_fusion.12
  233.1 1.9 constant_dynamic-update-slice_fusion.11
  235.4 7.7 %convert_dynamic-update-slice_fusion = (bf16[1024,2048]{1,0:T(8,128)(2,1)S(1)}, bf16[1024,512]{1,0:T(8,128)(2,1)}) fusion(bf16[1024,2048]{1,0:T(8,128)(2,1)S(1)} %broadcast_in_dim.41, s32[]{:T(128)S(6)} %select_n.156, bf16[1024,4096]{1,0:T(8,128)(2,1)S(1)} %constant_dynamic-update-slice_fusion.11, bf16[4096,512]{1,0:T(8,128)(2,1)} %constant_dynamic-update-slice_fusion.7), kind=kOutput, calls=%fused_computation.4 | convolution fusion | flops 4294967296 | bytes 14680068 | tf_op jit(solution)/shard_map/dot_general | solution.py:95
  243.4 3.7 collective-permute-start.5
  247.1 6.2 %convolution_convert_fusion = bf16[4096,512]{1,0:T(8,128)(2,1)S(1)} fusion(bf16[1024,4096]{1,0:T(8,128)(2,1)S(1)} %constant_dynamic-update-slice_fusion.11, bf16[1024,512]{1,0:T(8,128)(2,1)} %get-tuple-element.10), kind=kOutput, calls=%fused_computation | convolution fusion | flops 4297064448 | bytes 13631488 | tf_op jit(solution)/shard_map/dot_general | solution.py:13
  253.3 1.2 constant_dynamic-slice_fusion.3
  255.3 1.8 broadcast_select_fusion.1
  257.1 1.6 collective-permute-start.8
  258.7 1.1 constant_dynamic-update-slice_fusion.1
  259.8 1.1 constant_dynamic-update-slice_fusion
  260.9 24.4 %collective-permute-done.10 = bf16[1024,1024]{1,0:T(8,128)(2,1)S(1)} collective-permute-done((bf16[1024,1024]{1,0:T(8,128)(2,1)}, bf16[1024,1024]{1,0:T(8,128)(2,1)S(1)}, u32[]{:S(2)}, u32[]{:S(2)}) %collective-permute-start.10) | collective-permute-done | bytes 2097184 | tf_op jit(solution)/shard_map/ppermute | solution.py:61
  285.3 2.4 collective-permute-start.20
  287.7 1.8 broadcast_select_fusion
  289.5 1.4 collective-permute-start.11
  290.9 3.3 fusion.16
  294.4 1.3 collective-permute-start.16
  295.7 1.3 dynamic-slice_add_fusion
  297.1 3.7 collective-permute-done.20
  300.8 1.3 collective-permute-start.18
  302.1 1.4 constant_dynamic-update-slice_fusion.5
  303.6 2.5 fusion.6
  306.1 4.1 %fusion.4 = f32[1024,1024]{1,0:T(8,128)S(1)} fusion(bf16[1024,1024]{1,0:T(8,128)(2,1)} %collective-permute-done.6, bf16[1024,1024]{1,0:T(8,128)(2,1)S(1)} %broadcast_select_fusion.1, bf16[1024,1024]{1,0:T(8,128)(2,1)S(1)} %collective-permute-done.8, pred[]{:T(512)S(6)} %or.2), kind=kOutput, calls=%fused_computation.10 | convolution fusion | flops 2148532224 | bytes 10485761 | tf_op jit(solution)/shard_map/dot_general | solution.py:13
  310.2 6.0 %fusion.2 = f32[1024,1024]{1,0:T(8,128)} fusion(bf16[1024,1024]{1,0:T(8,128)(2,1)} %collective-permute-done.9, bf16[1024,1024]{1,0:T(8,128)(2,1)S(1)} %broadcast_select_fusion, bf16[1024,1024]{1,0:T(8,128)(2,1)S(1)} %collective-permute-done.11, pred[]{:T(512)S(6)} %or.2), kind=kOutput, calls=%fused_computation.8 | convolution fusion | flops 2148532224 | bytes 10485761 | tf_op jit(solution)/shard_map/dot_general | solution.py:13
  316.3 6.0 %add_convert_fusion.1 = bf16[1024,1024]{1,0:T(8,128)(2,1)S(1)} fusion(f32[1024,1024]{1,0:T(8,128)} %fusion.2, f32[1024,1024]{1,0:T(8,128)S(1)} %fusion.4, f32[1024,1024]{1,0:T(8,128)S(1)} %fusion.6, bf16[1024,1024]{1,0:T(8,128)(2,1)} %param.4, bf16[1024,4096]{1,0:T(8,128)(2,1)S(1)} %constant_dynamic-update-slice_fusion.11, s32[]{:T(128)S(6)} %select_n.133), kind=kOutput, calls=%fused_computation.2 | convolution fusion | flops 2151677952 | bytes 18874372 | tf_op jit(solution)/shard_map/dot_general | solution.py:13
  322.3 2.6 copy.7
  324.8 2.0 collective-permute-start.12
  326.8 2.3 constant_dynamic-update-slice_fusion.4
  329.2 6.2 %add_convert_fusion = bf16[2048,512]{1,0:T(8,128)(2,1)S(1)} fusion(f32[2048,512]{1,0:T(8,128)} %fusion.16, bf16[1024,2048]{1,0:T(8,128)(2,1)} %constant_dynamic-update-slice_fusion.4, bf16[1024,512]{1,0:T(8,128)(2,1)} %get-tuple-element.10), kind=kOutput, calls=%fused_computation.1 | convolution fusion | flops 2149580800 | bytes 11534336 | tf_op jit(solution)/shard_map/dot_general | solution.py:13
  335.3 1.4 copy-done.3
  337.6 5.0 %collective-permute-start.26 = (bf16[512,512]{1,0:T(8,128)(2,1)S(1)}, bf16[512,512]{1,0:T(8,128)(2,1)S(1)}, u32[]{:S(2)}, u32[]{:S(2)}) collective-permute-start(bf16[512,512]{1,0:T(8,128)(2,1)S(1)} %get-tuple-element.8), channel_id=1, source_target_pairs={{0,4},{1,5},{2,6},{3,7},{4,0},{5,1},{6,2},{7,3},{8,12},{9,13},{10,... | collective-permute-start | bytes 1572872 | tf_op jit(solution)/shard_map/ppermute | solution.py:61
  342.6 34.6 %collective-permute-done.26 = bf16[512,512]{1,0:T(8,128)(2,1)S(1)} collective-permute-done((bf16[512,512]{1,0:T(8,128)(2,1)S(1)}, bf16[512,512]{1,0:T(8,128)(2,1)S(1)}, u32[]{:S(2)}, u32[]{:S(2)}) %collective-permute-start.26) | collective-permute-done | bytes 524320 | tf_op jit(solution)/shard_map/ppermute | solution.py:61
  377.1 1.2 dynamic-slice_add_fusion.1
  378.4 3.4 select_convert_fusion
  381.8 1.1 collective-permute-done.25
  382.8 10.2 %collective-permute-done.27 = bf16[512,512]{1,0:T(8,128)(2,1)S(1)} collective-permute-done((bf16[512,512]{1,0:T(8,128)(2,1)S(1)}, bf16[512,512]{1,0:T(8,128)(2,1)S(1)}, u32[]{:S(2)}, u32[]{:S(2)}) %collective-permute-start.27) | collective-permute-done | bytes 524320 | tf_op jit(solution)/shard_map/ppermute | solution.py:61
  393.0 2.4 convert_add_fusion
  395.4 3.1 bitcast_select_fusion
  (42 shorter events, 4.6 us)
Async XLA Ops:
  0.6 85.2 %collective-permute-start.1 = (bf16[1024,1024]{1,0:T(8,128)(2,1)}, bf16[1024,1024]{1,0:T(8,128)(2,1)}, u32[]{:S(2)}, u32[]{:S(2)}) collective-permute-start(bf16[1024,1024]{1,0:T(8,128)(2,1)} %param.4), channel_id=1, source_target_pairs={{0,2},{4,6},{5,7},{8,10},{9,11},{10,8},{12,14},{13,15},{14,12},{15... | collective-permute-start | bytes 6291464 | tf_op jit(solution)/shard_map/ppermute | solution.py:61
  6.8 16.2 %collective-permute-start.22 = (bf16[512,512]{1,0:T(8,128)(2,1)}, bf16[512,512]{1,0:T(8,128)(2,1)S(1)}, u32[]{:S(2)}, u32[]{:S(2)}) collective-permute-start(bf16[512,512]{1,0:T(8,128)(2,1)} %param.5), channel_id=1, source_target_pairs={{0,1},{4,5},{5,4},{8,9},{9,8},{10,11},{12,13},{13,12},{14,15},{15,... | collective-permute-start | bytes 1572872 | tf_op jit(solution)/shard_map/ppermute | solution.py:61
  8.9 2.2 copy-start.4
  11.1 11.9 %copy-start.2 = (bf16[512,512]{1,0:T(8,128)(2,1)S(1)}, bf16[512,512]{1,0:T(8,128)(2,1)}, u32[]{:S(2)}) copy-start(bf16[512,512]{1,0:T(8,128)(2,1)} %param.5) | copy-start | bytes 1572868
  12.4 27.5 %collective-permute-start.13 = (bf16[1024,512]{1,0:T(8,128)(2,1)S(1)}, bf16[1024,512]{1,0:T(8,128)(2,1)}, u32[]{:S(2)}, u32[]{:S(2)}) collective-permute-start(bf16[1024,512]{1,0:T(8,128)(2,1)S(1)} %get-tuple-element.4), channel_id=1, source_target_pairs={{0,4},{1,5},{2,6},{3,7},{4,8},{5,9},{6,10},{7,11},{8,12},{9,13},{1... | collective-permute-start | bytes 3145736 | tf_op jit(solution)/shard_map/ppermute | solution.py:61
  17.4 45.0 %collective-permute-start.14 = (bf16[1024,512]{1,0:T(8,128)(2,1)S(1)}, bf16[1024,512]{1,0:T(8,128)(2,1)}, u32[]{:S(2)}, u32[]{:S(2)}) collective-permute-start(bf16[1024,512]{1,0:T(8,128)(2,1)S(1)} %get-tuple-element.4), channel_id=1, source_target_pairs={{0,8},{1,9},{2,10},{3,11},{4,12},{5,13},{6,14},{7,15},{16,24},{17,... | collective-permute-start | bytes 3145736 | tf_op jit(solution)/shard_map/ppermute | solution.py:61
  20.7 63.8 %collective-permute-start.15 = (bf16[1024,512]{1,0:T(8,128)(2,1)S(1)}, bf16[1024,512]{1,0:T(8,128)(2,1)}, u32[]{:S(2)}, u32[]{:S(2)}) collective-permute-start(bf16[1024,512]{1,0:T(8,128)(2,1)S(1)} %get-tuple-element.4), channel_id=1, source_target_pairs={{0,12},{1,13},{2,14},{3,15},{16,28},{17,29},{18,30},{19,31}} | collective-permute-start | bytes 3145736 | tf_op jit(solution)/shard_map/ppermute | solution.py:61
  23.0 11.9 %collective-permute-start.23 = (bf16[512,512]{1,0:T(8,128)(2,1)S(1)}, bf16[512,512]{1,0:T(8,128)(2,1)}, u32[]{:S(2)}, u32[]{:S(2)}) collective-permute-start(bf16[512,512]{1,0:T(8,128)(2,1)S(1)} %copy-done.2), channel_id=1, source_target_pairs={{0,2},{4,6},{5,7},{8,10},{9,11},{10,8},{12,14},{13,15},{14,12},{15... | collective-permute-start | bytes 1572872 | tf_op jit(solution)/shard_map/ppermute | solution.py:61
  34.8 63.1 %collective-permute-start = (bf16[1024,1024]{1,0:T(8,128)(2,1)}, bf16[1024,1024]{1,0:T(8,128)(2,1)}, u32[]{:S(2)}, u32[]{:S(2)}) collective-permute-start(bf16[1024,1024]{1,0:T(8,128)(2,1)} %param.4), channel_id=1, source_target_pairs={{0,1},{4,5},{5,4},{8,9},{9,8},{10,11},{12,13},{13,12},{14,15},{15,... | collective-permute-start | bytes 6291464 | tf_op jit(solution)/shard_map/ppermute | solution.py:61
  39.9 59.5 %collective-permute-start.3 = (bf16[1024,1024]{1,0:T(8,128)(2,1)}, bf16[1024,1024]{1,0:T(8,128)(2,1)S(1)}, u32[]{:S(2)}, u32[]{:S(2)}) collective-permute-start(bf16[1024,1024]{1,0:T(8,128)(2,1)} %param.4), channel_id=1, source_target_pairs={{4,0},{8,4},{9,5},{10,6},{12,8},{13,9},{14,10},{15,11},{20,16},{24... | collective-permute-start | bytes 6291464 | tf_op jit(solution)/shard_map/ppermute | solution.py:61
  62.4 142.4 %collective-permute-start.6 = (bf16[1024,1024]{1,0:T(8,128)(2,1)}, bf16[1024,1024]{1,0:T(8,128)(2,1)}, u32[]{:S(2)}, u32[]{:S(2)}) collective-permute-start(bf16[1024,1024]{1,0:T(8,128)(2,1)} %param.4), channel_id=1, source_target_pairs={{8,0},{10,2},{12,4},{13,5},{14,6},{15,7},{24,16},{26,18},{28,20},{... | collective-permute-start | bytes 6291464 | tf_op jit(solution)/shard_map/ppermute | solution.py:61
  84.5 143.4 %collective-permute-start.9 = (bf16[1024,1024]{1,0:T(8,128)(2,1)}, bf16[1024,1024]{1,0:T(8,128)(2,1)}, u32[]{:S(2)}, u32[]{:S(2)}) collective-permute-start(bf16[1024,1024]{1,0:T(8,128)(2,1)} %param.4), channel_id=1, source_target_pairs={{12,0},{14,2},{15,3},{28,16},{30,18},{31,19}} | collective-permute-start | bytes 6291464 | tf_op jit(solution)/shard_map/ppermute | solution.py:61
  85.8 147.3 %collective-permute-start.2 = (bf16[1024,1024]{1,0:T(8,128)(2,1)}, bf16[1024,1024]{1,0:T(8,128)(2,1)}, u32[]{:S(2)}, u32[]{:S(2)}) collective-permute-start(bf16[1024,1024]{1,0:T(8,128)(2,1)} %collective-permute-done.1), channel_id=1, source_target_pairs={{2,3},{6,7},{7,6},{8,9},{10,11},{11,10},{12,13},{13,12},{14,15},{1... | collective-permute-start | bytes 6291464 | tf_op jit(solution)/shard_map/ppermute | solution.py:61
  98.0 159.1 %collective-permute-start.24 = (bf16[512,512]{1,0:T(8,128)(2,1)}, bf16[512,512]{1,0:T(8,128)(2,1)}, u32[]{:S(2)}, u32[]{:S(2)}) collective-permute-start(bf16[512,512]{1,0:T(8,128)(2,1)} %collective-permute-done.23), channel_id=1, source_target_pairs={{2,3},{6,7},{7,6},{8,9},{10,11},{11,10},{12,13},{13,12},{14,15},{1... | collective-permute-start | bytes 1572872 | tf_op jit(solution)/shard_map/ppermute | solution.py:61
  99.5 143.7 %collective-permute-start.4 = (bf16[1024,1024]{1,0:T(8,128)(2,1)S(1)}, bf16[1024,1024]{1,0:T(8,128)(2,1)S(1)}, u32[]{:S(2)}, u32[]{:S(2)}) collective-permute-start(bf16[1024,1024]{1,0:T(8,128)(2,1)S(1)} %collective-permute-done.3), channel_id=1, source_target_pairs={{5,7},{10,8},{21,23},{26,24}} | collective-permute-start | bytes 6291464 | tf_op jit(solution)/shard_map/ppermute | solution.py:61
  204.9 49.7 %collective-permute-start.7 = (bf16[1024,1024]{1,0:T(8,128)(2,1)}, bf16[1024,1024]{1,0:T(8,128)(2,1)S(1)}, u32[]{:S(2)}, u32[]{:S(2)}) collective-permute-start(bf16[1024,1024]{1,0:T(8,128)(2,1)} %collective-permute-done.6), channel_id=1, source_target_pairs={{0,2},{5,7},{16,18},{21,23}} | collective-permute-start | bytes 6291464 | tf_op jit(solution)/shard_map/ppermute | solution.py:61
  227.9 57.4 %collective-permute-start.10 = (bf16[1024,1024]{1,0:T(8,128)(2,1)}, bf16[1024,1024]{1,0:T(8,128)(2,1)S(1)}, u32[]{:S(2)}, u32[]{:S(2)}) collective-permute-start(bf16[1024,1024]{1,0:T(8,128)(2,1)} %collective-permute-done.9), channel_id=1, source_target_pairs={{0,2},{16,18}} | collective-permute-start | bytes 6291464 | tf_op jit(solution)/shard_map/ppermute | solution.py:61
  243.1 46.4 %collective-permute-start.19 = (bf16[1024,512]{1,0:T(8,128)(2,1)}, bf16[1024,512]{1,0:T(8,128)(2,1)S(1)}, u32[]{:S(2)}, u32[]{:S(2)}) collective-permute-start(bf16[1024,512]{1,0:T(8,128)(2,1)} %get-tuple-element.10), channel_id=1, source_target_pairs={{0,1},{1,0},{2,3},{3,2},{4,5},{5,4},{6,7},{7,6},{8,9},{9,8},{10,11... | collective-permute-start | bytes 3145736 | tf_op jit(solution)/shard_map/ppermute | solution.py:61
  243.4 60.1 %collective-permute-start.5 = (bf16[1024,1024]{1,0:T(8,128)(2,1)S(1)}, bf16[1024,1024]{1,0:T(8,128)(2,1)}, u32[]{:S(2)}, u32[]{:S(2)}) collective-permute-start(bf16[1024,1024]{1,0:T(8,128)(2,1)S(1)} %broadcast_select_fusion.2), channel_id=1, source_target_pairs={{0,1},{2,3},{5,4},{7,6},{8,9},{10,11},{16,17},{18,19},{21,20},{23,... | collective-permute-start | bytes 6291464 | tf_op jit(solution)/shard_map/ppermute | solution.py:61
  253.3 42.4 %copy-start = (bf16[4096,512]{1,0:T(8,128)(2,1)}, bf16[4096,512]{1,0:T(8,128)(2,1)S(1)}, u32[]{:S(2)}) copy-start(bf16[4096,512]{1,0:T(8,128)(2,1)S(1)} %convolution_convert_fusion) | copy-start | bytes 12582916
  254.6 39.9 %collective-permute-start.17 = (bf16[1024,512]{1,0:T(8,128)(2,1)S(1)}, bf16[1024,512]{1,0:T(8,128)(2,1)S(1)}, u32[]{:S(2)}, u32[]{:S(2)}) collective-permute-start(bf16[1024,512]{1,0:T(8,128)(2,1)S(1)} %get-tuple-element.6), channel_id=1, source_target_pairs={{8,12},{9,13},{10,14},{11,15},{12,8},{13,9},{14,10},{15,11},{24,28... | collective-permute-start | bytes 3145736 | tf_op jit(solution)/shard_map/ppermute | solution.py:61
  257.1 49.0 %collective-permute-start.8 = (bf16[1024,1024]{1,0:T(8,128)(2,1)S(1)}, bf16[1024,1024]{1,0:T(8,128)(2,1)S(1)}, u32[]{:S(2)}, u32[]{:S(2)}) collective-permute-start(bf16[1024,1024]{1,0:T(8,128)(2,1)S(1)} %broadcast_select_fusion.1), channel_id=1, source_target_pairs={{0,1},{2,3},{5,4},{7,6},{16,17},{18,19},{21,20},{23,22}} | collective-permute-start | bytes 6291464 | tf_op jit(solution)/shard_map/ppermute | solution.py:61
  285.3 15.5 %collective-permute-start.20 = (bf16[1024,512]{1,0:T(8,128)(2,1)}, bf16[1024,512]{1,0:T(8,128)(2,1)}, u32[]{:S(2)}, u32[]{:S(2)}) collective-permute-start(bf16[1024,512]{1,0:T(8,128)(2,1)} %get-tuple-element.10), channel_id=1, source_target_pairs={{0,2},{1,3},{2,0},{3,1},{4,6},{5,7},{6,4},{7,5},{8,10},{9,11},{10,... | collective-permute-start | bytes 3145736 | tf_op jit(solution)/shard_map/ppermute | solution.py:61
  289.5 20.7 %collective-permute-start.11 = (bf16[1024,1024]{1,0:T(8,128)(2,1)S(1)}, bf16[1024,1024]{1,0:T(8,128)(2,1)S(1)}, u32[]{:S(2)}, u32[]{:S(2)}) collective-permute-start(bf16[1024,1024]{1,0:T(8,128)(2,1)S(1)} %broadcast_select_fusion), channel_id=1, source_target_pairs={{0,1},{2,3},{16,17},{18,19}} | collective-permute-start | bytes 6291464 | tf_op jit(solution)/shard_map/ppermute | solution.py:61
  294.4 84.0 %collective-permute-start.16 = (bf16[1024,512]{1,0:T(8,128)(2,1)}, bf16[1024,512]{1,0:T(8,128)(2,1)}, u32[]{:S(2)}, u32[]{:S(2)}) collective-permute-start(bf16[1024,512]{1,0:T(8,128)(2,1)} %get-tuple-element.5), channel_id=1, source_target_pairs={{4,0},{5,1},{6,2},{7,3},{12,8},{13,9},{14,10},{15,11},{20,16},{21,... | collective-permute-start | bytes 3145736 | tf_op jit(solution)/shard_map/ppermute | solution.py:61
  300.8 77.6 %collective-permute-start.18 = (bf16[1024,512]{1,0:T(8,128)(2,1)}, bf16[1024,512]{1,0:T(8,128)(2,1)}, u32[]{:S(2)}, u32[]{:S(2)}) collective-permute-start(bf16[1024,512]{1,0:T(8,128)(2,1)} %dynamic-slice_add_fusion), channel_id=1, source_target_pairs={{8,0},{9,1},{10,2},{11,3},{12,4},{13,5},{14,6},{15,7},{24,16},{25,... | collective-permute-start | bytes 3145736 | tf_op jit(solution)/shard_map/ppermute | solution.py:61
  303.5 2.6 copy-start.1
  303.5 23.3 %collective-permute-start.21 = (bf16[1024,512]{1,0:T(8,128)(2,1)}, bf16[1024,512]{1,0:T(8,128)(2,1)}, u32[]{:S(2)}, u32[]{:S(2)}) collective-permute-start(bf16[1024,512]{1,0:T(8,128)(2,1)} %collective-permute-done.20), channel_id=1, source_target_pairs={{0,1},{1,0},{2,3},{3,2},{4,5},{5,4},{6,7},{7,6},{8,9},{9,8},{10,11... | collective-permute-start | bytes 3145736 | tf_op jit(solution)/shard_map/ppermute | solution.py:61
  324.8 70.6 %collective-permute-start.12 = (bf16[1024,1024]{0,1:T(8,128)(2,1)}, bf16[1024,1024]{0,1:T(8,128)(2,1)}, u32[]{:S(2)}, u32[]{:S(2)}) collective-permute-start(bf16[1024,1024]{0,1:T(8,128)(2,1)} %copy.7), channel_id=1, source_target_pairs={{4,1},{20,17}} | collective-permute-start | bytes 6291464 | tf_op jit(solution)/shard_map/ppermute | solution.py:61
  335.3 1.4 copy-start.3
  337.6 39.6 %collective-permute-start.26 = (bf16[512,512]{1,0:T(8,128)(2,1)S(1)}, bf16[512,512]{1,0:T(8,128)(2,1)S(1)}, u32[]{:S(2)}, u32[]{:S(2)}) collective-permute-start(bf16[512,512]{1,0:T(8,128)(2,1)S(1)} %get-tuple-element.8), channel_id=1, source_target_pairs={{0,4},{1,5},{2,6},{3,7},{4,0},{5,1},{6,2},{7,3},{8,12},{9,13},{10,... | collective-permute-start | bytes 1572872 | tf_op jit(solution)/shard_map/ppermute | solution.py:61
  342.5 40.3 %collective-permute-start.25 = (bf16[512,512]{1,0:T(8,128)(2,1)}, bf16[512,512]{1,0:T(8,128)(2,1)}, u32[]{:S(2)}, u32[]{:S(2)}) collective-permute-start(bf16[512,512]{1,0:T(8,128)(2,1)} %get-tuple-element.7), channel_id=1, source_target_pairs={{0,4},{1,5},{2,6},{3,7},{4,0},{5,1},{6,2},{7,3},{8,12},{9,13},{10,... | collective-permute-start | bytes 1572872 | tf_op jit(solution)/shard_map/ppermute | solution.py:61
  378.3 14.7 %collective-permute-start.27 = (bf16[512,512]{1,0:T(8,128)(2,1)S(1)}, bf16[512,512]{1,0:T(8,128)(2,1)S(1)}, u32[]{:S(2)}, u32[]{:S(2)}) collective-permute-start(bf16[512,512]{1,0:T(8,128)(2,1)S(1)} %dynamic-slice_add_fusion.1), channel_id=1, source_target_pairs={{0,8},{1,9},{2,10},{3,11},{4,12},{5,13},{6,14},{7,15},{8,0},{9,1},... | collective-permute-start | bytes 1572872 | tf_op jit(solution)/shard_map/ppermute | solution.py:61

commit v2 on v1

v2 whole, which is shorter than its diff:
```python
import jax
import jax.numpy as jnp
from jax import lax
from jax.experimental import pallas as pl
from jax.sharding import PartitionSpec as P

BLOCK = 128
AXES = ("fields", "row", "col")
BF16 = jnp.bfloat16
F32 = jnp.float32


def inner_dot(left_part, right_part):
    return lax.dot_general(
        left_part, right_part, (((0,), (0,)), ((), ())), preferred_element_type=F32
    )


def mask_panel(panel, structure):
    kept_rows = jnp.repeat(structure, BLOCK)[:, None] > 0
    return kept_rows, jnp.where(kept_rows, panel, jnp.zeros_like(panel))


def gather_plan(root_inverse, child_inverse, panel, structure):
    kept_rows, panel_kept = mask_panel(panel, structure)
    root_full, child_rows, panel_full = (
        lax.all_gather(root_inverse, "col", axis=1, tiled=True),
        lax.all_gather(child_inverse, "col", axis=1, tiled=True),
        lax.all_gather(panel_kept, "col", axis=1, tiled=True),
    )
    root_sum = lax.psum_scatter(
        inner_dot(root_full, root_inverse), "row", scatter_dimension=0, tiled=True
    )
    sigma_root = root_sum.astype(BF16)
    sigma_rows = lax.all_gather(sigma_root, "col", axis=1, tiled=True)
    cross_sum = jnp.dot(
        sigma_rows,
        lax.all_gather(panel_kept, "row", axis=0, tiled=True),
        preferred_element_type=F32,
    )
    sigma_cross = jnp.where(kept_rows, -cross_sum, jnp.zeros_like(cross_sum)).astype(BF16)
    sigma_child = lax.psum_scatter(
        (inner_dot(child_rows, child_inverse) - inner_dot(panel_full, sigma_cross)).astype(BF16),
        "row",
        scatter_dimension=0,
        tiled=True,
    ).astype(F32)
    return (sigma_root, sigma_cross, sigma_child)


def square_plan(fields):
    n = 4

    def move(x, target):
        pairs = []
        for f in range(fields):
            for r in range(n):
                for c in range(n):
                    to = target(r, c)
                    if to is not None and 0 <= to[0] < n:
                        pairs.append(((f * n + r) * n + c, (f * n + to[0]) * n + to[1]))
        return lax.ppermute(x, AXES, pairs)

    def together(*arrays, earlier=()):
        k = len(arrays)
        anywhere = pl.BlockSpec(memory_space=pl.ANY)
        return pl.pallas_call(
            lambda *refs: None,
            out_shape=[jax.ShapeDtypeStruct(x.shape, x.dtype) for x in arrays],
            in_specs=[anywhere] * (k + len(earlier)),
            out_specs=[anywhere] * k,
            input_output_aliases={i: i for i in range(k)},
        )(*arrays, *earlier)

    def on_device(root_inverse, child_inverse, panel, structure):
        r, c = lax.axis_index("row"), lax.axis_index("col")
        kept_rows, panel_kept = mask_panel(panel, structure)
        h, w = panel.shape
        lower = lambda r, c: c <= r
        columns = lambda x, i, size: lax.dynamic_slice_in_dim(x, i * size, size, 1)

        def r_after(*earlier):
            return together(jnp.full((8, 128), r, jnp.int32), earlier=earlier)[0][0, 0]

        def up(x, s):
            return move(x, lambda r, c: (r + 1, c) if r >= s - 1 else None)

        def down(x, s):
            def target(r, c):
                k = r + s - 1
                return (r - 1, c) if k < n and c <= k and (r, c) != (1, 1) else None

            return move(x, target)

        child_row = lax.all_gather(child_inverse, "col", axis=1, tiled=True)
        panel_1 = up(panel_kept, 1)
        root_across = move(root_inverse, lambda r, c: (r, c ^ 2) if lower(r, c) else None)
        below_1 = down(root_inverse, 1)
        root_beside = move(root_inverse, lambda r, c: (r, c ^ 1) if lower(r, c) else None)
        (panel_1,) = together(panel_1, earlier=(root_beside,))
        panel_2 = up(panel_1, 2)
        root_row = jnp.zeros((h, n * h), BF16)
        for m, block in enumerate((root_inverse, root_beside)):
            root_row = lax.dynamic_update_slice(root_row, block, (0, (c ^ m) * h))
        panel_2, below_1, root_across, root_row = together(
            panel_2, below_1, root_across, root_row
        )
        panel_3 = up(panel_2, 3)
        half = h // 2
        below_2a = down(below_1[:half], 2)
        root_both = move(root_across, lambda r, c: (r, c ^ 1) if lower(r, c ^ 2) else None)
        across_1 = move(below_1, lambda r, c: (r, c ^ 2) if r == c and r in (1, 2) else None)

        panel_3, below_2a, across_1 = together(panel_3, below_2a, across_1)
        for m, block in ((2, root_across), (3, root_both)):
            root_row = lax.dynamic_update_slice(root_row, block, (0, (c ^ m) * h))
        t = jnp.zeros((h, w), F32)
        for s, block in enumerate((panel_kept, panel_1, panel_2, panel_3)):
            t = t + jnp.dot(columns(root_row, (r - s) % n, h), block, preferred_element_type=F32)
        t = t.astype(BF16)
        t_row = lax.all_gather(t, "col", axis=1, tiled=True)
        below_2b = down(below_1[half:], 2)
        below_3a = down(below_2a, 3)

        part = lambda i: inner_dot(columns(root_row, i, h), t)
        far_part = part(r ^ 3).astype(BF16)
        far = move(far_part, lambda r, c: (r ^ 1, c) if r >= 2 else None)
        near_part = part(r_after(far_part) ^ 1).astype(BF16)
        below_2b, below_3a = together(below_2b, below_3a, earlier=(near_part, far))
        below_2 = jnp.concatenate((below_2a, below_2b), 0)
        below_3b = down(below_2b, 3)
        r_cross = r_after(near_part, below_2b)
        onward = (part(r_cross ^ 2) + far.astype(F32)).astype(BF16)
        near = move(near_part, lambda r, c: (r ^ 1, c) if r % 2 else None)
        last = move(onward, lambda r, c: (r - 2, c))
        own = part(r_after(onward))
        cross_sum = own + near.astype(F32) + last.astype(F32)
        sigma_cross = jnp.where(kept_rows, -cross_sum, jnp.zeros_like(cross_sum)).astype(BF16)

        part = lambda i: inner_dot(columns(t_row, i, w), t) + inner_dot(
            columns(child_row, i, w), child_inverse
        )
        child_far = part(r_after(onward) ^ 3).astype(BF16)
        far = move(child_far, lambda r, c: (r ^ 1, c))
        child_near = part(r_after(child_far) ^ 1).astype(BF16)
        child_near_in = move(child_near, lambda r, c: (r ^ 1, c))
        r_child = r_after(child_near, far, near, below_3b)
        child_onward = (part(r_child ^ 2) + far.astype(F32)).astype(BF16)
        last = move(child_onward, lambda r, c: (r ^ 2, c))
        sigma_child = part(r_child) + child_near_in.astype(F32) + last.astype(F32)

        root_sum = inner_dot(columns(root_row, r_cross, h), root_inverse)
        (below_3a,) = together(below_3a, earlier=(child_onward,))
        below_3 = jnp.concatenate((below_3a, below_3b), 0)
        r_root = {1: r_after(onward), 2: r_after(child_near), 3: r_after(child_onward)}
        across = {
            1: across_1,
            2: move(below_2, lambda r, c: (r, c ^ 2) if r == c and r in (0, 1) else None),
            3: move(below_3, lambda r, c: (r, c ^ 2) if r == c == 0 else None),
        }
        for s, held in ((1, below_1), (2, below_2), (3, below_3)):
            have = jnp.where(c == r_root[s], held, across[s])
            beside = move(
                have, lambda r, c, s=s: (r, c ^ 1) if r in (c, c ^ 2) and r + s < n else None
            )
            left = jnp.where((c == r) | (c == (r ^ 2)), have, beside)
            if s == 3:
                mirror = move(
                    root_sum.astype(BF16), lambda r, c: (0, 1) if (r, c) == (1, 0) else None
                )
            root_sum = root_sum + inner_dot(left, held)
        sigma_root = jnp.where((r == 0) & (c == 1), mirror.T, root_sum.astype(BF16))
        return (sigma_root, sigma_cross, sigma_child)

    return on_device


def solution(mesh):
    square = mesh.shape["row"] == 4 and mesh.shape["col"] == 4
    spec = P(("fields", "row"), "col")
    return jax.shard_map(
        square_plan(mesh.shape["fields"]) if square else gather_plan,
        mesh=mesh,
        in_specs=(spec, spec, spec, P(("fields", "row"))),
        out_specs=(spec, spec, spec),
        check_vma=False,
    )
```

time: 400 us -> 331 us (0.83)
  waiting for transfers between devices: 232 us -> 90.6 us
  matrix products: 42 us -> 81.8 us
  between operations: 1.08 us -> 21.4 us
  local copies, waits for them, and re-layouts: 30.6 us -> 48 us
  starting transfers between devices: 76.1 us -> 68.8 us
    ppermute x28 -> x24, waiting for transfers between devices: 232 us -> 89.9 us  [move(): return lax.ppermute(x, AXES, pairs)]
    dot_general x7 -> x16, matrix products: 34.4 us -> 63.1 us  [inner_dot(): lax.dot_general(left_part, right_part, (((0,), (0,)), ((), ())), preferre...]
    slice x0 -> x8, local copies, waits for them, and re-layouts: none -> 11.4 us  [the longest x7 8.68 us: r_after(): return together(jnp.full((8, 128), r, jnp.int32), earlier=earlier)[0][0, 0]]
    dot_general x1 -> x4, matrix products: 7.66 us -> 18.8 us  [on_device(): jnp.dot(columns(root_row, (r - s) % n, h), block, preferred_element_type=...]
    dynamic_update_slice x14 -> x4, local copies, waits for them, and re-layouts: 20.4 us -> 12.8 us  [on_device(): root_row = lax.dynamic_update_slice(root_row, block, (0, (c ^ m) * h))]
    ppermute x28 -> x24, starting transfers between devices: 76.1 us -> 68.7 us  [move(): return lax.ppermute(x, AXES, pairs)]
    unnamed x10 -> x47, local copies, waits for them, and re-layouts: 1.39 us -> 8.27 us
    add x0 -> x1, local copies, waits for them, and re-layouts: none -> 4.69 us  [on_device(): root_sum = root_sum + inner_dot(left, held)]
  transfers between devices with their start and end apart: 28 -> 26, of which waited for: 10 -> 6; matrix products, arithmetic and copies ran while one was open for 21% -> 39% of each run, Pallas kernels for 0% -> 0%
where the time goes in v2:
time: 331 us; the launch traced here: 329 us
  waiting for transfers between devices  90.6 us (27%)
  matrix products  81.8 us (25%)
  starting transfers between devices  68.8 us (21%)
  local copies, waits for them, and re-layouts  48 us (15%)
  between operations  21.4 us (6%)
  other arithmetic  18.6 us (6%)
    ppermute x24, waiting for transfers between devices, move(): return lax.ppermute(x, AXES, pairs)  89.9 us
    ppermute x24, starting transfers between devices, move(): return lax.ppermute(x, AXES, pairs)  68.7 us
    dot_general x16, matrix products, inner_dot(): lax.dot_general(left_part, right_part, (((0,), (0,)), ((), ())), preferre...  63.1 us
    dot_general x4, matrix products, on_device(): jnp.dot(columns(root_row, (r - s) % n, h), block, preferred_element_type=...  18.8 us
    dynamic_update_slice x4, local copies, waits for them, and re-layouts, on_device(): root_row = lax.dynamic_update_slice(root_row, block, (0, (c ^ m) * h))  12.8 us
    slice x7, local copies, waits for them, and re-layouts, r_after(): return together(jnp.full((8, 128), r, jnp.int32), earlier=earlier)[0][0, 0]  8.68 us
    unnamed x47, local copies, waits for them, and re-layouts  8.27 us
    select_n x3, other arithmetic, on_device(): have = jnp.where(c == r_root[s], held, across[s])  8.22 us
  transfers between devices with their start and end apart: 26, of which 6 were waited for; matrix products, arithmetic and copies ran while one was open for 39% of the time, Pallas kernels for 0%

profile of v2, /device:TPU:0, one launch (start us, length us, event | category | flops | bytes accessed | tf_op | source)
XLA Modules:
  0.0 329.3 jit_solution(5946690869315378230)
XLA Ops:
  7.2 3.8 %collective-permute-start.1 = (bf16[1024,1024]{1,0:T(8,128)(2,1)}, bf16[1024,1024]{1,0:T(8,128)(2,1)}, u32[]{:S(2)}, u32[]{:S(2)}) collective-permute-start(bf16[1024,1024]{1,0:T(8,128)(2,1)} %param.4), channel_id=1, source_target_pairs={{0,1},{4,5},{5,4},{8,9},{9,8},{10,11},{12,13},{13,12},{14,15},{15,... | collective-permute-start | bytes 6291464 | tf_op jit(solution)/shard_map/ppermute | solution.py:62
  11.7 1.4 broadcast_select_fusion.3
  13.2 3.1 collective-permute-start
  16.3 4.9 %collective-permute-start.4 = (bf16[1024,1024]{1,0:T(8,128)(2,1)}, bf16[1024,1024]{1,0:T(8,128)(2,1)}, u32[]{:S(2)}, u32[]{:S(2)}) collective-permute-start(bf16[1024,1024]{1,0:T(8,128)(2,1)} %param.4), channel_id=1, source_target_pairs={{0,2},{4,6},{5,7},{8,10},{9,11},{10,8},{12,14},{13,15},{14,12},{15... | collective-permute-start | bytes 6291464 | tf_op jit(solution)/shard_map/ppermute | solution.py:62
  21.2 1.3 collective-permute-start.3
  22.5 16.8 %collective-permute-done.refs_0_ = bf16[1024,512]{1,0:T(8,128)(2,1)S(1)} collective-permute-done((bf16[1024,512]{1,0:T(8,128)(2,1)S(1)}, bf16[1024,512]{1,0:T(8,128)(2,1)S(1)}, u32[]{:S(2)}, u32[]{:S(2)}) %collective-permute-start) | collective-permute-done | bytes 1048608 | tf_op jit(solution)/shard_map/ppermute | solution.py:62
  41.0 4.4 %broadcast_in_dim.40 = bf16[1024,4096]{1,0:T(8,128)(2,1)} broadcast(bf16[]{:T(256)} %constant.56.clone.1), dimensions={} | broadcast | bytes 8388610 | tf_op jit(solution)/shard_map/broadcast_in_dim | solution.py:102
  45.4 3.2 constant_dynamic-update-slice_fusion.5
  48.6 3.1 constant_dynamic-update-slice_fusion.4.refs_3_
  51.7 1.3 copy-done.1
  54.0 2.1 collective-permute-start.5
  57.7 2.7 fusion.75
  60.4 1.3 collective-permute-start.7
  61.7 3.2 constant_dynamic-update-slice_fusion.3
  64.9 3.3 constant_dynamic-update-slice_fusion.2
  68.2 4.3 %fusion.17 = f32[1024,512]{1,0:T(8,128)} fusion(bf16[1024,512]{1,0:T(8,128)(2,1)S(1)} %copy-done.22, bf16[1024,4096]{1,0:T(8,128)(2,1)} %constant_dynamic-update-slice_fusion.2, s32[]{:T(128)S(6)} %select_n.134), kind=kOutput, calls=%fused_computation.23 | convolution fusion | flops 1073741824 | bytes 5242884 | tf_op jit(solution)/shard_map/dot_general | solution.py:119
  72.4 4.3 %fusion.19 = f32[1024,512]{1,0:T(8,128)} fusion(bf16[1024,512]{1,0:T(8,128)(2,1)S(1)} %copy-done.20, bf16[1024,4096]{1,0:T(8,128)(2,1)} %constant_dynamic-update-slice_fusion.2, s32[]{:T(128)S(6)} %select_n.132), kind=kOutput, calls=%fused_computation.25 | convolution fusion | flops 1073741824 | bytes 5242884 | tf_op jit(solution)/shard_map/dot_general | solution.py:119
  76.8 4.1 %fusion.21 = f32[1024,512]{1,0:T(8,128)} fusion(bf16[1024,512]{1,0:T(8,128)(2,1)S(1)} %copy-done.18, bf16[1024,4096]{1,0:T(8,128)(2,1)} %constant_dynamic-update-slice_fusion.2, s32[]{:T(128)S(6)} %select_n.130), kind=kOutput, calls=%fused_computation.27 | convolution fusion | flops 1073741824 | bytes 5242884 | tf_op jit(solution)/shard_map/dot_general | solution.py:119
  80.9 14.4 %collective-permute-done.7.refs_1_ = bf16[512,1024]{1,0:T(8,128)(2,1)S(1)} collective-permute-done((bf16[512,1024]{1,0:T(8,128)(2,1)S(1)}, bf16[512,1024]{1,0:T(8,128)(2,1)S(1)}, u32[]{:S(2)}, u32[]{:S(2)}) %collective-permute-start.7) | collective-permute-done | bytes 1048608 | tf_op jit(solution)/shard_map/ppermute | solution.py:62
  96.3 1.3 copy-done.7
  97.6 6.0 %add_convert_fusion.2 = bf16[1024,512]{1,0:T(8,128)(2,1)} fusion(f32[1024,512]{1,0:T(8,128)} %fusion.17, f32[1024,512]{1,0:T(8,128)} %fusion.21, f32[1024,512]{1,0:T(8,128)} %fusion.19, bf16[1024,512]{1,0:T(8,128)(2,1)} %get-tuple-element.16, bf16[1024,4096]{1,0:T(8,128)(2,1)} %constant_dynamic-update-slice_fusion.2, s32[]{:T(128)S(6)} %select_n.136), kind=kOutput, calls=%fused_computation.20 | convolution fusion | flops 1075838976 | bytes 10485764 | tf_op jit(solution)/shard_map/dot_general | solution.py:119
  104.5 1.4 collective-permute-start.9
  105.9 4.1 %fusion.32.refs_1_ = bf16[1024,512]{1,0:T(8,128)(2,1)} fusion(bf16[1024,512]{1,0:T(8,128)(2,1)} %add_convert_fusion.2, bf16[1024,4096]{1,0:T(8,128)(2,1)} %constant_dynamic-update-slice_fusion.2, s32[]{:T(128)S(6)} %select_n.128), kind=kOutput, calls=%fused_computation.37 | convolution fusion | flops 1074266112 | bytes 4194308 | tf_op jit(solution)/shard_map/dot_general | solution.py:14
  110.0 1.6 collective-permute-start.11
  111.7 1.3 collective-permute-start.10
  113.6 1.3 slice.30
  117.1 3.9 %fusion.35.refs_2_.refs_1_ = bf16[1024,512]{1,0:T(8,128)(2,1)} fusion(bf16[1024,512]{1,0:T(8,128)(2,1)S(1)} %copy-done.12, bf16[1024,4096]{1,0:T(8,128)(2,1)} %constant_dynamic-update-slice_fusion.2, s32[]{:T(128)S(6)} %select_n.137), kind=kOutput, calls=%fused_computation.38 | convolution fusion | flops 1074266112 | bytes 4194308 | tf_op jit(solution)/shard_map/dot_general | solution.py:14
  121.1 10.5 %collective-permute-done.9.refs_0_ = bf16[512,1024]{1,0:T(8,128)(2,1)S(1)} collective-permute-done((bf16[512,1024]{1,0:T(8,128)(2,1)}, bf16[512,1024]{1,0:T(8,128)(2,1)S(1)}, u32[]{:S(2)}, u32[]{:S(2)}) %collective-permute-start.9) | collective-permute-done | bytes 1048608 | tf_op jit(solution)/shard_map/ppermute | solution.py:62
  131.6 11.2 %collective-permute-done.10.refs_1_ = bf16[512,1024]{1,0:T(8,128)(2,1)S(1)} collective-permute-done((bf16[512,1024]{1,0:T(8,128)(2,1)S(1)}, bf16[512,1024]{1,0:T(8,128)(2,1)S(1)}, u32[]{:S(2)}, u32[]{:S(2)}) %collective-permute-start.10) | collective-permute-done | bytes 1048608 | tf_op jit(solution)/shard_map/ppermute | solution.py:62
  143.8 2.3 constant_dynamic-update-slice_fusion
  146.0 15.0 %collective-permute-start.13 = (bf16[1024,1024]{1,0:T(8,128)(2,1)}, bf16[1024,1024]{1,0:T(8,128)(2,1)}, u32[]{:S(2)}, u32[]{:S(2)}) collective-permute-start(bf16[1024,1024]{1,0:T(8,128)(2,1)} %constant_dynamic-update-slice_fusion), channel_id=1, source_target_pairs={{0,2},{5,7},{16,18},{21,23}} | collective-permute-start | bytes 6291464 | tf_op jit(solution)/shard_map/ppermute | solution.py:62
  161.0 1.3 collective-permute-start.17
  164.8 4.6 %add_convert_fusion.1.refs_1_ = bf16[1024,512]{1,0:T(8,128)(2,1)} fusion(bf16[1024,512]{1,0:T(8,128)(2,1)} %collective-permute-done.11.refs_3_, bf16[1024,512]{1,0:T(8,128)(2,1)} %add_convert_fusion.2, bf16[1024,4096]{1,0:T(8,128)(2,1)} %constant_dynamic-update-slice_fusion.2, s32[]{:T(128)S(6)} %select_n.140), kind=kOutput, calls=%fused_computation.13 | convolution fusion | flops 1075314688 | bytes 5242884 | tf_op jit(solution)/shard_map/dot_general | solution.py:14
  172.3 1.3 collective-permute-start.18
  173.7 1.5 broadcast_select_fusion.2
  175.2 2.8 collective-permute-start.12
  178.0 3.3 fusion.48
  181.3 2.6 fusion.40.refs_1_
  186.5 5.1 %collective-permute-start.16 = (bf16[512,512]{1,0:T(8,128)(2,1)}, bf16[512,512]{1,0:T(8,128)(2,1)S(1)}, u32[]{:S(2)}, u32[]{:S(2)}) collective-permute-start(bf16[512,512]{1,0:T(8,128)(2,1)} %fusion.40.refs_1_), channel_id=1, source_target_pairs={{0,4},{1,5},{2,6},{3,7},{4,0},{5,1},{6,2},{7,3},{8,12},{9,13},{10,... | collective-permute-start | bytes 1572872 | tf_op jit(solution)/shard_map/ppermute | solution.py:62
  191.5 2.3 fusion.46
  193.8 2.3 fusion.41.refs_1_
  198.7 3.2 broadcast_select_fusion.1
  201.9 5.3 %collective-permute-start.14 = (bf16[1024,1024]{1,0:T(8,128)(2,1)}, bf16[1024,1024]{1,0:T(8,128)(2,1)}, u32[]{:S(2)}, u32[]{:S(2)}) collective-permute-start(bf16[1024,1024]{1,0:T(8,128)(2,1)} %broadcast_select_fusion.1), channel_id=1, source_target_pairs={{0,1},{2,3},{5,4},{7,6},{16,17},{18,19},{21,20},{23,22}} | collective-permute-start | bytes 6291464 | tf_op jit(solution)/shard_map/ppermute | solution.py:62
  209.9 2.3 fusion.44
  212.2 2.3 add_convert_fusion.3.refs_1_
  214.5 3.0 pad_maximum_fusion
  217.5 6.5 %collective-permute-start.19 = (bf16[1024,1024]{1,0:T(8,128)(2,1)}, bf16[1024,1024]{1,0:T(8,128)(2,1)}, u32[]{:S(2)}, u32[]{:S(2)}) collective-permute-start(bf16[1024,1024]{1,0:T(8,128)(2,1)} %pad_maximum_fusion), channel_id=1, source_target_pairs={{0,2},{16,18}} | collective-permute-start | bytes 6291464 | tf_op jit(solution)/shard_map/ppermute | solution.py:62
  224.6 1.3 collective-permute-start.21
  225.9 6.6 %fusion.11 = f32[1024,1024]{1,0:T(8,128)} fusion(bf16[1024,1024]{1,0:T(8,128)(2,1)} %param.4, bf16[1024,4096]{1,0:T(8,128)(2,1)} %constant_dynamic-update-slice_fusion.2, s32[]{:T(128)S(6)} %select_n.138), kind=kOutput, calls=%fused_computation.16 | convolution fusion | flops 2147483648 | bytes 8388612 | tf_op jit(solution)/shard_map/dot_general | solution.py:14
  232.5 6.0 %fusion.7 = f32[1024,1024]{1,0:T(8,128)} fusion(bf16[1024,1024]{1,0:T(8,128)(2,1)S(1)} %copy-done.2, bf16[1024,1024]{1,0:T(8,128)(2,1)} %broadcast_select_fusion.2, bf16[1024,1024]{1,0:T(8,128)(2,1)} %collective-permute-done.12, pred[]{:T(512)S(6)} %or.2), kind=kOutput, calls=%fused_computation.11 | convolution fusion | flops 2148532224 | bytes 10485761 | tf_op jit(solution)/shard_map/dot_general | solution.py:14
  241.0 9.2 %add_add_fusion = f32[1024,1024]{1,0:T(8,128)} fusion(f32[1024,1024]{1,0:T(8,128)} %fusion.11, f32[1024,1024]{1,0:T(8,128)} %fusion.7, bf16[1024,1024]{1,0:T(8,128)(2,1)} %constant_dynamic-update-slice_fusion, bf16[1024,1024]{1,0:T(8,128)(2,1)} %broadcast_select_fusion.1, bf16[1024,1024]{1,0:T(8,128)(2,1)} %collective-permute-done.14, pred[]{:T(512)S(6)} %or.2), kind=kOutput, calls=%fused_computation.1 | convolution fusion | flops 2150629376 | bytes 18874368 | tf_op jit(solution)/shard_map/dot_general | solution.py:14
  250.2 4.7 %copy.25 = bf16[1024,1024]{0,1:T(8,128)(2,1)} copy(f32[1024,1024]{1,0:T(8,128)} %add_add_fusion) | data formatting | bytes 6291456 | tf_op jit(solution)/shard_map/add | solution.py:171
  254.8 2.1 collective-permute-start.15
  256.9 3.5 %broadcast_select_fusion = bf16[1024,1024]{1,0:T(8,128)(2,1)} fusion(bf16[1024,1024]{1,0:T(8,128)(2,1)} %collective-permute-done.19, pred[]{:T(512)S(6)} %eq.36, bf16[512,1024]{1,0:T(8,128)(2,1)} %collective-permute-done.18.refs_4_, bf16[512,1024]{1,0:T(8,128)(2,1)S(1)} %copy-done.4), kind=kLoop, calls=%fused_computation.31 | loop fusion | flops 5242880 | bytes 6291457 | tf_op jit(solution)/shard_map/jit(_where)/select_n | solution.py:162
  260.5 2.7 collective-permute-start.20
  263.7 2.9 fusion.1
  266.6 2.2 collective-permute-done.21
  268.8 3.0 select_convert_fusion
  272.5 2.4 collective-permute-start.23
  274.9 2.3 fusion.42
  277.2 1.7 convolution_add_fusion
  278.9 34.7 %collective-permute-done.22 = bf16[512,512]{1,0:T(8,128)(2,1)S(1)} collective-permute-done((bf16[512,512]{1,0:T(8,128)(2,1)S(1)}, bf16[512,512]{1,0:T(8,128)(2,1)S(1)}, u32[]{:S(2)}, u32[]{:S(2)}) %collective-permute-start.22) | collective-permute-done | bytes 524320 | tf_op jit(solution)/shard_map/ppermute | solution.py:62
  313.6 2.2 convert_add_fusion
  315.8 6.7 %fusion = bf16[1024,1024]{1,0:T(8,128)(2,1)} fusion(f32[1024,1024]{1,0:T(8,128)S(1)} %copy-done, bf16[1024,1024]{0,1:T(8,128)(2,1)} %collective-permute-done.15, pred[]{:T(512)S(6)} %and.22, bf16[1024,1024]{1,0:T(8,128)(2,1)} %broadcast_select_fusion, bf16[1024,1024]{1,0:T(8,128)(2,1)} %collective-permute-done.20, pred[]{:T(512)S(6)} %or.2, ...), kind=kOutput, calls=%fused_computation.2 | convolution fusion | flops 2155872256 | bytes 14680066 | tf_op jit(solution)/shard_map/dot_general | solution.py:14
  (100 shorter events, 21.1 us)
Async XLA Ops:
  7.2 170.8 %all-gather.3.cloned.1.call-start = ((), (), s32[]{:S(2)}) async-start(), calls=%async_computation | async-start | bytes 5242880 | tf_op jit(solution)/shard_map/all_gather | solution.py:121
  7.2 32.1 %collective-permute-start.1 = (bf16[1024,1024]{1,0:T(8,128)(2,1)}, bf16[1024,1024]{1,0:T(8,128)(2,1)}, u32[]{:S(2)}, u32[]{:S(2)}) collective-permute-start(bf16[1024,1024]{1,0:T(8,128)(2,1)} %param.4), channel_id=1, source_target_pairs={{0,1},{4,5},{5,4},{8,9},{9,8},{10,11},{12,13},{13,12},{14,15},{15,... | collective-permute-start | bytes 6291464 | tf_op jit(solution)/shard_map/ppermute | solution.py:62
  13.2 3.2 copy-start.17
  13.2 26.1 %collective-permute-start = (bf16[1024,512]{1,0:T(8,128)(2,1)S(1)}, bf16[1024,512]{1,0:T(8,128)(2,1)S(1)}, u32[]{:S(2)}, u32[]{:S(2)}) collective-permute-start(bf16[1024,512]{1,0:T(8,128)(2,1)S(1)} %broadcast_select_fusion.3), channel_id=1, source_target_pairs={{0,4},{1,5},{2,6},{3,7},{4,8},{5,9},{6,10},{7,11},{8,12},{9,13},{1... | collective-permute-start | bytes 3145736 | tf_op jit(solution)/shard_map/ppermute | solution.py:62
  16.3 35.4 %collective-permute-start.4 = (bf16[1024,1024]{1,0:T(8,128)(2,1)}, bf16[1024,1024]{1,0:T(8,128)(2,1)}, u32[]{:S(2)}, u32[]{:S(2)}) collective-permute-start(bf16[1024,1024]{1,0:T(8,128)(2,1)} %param.4), channel_id=1, source_target_pairs={{0,2},{4,6},{5,7},{8,10},{9,11},{10,8},{12,14},{13,15},{14,12},{15... | collective-permute-start | bytes 6291464 | tf_op jit(solution)/shard_map/ppermute | solution.py:62
  21.2 30.5 %collective-permute-start.3 = (bf16[1024,1024]{1,0:T(8,128)(2,1)}, bf16[1024,1024]{1,0:T(8,128)(2,1)S(1)}, u32[]{:S(2)}, u32[]{:S(2)}) collective-permute-start(bf16[1024,1024]{1,0:T(8,128)(2,1)} %param.4), channel_id=1, source_target_pairs={{4,0},{8,4},{9,5},{10,6},{12,8},{13,9},{14,10},{15,11},{20,16},{24... | collective-permute-start | bytes 6291464 | tf_op jit(solution)/shard_map/ppermute | solution.py:62
  39.3 1.0 copy-start.19
  40.3 11.4 %collective-permute-start.2 = (bf16[1024,512]{1,0:T(8,128)(2,1)}, bf16[1024,512]{1,0:T(8,128)(2,1)S(1)}, u32[]{:S(2)}, u32[]{:S(2)}) collective-permute-start(bf16[1024,512]{1,0:T(8,128)(2,1)} %shard_map.67), channel_id=1, source_target_pairs={{4,8},{5,9},{6,10},{7,11},{8,12},{9,13},{10,14},{11,15},{20,24},{2... | collective-permute-start | bytes 3145736 | tf_op jit(solution)/shard_map/ppermute | solution.py:62
  51.7 1.3 copy-start.1
  53.0 1.0 copy-start.21
  54.0 10.9 %collective-permute-start.5 = (bf16[1024,1024]{1,0:T(8,128)(2,1)}, bf16[1024,1024]{1,0:T(8,128)(2,1)}, u32[]{:S(2)}, u32[]{:S(2)}) collective-permute-start(bf16[1024,1024]{1,0:T(8,128)(2,1)} %get-tuple-element.13), channel_id=1, source_target_pairs={{2,3},{6,7},{7,6},{8,9},{10,11},{11,10},{12,13},{13,12},{14,15},{1... | collective-permute-start | bytes 6291464 | tf_op jit(solution)/shard_map/ppermute | solution.py:62
  56.1 39.3 %collective-permute-start.8 = (bf16[1024,1024]{1,0:T(8,128)(2,1)}, bf16[1024,1024]{1,0:T(8,128)(2,1)S(1)}, u32[]{:S(2)}, u32[]{:S(2)}) collective-permute-start(bf16[1024,1024]{1,0:T(8,128)(2,1)} %get-tuple-element.15), channel_id=1, source_target_pairs={{5,7},{10,8},{21,23},{26,24}} | collective-permute-start | bytes 6291464 | tf_op jit(solution)/shard_map/ppermute | solution.py:62
  57.0 24.0 %collective-permute-start.6 = (bf16[1024,512]{1,0:T(8,128)(2,1)}, bf16[1024,512]{1,0:T(8,128)(2,1)S(1)}, u32[]{:S(2)}, u32[]{:S(2)}) collective-permute-start(bf16[1024,512]{1,0:T(8,128)(2,1)} %get-tuple-element.14), channel_id=1, source_target_pairs={{8,12},{9,13},{10,14},{11,15},{24,28},{25,29},{26,30},{27,31}} | collective-permute-start | bytes 3145736 | tf_op jit(solution)/shard_map/ppermute | solution.py:62
  60.4 34.9 %collective-permute-start.7 = (bf16[512,1024]{1,0:T(8,128)(2,1)S(1)}, bf16[512,1024]{1,0:T(8,128)(2,1)S(1)}, u32[]{:S(2)}, u32[]{:S(2)}) collective-permute-start(bf16[512,1024]{1,0:T(8,128)(2,1)S(1)} %get-tuple-element.22), channel_id=1, source_target_pairs={{4,0},{6,2},{8,4},{9,5},{10,6},{11,7},{20,16},{22,18},{24,20},{25,... | collective-permute-start | bytes 3145736 | tf_op jit(solution)/shard_map/ppermute | solution.py:62
  64.9 3.3 copy-start.22
  68.2 4.3 %copy-start.20 = (bf16[1024,512]{1,0:T(8,128)(2,1)S(1)}, bf16[1024,512]{1,0:T(8,128)(2,1)}, u32[]{:S(2)}) copy-start(bf16[1024,512]{1,0:T(8,128)(2,1)} %shard_map.67) | copy-start | bytes 3145732
  72.4 4.4 %copy-start.18 = (bf16[1024,512]{1,0:T(8,128)(2,1)S(1)}, bf16[1024,512]{1,0:T(8,128)(2,1)}, u32[]{:S(2)}) copy-start(bf16[1024,512]{1,0:T(8,128)(2,1)} %copy-done.17) | copy-start | bytes 3145732
  80.9 14.4 %copy-start.14 = (bf16[1024,512]{1,0:T(8,128)(2,1)}, bf16[1024,512]{1,0:T(8,128)(2,1)S(1)}, u32[]{:S(2)}) copy-start(bf16[1024,512]{1,0:T(8,128)(2,1)S(1)} %collective-permute-done.6.refs_0_) | copy-start | bytes 3145732
  95.4 1.0 copy-start.10
  96.3 1.3 copy-start.7
  103.7 77.6 %all-gather.5.cloned.1.call-start = ((), (), s32[]{:S(2)}) async-start(), calls=%async_computation.1 | async-start | bytes 2621440 | tf_op jit(solution)/shard_map/all_gather | solution.py:95
  104.5 7.2 %copy-start.11 = (bf16[512,1024]{1,0:T(8,128)(2,1)S(1)}, bf16[512,1024]{1,0:T(8,128)(2,1)}, u32[]{:S(2)}) copy-start(bf16[512,1024]{1,0:T(8,128)(2,1)} %get-tuple-element.17) | copy-start | bytes 3145732
  104.5 27.1 %collective-permute-start.9 = (bf16[512,1024]{1,0:T(8,128)(2,1)}, bf16[512,1024]{1,0:T(8,128)(2,1)S(1)}, u32[]{:S(2)}, u32[]{:S(2)}) collective-permute-start(bf16[512,1024]{1,0:T(8,128)(2,1)} %get-tuple-element.21), channel_id=1, source_target_pairs={{4,0},{6,2},{8,4},{9,5},{10,6},{11,7},{20,16},{22,18},{24,20},{25,... | collective-permute-start | bytes 3145736 | tf_op jit(solution)/shard_map/ppermute | solution.py:62
  110.0 21.5 %collective-permute-start.11 = (bf16[1024,512]{1,0:T(8,128)(2,1)}, bf16[1024,512]{1,0:T(8,128)(2,1)}, u32[]{:S(2)}, u32[]{:S(2)}) collective-permute-start(bf16[1024,512]{1,0:T(8,128)(2,1)} %fusion.32.refs_1_), channel_id=1, source_target_pairs={{8,12},{9,13},{10,14},{11,15},{12,8},{13,9},{14,10},{15,11},{24,28... | collective-permute-start | bytes 3145736 | tf_op jit(solution)/shard_map/ppermute | solution.py:62
  111.7 31.1 %collective-permute-start.10 = (bf16[512,1024]{1,0:T(8,128)(2,1)S(1)}, bf16[512,1024]{1,0:T(8,128)(2,1)S(1)}, u32[]{:S(2)}, u32[]{:S(2)}) collective-permute-start(bf16[512,1024]{1,0:T(8,128)(2,1)S(1)} %copy-done.11), channel_id=1, source_target_pairs={{4,0},{6,2},{7,3},{20,16},{22,18},{23,19}} | collective-permute-start | bytes 3145736 | tf_op jit(solution)/shard_map/ppermute | solution.py:62
  115.5 1.6 copy-start.12
  131.6 11.2 %copy-start.6 = (bf16[512,1024]{1,0:T(8,128)(2,1)}, bf16[512,1024]{1,0:T(8,128)(2,1)S(1)}, u32[]{:S(2)}) copy-start(bf16[512,1024]{1,0:T(8,128)(2,1)S(1)} %collective-permute-done.9.refs_0_) | copy-start | bytes 3145732
  142.8 1.0 copy-start.3
  146.0 52.7 %collective-permute-start.13 = (bf16[1024,1024]{1,0:T(8,128)(2,1)}, bf16[1024,1024]{1,0:T(8,128)(2,1)}, u32[]{:S(2)}, u32[]{:S(2)}) collective-permute-start(bf16[1024,1024]{1,0:T(8,128)(2,1)} %constant_dynamic-update-slice_fusion), channel_id=1, source_target_pairs={{0,2},{5,7},{16,18},{21,23}} | collective-permute-start | bytes 6291464 | tf_op jit(solution)/shard_map/ppermute | solution.py:62
  161.0 46.2 %collective-permute-start.17 = (bf16[1024,512]{1,0:T(8,128)(2,1)}, bf16[1024,512]{1,0:T(8,128)(2,1)}, u32[]{:S(2)}, u32[]{:S(2)}) collective-permute-start(bf16[1024,512]{1,0:T(8,128)(2,1)} %fusion.35.refs_2_.refs_1_), channel_id=1, source_target_pairs={{4,0},{5,1},{6,2},{7,3},{12,8},{13,9},{14,10},{15,11},{20,16},{21,... | collective-permute-start | bytes 3145736 | tf_op jit(solution)/shard_map/ppermute | solution.py:62
  164.8 8.9 %copy-start.2 = (bf16[1024,1024]{1,0:T(8,128)(2,1)S(1)}, bf16[1024,1024]{1,0:T(8,128)(2,1)}, u32[]{:S(2)}) copy-start(bf16[1024,1024]{1,0:T(8,128)(2,1)} %get-tuple-element.15) | copy-start | bytes 6291460
  172.3 34.9 %collective-permute-start.18 = (bf16[512,1024]{1,0:T(8,128)(2,1)}, bf16[512,1024]{1,0:T(8,128)(2,1)}, u32[]{:S(2)}, u32[]{:S(2)}) collective-permute-start(bf16[512,1024]{1,0:T(8,128)(2,1)} %get-tuple-element.18.refs_2_), channel_id=1, source_target_pairs={{4,0},{6,2},{7,3},{20,16},{22,18},{23,19}} | collective-permute-start | bytes 3145736 | tf_op jit(solution)/shard_map/ppermute | solution.py:62
  175.2 6.1 %copy-start.5 = (bf16[512,512]{1,0:T(8,128)(2,1)S(1)}, bf16[512,512]{1,0:T(8,128)(2,1)}, u32[]{:S(2)}) copy-start(bf16[512,512]{1,0:T(8,128)(2,1)} %param.5) | copy-start | bytes 1572868
  175.2 57.3 %collective-permute-start.12 = (bf16[1024,1024]{1,0:T(8,128)(2,1)}, bf16[1024,1024]{1,0:T(8,128)(2,1)}, u32[]{:S(2)}, u32[]{:S(2)}) collective-permute-start(bf16[1024,1024]{1,0:T(8,128)(2,1)} %broadcast_select_fusion.2), channel_id=1, source_target_pairs={{0,1},{2,3},{5,4},{7,6},{8,9},{10,11},{16,17},{18,19},{21,20},{23,... | collective-permute-start | bytes 6291464 | tf_op jit(solution)/shard_map/ppermute | solution.py:62
  186.5 20.7 %collective-permute-start.16 = (bf16[512,512]{1,0:T(8,128)(2,1)}, bf16[512,512]{1,0:T(8,128)(2,1)S(1)}, u32[]{:S(2)}, u32[]{:S(2)}) collective-permute-start(bf16[512,512]{1,0:T(8,128)(2,1)} %fusion.40.refs_1_), channel_id=1, source_target_pairs={{0,4},{1,5},{2,6},{3,7},{4,0},{5,1},{6,2},{7,3},{8,12},{9,13},{10,... | collective-permute-start | bytes 1572872 | tf_op jit(solution)/shard_map/ppermute | solution.py:62
  201.9 39.1 %collective-permute-start.14 = (bf16[1024,1024]{1,0:T(8,128)(2,1)}, bf16[1024,1024]{1,0:T(8,128)(2,1)}, u32[]{:S(2)}, u32[]{:S(2)}) collective-permute-start(bf16[1024,1024]{1,0:T(8,128)(2,1)} %broadcast_select_fusion.1), channel_id=1, source_target_pairs={{0,1},{2,3},{5,4},{7,6},{16,17},{18,19},{21,20},{23,22}} | collective-permute-start | bytes 6291464 | tf_op jit(solution)/shard_map/ppermute | solution.py:62
  207.2 0.8 copy-start.15
  208.0 4.2 %copy-start.16 = (bf16[512,512]{1,0:T(8,128)(2,1)S(1)}, bf16[512,512]{1,0:T(8,128)(2,1)}, u32[]{:S(2)}) copy-start(bf16[512,512]{1,0:T(8,128)(2,1)} %copy-done.15) | copy-start | bytes 1572868
  217.5 39.4 %collective-permute-start.19 = (bf16[1024,1024]{1,0:T(8,128)(2,1)}, bf16[1024,1024]{1,0:T(8,128)(2,1)}, u32[]{:S(2)}, u32[]{:S(2)}) collective-permute-start(bf16[1024,1024]{1,0:T(8,128)(2,1)} %pad_maximum_fusion), channel_id=1, source_target_pairs={{0,2},{16,18}} | collective-permute-start | bytes 6291464 | tf_op jit(solution)/shard_map/ppermute | solution.py:62
  224.6 44.2 %collective-permute-start.21 = (bf16[1024,512]{1,0:T(8,128)(2,1)}, bf16[1024,512]{1,0:T(8,128)(2,1)}, u32[]{:S(2)}, u32[]{:S(2)}) collective-permute-start(bf16[1024,512]{1,0:T(8,128)(2,1)} %add_convert_fusion.1.refs_1_), channel_id=1, source_target_pairs={{8,0},{9,1},{10,2},{11,3},{12,4},{13,5},{14,6},{15,7},{24,16},{25,... | collective-permute-start | bytes 3145736 | tf_op jit(solution)/shard_map/ppermute | solution.py:62
  250.2 6.8 %copy-start.4 = (bf16[512,1024]{1,0:T(8,128)(2,1)S(1)}, bf16[512,1024]{1,0:T(8,128)(2,1)}, u32[]{:S(2)}) copy-start(bf16[512,1024]{1,0:T(8,128)(2,1)} %shard_map.78) | copy-start | bytes 3145732
  254.8 8.9 %copy-start.13 = (bf16[1024,512]{1,0:T(8,128)(2,1)S(1)}, bf16[1024,512]{1,0:T(8,128)(2,1)}, u32[]{:S(2)}) copy-start(bf16[1024,512]{1,0:T(8,128)(2,1)} %add_convert_fusion.2) | copy-start | bytes 3145732
  254.8 61.0 %collective-permute-start.15 = (bf16[1024,1024]{0,1:T(8,128)(2,1)}, bf16[1024,1024]{0,1:T(8,128)(2,1)}, u32[]{:S(2)}, u32[]{:S(2)}) collective-permute-start(bf16[1024,1024]{0,1:T(8,128)(2,1)} %copy.25), channel_id=1, source_target_pairs={{4,1},{20,17}} | collective-permute-start | bytes 6291464 | tf_op jit(solution)/shard_map/ppermute | solution.py:62
  260.5 55.4 %collective-permute-start.20 = (bf16[1024,1024]{1,0:T(8,128)(2,1)}, bf16[1024,1024]{1,0:T(8,128)(2,1)}, u32[]{:S(2)}, u32[]{:S(2)}) collective-permute-start(bf16[1024,1024]{1,0:T(8,128)(2,1)} %broadcast_select_fusion), channel_id=1, source_target_pairs={{0,1},{2,3},{16,17},{18,19}} | collective-permute-start | bytes 6291464 | tf_op jit(solution)/shard_map/ppermute | solution.py:62
  266.6 5.3 %copy-start.9 = (bf16[512,512]{1,0:T(8,128)(2,1)S(1)}, bf16[512,512]{1,0:T(8,128)(2,1)}, u32[]{:S(2)}) copy-start(bf16[512,512]{1,0:T(8,128)(2,1)} %fusion.41.refs_1_) | copy-start | bytes 1572868
  266.6 5.9 %copy-start.8 = (bf16[512,512]{1,0:T(8,128)(2,1)S(1)}, bf16[512,512]{1,0:T(8,128)(2,1)}, u32[]{:S(2)}) copy-start(bf16[512,512]{1,0:T(8,128)(2,1)} %add_convert_fusion.3.refs_1_) | copy-start | bytes 1572868
  271.9 41.7 %collective-permute-start.22 = (bf16[512,512]{1,0:T(8,128)(2,1)S(1)}, bf16[512,512]{1,0:T(8,128)(2,1)S(1)}, u32[]{:S(2)}, u32[]{:S(2)}) collective-permute-start(bf16[512,512]{1,0:T(8,128)(2,1)S(1)} %copy-done.9), channel_id=1, source_target_pairs={{0,4},{1,5},{2,6},{3,7},{4,0},{5,1},{6,2},{7,3},{8,12},{9,13},{10,... | collective-permute-start | bytes 1572872 | tf_op jit(solution)/shard_map/ppermute | solution.py:62
  272.5 41.1 %collective-permute-start.23 = (bf16[512,512]{1,0:T(8,128)(2,1)S(1)}, bf16[512,512]{1,0:T(8,128)(2,1)}, u32[]{:S(2)}, u32[]{:S(2)}) collective-permute-start(bf16[512,512]{1,0:T(8,128)(2,1)S(1)} %copy-done.8), channel_id=1, source_target_pairs={{0,8},{1,9},{2,10},{3,11},{4,12},{5,13},{6,14},{7,15},{8,0},{9,1},... | collective-permute-start | bytes 1572872 | tf_op jit(solution)/shard_map/ppermute | solution.py:62
  277.2 38.6 %copy-start = (f32[1024,1024]{1,0:T(8,128)S(1)}, f32[1024,1024]{1,0:T(8,128)}, u32[]{:S(2)}) copy-start(f32[1024,1024]{1,0:T(8,128)} %add_add_fusion) | copy-start | bytes 12582916
Sparse Core Ops, SparseCore 0:
  103.8 43.3 all-gather.2
  148.8 22.5 all-gather.4

commit v3 on v1

v3 whole, which is shorter than its diff:
```python
import jax
import jax.numpy as jnp
from jax import lax
from jax.experimental import pallas as pl
from jax.experimental.pallas import tpu as pltpu
from jax.sharding import PartitionSpec as P

BLOCK = 128
AXES = ("fields", "row", "col")
BF16 = jnp.bfloat16
F32 = jnp.float32
TILE = 256
N = 4
VMEM_BYTES = 40 * 1024 * 1024


def inner_dot(left_part, right_part):
    return lax.dot_general(
        left_part, right_part, (((0,), (0,)), ((), ())), preferred_element_type=F32
    )


def dot(a, b):
    return jnp.dot(a, b, preferred_element_type=F32)


def mask_panel(panel, structure):
    kept_rows = jnp.repeat(structure, BLOCK)[:, None] > 0
    return kept_rows, jnp.where(kept_rows, panel, jnp.zeros_like(panel))


def gather_plan(root_inverse, child_inverse, panel, structure):
    kept_rows, panel_kept = mask_panel(panel, structure)
    root_full, child_rows, panel_full = (
        lax.all_gather(root_inverse, "col", axis=1, tiled=True),
        lax.all_gather(child_inverse, "col", axis=1, tiled=True),
        lax.all_gather(panel_kept, "col", axis=1, tiled=True),
    )
    root_sum = lax.psum_scatter(
        inner_dot(root_full, root_inverse), "row", scatter_dimension=0, tiled=True
    )
    sigma_root = root_sum.astype(BF16)
    sigma_rows = lax.all_gather(sigma_root, "col", axis=1, tiled=True)
    cross_sum = jnp.dot(
        sigma_rows,
        lax.all_gather(panel_kept, "row", axis=0, tiled=True),
        preferred_element_type=F32,
    )
    sigma_cross = jnp.where(kept_rows, -cross_sum, jnp.zeros_like(cross_sum)).astype(BF16)
    sigma_child = lax.psum_scatter(
        (inner_dot(child_rows, child_inverse) - inner_dot(panel_full, sigma_cross)).astype(BF16),
        "row",
        scatter_dimension=0,
        tiled=True,
    ).astype(F32)
    return (sigma_root, sigma_cross, sigma_child)


def position():
    return lax.axis_index("row"), lax.axis_index("col")


def start(src, dst, sem):
    pltpu.make_async_copy(src, dst, sem).start()


def wait(src, dst, sem):
    pltpu.make_async_copy(src, dst, sem).wait()


def start_picked(refs, index, dst, sem):
    for m, ref in enumerate(refs):

        @pl.when(index == m)
        def _():
            start(ref, dst, sem)


def tile(i):
    return pl.ds(pl.multiple_of(i * TILE, TILE), TILE)


def product_kernel(
    l0, l1, l2, l3, p0, p1, p2, p3, _dep0, _dep1, _in, t_ref, tt_ref, far_ref, _out, rows, panels, acc, row_sems, panel_sems
):
    r, c = position()
    for m, ref in enumerate((l0, l1, l2, l3)):
        j = c ^ m

        @pl.when(j <= r)
        def _():
            start(ref, rows.at[r - j], row_sems.at[r - j])

    for s, ref in enumerate((p0, p1, p2, p3)):

        @pl.when(s <= r)
        def _():
            start(ref, panels.at[s], panel_sems.at[s])

    for s in range(N):

        @pl.when(s <= r)
        def _():
            wait(l0, rows.at[s], row_sems.at[s])
            wait(p0, panels.at[s], panel_sems.at[s])

            @pl.loop(0, acc.shape[0] // TILE)
            def _(i):
                term = dot(rows[s, tile(i), :], panels[s])
                if s > 0:
                    term = term + acc[tile(i), :]
                acc[tile(i), :] = term

    @pl.loop(0, acc.shape[0] // TILE)
    def _(i):
        value = acc[tile(i), :]
        t_ref[tile(i), :] = value.astype(BF16)
        tt_ref[:, tile(i)] = value.T.astype(BF16)

    @pl.when(r >= 2)
    def _():
        slot = r - (r ^ 3)

        @pl.loop(0, tt_ref.shape[0] // TILE)
        def _(i):
            far_ref[tile(i), :] = dot(tt_ref[tile(i), :], rows[slot]).astype(BF16)


def cross_kernel(l0, l1, l2, l3, tt_ref, near_ref, own_ref, blocks, sems):
    r, c = position()
    refs = (l0, l1, l2, l3)

    @pl.when(r % 2 == 1)
    def _():
        start_picked(refs, r ^ 1 ^ c, blocks.at[0], sems.at[0])

    start_picked(refs, r ^ c, blocks.at[1], sems.at[1])

    @pl.when(r % 2 == 1)
    def _():
        wait(l0, blocks.at[0], sems.at[0])

        @pl.loop(0, tt_ref.shape[0] // TILE)
        def _(i):
            near_ref[tile(i), :] = dot(tt_ref[tile(i), :], blocks[0]).astype(BF16)

    wait(l0, blocks.at[1], sems.at[1])

    @pl.loop(0, tt_ref.shape[0] // TILE)
    def _(i):
        own_ref[tile(i), :] = dot(tt_ref[tile(i), :], blocks[1])


def onward_kernel(l0, l1, l2, l3, tt_ref, far_ref, _dep0, _ina, _inb, onward_ref, _outa, _outb, block, sem):
    r, c = position()

    @pl.when(r >= 2)
    def _():
        start_picked((l0, l1, l2, l3), r ^ 2 ^ c, block, sem)
        wait(l0, block, sem)

        @pl.loop(0, tt_ref.shape[0] // TILE)
        def _(i):
            term = dot(tt_ref[tile(i), :], block[...])
            onward_ref[tile(i), :] = (term + far_ref[tile(i), :].astype(F32)).astype(BF16)


def child_kernel(tt_ref, t_row_ref, child_ref, child_row_ref, _dep, _in, out_ref, _out, child_t):
    w = child_ref.shape[1]
    child_t[...] = child_ref[...].astype(F32).T.astype(BF16)
    for i in range(N):
        columns = slice(i * w, (i + 1) * w)

        @pl.loop(0, w // TILE)
        def _(j):
            term = dot(tt_ref[tile(j), :], t_row_ref[:, columns])
            term = term + dot(child_t[tile(j), :], child_row_ref[:, columns])
            out_ref[i, tile(j), :] = term.astype(BF16)


def add_root(s, r, c, left, held, acc, first):
    @pl.when((r + s < N) & (c <= r + s))
    def _():
        @pl.loop(0, acc.shape[0] // TILE)
        def _(i):
            term = inner_dot(left[:, tile(i)], held[...])
            if not first:
                term = term + acc[tile(i), :]
            acc[tile(i), :] = term


def root_kernel(l0, l1, l2, l3, h1, x1, h2, x2, b12, _dep, acc_ref, left, held, left_sems, held_sems):
    r, c = position()
    start_picked((l0, l1, l2, l3), r ^ c, left.at[0], left_sems.at[0])
    start(l0, held.at[0], held_sems.at[0])
    b1, b2 = b12.at[: h1.shape[0]], b12.at[h1.shape[0] :]
    for s, refs in ((1, (h1, x1, b1)), (2, (h2, x2, b2))):
        start_picked(refs, source(r, c), left.at[s], left_sems.at[s])
        start(refs[0], held.at[s], held_sems.at[s])
    acc_ref[...] = jnp.zeros_like(acc_ref)
    for s in range(3):
        wait(l0, left.at[s], left_sems.at[s])
        wait(l0, held.at[s], held_sems.at[s])
        add_root(s, r, c, left.at[s], held.at[s], acc_ref, False)


def source(r, c):
    return jnp.where(c == r, 0, jnp.where(c == (r ^ 2), 1, 2))


def root_end_kernel(acc_ref, h3, x3, b3, out_ref, left, held, sems):
    r, c = position()

    @pl.when(r == 0)
    def _():
        start_picked((h3, x3, b3), source(r, c), left, sems.at[0])
        start(h3, held, sems.at[1])
        wait(h3, left, sems.at[0])
        wait(h3, held, sems.at[1])

        @pl.loop(0, left.shape[0] // TILE)
        def _(i):
            term = inner_dot(left[:, tile(i)], held[...])
            out_ref[tile(i), :] = (term + acc_ref[tile(i), :]).astype(BF16)

    @pl.when(r != 0)
    def _():
        out_ref[...] = acc_ref[...].astype(BF16)


def cross_end_kernel(structure, own_ref, near_ref, last_ref, out_ref):
    for b in range(own_ref.shape[1] // BLOCK):
        rows = slice(b * BLOCK, (b + 1) * BLOCK)
        total = own_ref[:, rows] + near_ref[:, rows].astype(F32) + last_ref[:, rows].astype(F32)
        kept = structure[b] > 0
        out_ref[rows, :] = jnp.where(kept, -total.T, jnp.zeros_like(total.T)).astype(BF16)


def child_end_kernel(sum_ref, _dep, out_ref):
    out_ref[...] = sum_ref[...].astype(F32).T


ANY = pl.BlockSpec(memory_space=pl.ANY)
VMEM = pl.BlockSpec(memory_space=pltpu.VMEM)
SMEM = pl.BlockSpec(memory_space=pltpu.SMEM)


def local_call(kernel, in_specs, outs, scratch, *args, gated=0):
    first = len(args) - gated
    outs = outs + [jax.ShapeDtypeStruct(x.shape, x.dtype) for x in args[first:]]
    return pl.pallas_call(
        kernel,
        out_shape=outs,
        in_specs=in_specs + [ANY] * (len(args) - len(in_specs)),
        out_specs=[VMEM] * (len(outs) - gated) + [ANY] * gated,
        scratch_shapes=scratch,
        input_output_aliases={first + i: len(outs) - gated + i for i in range(gated)},
        compiler_params=pltpu.CompilerParams(vmem_limit_bytes=VMEM_BYTES),
        cost_estimate=pl.CostEstimate(flops=1, bytes_accessed=1, transcendentals=0),
    )(*args)


def together(*arrays, earlier=()):
    k = len(arrays)
    return pl.pallas_call(
        lambda *refs: None,
        out_shape=[jax.ShapeDtypeStruct(x.shape, x.dtype) for x in arrays],
        in_specs=[ANY] * (k + len(earlier)),
        out_specs=[ANY] * k,
        input_output_aliases={i: i for i in range(k)},
    )(*arrays, *earlier)


def square_plan(fields):
    n = N

    def move(x, target):
        pairs = []
        for f in range(fields):
            for r in range(n):
                for c in range(n):
                    to = target(r, c)
                    if to is not None and 0 <= to[0] < n:
                        pairs.append(((f * n + r) * n + c, (f * n + to[0]) * n + to[1]))
        return lax.ppermute(x, AXES, pairs)

    def up(x, s):
        return move(x, lambda r, c: (r + 1, c) if r >= s - 1 else None)

    def down(x, s):
        def target(r, c):
            k = r + s - 1
            return (r - 1, c) if k < n and c <= k else None

        return move(x, target)

    def on_device(root_inverse, child_inverse, panel, structure):
        kept_rows, panel_kept = mask_panel(panel, structure)
        h, w = panel.shape
        half = h // 2
        lower = lambda r, c: c <= r
        shape = jax.ShapeDtypeStruct
        dma = pltpu.SemaphoreType.DMA

        child_row = lax.all_gather(child_inverse, "col", axis=1, tiled=True)
        panel_1 = up(panel_kept, 1)
        root_across = move(root_inverse, lambda r, c: (r, c ^ 2) if lower(r, c) else None)
        below_1 = down(root_inverse, 1)
        root_beside = move(root_inverse, lambda r, c: (r, c ^ 1) if lower(r, c) else None)
        panel_2 = up(panel_1, 2)
        (panel_2,) = together(panel_2, earlier=(below_1, root_across, root_beside))
        panel_3 = up(panel_2, 3)
        below_2a = down(below_1[:half], 2)
        root_both = move(root_across, lambda r, c: (r, c ^ 1) if lower(r, c ^ 2) else None)
        across_1 = move(below_1, lambda r, c: (r, c ^ 2) if r == c and r in (1, 2) else None)

        root_row = (root_inverse, root_beside, root_across, root_both)
        panels = (panel_kept, panel_1, panel_2, panel_3)
        t, t_t, far_part, below_1 = local_call(
            product_kernel,
            [ANY] * 10,
            [shape((h, w), BF16), shape((w, h), BF16), shape((w, h), BF16)],
            [
                pltpu.VMEM((n, h, h), BF16),
                pltpu.VMEM((n, h, w), BF16),
                pltpu.VMEM((h, w), F32),
                dma((n,)),
                dma((n,)),
            ],
            *root_row,
            *panels,
            below_2a,
            across_1,
            below_1,
            gated=1,
        )
        t_row = lax.all_gather(t, "col", axis=1, tiled=True)
        far = move(far_part, lambda r, c: (r ^ 1, c) if r >= 2 else None)
        below_2b = down(below_1[half:], 2)

        near_part, own = local_call(
            cross_kernel,
            [ANY] * 4 + [VMEM],
            [shape((w, h), BF16), shape((w, h), F32)],
            [pltpu.VMEM((2, h, h), BF16), dma((2,))],
            *root_row,
            t_t,
        )
        near = move(near_part, lambda r, c: (r ^ 1, c) if r % 2 else None)
        onward, below_2a, below_2b = local_call(
            onward_kernel,
            [ANY] * 4 + [VMEM, VMEM],
            [shape((w, h), BF16)],
            [pltpu.VMEM((h, h), BF16), dma],
            *root_row,
            t_t,
            far,
            near_part,
            below_2a,
            below_2b,
            gated=2,
        )
        last = move(onward, lambda r, c: (r - 2, c))
        below_2 = jnp.concatenate((below_2a, below_2b), 0)
        below_3 = down(below_2, 3)
        across_2 = move(below_2, lambda r, c: (r, c ^ 2) if r == c and r in (0, 1) else None)

        child_parts, across_1 = local_call(
            child_kernel,
            [VMEM] * 4,
            [shape((n, w, w), BF16)],
            [pltpu.VMEM((w, w), BF16)],
            t_t,
            t_row,
            child_inverse,
            child_row,
            onward,
            across_1,
            gated=1,
        )
        child_sum = lax.psum_scatter(child_parts, "row", scatter_dimension=0)

        r, c = lax.axis_index("row"), lax.axis_index("col")
        across_1, below_3 = together(across_1, below_3, earlier=(near, last))
        across_3 = move(below_3, lambda r, c: (r, c ^ 2) if r == c == 0 else None)
        held_12 = jnp.concatenate((below_1, below_2), 0)
        beside_12 = move(
            jnp.where(c == r, held_12, jnp.concatenate((across_1, across_2), 0)),
            lambda r, c: (r, c ^ 1) if r in (c, c ^ 2) and r < 3 else None,
        )
        (root_sum,) = local_call(
            root_kernel,
            [],
            [shape((h, h), F32)],
            [pltpu.VMEM((3, h, h), BF16), pltpu.VMEM((3, h, h), BF16), dma((3,)), dma((3,))],
            *root_row,
            below_1,
            across_1,
            below_2,
            across_2,
            beside_12,
            child_parts,
        )
        (sigma_cross,) = local_call(
            cross_end_kernel,
            [SMEM] + [VMEM] * 3,
            [shape((h, w), BF16)],
            [],
            structure,
            own,
            near,
            last,
        )
        beside_3 = move(
            jnp.where(c == r, below_3, across_3),
            lambda r, c: (r, c ^ 1) if r == 0 and c in (0, 2) else None,
        )
        (sigma_root,) = local_call(
            root_end_kernel,
            [VMEM],
            [shape((h, h), BF16)],
            [pltpu.VMEM((h, h), BF16), pltpu.VMEM((h, h), BF16), dma((2,))],
            root_sum,
            below_3,
            across_3,
            beside_3,
        )
        (sigma_child,) = local_call(
            child_end_kernel,
            [VMEM],
            [shape((w, w), F32)],
            [],
            child_sum,
            sigma_cross,
        )
        return (sigma_root, sigma_cross, sigma_child)

    return on_device


def solution(mesh):
    square = mesh.shape["row"] == N and mesh.shape["col"] == N
    spec = P(("fields", "row"), "col")
    return jax.shard_map(
        square_plan(mesh.shape["fields"]) if square else gather_plan,
        mesh=mesh,
        in_specs=(spec, spec, spec, P(("fields", "row"))),
        out_specs=(spec, spec, spec),
        check_vma=False,
    )
```

time: 400 us -> 318 us (0.80)
  matrix products: 42 us -> 0 us
  waiting for transfers between devices: 232 us -> 194 us
  starting transfers between devices: 76.1 us -> 41.7 us
  Pallas kernels: 0 us -> 33.3 us
  between operations: 1.08 us -> 14.1 us
  other arithmetic: 17.2 us -> 10.1 us
  local copies, waits for them, and re-layouts: 30.6 us -> 23.6 us
    ppermute x28 -> x18, waiting for transfers between devices: 232 us -> 183 us  [move(): return lax.ppermute(x, AXES, pairs)]
    dot_general x8 -> x0, matrix products: 42 us -> none  [the longest x7 34.4 us: inner_dot(): lax.dot_general(left_part, right_part, (((0,), (0,)), ((), ())), preferre...]
    ppermute x28 -> x18, starting transfers between devices: 76.1 us -> 41.6 us  [move(): return lax.ppermute(x, AXES, pairs)]
    pallas_call x0 -> x10, Pallas kernels: none -> 33.3 us  [the longest x8 33.3 us: local_call(): pl.pallas_call(kernel, out_shape=outs, in_specs=in_specs + [ANY] * (len(a...]
    dynamic_update_slice x14 -> x0, local copies, waits for them, and re-layouts: 20.4 us -> none  [the longest x11 13.6 us: in_row(): full = lax.dynamic_update_slice(full, part, (0, (c ^ m) * w))]
    unnamed x10 -> x51, local copies, waits for them, and re-layouts: 1.39 us -> 19.9 us
    reduce_scatter x0 -> x1, waiting for transfers between devices: none -> 9.86 us  [on_device(): child_sum = lax.psum_scatter(child_parts, 'row', scatter_dimension=0)]
    add x3 -> x0, other arithmetic: 4.88 us -> none  [the longest x1 2.37 us: on_device(): block(child, r, w).astype(F32) + near.astype(F32) + last.astype(F32)]
  transfers between devices with their start and end apart: 28 -> 21, of which waited for: 10 -> 8; matrix products, arithmetic and copies ran while one was open for 21% -> 5% of each run, Pallas kernels for 0% -> 8%
where the time goes in v3:
time: 318 us; the launch traced here: 317 us
  waiting for transfers between devices  194 us (61%)
  starting transfers between devices  41.7 us (13%)
  Pallas kernels  33.3 us (10%)
  local copies, waits for them, and re-layouts  23.6 us (7%)
  between operations  14.1 us (4%)
  other arithmetic  10.1 us (3%)
    ppermute x18, waiting for transfers between devices, move(): return lax.ppermute(x, AXES, pairs)  183 us
    ppermute x18, starting transfers between devices, move(): return lax.ppermute(x, AXES, pairs)  41.6 us
    pallas_call x8, Pallas kernels, local_call(): pl.pallas_call(kernel, out_shape=outs, in_specs=in_specs + [ANY] * (len(a...  33.3 us
    unnamed x51, local copies, waits for them, and re-layouts  19.9 us
    reduce_scatter x1, waiting for transfers between devices, on_device(): child_sum = lax.psum_scatter(child_parts, 'row', scatter_dimension=0)  9.86 us
  transfers between devices with their start and end apart: 21, of which 8 were waited for; matrix products, arithmetic and copies ran while one was open for 5% of the time, Pallas kernels for 8%

profile of v3, /device:TPU:0, one launch (start us, length us, event | category | flops | bytes accessed | tf_op | source)
XLA Modules:
  0.0 316.9 jit_solution(9460681212977823129)
XLA Ops:
  7.2 0.0 all-gather.5.cloned.1.call-start
  7.2 6.2 %collective-permute-start.1 = (bf16[1024,1024]{1,0:T(8,128)(2,1)}, bf16[1024,1024]{1,0:T(8,128)(2,1)}, u32[]{:S(2)}, u32[]{:S(2)}) collective-permute-start(bf16[1024,1024]{1,0:T(8,128)(2,1)} %l0.7), channel_id=1, source_target_pairs={{0,2},{4,6},{5,7},{8,10},{9,11},{10,8},{12,14},{13,15},{14,12},{15... | collective-permute-start | bytes 6291464 | tf_op jit(solution)/shard_map/ppermute | solution.py:285
  13.4 1.3 collective-permute-start.5
  14.7 2.7 collective-permute-start
  17.4 0.7 broadcast_compare_fusion
  18.0 0.1 broadcast_bitcast_fusion
  18.1 1.4 broadcast_select_fusion.1.p0
  19.6 4.7 %collective-permute-start.3 = (bf16[1024,512]{1,0:T(8,128)(2,1)S(1)}, bf16[1024,512]{1,0:T(8,128)(2,1)}, u32[]{:S(2)}, u32[]{:S(2)}) collective-permute-start(bf16[1024,512]{1,0:T(8,128)(2,1)S(1)} %broadcast_select_fusion.1.p0), channel_id=1, source_target_pairs={{0,4},{1,5},{2,6},{3,7},{4,8},{5,9},{6,10},{7,11},{8,12},{9,13},{1... | collective-permute-start | bytes 3145736 | tf_op jit(solution)/shard_map/ppermute | solution.py:285
  24.3 0.0 all-gather.5.cloned.1.call-update
  24.3 0.0 all-gather.3.cloned.1.call-start
  24.4 22.0 %collective-permute-done.3.p1 = bf16[1024,512]{1,0:T(8,128)(2,1)} collective-permute-done((bf16[1024,512]{1,0:T(8,128)(2,1)S(1)}, bf16[1024,512]{1,0:T(8,128)(2,1)}, u32[]{:S(2)}, u32[]{:S(2)}) %collective-permute-start.3) | collective-permute-done | bytes 1048608 | tf_op jit(solution)/shard_map/ppermute | solution.py:285
  46.4 1.7 collective-permute-start.4
  48.1 2.0 collective-permute-start.2
  50.1 12.4 %collective-permute-done.5.refs_1_._in = bf16[1024,1024]{1,0:T(8,128)(2,1)} collective-permute-done((bf16[1024,1024]{1,0:T(8,128)(2,1)}, bf16[1024,1024]{1,0:T(8,128)(2,1)}, u32[]{:S(2)}, u32[]{:S(2)}) %collective-permute-start.5) | collective-permute-done | bytes 2097184 | tf_op jit(solution)/shard_map/ppermute | solution.py:285
  62.5 0.8 collective-permute-start.8
  63.4 0.9 collective-permute-start.6
  64.2 1.3 slice.8
  65.5 1.3 collective-permute-start.7
  66.8 35.3 %collective-permute-done.7._dep0._ina = bf16[512,1024]{1,0:T(8,128)(2,1)S(1)} collective-permute-done((bf16[512,1024]{1,0:T(8,128)(2,1)S(1)}, bf16[512,1024]{1,0:T(8,128)(2,1)S(1)}, u32[]{:S(2)}, u32[]{:S(2)}) %collective-permute-start.7) | collective-permute-done | bytes 1048608 | tf_op jit(solution)/shard_map/ppermute | solution.py:285
  102.1 1.3 copy-done
  103.4 1.2 copy-done.14
  104.6 2.6 shard_map.68
  107.3 1.0 copy-done.9
  108.2 1.0 copy-done.21
  109.2 1.0 copy-done.24
  110.2 0.0 all-gather.3.cloned.1.call-update
  110.2 0.0 reduce-scatter.2.cloned.1.call-start
  110.3 0.9 collective-permute-start.9
  111.1 1.3 slice.7
  112.4 1.3 collective-permute-start.10
  113.8 1.9 shard_map.69
  115.7 1.3 copy-done.17
  117.1 24.7 %collective-permute-done.10._inb = bf16[512,1024]{1,0:T(8,128)(2,1)S(1)} collective-permute-done((bf16[512,1024]{1,0:T(8,128)(2,1)S(1)}, bf16[512,1024]{1,0:T(8,128)(2,1)S(1)}, u32[]{:S(2)}, u32[]{:S(2)}) %collective-permute-start.10) | collective-permute-done | bytes 1048608 | tf_op jit(solution)/shard_map/ppermute | solution.py:285
  141.8 1.0 shard_map.70
  142.8 1.0 constant_dynamic-update-slice_fusion.1
  143.8 1.0 constant_dynamic-update-slice_fusion.h2
  144.9 1.3 collective-permute-start.11
  146.1 2.6 collective-permute-start.14
  148.8 1.3 collective-permute-start.12
  150.1 1.3 collective-permute-start.13
  151.4 0.0 all-gather.5.cloned.1.call-done.child_row_ref
  151.4 1.2 all-gather.3.cloned.1.call-done.t_row_ref
  152.6 1.2 copy-done.11
  153.8 2.2 copy-done.15
  156.0 1.6 copy-done.19
  157.6 1.0 copy-done.20
  158.6 4.8 %shard_map.71 = (bf16[4,512,512]{2,1,0:T(8,128)(2,1)S(1)}, bf16[1024,1024]{1,0:T(8,128)(2,1)S(1)}) custom-call(bf16[512,1024]{1,0:T(8,128)(2,1)S(1)} %copy-done.11, bf16[1024,2048]{1,0:T(8,128)(2,1)S(1)} %copy-done.15, bf16[512,512]{1,0:T(8,128)(2,1)S(1)} %copy-done.20, bf16[512,2048]{1,0:T(8,128)(2,1)S(1)} %copy-done.19, ...), custom_call_target="tpu_custom_call", output_to_operand_aliasing={{1}: (5, {})} | custom-call | flops 1 | bytes 1 | tf_op jit(solution)/shard_map/pallas_call | solution.py:251
  163.4 1.4 copy-done.12
  164.8 74.4 %collective-permute-done.12.refs_2_.near_ref = bf16[512,1024]{1,0:T(8,128)(2,1)} collective-permute-done((bf16[512,1024]{1,0:T(8,128)(2,1)}, bf16[512,1024]{1,0:T(8,128)(2,1)}, u32[]{:S(2)}, u32[]{:S(2)}) %collective-permute-start.12) | collective-permute-done | bytes 1048608 | tf_op jit(solution)/shard_map/ppermute | solution.py:285
  239.2 5.4 %collective-permute-start.16 = (bf16[1024,1024]{1,0:T(8,128)(2,1)}, bf16[1024,1024]{1,0:T(8,128)(2,1)}, u32[]{:S(2)}, u32[]{:S(2)}) collective-permute-start(bf16[1024,1024]{1,0:T(8,128)(2,1)} %get-tuple-element.27.h3), channel_id=1, source_target_pairs={{0,2},{16,18}} | collective-permute-start | bytes 6291464 | tf_op jit(solution)/shard_map/ppermute | solution.py:285
  244.6 0.0 reduce-scatter.2.cloned.1.call-update
  244.6 4.8 %maximum_select_fusion = bf16[2048,1024]{1,0:T(8,128)(2,1)} fusion(bf16[512,1024]{1,0:T(8,128)(2,1)} %copy-done.8, bf16[512,1024]{1,0:T(8,128)(2,1)S(1)} %get-tuple-element.23, bf16[1024,1024]{1,0:T(8,128)(2,1)} %get-tuple-element.16.h1, bf16[1024,1024]{1,0:T(8,128)(2,1)} %collective-permute-done.14.x2, bf16[1024,1024]{1,0:T(8,128)(2,1)S(1)} %copy-done.3, ...), kind=kLoop, calls=%fused_computation | loop fusion | flops 23068672 | bytes 12582913 | tf_op jit(solution)/shard_map/jit(_where)/select_n | solution.py:388
  249.5 3.4 %collective-permute-start.15 = (bf16[2048,1024]{1,0:T(8,128)(2,1)}, bf16[2048,1024]{1,0:T(8,128)(2,1)}, u32[]{:S(2)}, u32[]{:S(2)}) collective-permute-start(bf16[2048,1024]{1,0:T(8,128)(2,1)} %maximum_select_fusion), channel_id=1, source_target_pairs={{0,1},{2,3},{5,4},{7,6},{8,9},{10,11},{16,17},{18,19},{21,20},{23,... | collective-permute-start | bytes 12582920 | tf_op jit(solution)/shard_map/ppermute | solution.py:285
  252.9 14.2 %collective-permute-done.16.x3 = bf16[1024,1024]{1,0:T(8,128)(2,1)} collective-permute-done((bf16[1024,1024]{1,0:T(8,128)(2,1)}, bf16[1024,1024]{1,0:T(8,128)(2,1)}, u32[]{:S(2)}, u32[]{:S(2)}) %collective-permute-start.16) | collective-permute-done | bytes 2097184 | tf_op jit(solution)/shard_map/ppermute | solution.py:285
  267.1 3.1 broadcast_select_fusion
  270.2 2.7 collective-permute-start.17
  272.9 3.2 %shard_map.75._dep = bf16[1024,512]{1,0:T(8,128)(2,1)} custom-call(s32[8]{0:T(128)S(1)} %copy-done.23, f32[512,1024]{1,0:T(8,128)S(1)} %copy-done.18, bf16[512,1024]{1,0:T(8,128)(2,1)} %collective-permute-done.12.refs_2_.near_ref, bf16[512,1024]{1,0:T(8,128)(2,1)} %collective-permute-done.13.refs_3_.last_ref), custom_call_target="tpu_custom_call" | custom-call | flops 1 | bytes 1 | tf_op jit(solution)/shard_map/pallas_call | solution.py:251
  276.1 9.9 %reduce-scatter.2.cloned.1.call-done = bf16[1,512,512]{2,1,0:T(8,128)(2,1)} async-done(((bf16[4,512,512]{2,1,0:T(8,128)(2,1)}), bf16[1,512,512]{2,1,0:T(8,128)(2,1)}) %reduce-scatter.2.cloned.1.call-update) | async-done | bytes 524304 | tf_op jit(solution)/shard_map/reduce_scatter | solution.py:381
  285.9 1.4 copy-done.16
  287.3 1.0 copy-done.22
  288.3 1.2 shard_map.76
  289.5 12.0 %shard_map.73.acc_ref = f32[1024,1024]{1,0:T(8,128)} custom-call(bf16[1024,1024]{1,0:T(8,128)(2,1)S(1)} %copy-done.6, bf16[1024,1024]{1,0:T(8,128)(2,1)} %collective-permute-done.refs_3_.l1, bf16[1024,1024]{1,0:T(8,128)(2,1)} %collective-permute-done.1.refs_2_.l2, bf16[1024,1024]{1,0:T(8,128)(2,1)} %collective-permute-done.2.l3, ...), custom_call_target="tpu_custom_call" | custom-call | flops 1 | bytes 1 | tf_op jit(solution)/shard_map/pallas_call | solution.py:251
  301.6 2.2 copy-done.7
  303.7 6.6 %shard_map.74 = bf16[1024,1024]{1,0:T(8,128)(2,1)} custom-call(f32[1024,1024]{1,0:T(8,128)S(1)} %copy-done.7, bf16[1024,1024]{1,0:T(8,128)(2,1)} %get-tuple-element.27.h3, bf16[1024,1024]{1,0:T(8,128)(2,1)} %collective-permute-done.16.x3, bf16[1024,1024]{1,0:T(8,128)(2,1)} %collective-permute-done.17.b3), custom_call_target="tpu_custom_call" | custom-call | flops 1 | bytes 1 | tf_op jit(solution)/shard_map/pallas_call | solution.py:251
  (50 shorter events, 0.1 us)
Async XLA Ops:
  7.2 144.2 %all-gather.5.cloned.1.call-start = ((), (), s32[]{:S(2)}) async-start(), calls=%async_computation.2 | async-start | bytes 2621440 | tf_op jit(solution)/shard_map/all_gather | solution.py:305
  7.2 40.9 %collective-permute-start.1 = (bf16[1024,1024]{1,0:T(8,128)(2,1)}, bf16[1024,1024]{1,0:T(8,128)(2,1)}, u32[]{:S(2)}, u32[]{:S(2)}) collective-permute-start(bf16[1024,1024]{1,0:T(8,128)(2,1)} %l0.7), channel_id=1, source_target_pairs={{0,2},{4,6},{5,7},{8,10},{9,11},{10,8},{12,14},{13,15},{14,12},{15... | collective-permute-start | bytes 6291464 | tf_op jit(solution)/shard_map/ppermute | solution.py:285
  13.4 49.1 %collective-permute-start.5 = (bf16[1024,1024]{1,0:T(8,128)(2,1)}, bf16[1024,1024]{1,0:T(8,128)(2,1)}, u32[]{:S(2)}, u32[]{:S(2)}) collective-permute-start(bf16[1024,1024]{1,0:T(8,128)(2,1)} %l0.7), channel_id=1, source_target_pairs={{4,0},{5,1},{8,4},{9,5},{10,6},{12,8},{13,9},{14,10},{15,11},{20,1... | collective-permute-start | bytes 6291464 | tf_op jit(solution)/shard_map/ppermute | solution.py:285
  14.7 48.6 %collective-permute-start = (bf16[1024,1024]{1,0:T(8,128)(2,1)}, bf16[1024,1024]{1,0:T(8,128)(2,1)}, u32[]{:S(2)}, u32[]{:S(2)}) collective-permute-start(bf16[1024,1024]{1,0:T(8,128)(2,1)} %l0.7), channel_id=1, source_target_pairs={{0,1},{4,5},{5,4},{8,9},{9,8},{10,11},{12,13},{13,12},{14,15},{15,... | collective-permute-start | bytes 6291464 | tf_op jit(solution)/shard_map/ppermute | solution.py:285
  19.6 43.8 %copy-start.13 = (bf16[1024,512]{1,0:T(8,128)(2,1)}, bf16[1024,512]{1,0:T(8,128)(2,1)S(1)}, u32[]{:S(2)}) copy-start(bf16[1024,512]{1,0:T(8,128)(2,1)S(1)} %broadcast_select_fusion.1.p0) | copy-start | bytes 3145732
  19.6 26.8 %collective-permute-start.3 = (bf16[1024,512]{1,0:T(8,128)(2,1)S(1)}, bf16[1024,512]{1,0:T(8,128)(2,1)}, u32[]{:S(2)}, u32[]{:S(2)}) collective-permute-start(bf16[1024,512]{1,0:T(8,128)(2,1)S(1)} %broadcast_select_fusion.1.p0), channel_id=1, source_target_pairs={{0,4},{1,5},{2,6},{3,7},{4,8},{5,9},{6,10},{7,11},{8,12},{9,13},{1... | collective-permute-start | bytes 3145736 | tf_op jit(solution)/shard_map/ppermute | solution.py:285
  24.3 128.3 %all-gather.3.cloned.1.call-start = ((), (), s32[]{:S(2)}) async-start(), calls=%async_computation.1 | async-start | bytes 5242880 | tf_op jit(solution)/shard_map/all_gather | solution.py:337
  46.4 16.9 %collective-permute-start.4 = (bf16[1024,512]{1,0:T(8,128)(2,1)}, bf16[1024,512]{1,0:T(8,128)(2,1)}, u32[]{:S(2)}, u32[]{:S(2)}) collective-permute-start(bf16[1024,512]{1,0:T(8,128)(2,1)} %collective-permute-done.3.p1), channel_id=1, source_target_pairs={{4,8},{5,9},{6,10},{7,11},{8,12},{9,13},{10,14},{11,15},{20,24},{2... | collective-permute-start | bytes 3145736 | tf_op jit(solution)/shard_map/ppermute | solution.py:285
  48.1 54.0 %collective-permute-start.2 = (bf16[1024,1024]{1,0:T(8,128)(2,1)}, bf16[1024,1024]{1,0:T(8,128)(2,1)}, u32[]{:S(2)}, u32[]{:S(2)}) collective-permute-start(bf16[1024,1024]{1,0:T(8,128)(2,1)} %collective-permute-done.1.refs_2_.l2), channel_id=1, source_target_pairs={{2,3},{6,7},{7,6},{8,9},{10,11},{11,10},{12,13},{13,12},{14,15},{1... | collective-permute-start | bytes 6291464 | tf_op jit(solution)/shard_map/ppermute | solution.py:285
  62.5 39.6 %collective-permute-start.8 = (bf16[1024,1024]{1,0:T(8,128)(2,1)}, bf16[1024,1024]{1,0:T(8,128)(2,1)S(1)}, u32[]{:S(2)}, u32[]{:S(2)}) collective-permute-start(bf16[1024,1024]{1,0:T(8,128)(2,1)} %collective-permute-done.5.refs_1_._in), channel_id=1, source_target_pairs={{5,7},{10,8},{21,23},{26,24}} | collective-permute-start | bytes 6291464 | tf_op jit(solution)/shard_map/ppermute | solution.py:285
  63.3 40.1 %copy-start.4 = (bf16[1024,1024]{1,0:T(8,128)(2,1)S(1)}, bf16[1024,1024]{1,0:T(8,128)(2,1)}, u32[]{:S(2)}) copy-start(bf16[1024,1024]{1,0:T(8,128)(2,1)} %l0.7) | copy-start | bytes 6291460
  63.4 3.5 %collective-permute-start.6 = (bf16[1024,512]{1,0:T(8,128)(2,1)}, bf16[1024,512]{1,0:T(8,128)(2,1)S(1)}, u32[]{:S(2)}, u32[]{:S(2)}) collective-permute-start(bf16[1024,512]{1,0:T(8,128)(2,1)} %shard_map.67.p2), channel_id=1, source_target_pairs={{8,12},{9,13},{10,14},{11,15},{24,28},{25,29},{26,30},{27,31}} | collective-permute-start | bytes 3145736 | tf_op jit(solution)/shard_map/ppermute | solution.py:285
  65.5 36.6 %collective-permute-start.7 = (bf16[512,1024]{1,0:T(8,128)(2,1)S(1)}, bf16[512,1024]{1,0:T(8,128)(2,1)S(1)}, u32[]{:S(2)}, u32[]{:S(2)}) collective-permute-start(bf16[512,1024]{1,0:T(8,128)(2,1)S(1)} %slice.8), channel_id=1, source_target_pairs={{4,0},{5,1},{6,2},{8,4},{9,5},{10,6},{11,7},{20,16},{21,17},{22,18... | collective-permute-start | bytes 3145736 | tf_op jit(solution)/shard_map/ppermute | solution.py:285
  102.1 1.3 copy-start
  103.4 1.2 copy-start.14
  107.3 1.0 copy-start.9
  108.2 1.0 copy-start.21
  109.2 1.0 copy-start.24
  110.2 3.6 %copy-start.5 = (bf16[1024,1024]{1,0:T(8,128)(2,1)S(1)}, bf16[1024,1024]{1,0:T(8,128)(2,1)}, u32[]{:S(2)}) copy-start(bf16[1024,1024]{1,0:T(8,128)(2,1)} %l0.7) | copy-start | bytes 6291460
  110.2 175.7 %reduce-scatter.2.cloned.1.call-start = ((), (), s32[]{:S(2)}) async-start(), calls=%async_computation.3 | async-start | bytes 2621440 | tf_op jit(solution)/shard_map/reduce_scatter | solution.py:381
  110.3 3.5 %copy-start.10 = (bf16[512,1024]{1,0:T(8,128)(2,1)S(1)}, bf16[512,1024]{1,0:T(8,128)(2,1)}, u32[]{:S(2)}) copy-start(bf16[512,1024]{1,0:T(8,128)(2,1)} %copy-done.9) | copy-start | bytes 3145732
  110.3 6.8 %collective-permute-start.9 = (bf16[512,1024]{1,0:T(8,128)(2,1)}, bf16[512,1024]{1,0:T(8,128)(2,1)S(1)}, u32[]{:S(2)}, u32[]{:S(2)}) collective-permute-start(bf16[512,1024]{1,0:T(8,128)(2,1)} %copy-done.24), channel_id=1, source_target_pairs={{8,12},{9,13},{10,14},{11,15},{12,8},{13,9},{14,10},{15,11},{24,28... | collective-permute-start | bytes 3145736 | tf_op jit(solution)/shard_map/ppermute | solution.py:285
  112.4 29.3 %collective-permute-start.10 = (bf16[512,1024]{1,0:T(8,128)(2,1)S(1)}, bf16[512,1024]{1,0:T(8,128)(2,1)S(1)}, u32[]{:S(2)}, u32[]{:S(2)}) collective-permute-start(bf16[512,1024]{1,0:T(8,128)(2,1)S(1)} %slice.7), channel_id=1, source_target_pairs={{4,0},{5,1},{6,2},{8,4},{9,5},{10,6},{11,7},{20,16},{21,17},{22,18... | collective-permute-start | bytes 3145736 | tf_op jit(solution)/shard_map/ppermute | solution.py:285
  115.7 1.3 copy-start.17
  142.8 2.1 copy-start.8
  142.8 9.8 %copy-start.1 = (bf16[1024,1024]{1,0:T(8,128)(2,1)S(1)}, bf16[1024,1024]{1,0:T(8,128)(2,1)}, u32[]{:S(2)}) copy-start(bf16[1024,1024]{1,0:T(8,128)(2,1)} %copy-done) | copy-start | bytes 6291460
  144.9 94.3 %collective-permute-start.11 = (bf16[1024,1024]{1,0:T(8,128)(2,1)}, bf16[1024,1024]{1,0:T(8,128)(2,1)}, u32[]{:S(2)}, u32[]{:S(2)}) collective-permute-start(bf16[1024,1024]{1,0:T(8,128)(2,1)} %constant_dynamic-update-slice_fusion.h2), channel_id=1, source_target_pairs={{4,0},{5,1},{6,2},{7,3},{20,16},{21,17},{22,18},{23,19}} | collective-permute-start | bytes 6291464 | tf_op jit(solution)/shard_map/ppermute | solution.py:285
  146.1 98.4 %collective-permute-start.14 = (bf16[1024,1024]{1,0:T(8,128)(2,1)}, bf16[1024,1024]{1,0:T(8,128)(2,1)}, u32[]{:S(2)}, u32[]{:S(2)}) collective-permute-start(bf16[1024,1024]{1,0:T(8,128)(2,1)} %constant_dynamic-update-slice_fusion.h2), channel_id=1, source_target_pairs={{0,2},{5,7},{16,18},{21,23}} | collective-permute-start | bytes 6291464 | tf_op jit(solution)/shard_map/ppermute | solution.py:285
  148.8 90.4 %collective-permute-start.12 = (bf16[512,1024]{1,0:T(8,128)(2,1)}, bf16[512,1024]{1,0:T(8,128)(2,1)}, u32[]{:S(2)}, u32[]{:S(2)}) collective-permute-start(bf16[512,1024]{1,0:T(8,128)(2,1)} %get-tuple-element.20._dep0), channel_id=1, source_target_pairs={{4,0},{5,1},{6,2},{7,3},{12,8},{13,9},{14,10},{15,11},{20,16},{21,... | collective-permute-start | bytes 3145736 | tf_op jit(solution)/shard_map/ppermute | solution.py:285
  150.1 89.1 %collective-permute-start.13 = (bf16[512,1024]{1,0:T(8,128)(2,1)}, bf16[512,1024]{1,0:T(8,128)(2,1)}, u32[]{:S(2)}, u32[]{:S(2)}) collective-permute-start(bf16[512,1024]{1,0:T(8,128)(2,1)} %get-tuple-element.21._dep), channel_id=1, source_target_pairs={{8,0},{9,1},{10,2},{11,3},{12,4},{13,5},{14,6},{15,7},{24,16},{25,... | collective-permute-start | bytes 3145736 | tf_op jit(solution)/shard_map/ppermute | solution.py:285
  152.6 1.2 copy-start.11
  153.8 2.2 copy-start.15
  156.0 1.6 copy-start.19
  157.6 1.0 copy-start.20
  163.4 1.4 copy-start.12
  164.8 74.4 %copy-start.2 = (bf16[1024,1024]{1,0:T(8,128)(2,1)}, bf16[1024,1024]{1,0:T(8,128)(2,1)S(1)}, u32[]{:S(2)}) copy-start(bf16[1024,1024]{1,0:T(8,128)(2,1)S(1)} %get-tuple-element.22.refs_0_) | copy-start | bytes 6291460
  239.2 5.4 %copy-start.3 = (bf16[1024,1024]{1,0:T(8,128)(2,1)S(1)}, bf16[1024,1024]{1,0:T(8,128)(2,1)}, u32[]{:S(2)}) copy-start(bf16[1024,1024]{1,0:T(8,128)(2,1)} %get-tuple-element.25.x1) | copy-start | bytes 6291460
  239.2 27.9 %collective-permute-start.16 = (bf16[1024,1024]{1,0:T(8,128)(2,1)}, bf16[1024,1024]{1,0:T(8,128)(2,1)}, u32[]{:S(2)}, u32[]{:S(2)}) collective-permute-start(bf16[1024,1024]{1,0:T(8,128)(2,1)} %get-tuple-element.27.h3), channel_id=1, source_target_pairs={{0,2},{16,18}} | collective-permute-start | bytes 6291464 | tf_op jit(solution)/shard_map/ppermute | solution.py:285
  249.5 23.4 %copy-start.18 = (f32[512,1024]{1,0:T(8,128)S(1)}, f32[512,1024]{1,0:T(8,128)}, u32[]{:S(2)}) copy-start(f32[512,1024]{1,0:T(8,128)} %copy-done.17) | copy-start | bytes 6291460
  249.5 23.4 %copy-start.23 = (s32[8]{0:T(128)S(1)}, s32[8]{0:T(128)}, u32[]{:S(2)}) copy-start(s32[8]{0:T(128)} %structure.1) | copy-start | bytes 100
  249.5 40.1 %collective-permute-start.15 = (bf16[2048,1024]{1,0:T(8,128)(2,1)}, bf16[2048,1024]{1,0:T(8,128)(2,1)}, u32[]{:S(2)}, u32[]{:S(2)}) collective-permute-start(bf16[2048,1024]{1,0:T(8,128)(2,1)} %maximum_select_fusion), channel_id=1, source_target_pairs={{0,1},{2,3},{5,4},{7,6},{8,9},{10,11},{16,17},{18,19},{21,20},{23,... | collective-permute-start | bytes 12582920 | tf_op jit(solution)/shard_map/ppermute | solution.py:285
  270.2 31.3 %collective-permute-start.17 = (bf16[1024,1024]{1,0:T(8,128)(2,1)}, bf16[1024,1024]{1,0:T(8,128)(2,1)}, u32[]{:S(2)}, u32[]{:S(2)}) collective-permute-start(bf16[1024,1024]{1,0:T(8,128)(2,1)} %broadcast_select_fusion), channel_id=1, source_target_pairs={{0,1},{2,3},{16,17},{18,19}} | collective-permute-start | bytes 6291464 | tf_op jit(solution)/shard_map/ppermute | solution.py:285
  285.9 3.6 %copy-start.6 = (bf16[1024,1024]{1,0:T(8,128)(2,1)S(1)}, bf16[1024,1024]{1,0:T(8,128)(2,1)}, u32[]{:S(2)}) copy-start(bf16[1024,1024]{1,0:T(8,128)(2,1)} %l0.7) | copy-start | bytes 6291460
  285.9 1.4 copy-start.16
  287.3 1.0 copy-start.22
  301.5 2.2 copy-start.7
Sparse Core Ops, SparseCore 0:
  24.5 22.6 all-gather.4
  110.3 42.2 all-gather.2
  244.7 41.1 reduce-scatter.1

commit v4 on v3

v4 whole, which is shorter than its diff:
```python
import functools

import jax
import jax.numpy as jnp
from jax import lax
from jax.experimental import pallas as pl
from jax.experimental.pallas import tpu as pltpu
from jax.sharding import PartitionSpec as P

BLOCK = 128
AXES = ("fields", "row", "col")
BF16 = jnp.bfloat16
F32 = jnp.float32
TILE = 256
N = 4
VMEM_BYTES = 40 * 1024 * 1024


def inner_dot(left_part, right_part):
    return lax.dot_general(
        left_part, right_part, (((0,), (0,)), ((), ())), preferred_element_type=F32
    )


def dot(a, b):
    return jnp.dot(a, b, preferred_element_type=F32)


def mask_panel(panel, structure):
    kept_rows = jnp.repeat(structure, BLOCK)[:, None] > 0
    return kept_rows, jnp.where(kept_rows, panel, jnp.zeros_like(panel))


def gather_plan(root_inverse, child_inverse, panel, structure):
    kept_rows, panel_kept = mask_panel(panel, structure)
    root_full, child_rows, panel_full = (
        lax.all_gather(root_inverse, "col", axis=1, tiled=True),
        lax.all_gather(child_inverse, "col", axis=1, tiled=True),
        lax.all_gather(panel_kept, "col", axis=1, tiled=True),
    )
    root_sum = lax.psum_scatter(
        inner_dot(root_full, root_inverse), "row", scatter_dimension=0, tiled=True
    )
    sigma_root = root_sum.astype(BF16)
    sigma_rows = lax.all_gather(sigma_root, "col", axis=1, tiled=True)
    cross_sum = jnp.dot(
        sigma_rows,
        lax.all_gather(panel_kept, "row", axis=0, tiled=True),
        preferred_element_type=F32,
    )
    sigma_cross = jnp.where(kept_rows, -cross_sum, jnp.zeros_like(cross_sum)).astype(BF16)
    sigma_child = lax.psum_scatter(
        (inner_dot(child_rows, child_inverse) - inner_dot(panel_full, sigma_cross)).astype(BF16),
        "row",
        scatter_dimension=0,
        tiled=True,
    ).astype(F32)
    return (sigma_root, sigma_cross, sigma_child)


def position():
    return lax.axis_index("row"), lax.axis_index("col")


def start(src, dst, sem):
    pltpu.make_async_copy(src, dst, sem).start()


def wait(src, dst, sem):
    pltpu.make_async_copy(src, dst, sem).wait()


def start_picked(refs, index, dst, sem):
    for m, ref in enumerate(refs):

        @pl.when(index == m)
        def _():
            start(ref, dst, sem)


def tile(i):
    return pl.ds(pl.multiple_of(i * TILE, TILE), TILE)


def far_block(r):
    return jnp.where(r == 1, 0, r ^ 3)


def product_kernel(
    structure, l0, l1, l2, l3, p0, p1, p2, p3, *refs, deps, gated
):
    t_ref, tt_ref, far_ref = refs[deps + gated : deps + gated + 3]
    rows, panels, acc, row_sems, panel_sems = refs[deps + 2 * gated + 3 :]
    r, c = position()
    blocks = panels.shape[1] // BLOCK
    for m, ref in enumerate((l0, l1, l2, l3)):
        j = c ^ m

        @pl.when(j <= r)
        def _():
            start(ref, rows.at[r - j], row_sems.at[r - j])

    for s, ref in enumerate((p0, p1, p2, p3)):

        @pl.when(s <= r)
        def _():
            start(ref, panels.at[s], panel_sems.at[s])

    for s in range(N):

        @pl.when(s <= r)
        def _():
            wait(p0, panels.at[s], panel_sems.at[s])
            for b in range(blocks):

                @pl.when(structure[(r - s) * blocks + b] == 0)
                def _():
                    panels[s, b * BLOCK : (b + 1) * BLOCK, :] = jnp.zeros(
                        (BLOCK, panels.shape[2]), BF16
                    )

            wait(l0, rows.at[s], row_sems.at[s])

            @pl.loop(0, acc.shape[0] // TILE)
            def _(i):
                term = dot(rows[s, tile(i), :], panels[s])
                if s > 0:
                    term = term + acc[tile(i), :]
                acc[tile(i), :] = term

    @pl.loop(0, acc.shape[0] // TILE)
    def _(i):
        value = acc[tile(i), :]
        t_ref[tile(i), :] = value.astype(BF16)
        tt_ref[:, tile(i)] = value.T.astype(BF16)

    @pl.when(r >= 1)
    def _():
        slot = r - far_block(r)

        @pl.loop(0, tt_ref.shape[0] // TILE)
        def _(i):
            far_ref[tile(i), :] = dot(tt_ref[tile(i), :], rows[slot]).astype(BF16)


def cross_kernel(l0, l1, l2, l3, tt_ref, near_ref, own_ref, blocks, sems):
    r, c = position()
    refs = (l0, l1, l2, l3)

    @pl.when(r == 3)
    def _():
        start_picked(refs, r ^ 1 ^ c, blocks.at[0], sems.at[0])

    start_picked(refs, r ^ c, blocks.at[1], sems.at[1])

    @pl.when(r == 3)
    def _():
        wait(l0, blocks.at[0], sems.at[0])

        @pl.loop(0, tt_ref.shape[0] // TILE)
        def _(i):
            near_ref[tile(i), :] = dot(tt_ref[tile(i), :], blocks[0]).astype(BF16)

    wait(l0, blocks.at[1], sems.at[1])

    @pl.loop(0, tt_ref.shape[0] // TILE)
    def _(i):
        own_ref[tile(i), :] = dot(tt_ref[tile(i), :], blocks[1])


def onward_kernel(l0, l1, l2, l3, tt_ref, far_ref, *refs, deps):
    onward_ref, _, block, sem = refs[deps:]
    r, c = position()

    @pl.when(r >= 2)
    def _():
        start_picked((l0, l1, l2, l3), r ^ 2 ^ c, block, sem)
        wait(l0, block, sem)

        @pl.loop(0, tt_ref.shape[0] // TILE)
        def _(i):
            term = dot(tt_ref[tile(i), :], block[...])
            onward_ref[tile(i), :] = (term + far_ref[tile(i), :].astype(F32)).astype(BF16)


def child_kernel(
    tt_ref, t_row_ref, child_ref, child_row_ref, _dep, far_ref, near_ref, onward_ref, own_ref, child_t
):
    r, _ = position()
    w = child_ref.shape[1]
    child_t[...] = child_ref[...].astype(F32).T.astype(BF16)
    for flip, ref in ((3, far_ref), (1, near_ref), (2, onward_ref), (0, own_ref)):
        columns = pl.ds(pl.multiple_of((r ^ flip) * w, w), w)

        @pl.loop(0, w // TILE)
        def _(i):
            term = dot(tt_ref[tile(i), :], t_row_ref[:, columns])
            term = term + dot(child_t[tile(i), :], child_row_ref[:, columns])
            ref[tile(i), :] = term.astype(ref.dtype)


def child_onward_kernel(own_ref, far_ref, _dep0, _dep1, _dep2, out_ref):
    out_ref[...] = (own_ref[...] + far_ref[...].astype(F32)).astype(BF16)


def diagonal_kernel(l0, l1, l2, l3, _dep, acc_ref, left, held, sems):
    r, c = position()

    @pl.when(c <= r)
    def _():
        start_picked((l0, l1, l2, l3), r ^ c, left, sems.at[0])
        start(l0, held, sems.at[1])
        wait(l0, left, sems.at[0])
        wait(l0, held, sems.at[1])

        @pl.loop(0, acc_ref.shape[0] // TILE)
        def _(i):
            acc_ref[tile(i), :] = inner_dot(left[:, tile(i)], held[...])

    @pl.when(c > r)
    def _():
        acc_ref[...] = jnp.zeros_like(acc_ref)


def pick_kernel(h1, h2, h3, x1, x2, x3, _dep, out_ref, sems):
    r, c = position()
    rows = h1.shape[0]
    for refs, holds in (((h1, h2, h3), c == r), ((x1, x2, x3), c == (r ^ 2))):

        @pl.when(holds)
        def _():
            for act in (start, wait):
                for s, ref in enumerate(refs):
                    act(ref, out_ref.at[s * rows : (s + 1) * rows], sems.at[s])


def root_kernel(acc_ref, h1, h2, h3, x1, x2, x3, beside, out_ref, acc, left, held, left_sems, held_sems):
    r, c = position()
    rows = h1.shape[0]
    refs = ((h1, x1), (h2, x2), (h3, x3))
    needed = [(r + s < N) & (c <= r + s) for s in (1, 2, 3)]
    for s, (own, other) in enumerate(refs):

        @pl.when(needed[s])
        def _():
            places = (own, other, beside.at[s * rows : (s + 1) * rows])
            start_picked(places, source(r, c), left.at[s], left_sems.at[s])
            start(own, held.at[s], held_sems.at[s])

    acc[...] = acc_ref[...]
    for s in range(3):

        @pl.when(needed[s])
        def _():
            wait(h1, left.at[s], left_sems.at[s])
            wait(h1, held.at[s], held_sems.at[s])

            @pl.loop(0, acc.shape[0] // TILE)
            def _(i):
                acc[tile(i), :] += inner_dot(left[s, :, tile(i)], held[s])

    out_ref[...] = acc[...].astype(BF16)


def source(r, c):
    return jnp.where(c == r, 0, jnp.where(c == (r ^ 2), 1, 2))


def cross_end_kernel(structure, own_ref, far_ref, near_ref, last_ref, out_ref):
    first = position()[0] == 0
    for b in range(own_ref.shape[1] // BLOCK):
        rows = slice(b * BLOCK, (b + 1) * BLOCK)
        total = own_ref[:, rows] + near_ref[:, rows].astype(F32) + last_ref[:, rows].astype(F32)
        total = total + jnp.where(first, far_ref[:, rows].astype(F32), jnp.zeros_like(total))
        kept = structure[b] > 0
        out_ref[rows, :] = jnp.where(kept, -total.T, jnp.zeros_like(total.T)).astype(BF16)


def child_end_kernel(own_ref, near_ref, last_ref, out_ref):
    total = own_ref[...] + near_ref[...].astype(F32) + last_ref[...].astype(F32)
    out_ref[...] = total.T


ANY = pl.BlockSpec(memory_space=pl.ANY)
VMEM = pl.BlockSpec(memory_space=pltpu.VMEM)
SMEM = pl.BlockSpec(memory_space=pltpu.SMEM)


def local_call(kernel, in_specs, outs, scratch, *args, gated=0, out_specs=None):
    first = len(args) - gated
    outs = outs + [jax.ShapeDtypeStruct(x.shape, x.dtype) for x in args[first:]]
    return pl.pallas_call(
        kernel,
        out_shape=outs,
        in_specs=in_specs + [ANY] * (len(args) - len(in_specs)),
        out_specs=(out_specs or [VMEM] * (len(outs) - gated)) + [ANY] * gated,
        scratch_shapes=scratch,
        input_output_aliases={first + i: len(outs) - gated + i for i in range(gated)},
        compiler_params=pltpu.CompilerParams(vmem_limit_bytes=VMEM_BYTES),
        cost_estimate=pl.CostEstimate(flops=1, bytes_accessed=1, transcendentals=0),
    )(*args)


def together(*arrays, earlier=()):
    k = len(arrays)
    return pl.pallas_call(
        lambda *refs: None,
        out_shape=[jax.ShapeDtypeStruct(x.shape, x.dtype) for x in arrays],
        in_specs=[ANY] * (k + len(earlier)),
        out_specs=[ANY] * k,
        input_output_aliases={i: i for i in range(k)},
    )(*arrays, *earlier)


def square_plan(fields):
    n = N

    def move(x, target):
        pairs = []
        for f in range(fields):
            for r in range(n):
                for c in range(n):
                    to = target(r, c)
                    if to is not None and 0 <= to[0] < n:
                        pairs.append(((f * n + r) * n + c, (f * n + to[0]) * n + to[1]))
        return lax.ppermute(x, AXES, pairs)

    def up(x, s):
        return move(x, lambda r, c: (r + 1, c) if r >= s - 1 else None)

    def down(x, s):
        def target(r, c):
            k = r + s - 1
            return (r - 1, c) if k < n and c <= k else None

        return move(x, target)

    def on_device(root_inverse, child_inverse, panel, structure):
        h, w = panel.shape
        half = h // 2
        lower = lambda r, c: c <= r
        shape = jax.ShapeDtypeStruct
        dma = pltpu.SemaphoreType.DMA
        t_block, child_block = shape((w, h), BF16), shape((w, w), BF16)

        panel_1 = up(panel, 1)
        below_1a = down(root_inverse[:half], 1)
        root_across = move(root_inverse, lambda r, c: (r, c ^ 2) if lower(r, c) else None)
        root_beside = move(root_inverse, lambda r, c: (r, c ^ 1) if lower(r, c) else None)
        structure_all = lax.all_gather(structure, "row", tiled=True)
        child_row = lax.all_gather(child_inverse, "col", axis=1, tiled=True)
        panel_1, lower_half = together(
            panel_1, root_inverse[half:], earlier=(below_1a, root_beside)
        )
        panel_2 = up(panel_1, 2)
        below_1b = down(lower_half, 1)
        below_2a = down(below_1a, 2)
        (panel_2,) = together(panel_2, earlier=(root_across,))
        panel_3 = up(panel_2, 3)
        root_both = move(root_across, lambda r, c: (r, c ^ 1) if lower(r, c ^ 2) else None)
        below_2b = down(below_1b, 2)
        below_1 = jnp.concatenate((below_1a, below_1b), 0)
        across_1 = move(below_1, lambda r, c: (r, c ^ 2) if r == c and r in (1, 2) else None)

        root_row = (root_inverse, root_beside, root_across, root_both)
        panels = (panel, panel_1, panel_2, panel_3)
        t, t_t, far_part, below_2a, below_2b, root_across_late = local_call(
            functools.partial(product_kernel, deps=1, gated=3),
            [SMEM] + [ANY] * 8,
            [shape((h, w), BF16), t_block, t_block],
            [
                pltpu.VMEM((n, h, h), BF16),
                pltpu.VMEM((n, h, w), BF16),
                pltpu.VMEM((h, w), F32),
                dma((n,)),
                dma((n,)),
            ],
            structure_all,
            *root_row,
            *panels,
            across_1,
            below_2a,
            below_2b,
            root_across,
            gated=3,
        )
        root_row = (root_inverse, root_beside, root_across_late, root_both)
        t_row = lax.all_gather(t, "col", axis=1, tiled=True)
        far = move(far_part, lambda r, c: (r ^ 1, c) if r >= 1 else None)
        below_3a = down(below_2a, 3)
        below_2 = jnp.concatenate((below_2a, below_2b), 0)
        across_2 = move(below_2, lambda r, c: (r, c ^ 2) if r == c and r in (0, 1) else None)
        across_3 = move(root_across_late, lambda r, c: (0, 2) if (r, c) == (3, 2) else None)

        near_part, own = local_call(
            cross_kernel,
            [ANY] * 4 + [VMEM],
            [t_block, shape((w, h), F32)],
            [pltpu.VMEM((2, h, h), BF16), dma((2,))],
            *root_row,
            t_t,
        )
        onward, below_2b = local_call(
            functools.partial(onward_kernel, deps=5),
            [ANY] * 4 + [VMEM, VMEM],
            [t_block],
            [pltpu.VMEM((h, h), BF16), dma],
            *root_row,
            t_t,
            far,
            near_part,
            across_2,
            across_3,
            below_3a,
            below_2b,
            gated=1,
        )
        last = move(onward, lambda r, c: (r - 2, c))
        near = move(near_part, lambda r, c: (r - 1, c) if r == 3 else None)
        below_3b = down(below_2b, 3)

        far_part, child_near_part, child_on, child_own = local_call(
            child_kernel,
            [VMEM] * 4,
            [child_block, child_block, shape((w, w), F32), shape((w, w), F32)],
            [pltpu.VMEM((w, w), BF16)],
            t_t,
            t_row,
            child_inverse,
            child_row,
            onward,
        )
        child_far = move(far_part, lambda r, c: (r ^ 1, c))
        (root_sum,) = local_call(
            diagonal_kernel,
            [],
            [shape((h, h), F32)],
            [pltpu.VMEM((h, h), BF16), pltpu.VMEM((h, h), BF16), dma((2,))],
            *root_row,
            far_part,
        )
        (child_onward,) = local_call(
            child_onward_kernel,
            [VMEM] * 2,
            [child_block],
            [],
            child_on,
            child_far,
            near,
            last,
            below_3b,
        )
        child_last = move(child_onward, lambda r, c: (r ^ 2, c))
        child_near = move(child_near_part, lambda r, c: (r ^ 1, c))

        below_3 = jnp.concatenate((below_3a, below_3b), 0)
        held = (below_1, below_2, below_3)
        across = (across_1, across_2, across_3)
        (picked,) = local_call(
            pick_kernel,
            [],
            [shape((3 * h, h), BF16)],
            [dma((3,))],
            *held,
            *across,
            child_onward,
            out_specs=[ANY],
        )
        beside = move(picked, lambda r, c: (r, c ^ 1) if r in (c, c ^ 2) and r < 3 else None)
        (sigma_cross,) = local_call(
            cross_end_kernel,
            [SMEM] + [VMEM] * 4,
            [shape((h, w), BF16)],
            [],
            structure,
            own,
            far,
            near,
            last,
        )
        (sigma_root,) = local_call(
            root_kernel,
            [VMEM],
            [shape((h, h), BF16)],
            [
                pltpu.VMEM((h, h), F32),
                pltpu.VMEM((3, h, h), BF16),
                pltpu.VMEM((3, h, h), BF16),
                dma((3,)),
                dma((3,)),
            ],
            root_sum,
            *held,
            *across,
            beside,
        )
        (sigma_child,) = local_call(
            child_end_kernel,
            [VMEM] * 3,
            [shape((w, w), F32)],
            [],
            child_own,
            child_near,
            child_last,
        )
        return (sigma_root, sigma_cross, sigma_child)

    return on_device


def solution(mesh):
    square = mesh.shape["row"] == N and mesh.shape["col"] == N
    spec = P(("fields", "row"), "col")
    return jax.shard_map(
        square_plan(mesh.shape["fields"]) if square else gather_plan,
        mesh=mesh,
        in_specs=(spec, spec, spec, P(("fields", "row"))),
        out_specs=(spec, spec, spec),
        check_vma=False,
    )
```

time: 318 us -> 396 us (1.25)
  the two profiles are of different devices: /device:TPU:0 before, /device:TPU:2 now
where the time goes in v4:
time: 396 us; the launch traced here: 395 us
  waiting for transfers between devices  138 us (35%)
  Pallas kernels  93.2 us (24%)
  blocking collectives  77 us (19%)
  starting transfers between devices  36.9 us (9%)
  local copies, waits for them, and re-layouts  34.7 us (9%)
  between operations  15.2 us (4%)
    ppermute x22, waiting for transfers between devices, move(): return lax.ppermute(x, AXES, pairs)  138 us
    pallas_call x10, Pallas kernels, local_call(): pl.pallas_call(kernel, out_shape=outs, in_specs=in_specs + [ANY] * (len(a...  93.2 us
    unnamed x1, blocking collectives  77 us
    ppermute x22, starting transfers between devices, move(): return lax.ppermute(x, AXES, pairs)  36.8 us
    unnamed x73, local copies, waits for them, and re-layouts  27 us
  transfers between devices with their start and end apart: 24, of which 7 were waited for; matrix products, arithmetic and copies ran while one was open for 4% of the time, Pallas kernels for 4%

profile of v4, /device:TPU:2, one launch (start us, length us, event | category | flops | bytes accessed | tf_op | source)
XLA Modules:
  0.0 394.9 jit_solution(15291880217760322793)
XLA Ops:
  7.2 2.1 collective-permute-start
  9.4 2.7 fusion
  12.0 1.7 collective-permute-start.4
  13.7 3.2 collective-permute-start.3
  16.9 1.3 collective-permute-start.1
  18.2 21.7 %collective-permute-done.3.refs_0_ = bf16[1024,512]{1,0:T(8,128)(2,1)S(1)} collective-permute-done((bf16[1024,512]{1,0:T(8,128)(2,1)}, bf16[1024,512]{1,0:T(8,128)(2,1)S(1)}, u32[]{:S(2)}, u32[]{:S(2)}) %collective-permute-start.3) | collective-permute-done | bytes 1048608 | tf_op jit(solution)/shard_map/ppermute | solution.py:326
  39.9 1.0 copy-done.16
  40.9 1.8 collective-permute-start.7
  42.8 2.3 constant_dynamic-update-slice_fusion.1
  45.0 1.6 collective-permute-start.5
  46.7 2.7 collective-permute-start.2
  49.4 2.3 constant_dynamic-update-slice_fusion.h1
  51.6 2.1 collective-permute-start.8
  53.8 1.3 collective-permute-start.9
  55.1 0.7 collective-permute-start.6
  55.8 1.3 collective-permute-start.10
  57.1 0.6 dynamic-slice
  58.4 0.2 dynamic-update-slice
  58.6 77.0 %all-reduce.structure = s32[32]{0:T(128)S(1)} all-reduce(s32[32]{0:T(128)S(1)} %dynamic-update-slice), channel_id=1, replica_groups=mesh['fields'=2,'row'=4,'col'=4] {'row'}, use_global_device_ids=true, to_apply=%add | all-reduce | flops 32 | bytes 256
  135.6 1.7 copy.21.refs_3_
  137.4 1.0 copy-done.27
  138.4 1.2 copy-done.28
  139.6 4.6 %shard_map.69 = (bf16[1024,512]{1,0:T(8,128)(2,1)S(1)}, bf16[512,1024]{1,0:T(8,128)(2,1)S(1)}, bf16[512,1024]{1,0:T(8,128)(2,1)S(1)}, bf16[512,1024]{1,0:T(8,128...) custom-call(s32[32]{0:T(128)S(1)} %all-reduce.structure, ...), custom_call_target="tpu_custom_call", output_to_operand_aliasing={{3}: (10, {}), {4}: (11, {}), {5}: (12, {})} | custom-call | flops 1 | bytes 1 | tf_op jit(solution)/shard_map/pallas_call | solution.py:292
  144.2 1.3 copy-done.1
  145.5 1.0 copy-done.25
  146.5 1.0 copy-done.30
  147.5 1.4 constant_dynamic-update-slice_fusion.3
  148.9 1.3 constant_dynamic-update-slice_fusion.2.h2
  150.2 1.3 collective-permute-start.12
  151.5 1.3 collective-permute-start.13
  152.8 1.3 collective-permute-start.14
  154.2 1.3 collective-permute-start.11
  155.5 1.9 shard_map.70
  157.4 1.3 copy-done.20
  158.7 44.8 %collective-permute-done.14.refs_3_ = bf16[512,1024]{1,0:T(8,128)(2,1)S(1)} collective-permute-done((bf16[512,1024]{1,0:T(8,128)(2,1)}, bf16[512,1024]{1,0:T(8,128)(2,1)S(1)}, u32[]{:S(2)}, u32[]{:S(2)}) %collective-permute-start.14) | collective-permute-done | bytes 1048608 | tf_op jit(solution)/shard_map/ppermute | solution.py:326
  203.5 18.6 %collective-permute-done.11.far_ref = bf16[512,1024]{1,0:T(8,128)(2,1)S(1)} collective-permute-done((bf16[512,1024]{1,0:T(8,128)(2,1)S(1)}, bf16[512,1024]{1,0:T(8,128)(2,1)S(1)}, u32[]{:S(2)}, u32[]{:S(2)}) %collective-permute-start.11) | collective-permute-done | bytes 1048608 | tf_op jit(solution)/shard_map/ppermute | solution.py:326
  222.1 1.3 copy-done.4
  223.4 0.6 copy-done.6
  224.0 1.0 shard_map.71
  225.0 1.0 copy-done.11
  226.0 1.0 copy-done.13
  227.0 1.3 collective-permute-start.15
  228.3 1.7 collective-permute-start.17
  229.9 1.3 collective-permute-start.18
  231.3 2.2 copy-done.15
  233.5 1.6 copy-done.19
  235.1 1.0 copy-done.22
  236.1 5.1 %shard_map.72 = (bf16[512,512]{1,0:T(8,128)(2,1)S(1)}, bf16[512,512]{1,0:T(8,128)(2,1)}, f32[512,512]{1,0:T(8,128)S(1)}, f32[512,512]{1,0:T(8,128)S(1)}) custom-call(bf16[512,1024]{1,0:T(8,128)(2,1)S(1)} %get-tuple-element.22.tt_ref, bf16[1024,2048]{1,0:T(8,128)(2,1)S(1)} %copy-done.15, bf16[512,512]{1,0:T(8,128)(2,1)S(1)} %copy-done.22, ...), custom_call_target="tpu_custom_call" | custom-call | flops 1 | bytes 1 | tf_op jit(solution)/shard_map/pallas_call | solution.py:292
  241.2 3.7 collective-permute-start.16
  244.9 32.0 %collective-permute-done.15._dep2 = bf16[512,1024]{1,0:T(8,128)(2,1)} collective-permute-done((bf16[512,1024]{1,0:T(8,128)(2,1)}, bf16[512,1024]{1,0:T(8,128)(2,1)}, u32[]{:S(2)}, u32[]{:S(2)}) %collective-permute-start.15) | collective-permute-done | bytes 1048608 | tf_op jit(solution)/shard_map/ppermute | solution.py:326
  277.0 1.4 constant_dynamic-update-slice_fusion.4.h3
  278.4 5.6 %collective-permute-done.16.far_ref = bf16[512,512]{1,0:T(8,128)(2,1)S(1)} collective-permute-done((bf16[512,512]{1,0:T(8,128)(2,1)S(1)}, bf16[512,512]{1,0:T(8,128)(2,1)S(1)}, u32[]{:S(2)}, u32[]{:S(2)}) %collective-permute-start.16) | collective-permute-done | bytes 524320 | tf_op jit(solution)/shard_map/ppermute | solution.py:326
  284.1 0.1 shard_map.74._dep
  284.2 1.5 copy-done.5
  285.7 0.6 copy-done.7
  286.3 64.7 %shard_map.75 = bf16[3072,1024]{1,0:T(8,128)(2,1)} custom-call(bf16[1024,1024]{1,0:T(8,128)(2,1)} %constant_dynamic-update-slice_fusion.h1, bf16[1024,1024]{1,0:T(8,128)(2,1)S(1)} %copy-done.10, bf16[1024,1024]{1,0:T(8,128)(2,1)S(1)} %constant_dynamic-update-slice_fusion.4.h3, bf16[1024,1024]{1,0:T(8,128)(2,1)} %collective-permute-done.8.refs_0_.x1, ...), custom_call_target="tpu_custom_call" | custom-call | flops 1 | bytes 1 | tf_op jit(solution)/shard_map/pallas_call | solution.py:292
  351.0 3.9 collective-permute-start.19
  354.9 3.6 shard_map.77
  358.5 0.3 shard_map.73.acc_ref
  358.8 2.1 copy-done.8
  360.9 6.6 %collective-permute-done.20.near_ref = bf16[512,512]{1,0:T(8,128)(2,1)S(1)} collective-permute-done((bf16[512,512]{1,0:T(8,128)(2,1)}, bf16[512,512]{1,0:T(8,128)(2,1)S(1)}, u32[]{:S(2)}, u32[]{:S(2)}) %collective-permute-start.20) | collective-permute-done | bytes 524320 | tf_op jit(solution)/shard_map/ppermute | solution.py:326
  367.5 8.5 %collective-permute-done.21.last_ref = bf16[512,512]{1,0:T(8,128)(2,1)S(1)} collective-permute-done((bf16[512,512]{1,0:T(8,128)(2,1)S(1)}, bf16[512,512]{1,0:T(8,128)(2,1)S(1)}, u32[]{:S(2)}, u32[]{:S(2)}) %collective-permute-start.21) | collective-permute-done | bytes 524320 | tf_op jit(solution)/shard_map/ppermute | solution.py:326
  376.0 1.3 shard_map.78
  377.3 10.7 %shard_map.76 = bf16[1024,1024]{1,0:T(8,128)(2,1)} custom-call(f32[1024,1024]{1,0:T(8,128)} %copy-done.8, bf16[1024,1024]{1,0:T(8,128)(2,1)} %constant_dynamic-update-slice_fusion.h1, bf16[1024,1024]{1,0:T(8,128)(2,1)S(1)} %copy-done.10, bf16[1024,1024]{1,0:T(8,128)(2,1)S(1)} %constant_dynamic-update-slice_fusion.4.h3, ...), custom_call_target="tpu_custom_call" | custom-call | flops 1 | bytes 1 | tf_op jit(solution)/shard_map/pallas_call | solution.py:292
  (76 shorter events, 0.4 us)
Async XLA Ops:
  7.2 9.7 %copy-start = (bf16[1024,1024]{1,0:T(8,128)(2,1)S(1)}, bf16[1024,1024]{1,0:T(8,128)(2,1)}, u32[]{:S(2)}) copy-start(bf16[1024,1024]{1,0:T(8,128)(2,1)} %l0.7) | copy-start | bytes 6291460
  7.2 224.1 %all-gather.5.cloned.1.call-start = ((), (), s32[]{:S(2)}) async-start(), calls=%async_computation.1 | async-start | bytes 2621440 | tf_op jit(solution)/shard_map/all_gather | solution.py:351
  7.2 32.7 %collective-permute-start = (bf16[1024,1024]{1,0:T(8,128)(2,1)}, bf16[1024,1024]{1,0:T(8,128)(2,1)}, u32[]{:S(2)}, u32[]{:S(2)}) collective-permute-start(bf16[1024,1024]{1,0:T(8,128)(2,1)} %l0.7), channel_id=1, source_target_pairs={{0,1},{4,5},{5,4},{8,9},{9,8},{10,11},{12,13},{13,12},{14,15},{15,... | collective-permute-start | bytes 6291464 | tf_op jit(solution)/shard_map/ppermute | solution.py:326
  12.0 6.2 %collective-permute-start.4 = (bf16[512,1024]{1,0:T(8,128)(2,1)S(1)}, bf16[512,1024]{1,0:T(8,128)(2,1)}, u32[]{:S(2)}, u32[]{:S(2)}) collective-permute-start(bf16[512,1024]{1,0:T(8,128)(2,1)S(1)} %get-tuple-element.35), channel_id=1, source_target_pairs={{4,0},{5,1},{8,4},{9,5},{10,6},{12,8},{13,9},{14,10},{15,11},{20,1... | collective-permute-start | bytes 3145736 | tf_op jit(solution)/shard_map/ppermute | solution.py:326
  13.7 26.2 %collective-permute-start.3 = (bf16[1024,512]{1,0:T(8,128)(2,1)}, bf16[1024,512]{1,0:T(8,128)(2,1)S(1)}, u32[]{:S(2)}, u32[]{:S(2)}) collective-permute-start(bf16[1024,512]{1,0:T(8,128)(2,1)} %p0.1), channel_id=1, source_target_pairs={{0,4},{1,5},{2,6},{3,7},{4,8},{5,9},{6,10},{7,11},{8,12},{9,13},{1... | collective-permute-start | bytes 3145736 | tf_op jit(solution)/shard_map/ppermute | solution.py:326
  16.9 29.8 %collective-permute-start.1 = (bf16[1024,1024]{1,0:T(8,128)(2,1)S(1)}, bf16[1024,1024]{1,0:T(8,128)(2,1)}, u32[]{:S(2)}, u32[]{:S(2)}) collective-permute-start(bf16[1024,1024]{1,0:T(8,128)(2,1)S(1)} %copy-done), channel_id=1, source_target_pairs={{0,2},{4,6},{5,7},{8,10},{9,11},{10,8},{12,14},{13,15},{14,12},{15... | collective-permute-start | bytes 6291464 | tf_op jit(solution)/shard_map/ppermute | solution.py:326
  39.9 1.0 copy-start.16
  40.9 4.2 %copy-start.17 = (bf16[1024,512]{1,0:T(8,128)(2,1)S(1)}, bf16[1024,512]{1,0:T(8,128)(2,1)}, u32[]{:S(2)}) copy-start(bf16[1024,512]{1,0:T(8,128)(2,1)} %get-tuple-element.19.p1) | copy-start | bytes 3145732
  40.9 8.5 %collective-permute-start.7 = (bf16[512,1024]{1,0:T(8,128)(2,1)}, bf16[512,1024]{1,0:T(8,128)(2,1)}, u32[]{:S(2)}, u32[]{:S(2)}) collective-permute-start(bf16[512,1024]{1,0:T(8,128)(2,1)} %get-tuple-element.20), channel_id=1, source_target_pairs={{4,0},{5,1},{8,4},{9,5},{10,6},{12,8},{13,9},{14,10},{15,11},{20,1... | collective-permute-start | bytes 3145736 | tf_op jit(solution)/shard_map/ppermute | solution.py:326
  42.7 188.6 %all-gather.3.cloned.1.call-start = ((), (), s32[]{:S(2)}) async-start(), calls=%async_computation | async-start | bytes 5242880 | tf_op jit(solution)/shard_map/all_gather | solution.py:388
  45.0 10.0 %collective-permute-start.5 = (bf16[1024,512]{1,0:T(8,128)(2,1)S(1)}, bf16[1024,512]{1,0:T(8,128)(2,1)}, u32[]{:S(2)}, u32[]{:S(2)}) collective-permute-start(bf16[1024,512]{1,0:T(8,128)(2,1)S(1)} %copy-done.17), channel_id=1, source_target_pairs={{4,8},{5,9},{6,10},{7,11},{8,12},{9,13},{10,14},{11,15},{20,24},{2... | collective-permute-start | bytes 3145736 | tf_op jit(solution)/shard_map/ppermute | solution.py:326
  46.7 91.6 %collective-permute-start.2 = (bf16[1024,1024]{1,0:T(8,128)(2,1)}, bf16[1024,1024]{1,0:T(8,128)(2,1)}, u32[]{:S(2)}, u32[]{:S(2)}) collective-permute-start(bf16[1024,1024]{1,0:T(8,128)(2,1)} %collective-permute-done.1.refs_1_.l2), channel_id=1, source_target_pairs={{2,3},{6,7},{7,6},{8,9},{10,11},{11,10},{12,13},{13,12},{14,15},{1... | collective-permute-start | bytes 6291464 | tf_op jit(solution)/shard_map/ppermute | solution.py:326
  51.6 5.5 %copy-start.32 = (u32[32]{0:T(128)S(1)}, u32[32]{0:T(128)}, u32[]{:S(2)}) copy-start(u32[32]{0:T(128)} %constant.2) | copy-start | bytes 388
  51.6 6.8 %copy-start.29 = (s32[8]{0:T(128)S(1)}, s32[8]{0:T(128)}, u32[]{:S(2)}) copy-start(s32[8]{0:T(128)} %structure.1) | copy-start | bytes 100
  51.6 86.7 %collective-permute-start.8 = (bf16[1024,1024]{1,0:T(8,128)(2,1)}, bf16[1024,1024]{1,0:T(8,128)(2,1)}, u32[]{:S(2)}, u32[]{:S(2)}) collective-permute-start(bf16[1024,1024]{1,0:T(8,128)(2,1)} %constant_dynamic-update-slice_fusion.h1), channel_id=1, source_target_pairs={{5,7},{10,8},{21,23},{26,24}} | collective-permute-start | bytes 6291464 | tf_op jit(solution)/shard_map/ppermute | solution.py:326
  53.8 83.6 %collective-permute-start.9 = (bf16[512,1024]{1,0:T(8,128)(2,1)}, bf16[512,1024]{1,0:T(8,128)(2,1)}, u32[]{:S(2)}, u32[]{:S(2)}) collective-permute-start(bf16[512,1024]{1,0:T(8,128)(2,1)} %collective-permute-done.4.refs_2_), channel_id=1, source_target_pairs={{4,0},{5,1},{6,2},{8,4},{9,5},{10,6},{11,7},{20,16},{21,17},{22,18... | collective-permute-start | bytes 3145736 | tf_op jit(solution)/shard_map/ppermute | solution.py:326
  55.1 82.3 %collective-permute-start.6 = (bf16[1024,512]{1,0:T(8,128)(2,1)}, bf16[1024,512]{1,0:T(8,128)(2,1)S(1)}, u32[]{:S(2)}, u32[]{:S(2)}) collective-permute-start(bf16[1024,512]{1,0:T(8,128)(2,1)} %shard_map.68.p2), channel_id=1, source_target_pairs={{8,12},{9,13},{10,14},{11,15},{24,28},{25,29},{26,30},{27,31}} | collective-permute-start | bytes 3145736 | tf_op jit(solution)/shard_map/ppermute | solution.py:326
  55.8 82.5 %collective-permute-start.10 = (bf16[512,1024]{1,0:T(8,128)(2,1)}, bf16[512,1024]{1,0:T(8,128)(2,1)}, u32[]{:S(2)}, u32[]{:S(2)}) collective-permute-start(bf16[512,1024]{1,0:T(8,128)(2,1)} %collective-permute-done.7), channel_id=1, source_target_pairs={{4,0},{5,1},{6,2},{8,4},{9,5},{10,6},{11,7},{20,16},{21,17},{22,18... | collective-permute-start | bytes 3145736 | tf_op jit(solution)/shard_map/ppermute | solution.py:326
  135.6 2.7 copy-start.18
  135.6 2.7 copy-start.26
  137.4 1.0 copy-start.27
  138.4 1.2 copy-start.28
  144.2 1.3 copy-start.1
  145.5 1.0 copy-start.25
  146.5 1.0 copy-start.30
  147.5 4.1 %copy-start.2 = (bf16[1024,1024]{1,0:T(8,128)(2,1)S(1)}, bf16[1024,1024]{1,0:T(8,128)(2,1)}, u32[]{:S(2)}) copy-start(bf16[1024,1024]{1,0:T(8,128)(2,1)} %copy-done.1) | copy-start | bytes 6291460
  147.5 6.7 %copy-start.31 = (bf16[512,1024]{1,0:T(8,128)(2,1)S(1)}, bf16[512,1024]{1,0:T(8,128)(2,1)}, u32[]{:S(2)}) copy-start(bf16[512,1024]{1,0:T(8,128)(2,1)} %copy-done.30) | copy-start | bytes 3145732
  150.2 7.1 %copy-start.9 = (bf16[1024,1024]{1,0:T(8,128)(2,1)}, bf16[1024,1024]{1,0:T(8,128)(2,1)S(1)}, u32[]{:S(2)}) copy-start(bf16[1024,1024]{1,0:T(8,128)(2,1)S(1)} %constant_dynamic-update-slice_fusion.2.h2) | copy-start | bytes 6291460
  150.2 71.9 %collective-permute-start.12 = (bf16[1024,1024]{1,0:T(8,128)(2,1)S(1)}, bf16[1024,1024]{1,0:T(8,128)(2,1)S(1)}, u32[]{:S(2)}, u32[]{:S(2)}) collective-permute-start(bf16[1024,1024]{1,0:T(8,128)(2,1)S(1)} %constant_dynamic-update-slice_fusion.2.h2), channel_id=1, source_target_pairs={{0,2},{5,7},{16,18},{21,23}} | collective-permute-start | bytes 6291464 | tf_op jit(solution)/shard_map/ppermute | solution.py:326
  151.5 70.6 %collective-permute-start.13 = (bf16[1024,1024]{1,0:T(8,128)(2,1)S(1)}, bf16[1024,1024]{1,0:T(8,128)(2,1)S(1)}, u32[]{:S(2)}, u32[]{:S(2)}) collective-permute-start(bf16[1024,1024]{1,0:T(8,128)(2,1)S(1)} %copy-done.2), channel_id=1, source_target_pairs={{14,2},{30,18}} | collective-permute-start | bytes 6291464 | tf_op jit(solution)/shard_map/ppermute | solution.py:326
  152.8 50.7 %collective-permute-start.14 = (bf16[512,1024]{1,0:T(8,128)(2,1)}, bf16[512,1024]{1,0:T(8,128)(2,1)S(1)}, u32[]{:S(2)}, u32[]{:S(2)}) collective-permute-start(bf16[512,1024]{1,0:T(8,128)(2,1)} %get-tuple-element.26), channel_id=1, source_target_pairs={{4,0},{5,1},{6,2},{7,3},{20,16},{21,17},{22,18},{23,19}} | collective-permute-start | bytes 3145736 | tf_op jit(solution)/shard_map/ppermute | solution.py:326
  154.2 67.9 %collective-permute-start.11 = (bf16[512,1024]{1,0:T(8,128)(2,1)S(1)}, bf16[512,1024]{1,0:T(8,128)(2,1)S(1)}, u32[]{:S(2)}, u32[]{:S(2)}) collective-permute-start(bf16[512,1024]{1,0:T(8,128)(2,1)S(1)} %copy-done.31), channel_id=1, source_target_pairs={{4,0},{5,1},{6,2},{7,3},{8,12},{9,13},{10,14},{11,15},{12,8},{13,9... | collective-permute-start | bytes 3145736 | tf_op jit(solution)/shard_map/ppermute | solution.py:326
  157.4 1.3 copy-start.20
  222.1 1.3 copy-start.4
  222.1 1.9 copy-start.6
  225.0 1.0 copy-start.11
  226.0 1.0 copy-start.13
  227.0 50.0 %collective-permute-start.15 = (bf16[512,1024]{1,0:T(8,128)(2,1)}, bf16[512,1024]{1,0:T(8,128)(2,1)}, u32[]{:S(2)}, u32[]{:S(2)}) collective-permute-start(bf16[512,1024]{1,0:T(8,128)(2,1)} %get-tuple-element.30), channel_id=1, source_target_pairs={{4,0},{5,1},{6,2},{7,3},{20,16},{21,17},{22,18},{23,19}} | collective-permute-start | bytes 3145736 | tf_op jit(solution)/shard_map/ppermute | solution.py:326
  228.3 50.2 %collective-permute-start.17 = (bf16[512,1024]{1,0:T(8,128)(2,1)}, bf16[512,1024]{1,0:T(8,128)(2,1)}, u32[]{:S(2)}, u32[]{:S(2)}) collective-permute-start(bf16[512,1024]{1,0:T(8,128)(2,1)} %get-tuple-element.25.refs_0_), channel_id=1, source_target_pairs={{12,8},{13,9},{14,10},{15,11},{28,24},{29,25},{30,26},{31,27}} | collective-permute-start | bytes 3145736 | tf_op jit(solution)/shard_map/ppermute | solution.py:326
  229.9 48.5 %collective-permute-start.18 = (bf16[512,1024]{1,0:T(8,128)(2,1)}, bf16[512,1024]{1,0:T(8,128)(2,1)}, u32[]{:S(2)}, u32[]{:S(2)}) collective-permute-start(bf16[512,1024]{1,0:T(8,128)(2,1)} %get-tuple-element.28._dep), channel_id=1, source_target_pairs={{8,0},{9,1},{10,2},{11,3},{12,4},{13,5},{14,6},{15,7},{24,16},{25,... | collective-permute-start | bytes 3145736 | tf_op jit(solution)/shard_map/ppermute | solution.py:326
  231.3 2.2 copy-start.15
  233.5 1.6 copy-start.19
  235.1 1.0 copy-start.22
  236.1 8.7 %copy-start.14 = (bf16[512,1024]{1,0:T(8,128)(2,1)S(1)}, bf16[512,1024]{1,0:T(8,128)(2,1)}, u32[]{:S(2)}) copy-start(bf16[512,1024]{1,0:T(8,128)(2,1)} %copy-done.13) | copy-start | bytes 3145732
  241.2 37.2 %copy-start.23 = (f32[512,512]{1,0:T(8,128)}, f32[512,512]{1,0:T(8,128)S(1)}, u32[]{:S(2)}) copy-start(f32[512,512]{1,0:T(8,128)S(1)} %get-tuple-element.33.own_ref) | copy-start | bytes 3145732
  241.2 42.9 %collective-permute-start.16 = (bf16[512,512]{1,0:T(8,128)(2,1)S(1)}, bf16[512,512]{1,0:T(8,128)(2,1)S(1)}, u32[]{:S(2)}, u32[]{:S(2)}) collective-permute-start(bf16[512,512]{1,0:T(8,128)(2,1)S(1)} %get-tuple-element.29._dep), channel_id=1, source_target_pairs={{0,4},{1,5},{2,6},{3,7},{4,0},{5,1},{6,2},{7,3},{8,12},{9,13},{10,... | collective-permute-start | bytes 1572872 | tf_op jit(solution)/shard_map/ppermute | solution.py:326
  277.0 7.2 %copy-start.10 = (bf16[1024,1024]{1,0:T(8,128)(2,1)S(1)}, bf16[1024,1024]{1,0:T(8,128)(2,1)}, u32[]{:S(2)}) copy-start(bf16[1024,1024]{1,0:T(8,128)(2,1)} %copy-done.9) | copy-start | bytes 6291460
  284.1 1.6 copy-start.5
  284.1 2.2 copy-start.7
  286.3 68.5 %copy-start.12 = (bf16[512,1024]{1,0:T(8,128)(2,1)S(1)}, bf16[512,1024]{1,0:T(8,128)(2,1)}, u32[]{:S(2)}) copy-start(bf16[512,1024]{1,0:T(8,128)(2,1)} %copy-done.11) | copy-start | bytes 3145732
  286.3 68.6 %copy-start.21 = (f32[512,1024]{1,0:T(8,128)S(1)}, f32[512,1024]{1,0:T(8,128)}, u32[]{:S(2)}) copy-start(f32[512,1024]{1,0:T(8,128)} %copy-done.20) | copy-start | bytes 6291460
  351.0 26.4 %collective-permute-start.19 = (bf16[3072,1024]{1,0:T(8,128)(2,1)}, bf16[3072,1024]{1,0:T(8,128)(2,1)}, u32[]{:S(2)}, u32[]{:S(2)}) collective-permute-start(bf16[3072,1024]{1,0:T(8,128)(2,1)} %shard_map.75), channel_id=1, source_target_pairs={{0,1},{2,3},{5,4},{7,6},{8,9},{10,11},{16,17},{18,19},{21,20},{23,... | collective-permute-start | bytes 18874376 | tf_op jit(solution)/shard_map/ppermute | solution.py:326
  354.8 12.7 %collective-permute-start.20 = (bf16[512,512]{1,0:T(8,128)(2,1)}, bf16[512,512]{1,0:T(8,128)(2,1)S(1)}, u32[]{:S(2)}, u32[]{:S(2)}) collective-permute-start(bf16[512,512]{1,0:T(8,128)(2,1)} %get-tuple-element.34), channel_id=1, source_target_pairs={{0,4},{1,5},{2,6},{3,7},{4,0},{5,1},{6,2},{7,3},{8,12},{9,13},{10,... | collective-permute-start | bytes 1572872 | tf_op jit(solution)/shard_map/ppermute | solution.py:326
  354.8 21.2 %collective-permute-start.21 = (bf16[512,512]{1,0:T(8,128)(2,1)S(1)}, bf16[512,512]{1,0:T(8,128)(2,1)S(1)}, u32[]{:S(2)}, u32[]{:S(2)}) collective-permute-start(bf16[512,512]{1,0:T(8,128)(2,1)S(1)} %shard_map.74._dep), channel_id=1, source_target_pairs={{0,8},{1,9},{2,10},{3,11},{4,12},{5,13},{6,14},{7,15},{8,0},{9,1},... | collective-permute-start | bytes 1572872 | tf_op jit(solution)/shard_map/ppermute | solution.py:326
  354.8 3.6 copy-start.3
  358.5 17.5 %copy-start.24 = (f32[512,512]{1,0:T(8,128)S(1)}, f32[512,512]{1,0:T(8,128)}, u32[]{:S(2)}) copy-start(f32[512,512]{1,0:T(8,128)} %copy-done.23) | copy-start | bytes 3145732
  358.8 2.1 copy-start.8
Sparse Core Ops, SparseCore 0:
  42.8 25.5 all-gather.4
  147.6 47.3 all-gather.2

commit v5 on v4

--- a/solution.py
+++ b/solution.py
@@ -82,17 +82,10 @@
     return pl.ds(pl.multiple_of(i * TILE, TILE), TILE)
 
 
-def far_block(r):
-    return jnp.where(r == 1, 0, r ^ 3)
-
-
-def product_kernel(
-    structure, l0, l1, l2, l3, p0, p1, p2, p3, *refs, deps, gated
-):
-    t_ref, tt_ref, far_ref = refs[deps + gated : deps + gated + 3]
+def product_kernel(l0, l1, l2, l3, p0, p1, p2, p3, *refs, deps, gated):
+    t_ref, tt_ref, sent_ref = refs[deps + gated : deps + gated + 3]
     rows, panels, acc, row_sems, panel_sems = refs[deps + 2 * gated + 3 :]
     r, c = position()
-    blocks = panels.shape[1] // BLOCK
     for m, ref in enumerate((l0, l1, l2, l3)):
         j = c ^ m
 
@@ -110,16 +103,8 @@
 
         @pl.when(s <= r)
         def _():
+            wait(l0, rows.at[s], row_sems.at[s])
             wait(p0, panels.at[s], panel_sems.at[s])
-            for b in range(blocks):
-
-                @pl.when(structure[(r - s) * blocks + b] == 0)
-                def _():
-                    panels[s, b * BLOCK : (b + 1) * BLOCK, :] = jnp.zeros(
-                        (BLOCK, panels.shape[2]), BF16
-                    )
-
-            wait(l0, rows.at[s], row_sems.at[s])
 
             @pl.loop(0, acc.shape[0] // TILE)
             def _(i):
@@ -134,53 +119,46 @@
         t_ref[tile(i), :] = value.astype(BF16)
         tt_ref[:, tile(i)] = value.T.astype(BF16)
 
-    @pl.when(r >= 1)
+    @pl.when(r == 3)
     def _():
-        slot = r - far_block(r)
-
         @pl.loop(0, tt_ref.shape[0] // TILE)
         def _(i):
-            far_ref[tile(i), :] = dot(tt_ref[tile(i), :], rows[slot]).astype(BF16)
-
-
-def cross_kernel(l0, l1, l2, l3, tt_ref, near_ref, own_ref, blocks, sems):
+            sent_ref[tile(i), :] = dot(tt_ref[tile(i), :], rows[3]).astype(BF16)
+
+
+def own_kernel(l0, l1, l2, l3, tt_ref, own_ref, block, sem):
     r, c = position()
-    refs = (l0, l1, l2, l3)
-
-    @pl.when(r == 3)
-    def _():
-        start_picked(refs, r ^ 1 ^ c, blocks.at[0], sems.at[0])
-
-    start_picked(refs, r ^ c, blocks.at[1], sems.at[1])
-
-    @pl.when(r == 3)
-    def _():
-        wait(l0, blocks.at[0], sems.at[0])
-
-        @pl.loop(0, tt_ref.shape[0] // TILE)
-        def _(i):
-            near_ref[tile(i), :] = dot(tt_ref[tile(i), :], blocks[0]).astype(BF16)
-
-    wait(l0, blocks.at[1], sems.at[1])
+    start_picked((l0, l1, l2, l3), r ^ c, block, sem)
+    wait(l0, block, sem)
 
     @pl.loop(0, tt_ref.shape[0] // TILE)
     def _(i):
-        own_ref[tile(i), :] = dot(tt_ref[tile(i), :], blocks[1])
-
-
-def onward_kernel(l0, l1, l2, l3, tt_ref, far_ref, *refs, deps):
-    onward_ref, _, block, sem = refs[deps:]
+        own_ref[tile(i), :] = dot(tt_ref[tile(i), :], block[...])
+
+
+def chain_kernel(l0, l1, l2, l3, tt_ref, came_ref, *refs, step, deps, gated):
+    sent_ref = refs[deps + gated]
+    block, sem = refs[deps + 2 * gated + 1 :]
     r, c = position()
-
-    @pl.when(r >= 2)
+    i = step + r - 3
+
+    @pl.when(i >= 0)
     def _():
-        start_picked((l0, l1, l2, l3), r ^ 2 ^ c, block, sem)
+        start_picked((l0, l1, l2, l3), i ^ c, block, sem)
         wait(l0, block, sem)
 
-        @pl.loop(0, tt_ref.shape[0] // TILE)
-        def _(i):
-            term = dot(tt_ref[tile(i), :], block[...])
-            onward_ref[tile(i), :] = (term + far_ref[tile(i), :].astype(F32)).astype(BF16)
+        @pl.when(r == 3)
+        def _():
+            @pl.loop(0, tt_ref.shape[0] // TILE)
+            def _(j):
+                sent_ref[tile(j), :] = dot(tt_ref[tile(j), :], block[...]).astype(BF16)
+
+        @pl.when(r < 3)
+        def _():
+            @pl.loop(0, tt_ref.shape[0] // TILE)
+            def _(j):
+                term = dot(tt_ref[tile(j), :], block[...])
+                sent_ref[tile(j), :] = (term + came_ref[tile(j), :].astype(F32)).astype(BF16)
 
 
 def child_kernel(
@@ -199,7 +177,7 @@
             ref[tile(i), :] = term.astype(ref.dtype)
 
 
-def child_onward_kernel(own_ref, far_ref, _dep0, _dep1, _dep2, out_ref):
+def child_onward_kernel(own_ref, far_ref, _dep, out_ref):
     out_ref[...] = (own_ref[...] + far_ref[...].astype(F32)).astype(BF16)
 
 
@@ -222,30 +200,17 @@
         acc_ref[...] = jnp.zeros_like(acc_ref)
 
 
-def pick_kernel(h1, h2, h3, x1, x2, x3, _dep, out_ref, sems):
+def root_kernel(acc_ref, h1, h2, h3, x1, x2, x3, b1, b23, out_ref, acc, left, held, left_sems, held_sems):
     r, c = position()
     rows = h1.shape[0]
-    for refs, holds in (((h1, h2, h3), c == r), ((x1, x2, x3), c == (r ^ 2))):
-
-        @pl.when(holds)
-        def _():
-            for act in (start, wait):
-                for s, ref in enumerate(refs):
-                    act(ref, out_ref.at[s * rows : (s + 1) * rows], sems.at[s])
-
-
-def root_kernel(acc_ref, h1, h2, h3, x1, x2, x3, beside, out_ref, acc, left, held, left_sems, held_sems):
-    r, c = position()
-    rows = h1.shape[0]
-    refs = ((h1, x1), (h2, x2), (h3, x3))
+    refs = ((h1, x1, b1), (h2, x2, b23.at[:rows]), (h3, x3, b23.at[rows:]))
     needed = [(r + s < N) & (c <= r + s) for s in (1, 2, 3)]
-    for s, (own, other) in enumerate(refs):
+    for s, places in enumerate(refs):
 
         @pl.when(needed[s])
         def _():
-            places = (own, other, beside.at[s * rows : (s + 1) * rows])
             start_picked(places, source(r, c), left.at[s], left_sems.at[s])
-            start(own, held.at[s], held_sems.at[s])
+            start(places[0], held.at[s], held_sems.at[s])
 
     acc[...] = acc_ref[...]
     for s in range(3):
@@ -266,12 +231,10 @@
     return jnp.where(c == r, 0, jnp.where(c == (r ^ 2), 1, 2))
 
 
-def cross_end_kernel(structure, own_ref, far_ref, near_ref, last_ref, out_ref):
-    first = position()[0] == 0
+def cross_end_kernel(structure, own_ref, came_ref, out_ref):
     for b in range(own_ref.shape[1] // BLOCK):
         rows = slice(b * BLOCK, (b + 1) * BLOCK)
-        total = own_ref[:, rows] + near_ref[:, rows].astype(F32) + last_ref[:, rows].astype(F32)
-        total = total + jnp.where(first, far_ref[:, rows].astype(F32), jnp.zeros_like(total))
+        total = own_ref[:, rows] + came_ref[:, rows].astype(F32)
         kept = structure[b] > 0
         out_ref[rows, :] = jnp.where(kept, -total.T, jnp.zeros_like(total.T)).astype(BF16)
 
@@ -343,30 +306,25 @@
         dma = pltpu.SemaphoreType.DMA
         t_block, child_block = shape((w, h), BF16), shape((w, w), BF16)
 
-        panel_1 = up(panel, 1)
-        below_1a = down(root_inverse[:half], 1)
+        _, panel_kept = mask_panel(panel, structure)
+        child_row = lax.all_gather(child_inverse, "col", axis=1, tiled=True)
+        panel_1 = up(panel_kept, 1)
         root_across = move(root_inverse, lambda r, c: (r, c ^ 2) if lower(r, c) else None)
+        below_1 = down(root_inverse, 1)
         root_beside = move(root_inverse, lambda r, c: (r, c ^ 1) if lower(r, c) else None)
-        structure_all = lax.all_gather(structure, "row", tiled=True)
-        child_row = lax.all_gather(child_inverse, "col", axis=1, tiled=True)
-        panel_1, lower_half = together(
-            panel_1, root_inverse[half:], earlier=(below_1a, root_beside)
-        )
         panel_2 = up(panel_1, 2)
-        below_1b = down(lower_half, 1)
-        below_2a = down(below_1a, 2)
-        (panel_2,) = together(panel_2, earlier=(root_across,))
+        (panel_2,) = together(panel_2, earlier=(below_1, root_across, root_beside))
         panel_3 = up(panel_2, 3)
         root_both = move(root_across, lambda r, c: (r, c ^ 1) if lower(r, c ^ 2) else None)
-        below_2b = down(below_1b, 2)
-        below_1 = jnp.concatenate((below_1a, below_1b), 0)
+        below_2a = down(below_1[:half], 2)
         across_1 = move(below_1, lambda r, c: (r, c ^ 2) if r == c and r in (1, 2) else None)
+        across_3 = move(root_across, lambda r, c: (0, 2) if (r, c) == (3, 2) else None)
 
         root_row = (root_inverse, root_beside, root_across, root_both)
-        panels = (panel, panel_1, panel_2, panel_3)
-        t, t_t, far_part, below_2a, below_2b, root_across_late = local_call(
-            functools.partial(product_kernel, deps=1, gated=3),
-            [SMEM] + [ANY] * 8,
+        panels = (panel_kept, panel_1, panel_2, panel_3)
+        t, t_t, sent, below_1, below_2a = local_call(
+            functools.partial(product_kernel, deps=1, gated=2),
+            [ANY] * 8,
             [shape((h, w), BF16), t_block, t_block],
             [
                 pltpu.VMEM((n, h, h), BF16),
@@ -375,51 +333,57 @@
                 dma((n,)),
                 dma((n,)),
             ],
-            structure_all,
             *root_row,
             *panels,
             across_1,
+            below_1,
             below_2a,
-            below_2b,
-            root_across,
-            gated=3,
-        )
-        root_row = (root_inverse, root_beside, root_across_late, root_both)
+            gated=2,
+        )
         t_row = lax.all_gather(t, "col", axis=1, tiled=True)
-        far = move(far_part, lambda r, c: (r ^ 1, c) if r >= 1 else None)
+        step = lambda x, q: move(x, lambda r, c: (r - 1, c) if q + r - 3 >= 0 else None)
+        chain = [ANY] * 4 + [VMEM] * 2
+        came = step(sent, 0)
+        below_2b = down(below_1[half:], 2)
         below_3a = down(below_2a, 3)
-        below_2 = jnp.concatenate((below_2a, below_2b), 0)
-        across_2 = move(below_2, lambda r, c: (r, c ^ 2) if r == c and r in (0, 1) else None)
-        across_3 = move(root_across_late, lambda r, c: (0, 2) if (r, c) == (3, 2) else None)
-
-        near_part, own = local_call(
-            cross_kernel,
+        (own,) = local_call(
+            own_kernel,
             [ANY] * 4 + [VMEM],
-            [t_block, shape((w, h), F32)],
-            [pltpu.VMEM((2, h, h), BF16), dma((2,))],
+            [shape((w, h), F32)],
+            [pltpu.VMEM((h, h), BF16), dma],
             *root_row,
             t_t,
         )
-        onward, below_2b = local_call(
-            functools.partial(onward_kernel, deps=5),
-            [ANY] * 4 + [VMEM, VMEM],
+        sent, below_2b, across_1 = local_call(
+            functools.partial(chain_kernel, step=1, deps=3, gated=2),
+            chain,
             [t_block],
             [pltpu.VMEM((h, h), BF16), dma],
             *root_row,
             t_t,
-            far,
-            near_part,
-            across_2,
+            came,
+            own,
+            below_3a,
             across_3,
-            below_3a,
             below_2b,
-            gated=1,
-        )
-        last = move(onward, lambda r, c: (r - 2, c))
-        near = move(near_part, lambda r, c: (r - 1, c) if r == 3 else None)
+            across_1,
+            gated=2,
+        )
+        came = step(sent, 1)
         below_3b = down(below_2b, 3)
-
-        far_part, child_near_part, child_on, child_own = local_call(
+        below_2 = jnp.concatenate((below_2a, below_2b), 0)
+        across_2 = move(below_2, lambda r, c: (r, c ^ 2) if r == c and r in (0, 1) else None)
+        c_is_r = lax.axis_index("col") == lax.axis_index("row")
+
+        def to_beside(held, across, last_row):
+            return move(
+                jnp.where(c_is_r, held, across),
+                lambda r, c: (r, c ^ 1) if r in (c, c ^ 2) and r <= last_row else None,
+            )
+
+        beside_1 = to_beside(below_1, across_1, 2)
+
+        far_part, near_part, child_on, child_own = local_call(
             child_kernel,
             [VMEM] * 4,
             [child_block, child_block, shape((w, w), F32), shape((w, w), F32)],
@@ -428,7 +392,7 @@
             t_row,
             child_inverse,
             child_row,
-            onward,
+            sent,
         )
         child_far = move(far_part, lambda r, c: (r ^ 1, c))
         (root_sum,) = local_call(
@@ -439,44 +403,38 @@
             *root_row,
             far_part,
         )
+        sent, across_2 = local_call(
+            functools.partial(chain_kernel, step=2, deps=3, gated=1),
+            chain,
+            [t_block],
+            [pltpu.VMEM((h, h), BF16), dma],
+            *root_row,
+            t_t,
+            came,
+            below_3b,
+            child_far,
+            beside_1,
+            across_2,
+            gated=1,
+        )
+        came = step(sent, 2)
         (child_onward,) = local_call(
-            child_onward_kernel,
-            [VMEM] * 2,
-            [child_block],
-            [],
-            child_on,
-            child_far,
-            near,
-            last,
-            below_3b,
+            child_onward_kernel, [VMEM] * 2, [child_block], [], child_on, child_far, sent
         )
         child_last = move(child_onward, lambda r, c: (r ^ 2, c))
-        child_near = move(child_near_part, lambda r, c: (r ^ 1, c))
-
+        child_near = move(near_part, lambda r, c: (r ^ 1, c))
         below_3 = jnp.concatenate((below_3a, below_3b), 0)
-        held = (below_1, below_2, below_3)
-        across = (across_1, across_2, across_3)
-        (picked,) = local_call(
-            pick_kernel,
-            [],
-            [shape((3 * h, h), BF16)],
-            [dma((3,))],
-            *held,
-            *across,
-            child_onward,
-            out_specs=[ANY],
-        )
-        beside = move(picked, lambda r, c: (r, c ^ 1) if r in (c, c ^ 2) and r < 3 else None)
+        beside_23 = to_beside(
+            jnp.concatenate((below_2, below_3), 0), jnp.concatenate((across_2, across_3), 0), 1
+        )
         (sigma_cross,) = local_call(
             cross_end_kernel,
-            [SMEM] + [VMEM] * 4,
+            [SMEM] + [VMEM] * 2,
             [shape((h, w), BF16)],
             [],
             structure,
             own,
-            far,
-            near,
-            last,
+            came,
         )
         (sigma_root,) = local_call(
             root_kernel,
@@ -490,9 +448,14 @@
                 dma((3,)),
             ],
             root_sum,
-            *held,
-            *across,
-            beside,
+            below_1,
+            below_2,
+            below_3,
+            across_1,
+            across_2,
+            across_3,
+            beside_1,
+            beside_23,
         )
         (sigma_child,) = local_call(
             child_end_kernel,

time: 396 us -> 319 us (0.81)
  the two profiles are of different devices: /device:TPU:2 before, /device:TPU:0 now
where the time goes in v5:
time: 319 us; the launch traced here: 318 us
  waiting for transfers between devices  169 us (53%)
  starting transfers between devices  61.1 us (19%)
  Pallas kernels  36.8 us (12%)
  local copies, waits for them, and re-layouts  24.4 us (8%)
  between operations  14.3 us (4%)
  other arithmetic  12.2 us (4%)
    ppermute x22, waiting for transfers between devices, move(): return lax.ppermute(x, AXES, pairs)  169 us
    ppermute x22, starting transfers between devices, move(): return lax.ppermute(x, AXES, pairs)  61.1 us
    pallas_call x10, Pallas kernels, local_call(): pl.pallas_call(kernel, out_shape=outs, in_specs=in_specs + [ANY] * (len(a...  36.8 us
    unnamed x43, local copies, waits for them, and re-layouts  18.4 us
    select_n x2, other arithmetic, to_beside(): jnp.where(c_is_r, held, across)  8.4 us
  transfers between devices with their start and end apart: 24, of which 8 were waited for; matrix products, arithmetic and copies ran while one was open for 4% of the time, Pallas kernels for 6%

profile of v5, /device:TPU:0, one launch (start us, length us, event | category | flops | bytes accessed | tf_op | source)
XLA Modules:
  0.0 317.9 jit_solution(7866824101793658963)
XLA Ops:
  7.2 6.2 %collective-permute-start.1 = (bf16[1024,1024]{1,0:T(8,128)(2,1)}, bf16[1024,1024]{1,0:T(8,128)(2,1)}, u32[]{:S(2)}, u32[]{:S(2)}) collective-permute-start(bf16[1024,1024]{1,0:T(8,128)(2,1)} %l0.9), channel_id=1, source_target_pairs={{0,2},{4,6},{5,7},{8,10},{9,11},{10,8},{12,14},{13,15},{14,12},{15... | collective-permute-start | bytes 6291464 | tf_op jit(solution)/shard_map/ppermute | solution.py:289
  13.4 1.3 collective-permute-start.5
  14.7 1.4 collective-permute-start
  16.1 0.7 broadcast_compare_fusion
  16.8 0.1 broadcast_bitcast_fusion
  16.9 1.4 broadcast_select_fusion.1.p0
  18.3 6.1 %collective-permute-start.3 = (bf16[1024,512]{1,0:T(8,128)(2,1)S(1)}, bf16[1024,512]{1,0:T(8,128)(2,1)}, u32[]{:S(2)}, u32[]{:S(2)}) collective-permute-start(bf16[1024,512]{1,0:T(8,128)(2,1)S(1)} %broadcast_select_fusion.1.p0), channel_id=1, source_target_pairs={{0,4},{1,5},{2,6},{3,7},{4,8},{5,9},{6,10},{7,11},{8,12},{9,13},{1... | collective-permute-start | bytes 3145736 | tf_op jit(solution)/shard_map/ppermute | solution.py:289
  24.4 1.0 copy-done.12
  25.4 0.0 all-gather.3.cloned.1.call-start
  25.4 21.0 %collective-permute-done.3.p1 = bf16[1024,512]{1,0:T(8,128)(2,1)} collective-permute-done((bf16[1024,512]{1,0:T(8,128)(2,1)S(1)}, bf16[1024,512]{1,0:T(8,128)(2,1)}, u32[]{:S(2)}, u32[]{:S(2)}) %collective-permute-start.3) | collective-permute-done | bytes 1048608 | tf_op jit(solution)/shard_map/ppermute | solution.py:289
  46.4 0.7 collective-permute-start.4
  47.2 2.1 collective-permute-start.2
  49.2 13.3 %collective-permute-done.5.refs_1_ = bf16[1024,1024]{1,0:T(8,128)(2,1)} collective-permute-done((bf16[1024,1024]{1,0:T(8,128)(2,1)}, bf16[1024,1024]{1,0:T(8,128)(2,1)}, u32[]{:S(2)}, u32[]{:S(2)}) %collective-permute-start.5) | collective-permute-done | bytes 2097184 | tf_op jit(solution)/shard_map/ppermute | solution.py:289
  62.6 2.0 collective-permute-start.7
  64.6 1.3 copy-done
  65.9 1.0 copy-done.15
  66.8 0.8 collective-permute-start.6
  67.7 1.3 slice.8
  69.0 1.3 collective-permute-start.8
  70.3 31.0 %collective-permute-done.8.refs_2_ = bf16[512,1024]{1,0:T(8,128)(2,1)S(1)} collective-permute-done((bf16[512,1024]{1,0:T(8,128)(2,1)S(1)}, bf16[512,1024]{1,0:T(8,128)(2,1)S(1)}, u32[]{:S(2)}, u32[]{:S(2)}) %collective-permute-start.8) | collective-permute-done | bytes 1048608 | tf_op jit(solution)/shard_map/ppermute | solution.py:289
  101.3 1.2 copy-done.13
  102.5 1.2 copy-done.16
  103.7 3.6 %shard_map.68 = (bf16[1024,512]{1,0:T(8,128)(2,1)S(1)}, bf16[512,1024]{1,0:T(8,128)(2,1)S(1)}, bf16[512,1024]{1,0:T(8,128)(2,1)}, bf16[1024,1024]{1,0:T(8,128)(2,1)}, bf16[512,1024]{1,0:T(8,128)(2,1)S(1)}) custom-call(bf16[1024,1024]{1,0:T(8,128)(2,1)S(1)} %copy-done.2, bf16[1024,1024]{1,0:T(8,128)(2,1)} %copy-done, ...), custom_call_target="tpu_custom_call", output_to_operand_aliasing={{3}: (9, {}), {4}: (10, {})} | custom-call | flops 1 | bytes 1 | tf_op jit(solution)/shard_map/pallas_call | solution.py:255
  107.3 1.0 copy-done.9
  108.3 1.0 copy-done.19
  109.3 2.1 collective-permute-start.11
  111.4 1.3 collective-permute-start.10
  112.7 2.3 slice.7
  115.0 1.3 collective-permute-start.12
  116.3 1.6 collective-permute-start.9
  117.9 1.6 copy-done.3
  119.5 1.6 shard_map.69.refs_0_.own_ref
  121.1 1.3 copy-done.6
  122.4 1.0 constant_dynamic-update-slice_fusion.1
  123.5 24.5 %collective-permute-done.10.refs_1_ = bf16[512,1024]{1,0:T(8,128)(2,1)} collective-permute-done((bf16[512,1024]{1,0:T(8,128)(2,1)}, bf16[512,1024]{1,0:T(8,128)(2,1)}, u32[]{:S(2)}, u32[]{:S(2)}) %collective-permute-start.10) | collective-permute-done | bytes 1048608 | tf_op jit(solution)/shard_map/ppermute | solution.py:289
  147.9 20.4 %collective-permute-done.12.refs_3_ = bf16[512,1024]{1,0:T(8,128)(2,1)} collective-permute-done((bf16[512,1024]{1,0:T(8,128)(2,1)}, bf16[512,1024]{1,0:T(8,128)(2,1)}, u32[]{:S(2)}, u32[]{:S(2)}) %collective-permute-start.12) | collective-permute-done | bytes 1048608 | tf_op jit(solution)/shard_map/ppermute | solution.py:289
  168.3 2.2 shard_map.70
  170.5 3.2 %broadcast_select_fusion = bf16[1024,1024]{1,0:T(8,128)(2,1)} fusion(bf16[1024,1024]{1,0:T(8,128)(2,1)} %get-tuple-element.21.h1, bf16[1024,1024]{1,0:T(8,128)(2,1)} %get-tuple-element.25.x1, pred[]{:T(512)S(6)} %eq.3), kind=kLoop, calls=%fused_computation.2 | loop fusion | flops 1048576 | bytes 6291457 | tf_op jit(solution)/shard_map/jit(_where)/select_n | solution.py:380
  173.7 2.6 collective-permute-start.16
  176.3 2.3 constant_dynamic-update-slice_fusion.h2
  178.6 16.7 %collective-permute-start.17 = (bf16[1024,1024]{1,0:T(8,128)(2,1)}, bf16[1024,1024]{1,0:T(8,128)(2,1)}, u32[]{:S(2)}, u32[]{:S(2)}) collective-permute-start(bf16[1024,1024]{1,0:T(8,128)(2,1)} %constant_dynamic-update-slice_fusion.h2), channel_id=1, source_target_pairs={{0,2},{5,7},{16,18},{21,23}} | collective-permute-start | bytes 6291464 | tf_op jit(solution)/shard_map/ppermute | solution.py:289
  195.3 1.3 collective-permute-start.13
  196.6 1.6 collective-permute-start.14
  198.2 2.2 copy-done.14
  200.4 1.6 copy-done.17
  202.0 1.0 copy-done.18
  203.0 4.8 %shard_map.71 = (bf16[512,512]{1,0:T(8,128)(2,1)S(1)}, bf16[512,512]{1,0:T(8,128)(2,1)S(1)}, f32[512,512]{1,0:T(8,128)S(1)}, f32[512,512]{1,0:T(8,128)S(1)}) custom-call(bf16[512,1024]{1,0:T(8,128)(2,1)S(1)} %get-tuple-element.17.tt_ref, bf16[1024,2048]{1,0:T(8,128)(2,1)S(1)} %copy-done.14, bf16[512,512]{1,0:T(8,128)(2,1)S(1)} %copy-done.18, ...), custom_call_target="tpu_custom_call" | custom-call | flops 1 | bytes 1 | tf_op jit(solution)/shard_map/pallas_call | solution.py:255
  207.9 3.4 %collective-permute-start.15 = (bf16[512,512]{1,0:T(8,128)(2,1)S(1)}, bf16[512,512]{1,0:T(8,128)(2,1)S(1)}, u32[]{:S(2)}, u32[]{:S(2)}) collective-permute-start(bf16[512,512]{1,0:T(8,128)(2,1)S(1)} %get-tuple-element.23._dep), channel_id=1, source_target_pairs={{0,4},{1,5},{2,6},{3,7},{4,0},{5,1},{6,2},{7,3},{8,12},{9,13},{10,... | collective-permute-start | bytes 1572872 | tf_op jit(solution)/shard_map/ppermute | solution.py:289
  211.2 12.4 %collective-permute-done.13.refs_0_ = bf16[512,1024]{1,0:T(8,128)(2,1)} collective-permute-done((bf16[512,1024]{1,0:T(8,128)(2,1)}, bf16[512,1024]{1,0:T(8,128)(2,1)}, u32[]{:S(2)}, u32[]{:S(2)}) %collective-permute-start.13) | collective-permute-done | bytes 1048608 | tf_op jit(solution)/shard_map/ppermute | solution.py:289
  223.6 8.1 %collective-permute-done.15.refs_1_.far_ref = bf16[512,512]{1,0:T(8,128)(2,1)S(1)} collective-permute-done((bf16[512,512]{1,0:T(8,128)(2,1)S(1)}, bf16[512,512]{1,0:T(8,128)(2,1)S(1)}, u32[]{:S(2)}, u32[]{:S(2)}) %collective-permute-start.15) | collective-permute-done | bytes 524320 | tf_op jit(solution)/shard_map/ppermute | solution.py:289
  231.7 1.2 shard_map.73
  233.0 5.2 %maximum_select_fusion = bf16[2048,1024]{1,0:T(8,128)(2,1)} fusion(bf16[512,1024]{1,0:T(8,128)(2,1)} %collective-permute-done.13.refs_0_, bf16[512,1024]{1,0:T(8,128)(2,1)} %collective-permute-done.10.refs_1_, bf16[512,1024]{1,0:T(8,128)(2,1)} %get-tuple-element.24, bf16[512,1024]{1,0:T(8,128)(2,1)S(1)} %copy-done.11, ...), kind=kLoop, calls=%fused_computation | loop fusion | flops 27262976 | bytes 12582913 | tf_op jit(solution)/shard_map/jit(_where)/select_n | solution.py:380
  238.1 3.2 %collective-permute-start.18 = (bf16[2048,1024]{1,0:T(8,128)(2,1)}, bf16[2048,1024]{1,0:T(8,128)(2,1)}, u32[]{:S(2)}, u32[]{:S(2)}) collective-permute-start(bf16[2048,1024]{1,0:T(8,128)(2,1)} %maximum_select_fusion), channel_id=1, source_target_pairs={{0,1},{2,3},{5,4},{7,6},{16,17},{18,19},{21,20},{23,22}} | collective-permute-start | bytes 12582920 | tf_op jit(solution)/shard_map/ppermute | solution.py:289
  241.4 1.3 collective-permute-start.19
  242.7 2.7 collective-permute-start.20
  245.4 0.1 shard_map.76
  245.5 0.1 collective-permute-start.21
  245.5 1.7 pad_maximum_fusion.h3
  247.3 3.5 %shard_map.72.acc_ref = f32[1024,1024]{1,0:T(8,128)S(1)} custom-call(bf16[1024,1024]{1,0:T(8,128)(2,1)S(1)} %copy-done.5, bf16[1024,1024]{1,0:T(8,128)(2,1)S(1)} %copy-done.1, bf16[1024,1024]{1,0:T(8,128)(2,1)} %collective-permute-done.1.refs_2_.l2, bf16[1024,1024]{1,0:T(8,128)(2,1)} %collective-permute-done.2.l3, bf16[512,512]{1,0:T(8,128)(2,1)S(1)} %get-tuple-element.23._dep), custom_call_target="tpu_custom_call" | custom-call | flops 1 | bytes 1 | tf_op jit(solution)/shard_map/pallas_call | solution.py:255
  250.8 2.0 copy-done.8
  252.8 38.5 %collective-permute-done.20.near_ref = bf16[512,512]{1,0:T(8,128)(2,1)S(1)} collective-permute-done((bf16[512,512]{1,0:T(8,128)(2,1)S(1)}, bf16[512,512]{1,0:T(8,128)(2,1)S(1)}, u32[]{:S(2)}, u32[]{:S(2)}) %collective-permute-start.20) | collective-permute-done | bytes 524320 | tf_op jit(solution)/shard_map/ppermute | solution.py:289
  291.3 1.3 shard_map.77
  292.6 2.1 shard_map.75
  294.8 16.3 %shard_map.74 = bf16[1024,1024]{1,0:T(8,128)(2,1)} custom-call(f32[1024,1024]{1,0:T(8,128)} %copy-done.8, bf16[1024,1024]{1,0:T(8,128)(2,1)} %get-tuple-element.21.h1, bf16[1024,1024]{1,0:T(8,128)(2,1)} %constant_dynamic-update-slice_fusion.h2, bf16[1024,1024]{1,0:T(8,128)(2,1)S(1)} %pad_maximum_fusion.h3, bf16[1024,1024]{1,0:T(8,128)(2,1)} %get-tuple-element.25.x1, ...), custom_call_target="tpu_custom_call" | custom-call | flops 1 | bytes 1 | tf_op jit(solution)/shard_map/pallas_call | solution.py:255
  (49 shorter events, 0.2 us)
Async XLA Ops:
  7.2 191.0 %all-gather.5.cloned.1.call-start = ((), (), s32[]{:S(2)}) async-start(), calls=%async_computation.1 | async-start | bytes 2621440 | tf_op jit(solution)/shard_map/all_gather | solution.py:310
  7.2 40.0 %collective-permute-start.1 = (bf16[1024,1024]{1,0:T(8,128)(2,1)}, bf16[1024,1024]{1,0:T(8,128)(2,1)}, u32[]{:S(2)}, u32[]{:S(2)}) collective-permute-start(bf16[1024,1024]{1,0:T(8,128)(2,1)} %l0.9), channel_id=1, source_target_pairs={{0,2},{4,6},{5,7},{8,10},{9,11},{10,8},{12,14},{13,15},{14,12},{15... | collective-permute-start | bytes 6291464 | tf_op jit(solution)/shard_map/ppermute | solution.py:289
  13.4 49.1 %collective-permute-start.5 = (bf16[1024,1024]{1,0:T(8,128)(2,1)}, bf16[1024,1024]{1,0:T(8,128)(2,1)}, u32[]{:S(2)}, u32[]{:S(2)}) collective-permute-start(bf16[1024,1024]{1,0:T(8,128)(2,1)} %l0.9), channel_id=1, source_target_pairs={{4,0},{5,1},{8,4},{9,5},{10,6},{12,8},{13,9},{14,10},{15,11},{20,1... | collective-permute-start | bytes 6291464 | tf_op jit(solution)/shard_map/ppermute | solution.py:289
  14.7 49.8 %collective-permute-start = (bf16[1024,1024]{1,0:T(8,128)(2,1)}, bf16[1024,1024]{1,0:T(8,128)(2,1)S(1)}, u32[]{:S(2)}, u32[]{:S(2)}) collective-permute-start(bf16[1024,1024]{1,0:T(8,128)(2,1)} %l0.9), channel_id=1, source_target_pairs={{0,1},{4,5},{5,4},{8,9},{9,8},{10,11},{12,13},{13,12},{14,15},{15,... | collective-permute-start | bytes 6291464 | tf_op jit(solution)/shard_map/ppermute | solution.py:289
  18.3 28.1 %collective-permute-start.3 = (bf16[1024,512]{1,0:T(8,128)(2,1)S(1)}, bf16[1024,512]{1,0:T(8,128)(2,1)}, u32[]{:S(2)}, u32[]{:S(2)}) collective-permute-start(bf16[1024,512]{1,0:T(8,128)(2,1)S(1)} %broadcast_select_fusion.1.p0), channel_id=1, source_target_pairs={{0,4},{1,5},{2,6},{3,7},{4,8},{5,9},{6,10},{7,11},{8,12},{9,13},{1... | collective-permute-start | bytes 3145736 | tf_op jit(solution)/shard_map/ppermute | solution.py:289
  24.4 1.0 copy-start.12
  25.4 172.8 %all-gather.3.cloned.1.call-start = ((), (), s32[]{:S(2)}) async-start(), calls=%async_computation | async-start | bytes 5242880 | tf_op jit(solution)/shard_map/all_gather | solution.py:343
  46.4 18.1 %collective-permute-start.4 = (bf16[1024,512]{1,0:T(8,128)(2,1)}, bf16[1024,512]{1,0:T(8,128)(2,1)S(1)}, u32[]{:S(2)}, u32[]{:S(2)}) collective-permute-start(bf16[1024,512]{1,0:T(8,128)(2,1)} %collective-permute-done.3.p1), channel_id=1, source_target_pairs={{4,8},{5,9},{6,10},{7,11},{8,12},{9,13},{10,14},{11,15},{20,24},{2... | collective-permute-start | bytes 3145736 | tf_op jit(solution)/shard_map/ppermute | solution.py:289
  47.2 54.1 %collective-permute-start.2 = (bf16[1024,1024]{1,0:T(8,128)(2,1)}, bf16[1024,1024]{1,0:T(8,128)(2,1)}, u32[]{:S(2)}, u32[]{:S(2)}) collective-permute-start(bf16[1024,1024]{1,0:T(8,128)(2,1)} %collective-permute-done.1.refs_2_.l2), channel_id=1, source_target_pairs={{2,3},{6,7},{7,6},{8,9},{10,11},{11,10},{12,13},{13,12},{14,15},{1... | collective-permute-start | bytes 6291464 | tf_op jit(solution)/shard_map/ppermute | solution.py:289
  62.6 38.7 %collective-permute-start.7 = (bf16[1024,1024]{1,0:T(8,128)(2,1)}, bf16[1024,1024]{1,0:T(8,128)(2,1)}, u32[]{:S(2)}, u32[]{:S(2)}) collective-permute-start(bf16[1024,1024]{1,0:T(8,128)(2,1)} %collective-permute-done.5.refs_1_), channel_id=1, source_target_pairs={{5,7},{10,8},{21,23},{26,24}} | collective-permute-start | bytes 6291464 | tf_op jit(solution)/shard_map/ppermute | solution.py:289
  64.6 1.3 copy-start
  65.9 1.0 copy-start.15
  66.8 34.4 %copy-start.2 = (bf16[1024,1024]{1,0:T(8,128)(2,1)S(1)}, bf16[1024,1024]{1,0:T(8,128)(2,1)}, u32[]{:S(2)}) copy-start(bf16[1024,1024]{1,0:T(8,128)(2,1)} %l0.9) | copy-start | bytes 6291460
  66.8 3.5 %collective-permute-start.6 = (bf16[1024,512]{1,0:T(8,128)(2,1)}, bf16[1024,512]{1,0:T(8,128)(2,1)S(1)}, u32[]{:S(2)}, u32[]{:S(2)}) collective-permute-start(bf16[1024,512]{1,0:T(8,128)(2,1)} %shard_map.67.p2), channel_id=1, source_target_pairs={{8,12},{9,13},{10,14},{11,15},{24,28},{25,29},{26,30},{27,31}} | collective-permute-start | bytes 3145736 | tf_op jit(solution)/shard_map/ppermute | solution.py:289
  69.0 32.3 %collective-permute-start.8 = (bf16[512,1024]{1,0:T(8,128)(2,1)S(1)}, bf16[512,1024]{1,0:T(8,128)(2,1)S(1)}, u32[]{:S(2)}, u32[]{:S(2)}) collective-permute-start(bf16[512,1024]{1,0:T(8,128)(2,1)S(1)} %slice.8), channel_id=1, source_target_pairs={{4,0},{5,1},{6,2},{8,4},{9,5},{10,6},{11,7},{20,16},{21,17},{22,18... | collective-permute-start | bytes 3145736 | tf_op jit(solution)/shard_map/ppermute | solution.py:289
  101.3 1.2 copy-start.13
  102.5 1.2 copy-start.16
  107.3 1.0 copy-start.9
  108.3 1.0 copy-start.19
  109.3 8.7 %copy-start.1 = (bf16[1024,1024]{1,0:T(8,128)(2,1)S(1)}, bf16[1024,1024]{1,0:T(8,128)(2,1)}, u32[]{:S(2)}) copy-start(bf16[1024,1024]{1,0:T(8,128)(2,1)} %copy-done) | copy-start | bytes 6291460
  109.3 14.2 %collective-permute-start.11 = (bf16[1024,1024]{1,0:T(8,128)(2,1)}, bf16[1024,1024]{1,0:T(8,128)(2,1)}, u32[]{:S(2)}, u32[]{:S(2)}) collective-permute-start(bf16[1024,1024]{1,0:T(8,128)(2,1)} %collective-permute-done.1.refs_2_.l2), channel_id=1, source_target_pairs={{14,2},{30,18}} | collective-permute-start | bytes 6291464 | tf_op jit(solution)/shard_map/ppermute | solution.py:289
  111.4 36.5 %collective-permute-start.10 = (bf16[512,1024]{1,0:T(8,128)(2,1)}, bf16[512,1024]{1,0:T(8,128)(2,1)}, u32[]{:S(2)}, u32[]{:S(2)}) collective-permute-start(bf16[512,1024]{1,0:T(8,128)(2,1)} %copy-done.9), channel_id=1, source_target_pairs={{4,0},{5,1},{6,2},{7,3},{20,16},{21,17},{22,18},{23,19}} | collective-permute-start | bytes 3145736 | tf_op jit(solution)/shard_map/ppermute | solution.py:289
  115.0 53.3 %collective-permute-start.12 = (bf16[512,1024]{1,0:T(8,128)(2,1)}, bf16[512,1024]{1,0:T(8,128)(2,1)}, u32[]{:S(2)}, u32[]{:S(2)}) collective-permute-start(bf16[512,1024]{1,0:T(8,128)(2,1)} %slice.7), channel_id=1, source_target_pairs={{4,0},{5,1},{6,2},{8,4},{9,5},{10,6},{11,7},{20,16},{21,17},{22,18... | collective-permute-start | bytes 3145736 | tf_op jit(solution)/shard_map/ppermute | solution.py:289
  116.3 52.0 %collective-permute-start.9 = (bf16[512,1024]{1,0:T(8,128)(2,1)}, bf16[512,1024]{1,0:T(8,128)(2,1)}, u32[]{:S(2)}, u32[]{:S(2)}) collective-permute-start(bf16[512,1024]{1,0:T(8,128)(2,1)} %get-tuple-element.19), channel_id=1, source_target_pairs={{12,8},{13,9},{14,10},{15,11},{28,24},{29,25},{30,26},{31,27}} | collective-permute-start | bytes 3145736 | tf_op jit(solution)/shard_map/ppermute | solution.py:289
  117.9 1.6 copy-start.3
  119.5 2.9 copy-start.10
  121.1 1.3 copy-start.6
  122.4 45.9 %copy-start.4 = (bf16[1024,1024]{1,0:T(8,128)(2,1)S(1)}, bf16[1024,1024]{1,0:T(8,128)(2,1)}, u32[]{:S(2)}) copy-start(bf16[1024,1024]{1,0:T(8,128)(2,1)} %l0.9) | copy-start | bytes 6291460
  173.7 49.8 %collective-permute-start.16 = (bf16[1024,1024]{1,0:T(8,128)(2,1)}, bf16[1024,1024]{1,0:T(8,128)(2,1)}, u32[]{:S(2)}, u32[]{:S(2)}) collective-permute-start(bf16[1024,1024]{1,0:T(8,128)(2,1)} %broadcast_select_fusion), channel_id=1, source_target_pairs={{0,1},{2,3},{5,4},{7,6},{8,9},{10,11},{16,17},{18,19},{21,20},{23,... | collective-permute-start | bytes 6291464 | tf_op jit(solution)/shard_map/ppermute | solution.py:289
  178.6 45.0 %collective-permute-start.17 = (bf16[1024,1024]{1,0:T(8,128)(2,1)}, bf16[1024,1024]{1,0:T(8,128)(2,1)}, u32[]{:S(2)}, u32[]{:S(2)}) collective-permute-start(bf16[1024,1024]{1,0:T(8,128)(2,1)} %constant_dynamic-update-slice_fusion.h2), channel_id=1, source_target_pairs={{0,2},{5,7},{16,18},{21,23}} | collective-permute-start | bytes 6291464 | tf_op jit(solution)/shard_map/ppermute | solution.py:289
  195.3 28.3 %collective-permute-start.13 = (bf16[512,1024]{1,0:T(8,128)(2,1)}, bf16[512,1024]{1,0:T(8,128)(2,1)}, u32[]{:S(2)}, u32[]{:S(2)}) collective-permute-start(bf16[512,1024]{1,0:T(8,128)(2,1)} %get-tuple-element.24), channel_id=1, source_target_pairs={{4,0},{5,1},{6,2},{7,3},{20,16},{21,17},{22,18},{23,19}} | collective-permute-start | bytes 3145736 | tf_op jit(solution)/shard_map/ppermute | solution.py:289
  196.6 27.0 %collective-permute-start.14 = (bf16[512,1024]{1,0:T(8,128)(2,1)}, bf16[512,1024]{1,0:T(8,128)(2,1)}, u32[]{:S(2)}, u32[]{:S(2)}) collective-permute-start(bf16[512,1024]{1,0:T(8,128)(2,1)} %get-tuple-element.22._dep), channel_id=1, source_target_pairs={{8,4},{9,5},{10,6},{11,7},{12,8},{13,9},{14,10},{15,11},{24,20},{2... | collective-permute-start | bytes 3145736 | tf_op jit(solution)/shard_map/ppermute | solution.py:289
  198.2 2.2 copy-start.14
  200.4 1.6 copy-start.17
  202.0 1.0 copy-start.18
  203.0 28.7 %copy-start.5 = (bf16[1024,1024]{1,0:T(8,128)(2,1)S(1)}, bf16[1024,1024]{1,0:T(8,128)(2,1)}, u32[]{:S(2)}) copy-start(bf16[1024,1024]{1,0:T(8,128)(2,1)} %l0.9) | copy-start | bytes 6291460
  207.8 25.1 %copy-start.11 = (bf16[512,1024]{1,0:T(8,128)(2,1)S(1)}, bf16[512,1024]{1,0:T(8,128)(2,1)}, u32[]{:S(2)}) copy-start(bf16[512,1024]{1,0:T(8,128)(2,1)} %copy-done.9) | copy-start | bytes 3145732
  207.9 23.8 %collective-permute-start.15 = (bf16[512,512]{1,0:T(8,128)(2,1)S(1)}, bf16[512,512]{1,0:T(8,128)(2,1)S(1)}, u32[]{:S(2)}, u32[]{:S(2)}) collective-permute-start(bf16[512,512]{1,0:T(8,128)(2,1)S(1)} %get-tuple-element.23._dep), channel_id=1, source_target_pairs={{0,4},{1,5},{2,6},{3,7},{4,0},{5,1},{6,2},{7,3},{8,12},{9,13},{10,... | collective-permute-start | bytes 1572872 | tf_op jit(solution)/shard_map/ppermute | solution.py:289
  238.1 56.6 %collective-permute-start.18 = (bf16[2048,1024]{1,0:T(8,128)(2,1)}, bf16[2048,1024]{1,0:T(8,128)(2,1)}, u32[]{:S(2)}, u32[]{:S(2)}) collective-permute-start(bf16[2048,1024]{1,0:T(8,128)(2,1)} %maximum_select_fusion), channel_id=1, source_target_pairs={{0,1},{2,3},{5,4},{7,6},{16,17},{18,19},{21,20},{23,22}} | collective-permute-start | bytes 12582920 | tf_op jit(solution)/shard_map/ppermute | solution.py:289
  241.4 51.2 %collective-permute-start.19 = (bf16[512,1024]{1,0:T(8,128)(2,1)S(1)}, bf16[512,1024]{1,0:T(8,128)(2,1)S(1)}, u32[]{:S(2)}, u32[]{:S(2)}) collective-permute-start(bf16[512,1024]{1,0:T(8,128)(2,1)S(1)} %get-tuple-element.27._dep), channel_id=1, source_target_pairs={{4,0},{5,1},{6,2},{7,3},{8,4},{9,5},{10,6},{11,7},{12,8},{13,9},{1... | collective-permute-start | bytes 3145736 | tf_op jit(solution)/shard_map/ppermute | solution.py:289
  242.7 48.6 %collective-permute-start.20 = (bf16[512,512]{1,0:T(8,128)(2,1)S(1)}, bf16[512,512]{1,0:T(8,128)(2,1)S(1)}, u32[]{:S(2)}, u32[]{:S(2)}) collective-permute-start(bf16[512,512]{1,0:T(8,128)(2,1)S(1)} %get-tuple-element.29), channel_id=1, source_target_pairs={{0,4},{1,5},{2,6},{3,7},{4,0},{5,1},{6,2},{7,3},{8,12},{9,13},{10,... | collective-permute-start | bytes 1572872 | tf_op jit(solution)/shard_map/ppermute | solution.py:289
  245.5 45.8 %collective-permute-start.21 = (bf16[512,512]{1,0:T(8,128)(2,1)S(1)}, bf16[512,512]{1,0:T(8,128)(2,1)S(1)}, u32[]{:S(2)}, u32[]{:S(2)}) collective-permute-start(bf16[512,512]{1,0:T(8,128)(2,1)S(1)} %shard_map.76), channel_id=1, source_target_pairs={{0,8},{1,9},{2,10},{3,11},{4,12},{5,13},{6,14},{7,15},{8,0},{9,1},... | collective-permute-start | bytes 1572872 | tf_op jit(solution)/shard_map/ppermute | solution.py:289
  250.8 2.0 copy-start.8
  252.8 39.8 %copy-start.7 = (f32[512,1024]{1,0:T(8,128)S(1)}, f32[512,1024]{1,0:T(8,128)}, u32[]{:S(2)}) copy-start(f32[512,1024]{1,0:T(8,128)} %copy-done.6) | copy-start | bytes 6291460
  252.8 39.8 %copy-start.20 = (s32[8]{0:T(128)S(1)}, s32[8]{0:T(128)}, u32[]{:S(2)}) copy-start(s32[8]{0:T(128)} %structure.1) | copy-start | bytes 100
Sparse Core Ops, SparseCore 0:
  25.5 21.6 all-gather.4
  109.4 46.4 all-gather.2

commit v6 on v5

--- a/solution.py
+++ b/solution.py
@@ -83,9 +83,16 @@
 
 
 def product_kernel(l0, l1, l2, l3, p0, p1, p2, p3, *refs, deps, gated):
+    below = refs[deps]
     t_ref, tt_ref, sent_ref = refs[deps + gated : deps + gated + 3]
-    rows, panels, acc, row_sems, panel_sems = refs[deps + 2 * gated + 3 :]
+    rows, panels, acc, row_sems, panel_sems, sem = refs[deps + 2 * gated + 3 :]
     r, c = position()
+    half = below.at[sent_ref.shape[0] :]
+
+    @pl.when((r == 1) | (r == 2))
+    def _():
+        start(half, sent_ref, sem)
+
     for m, ref in enumerate((l0, l1, l2, l3)):
         j = c ^ m
 
@@ -125,6 +132,10 @@
         def _(i):
             sent_ref[tile(i), :] = dot(tt_ref[tile(i), :], rows[3]).astype(BF16)
 
+    @pl.when((r == 1) | (r == 2))
+    def _():
+        wait(half, sent_ref, sem)
+
 
 def own_kernel(l0, l1, l2, l3, tt_ref, own_ref, block, sem):
     r, c = position()
@@ -159,6 +170,10 @@
             def _(j):
                 term = dot(tt_ref[tile(j), :], block[...])
                 sent_ref[tile(j), :] = (term + came_ref[tile(j), :].astype(F32)).astype(BF16)
+
+    @pl.when((i < 0) & (r == 1))
+    def _():
+        sent_ref[...] = came_ref[...]
 
 
 def child_kernel(
@@ -200,16 +215,15 @@
         acc_ref[...] = jnp.zeros_like(acc_ref)
 
 
-def root_kernel(acc_ref, h1, h2, h3, x1, x2, x3, b1, b23, out_ref, acc, left, held, left_sems, held_sems):
+def root_kernel(acc_ref, h1, h2, h3, b1, b2, b3, x1, x2, x3, f1, f2, f3, out_ref, acc, left, held, left_sems, held_sems):
     r, c = position()
-    rows = h1.shape[0]
-    refs = ((h1, x1, b1), (h2, x2, b23.at[:rows]), (h3, x3, b23.at[rows:]))
+    refs = ((h1, b1, x1, f1), (h2, b2, x2, f2), (h3, b3, x3, f3))
     needed = [(r + s < N) & (c <= r + s) for s in (1, 2, 3)]
     for s, places in enumerate(refs):
 
         @pl.when(needed[s])
         def _():
-            start_picked(places, source(r, c), left.at[s], left_sems.at[s])
+            start_picked(places, r ^ c, left.at[s], left_sems.at[s])
             start(places[0], held.at[s], held_sems.at[s])
 
     acc[...] = acc_ref[...]
@@ -225,10 +239,6 @@
                 acc[tile(i), :] += inner_dot(left[s, :, tile(i)], held[s])
 
     out_ref[...] = acc[...].astype(BF16)
-
-
-def source(r, c):
-    return jnp.where(c == r, 0, jnp.where(c == (r ^ 2), 1, 2))
 
 
 def cross_end_kernel(structure, own_ref, came_ref, out_ref):
@@ -239,7 +249,7 @@
         out_ref[rows, :] = jnp.where(kept, -total.T, jnp.zeros_like(total.T)).astype(BF16)
 
 
-def child_end_kernel(own_ref, near_ref, last_ref, out_ref):
+def child_end_kernel(own_ref, near_ref, last_ref, _dep, out_ref):
     total = own_ref[...] + near_ref[...].astype(F32) + last_ref[...].astype(F32)
     out_ref[...] = total.T
 
@@ -311,19 +321,31 @@
         panel_1 = up(panel_kept, 1)
         root_across = move(root_inverse, lambda r, c: (r, c ^ 2) if lower(r, c) else None)
         below_1 = down(root_inverse, 1)
-        root_beside = move(root_inverse, lambda r, c: (r, c ^ 1) if lower(r, c) else None)
+        (root_late,) = together(root_inverse, earlier=(panel_1,))
+        root_beside = move(root_late, lambda r, c: (r, c ^ 1) if lower(r, c) else None)
+        across_3 = move(root_late, lambda r, c: (0, 2) if (r, c) == (3, 0) else None)
         panel_2 = up(panel_1, 2)
         (panel_2,) = together(panel_2, earlier=(below_1, root_across, root_beside))
         panel_3 = up(panel_2, 3)
         root_both = move(root_across, lambda r, c: (r, c ^ 1) if lower(r, c ^ 2) else None)
         below_2a = down(below_1[:half], 2)
-        across_1 = move(below_1, lambda r, c: (r, c ^ 2) if r == c and r in (1, 2) else None)
-        across_3 = move(root_across, lambda r, c: (0, 2) if (r, c) == (3, 2) else None)
+
+        def to_across(x, rows):
+            return move(x, lambda r, c: (r, c ^ 2) if r == c and r in rows else None)
+
+        def to_beside(x, rows):
+            return move(x, lambda r, c: (r, c ^ 1) if r == c and r in rows else None)
+
+        def on_beside(x, rows):
+            return move(x, lambda r, c: (r, c ^ 1) if r == c ^ 2 and r in rows else None)
+
+        across_1 = to_across(below_1, (1, 2))
+        beside_1 = to_beside(below_1, (0, 1, 2))
 
         root_row = (root_inverse, root_beside, root_across, root_both)
         panels = (panel_kept, panel_1, panel_2, panel_3)
         t, t_t, sent, below_1, below_2a = local_call(
-            functools.partial(product_kernel, deps=1, gated=2),
+            functools.partial(product_kernel, deps=2, gated=2),
             [ANY] * 8,
             [shape((h, w), BF16), t_block, t_block],
             [
@@ -332,20 +354,22 @@
                 pltpu.VMEM((h, w), F32),
                 dma((n,)),
                 dma((n,)),
+                dma,
             ],
             *root_row,
             *panels,
             across_1,
+            beside_1,
             below_1,
             below_2a,
             gated=2,
         )
         t_row = lax.all_gather(t, "col", axis=1, tiled=True)
-        step = lambda x, q: move(x, lambda r, c: (r - 1, c) if q + r - 3 >= 0 else None)
+        step = lambda x: move(x, lambda r, c: (r - 1, c))
         chain = [ANY] * 4 + [VMEM] * 2
-        came = step(sent, 0)
-        below_2b = down(below_1[half:], 2)
+        below_2b = came = step(sent)
         below_3a = down(below_2a, 3)
+        far_1 = on_beside(across_1, (1, 2))
         (own,) = local_call(
             own_kernel,
             [ANY] * 4 + [VMEM],
@@ -354,8 +378,8 @@
             *root_row,
             t_t,
         )
-        sent, below_2b, across_1 = local_call(
-            functools.partial(chain_kernel, step=1, deps=3, gated=2),
+        sent, below_2a = local_call(
+            functools.partial(chain_kernel, step=1, deps=4, gated=1),
             chain,
             [t_block],
             [pltpu.VMEM((h, h), BF16), dma],
@@ -364,24 +388,15 @@
             came,
             own,
             below_3a,
+            far_1,
             across_3,
-            below_2b,
-            across_1,
-            gated=2,
-        )
-        came = step(sent, 1)
-        below_3b = down(below_2b, 3)
+            below_2a,
+            gated=1,
+        )
         below_2 = jnp.concatenate((below_2a, below_2b), 0)
-        across_2 = move(below_2, lambda r, c: (r, c ^ 2) if r == c and r in (0, 1) else None)
-        c_is_r = lax.axis_index("col") == lax.axis_index("row")
-
-        def to_beside(held, across, last_row):
-            return move(
-                jnp.where(c_is_r, held, across),
-                lambda r, c: (r, c ^ 1) if r in (c, c ^ 2) and r <= last_row else None,
-            )
-
-        beside_1 = to_beside(below_1, across_1, 2)
+        below_3b = came = step(sent)
+        across_2 = to_across(below_2, (0, 1))
+        beside_2 = to_beside(below_2, (0, 1))
 
         far_part, near_part, child_on, child_own = local_call(
             child_kernel,
@@ -395,6 +410,7 @@
             sent,
         )
         child_far = move(far_part, lambda r, c: (r ^ 1, c))
+        child_near = move(near_part, lambda r, c: (r ^ 1, c))
         (root_sum,) = local_call(
             diagonal_kernel,
             [],
@@ -403,30 +419,31 @@
             *root_row,
             far_part,
         )
-        sent, across_2 = local_call(
-            functools.partial(chain_kernel, step=2, deps=3, gated=1),
+        sent, across_2, across_3, below_3a = local_call(
+            functools.partial(chain_kernel, step=2, deps=3, gated=3),
             chain,
             [t_block],
             [pltpu.VMEM((h, h), BF16), dma],
             *root_row,
             t_t,
             came,
-            below_3b,
             child_far,
-            beside_1,
+            child_near,
+            beside_2,
             across_2,
-            gated=1,
-        )
-        came = step(sent, 2)
+            across_3,
+            below_3a,
+            gated=3,
+        )
+        came = step(sent)
         (child_onward,) = local_call(
             child_onward_kernel, [VMEM] * 2, [child_block], [], child_on, child_far, sent
         )
         child_last = move(child_onward, lambda r, c: (r ^ 2, c))
-        child_near = move(near_part, lambda r, c: (r ^ 1, c))
         below_3 = jnp.concatenate((below_3a, below_3b), 0)
-        beside_23 = to_beside(
-            jnp.concatenate((below_2, below_3), 0), jnp.concatenate((across_2, across_3), 0), 1
-        )
+        beside_3 = to_beside(below_3, (0,))
+        far_2 = on_beside(across_2, (0, 1))
+        far_3 = on_beside(across_3, (0,))
         (sigma_cross,) = local_call(
             cross_end_kernel,
             [SMEM] + [VMEM] * 2,
@@ -451,11 +468,15 @@
             below_1,
             below_2,
             below_3,
+            beside_1,
+            beside_2,
+            beside_3,
             across_1,
             across_2,
             across_3,
-            beside_1,
-            beside_23,
+            far_1,
+            far_2,
+            far_3,
         )
         (sigma_child,) = local_call(
             child_end_kernel,
@@ -465,6 +486,7 @@
             child_own,
             child_near,
             child_last,
+            sigma_root,
         )
         return (sigma_root, sigma_cross, sigma_child)
 

time: 319 us -> 320 us (level)
  waiting for transfers between devices: 169 us -> 190 us
  starting transfers between devices: 61.1 us -> 47.8 us
  other arithmetic: 12.2 us -> 2.23 us
    ppermute x22 -> x24, waiting for transfers between devices: 169 us -> 190 us  [move(): return lax.ppermute(x, AXES, pairs)]
    ppermute x22 -> x24, starting transfers between devices: 61.1 us -> 47.8 us  [move(): return lax.ppermute(x, AXES, pairs)]
    select_n x2 -> x0, other arithmetic: 8.4 us -> none  [to_beside(): jnp.where(c_is_r, held, across)]
    unnamed x43 -> x57, local copies, waits for them, and re-layouts: 18.4 us -> 20.2 us
  transfers between devices with their start and end apart: 24 -> 26, of which waited for: 8 -> 10; matrix products, arithmetic and copies ran while one was open for 4% -> 2% of each run, Pallas kernels for 6% -> 10%
where the time goes in v6:
time: 320 us; the launch traced here: 316 us
  waiting for transfers between devices  190 us (59%)
  starting transfers between devices  47.8 us (15%)
  Pallas kernels  36 us (11%)
  local copies, waits for them, and re-layouts  25.5 us (8%)
  between operations  14.4 us (4%)
    ppermute x24, waiting for transfers between devices, move(): return lax.ppermute(x, AXES, pairs)  190 us
    ppermute x24, starting transfers between devices, move(): return lax.ppermute(x, AXES, pairs)  47.8 us
    pallas_call x10, Pallas kernels, local_call(): pl.pallas_call(kernel, out_shape=outs, in_specs=in_specs + [ANY] * (len(a...  36 us
    unnamed x57, local copies, waits for them, and re-layouts  20.2 us
  transfers between devices with their start and end apart: 26, of which 10 were waited for; matrix products, arithmetic and copies ran while one was open for 2% of the time, Pallas kernels for 10%

profile of v6, /device:TPU:0, one launch (start us, length us, event | category | flops | bytes accessed | tf_op | source)
XLA Modules:
  0.0 316.3 jit_solution(12941031869653828393)
XLA Ops:
  7.2 0.8 broadcast_compare_fusion
  8.1 1.4 broadcast_select_fusion.p0
  9.5 5.0 %collective-permute-start = (bf16[1024,512]{1,0:T(8,128)(2,1)S(1)}, bf16[1024,512]{1,0:T(8,128)(2,1)S(1)}, u32[]{:S(2)}, u32[]{:S(2)}) collective-permute-start(bf16[1024,512]{1,0:T(8,128)(2,1)S(1)} %broadcast_select_fusion.p0), channel_id=1, source_target_pairs={{0,4},{1,5},{2,6},{3,7},{4,8},{5,9},{6,10},{7,11},{8,12},{9,13},{1... | collective-permute-start | bytes 3145736 | tf_op jit(solution)/shard_map/ppermute | solution.py:299
  14.6 1.3 collective-permute-start.5
  15.9 5.4 %collective-permute-start.2 = (bf16[1024,1024]{1,0:T(8,128)(2,1)S(1)}, bf16[1024,1024]{1,0:T(8,128)(2,1)}, u32[]{:S(2)}, u32[]{:S(2)}) collective-permute-start(bf16[1024,1024]{1,0:T(8,128)(2,1)S(1)} %copy-done), channel_id=1, source_target_pairs={{0,2},{4,6},{5,7},{8,10},{9,11},{10,8},{12,14},{13,15},{14,12},{15... | collective-permute-start | bytes 6291464 | tf_op jit(solution)/shard_map/ppermute | solution.py:299
  21.3 1.3 copy.15.refs_0_
  22.6 14.3 %collective-permute-done.refs_1_.p1 = bf16[1024,512]{1,0:T(8,128)(2,1)S(1)} collective-permute-done((bf16[1024,512]{1,0:T(8,128)(2,1)S(1)}, bf16[1024,512]{1,0:T(8,128)(2,1)S(1)}, u32[]{:S(2)}, u32[]{:S(2)}) %collective-permute-start) | collective-permute-done | bytes 1048608 | tf_op jit(solution)/shard_map/ppermute | solution.py:299
  36.9 1.0 copy-done.14
  37.8 2.7 collective-permute-start.1
  40.6 1.7 collective-permute-start.4
  42.2 21.4 %collective-permute-done.5.refs_1_.refs_2_ = bf16[1024,1024]{1,0:T(8,128)(2,1)} collective-permute-done((bf16[1024,1024]{1,0:T(8,128)(2,1)S(1)}, bf16[1024,1024]{1,0:T(8,128)(2,1)}, u32[]{:S(2)}, u32[]{:S(2)}) %collective-permute-start.5) | collective-permute-done | bytes 2097184 | tf_op jit(solution)/shard_map/ppermute | solution.py:299
  63.6 2.6 collective-permute-start.8
  66.3 2.0 collective-permute-start.7
  68.3 2.1 collective-permute-start.3
  70.4 2.3 slice.4
  72.7 1.3 collective-permute-start.9
  74.0 0.7 collective-permute-start.6
  74.7 31.8 %collective-permute-done.9.refs_3_ = bf16[512,1024]{1,0:T(8,128)(2,1)S(1)} collective-permute-done((bf16[512,1024]{1,0:T(8,128)(2,1)}, bf16[512,1024]{1,0:T(8,128)(2,1)S(1)}, u32[]{:S(2)}, u32[]{:S(2)}) %collective-permute-start.9) | collective-permute-done | bytes 1048608 | tf_op jit(solution)/shard_map/ppermute | solution.py:299
  106.5 1.0 copy-done.9
  107.5 1.2 copy-done.10
  108.8 1.2 copy-done.15
  110.0 1.2 copy-done.17
  111.2 2.6 shard_map.69
  113.9 1.0 copy-done.11
  114.9 1.0 copy-done.21
  115.8 1.0 copy-done.25
  116.8 0.8 collective-permute-start.13
  117.6 0.8 collective-permute-start.12
  118.4 1.3 collective-permute-start.10
  119.7 1.3 collective-permute-start.11
  121.0 1.6 shard_map.70.refs_0_.own_ref
  122.6 1.4 copy-done.1
  124.0 48.3 %collective-permute-done.10.came_ref = bf16[512,1024]{1,0:T(8,128)(2,1)S(1)} collective-permute-done((bf16[512,1024]{1,0:T(8,128)(2,1)}, bf16[512,1024]{1,0:T(8,128)(2,1)S(1)}, u32[]{:S(2)}, u32[]{:S(2)}) %collective-permute-start.10) | collective-permute-done | bytes 1048608 | tf_op jit(solution)/shard_map/ppermute | solution.py:299
  172.3 17.9 %collective-permute-done.11.refs_1_.refs_5_ = bf16[512,1024]{1,0:T(8,128)(2,1)S(1)} collective-permute-done((bf16[512,1024]{1,0:T(8,128)(2,1)}, bf16[512,1024]{1,0:T(8,128)(2,1)S(1)}, u32[]{:S(2)}, u32[]{:S(2)}) %collective-permute-start.11) | collective-permute-done | bytes 1048608 | tf_op jit(solution)/shard_map/ppermute | solution.py:299
  190.3 1.3 copy-done.26
  191.6 1.0 shard_map.71
  192.6 1.1 constant_dynamic-update-slice_fusion.1
  193.7 1.0 constant_dynamic-update-slice_fusion.h2
  194.7 2.6 collective-permute-start.18
  197.4 2.7 collective-permute-start.17
  200.0 1.3 collective-permute-start.14
  201.4 2.2 copy-done.18
  203.5 1.6 copy-done.19
  205.1 1.0 copy-done.20
  206.2 4.8 %shard_map.72 = (bf16[512,512]{1,0:T(8,128)(2,1)S(1)}, bf16[512,512]{1,0:T(8,128)(2,1)S(1)}, f32[512,512]{1,0:T(8,128)S(1)}, f32[512,512]{1,0:T(8,128)S(1)}) custom-call(bf16[512,1024]{1,0:T(8,128)(2,1)S(1)} %get-tuple-element.18.tt_ref, bf16[1024,2048]{1,0:T(8,128)(2,1)S(1)} %copy-done.18, bf16[512,512]{1,0:T(8,128)(2,1)S(1)} %copy-done.20, ...), custom_call_target="tpu_custom_call" | custom-call | flops 1 | bytes 1 | tf_op jit(solution)/shard_map/pallas_call | solution.py:265
  211.0 2.7 collective-permute-start.16
  213.8 14.5 %collective-permute-done.14.came_ref = bf16[512,1024]{1,0:T(8,128)(2,1)} collective-permute-done((bf16[512,1024]{1,0:T(8,128)(2,1)}, bf16[512,1024]{1,0:T(8,128)(2,1)}, u32[]{:S(2)}, u32[]{:S(2)}) %collective-permute-start.14) | collective-permute-done | bytes 1048608 | tf_op jit(solution)/shard_map/ppermute | solution.py:299
  228.3 11.1 %collective-permute-done.16.refs_1_.near_ref = bf16[512,512]{1,0:T(8,128)(2,1)S(1)} collective-permute-done((bf16[512,512]{1,0:T(8,128)(2,1)S(1)}, bf16[512,512]{1,0:T(8,128)(2,1)S(1)}, u32[]{:S(2)}, u32[]{:S(2)}) %collective-permute-start.16) | collective-permute-done | bytes 524320 | tf_op jit(solution)/shard_map/ppermute | solution.py:299
  239.4 8.7 %collective-permute-done.15.refs_0_.far_ref = bf16[512,512]{1,0:T(8,128)(2,1)S(1)} collective-permute-done((bf16[512,512]{1,0:T(8,128)(2,1)S(1)}, bf16[512,512]{1,0:T(8,128)(2,1)S(1)}, u32[]{:S(2)}, u32[]{:S(2)}) %collective-permute-start.15) | collective-permute-done | bytes 524320 | tf_op jit(solution)/shard_map/ppermute | solution.py:299
  248.1 2.2 shard_map.74
  250.4 2.0 constant_dynamic-update-slice_fusion.2.h3
  252.4 1.6 collective-permute-start.19
  254.0 2.0 collective-permute-start.20
  255.9 2.1 collective-permute-start.21
  258.0 1.3 collective-permute-start.22
  259.3 0.9 shard_map.77
  260.2 2.6 collective-permute-start.23
  262.8 3.3 %shard_map.73.acc_ref = f32[1024,1024]{1,0:T(8,128)S(1)} custom-call(bf16[1024,1024]{1,0:T(8,128)(2,1)S(1)} %copy-done, bf16[1024,1024]{1,0:T(8,128)(2,1)} %collective-permute-done.1.refs_3_.l1, bf16[1024,1024]{1,0:T(8,128)(2,1)} %collective-permute-done.2.refs_2_.l2, bf16[1024,1024]{1,0:T(8,128)(2,1)} %collective-permute-done.3.l3, ...), custom_call_target="tpu_custom_call" | custom-call | flops 1 | bytes 1 | tf_op jit(solution)/shard_map/pallas_call | solution.py:265
  266.1 16.8 %collective-permute-done.22.came_ref = bf16[512,1024]{1,0:T(8,128)(2,1)S(1)} collective-permute-done((bf16[512,1024]{1,0:T(8,128)(2,1)}, bf16[512,1024]{1,0:T(8,128)(2,1)S(1)}, u32[]{:S(2)}, u32[]{:S(2)}) %collective-permute-start.22) | collective-permute-done | bytes 1048608 | tf_op jit(solution)/shard_map/ppermute | solution.py:299
  282.9 2.1 shard_map.76
  285.1 16.1 %shard_map.75._dep = bf16[1024,1024]{1,0:T(8,128)(2,1)} custom-call(f32[1024,1024]{1,0:T(8,128)} %copy-done.6, bf16[1024,1024]{1,0:T(8,128)(2,1)} %get-tuple-element.24.h1, bf16[1024,1024]{1,0:T(8,128)(2,1)} %constant_dynamic-update-slice_fusion.h2, bf16[1024,1024]{1,0:T(8,128)(2,1)S(1)} %constant_dynamic-update-slice_fusion.2.h3, ...), custom_call_target="tpu_custom_call" | custom-call | flops 1 | bytes 1 | tf_op jit(solution)/shard_map/pallas_call | solution.py:265
  301.2 5.4 %collective-permute-done.23.last_ref = bf16[512,512]{1,0:T(8,128)(2,1)S(1)} collective-permute-done((bf16[512,512]{1,0:T(8,128)(2,1)}, bf16[512,512]{1,0:T(8,128)(2,1)S(1)}, u32[]{:S(2)}, u32[]{:S(2)}) %collective-permute-start.23) | collective-permute-done | bytes 524320 | tf_op jit(solution)/shard_map/ppermute | solution.py:299
  306.6 1.6 copy-done.13
  308.2 1.3 shard_map.78
  (65 shorter events, 0.5 us)
Async XLA Ops:
  7.2 7.4 %copy-start = (bf16[1024,1024]{1,0:T(8,128)(2,1)S(1)}, bf16[1024,1024]{1,0:T(8,128)(2,1)}, u32[]{:S(2)}) copy-start(bf16[1024,1024]{1,0:T(8,128)(2,1)} %l0.9) | copy-start | bytes 6291460
  7.2 194.1 %all-gather.5.cloned.1.call-start = ((), (), s32[]{:S(2)}) async-start(), calls=%async_computation.1 | async-start | bytes 2621440 | tf_op jit(solution)/shard_map/all_gather | solution.py:320
  9.5 13.1 %copy-start.16 = (bf16[1024,512]{1,0:T(8,128)(2,1)}, bf16[1024,512]{1,0:T(8,128)(2,1)S(1)}, u32[]{:S(2)}) copy-start(bf16[1024,512]{1,0:T(8,128)(2,1)S(1)} %broadcast_select_fusion.p0) | copy-start | bytes 3145732
  9.5 27.3 %collective-permute-start = (bf16[1024,512]{1,0:T(8,128)(2,1)S(1)}, bf16[1024,512]{1,0:T(8,128)(2,1)S(1)}, u32[]{:S(2)}, u32[]{:S(2)}) collective-permute-start(bf16[1024,512]{1,0:T(8,128)(2,1)S(1)} %broadcast_select_fusion.p0), channel_id=1, source_target_pairs={{0,4},{1,5},{2,6},{3,7},{4,8},{5,9},{6,10},{7,11},{8,12},{9,13},{1... | collective-permute-start | bytes 3145736 | tf_op jit(solution)/shard_map/ppermute | solution.py:299
  14.6 49.1 %collective-permute-start.5 = (bf16[1024,1024]{1,0:T(8,128)(2,1)S(1)}, bf16[1024,1024]{1,0:T(8,128)(2,1)}, u32[]{:S(2)}, u32[]{:S(2)}) collective-permute-start(bf16[1024,1024]{1,0:T(8,128)(2,1)S(1)} %copy-done), channel_id=1, source_target_pairs={{4,0},{5,1},{8,4},{9,5},{10,6},{12,8},{13,9},{14,10},{15,11},{20,1... | collective-permute-start | bytes 6291464 | tf_op jit(solution)/shard_map/ppermute | solution.py:299
  15.9 52.5 %collective-permute-start.2 = (bf16[1024,1024]{1,0:T(8,128)(2,1)S(1)}, bf16[1024,1024]{1,0:T(8,128)(2,1)}, u32[]{:S(2)}, u32[]{:S(2)}) collective-permute-start(bf16[1024,1024]{1,0:T(8,128)(2,1)S(1)} %copy-done), channel_id=1, source_target_pairs={{0,2},{4,6},{5,7},{8,10},{9,11},{10,8},{12,14},{13,15},{14,12},{15... | collective-permute-start | bytes 6291464 | tf_op jit(solution)/shard_map/ppermute | solution.py:299
  36.9 1.0 copy-start.14
  37.8 36.1 %collective-permute-start.1 = (bf16[1024,1024]{1,0:T(8,128)(2,1)}, bf16[1024,1024]{1,0:T(8,128)(2,1)}, u32[]{:S(2)}, u32[]{:S(2)}) collective-permute-start(bf16[1024,1024]{1,0:T(8,128)(2,1)} %shard_map.67), channel_id=1, source_target_pairs={{0,1},{4,5},{5,4},{8,9},{9,8},{10,11},{12,13},{13,12},{14,15},{15,... | collective-permute-start | bytes 6291464 | tf_op jit(solution)/shard_map/ppermute | solution.py:299
  40.5 160.8 %all-gather.3.cloned.1.call-start = ((), (), s32[]{:S(2)}) async-start(), calls=%async_computation | async-start | bytes 5242880 | tf_op jit(solution)/shard_map/all_gather | solution.py:367
  40.6 32.1 %collective-permute-start.4 = (bf16[1024,512]{1,0:T(8,128)(2,1)}, bf16[1024,512]{1,0:T(8,128)(2,1)}, u32[]{:S(2)}, u32[]{:S(2)}) collective-permute-start(bf16[1024,512]{1,0:T(8,128)(2,1)} %copy-done.14), channel_id=1, source_target_pairs={{4,8},{5,9},{6,10},{7,11},{8,12},{9,13},{10,14},{11,15},{20,24},{2... | collective-permute-start | bytes 3145736 | tf_op jit(solution)/shard_map/ppermute | solution.py:299
  63.6 43.9 %collective-permute-start.8 = (bf16[1024,1024]{1,0:T(8,128)(2,1)}, bf16[1024,1024]{1,0:T(8,128)(2,1)}, u32[]{:S(2)}, u32[]{:S(2)}) collective-permute-start(bf16[1024,1024]{1,0:T(8,128)(2,1)} %collective-permute-done.5.refs_1_.refs_2_), channel_id=1, source_target_pairs={{0,1},{5,4},{10,11},{16,17},{21,20},{26,27}} | collective-permute-start | bytes 6291464 | tf_op jit(solution)/shard_map/ppermute | solution.py:299
  66.3 41.2 %collective-permute-start.7 = (bf16[1024,1024]{1,0:T(8,128)(2,1)}, bf16[1024,1024]{1,0:T(8,128)(2,1)}, u32[]{:S(2)}, u32[]{:S(2)}) collective-permute-start(bf16[1024,1024]{1,0:T(8,128)(2,1)} %collective-permute-done.5.refs_1_.refs_2_), channel_id=1, source_target_pairs={{5,7},{10,8},{21,23},{26,24}} | collective-permute-start | bytes 6291464 | tf_op jit(solution)/shard_map/ppermute | solution.py:299
  68.3 39.2 %collective-permute-start.3 = (bf16[1024,1024]{1,0:T(8,128)(2,1)}, bf16[1024,1024]{1,0:T(8,128)(2,1)}, u32[]{:S(2)}, u32[]{:S(2)}) collective-permute-start(bf16[1024,1024]{1,0:T(8,128)(2,1)} %collective-permute-done.2.refs_2_.l2), channel_id=1, source_target_pairs={{2,3},{6,7},{7,6},{8,9},{10,11},{11,10},{12,13},{13,12},{14,15},{1... | collective-permute-start | bytes 6291464 | tf_op jit(solution)/shard_map/ppermute | solution.py:299
  72.7 33.9 %collective-permute-start.9 = (bf16[512,1024]{1,0:T(8,128)(2,1)}, bf16[512,1024]{1,0:T(8,128)(2,1)S(1)}, u32[]{:S(2)}, u32[]{:S(2)}) collective-permute-start(bf16[512,1024]{1,0:T(8,128)(2,1)} %slice.4), channel_id=1, source_target_pairs={{4,0},{5,1},{6,2},{8,4},{9,5},{10,6},{11,7},{20,16},{21,17},{22,18... | collective-permute-start | bytes 3145736 | tf_op jit(solution)/shard_map/ppermute | solution.py:299
  74.0 33.5 %collective-permute-start.6 = (bf16[1024,512]{1,0:T(8,128)(2,1)}, bf16[1024,512]{1,0:T(8,128)(2,1)S(1)}, u32[]{:S(2)}, u32[]{:S(2)}) collective-permute-start(bf16[1024,512]{1,0:T(8,128)(2,1)} %shard_map.68.p2), channel_id=1, source_target_pairs={{8,12},{9,13},{10,14},{11,15},{24,28},{25,29},{26,30},{27,31}} | collective-permute-start | bytes 3145736 | tf_op jit(solution)/shard_map/ppermute | solution.py:299
  106.5 1.0 copy-start.9
  107.5 1.2 copy-start.10
  108.8 1.2 copy-start.15
  110.0 1.2 copy-start.17
  113.8 1.0 copy-start.11
  114.9 1.0 copy-start.21
  115.8 1.0 copy-start.25
  116.8 7.2 %collective-permute-start.13 = (bf16[1024,1024]{1,0:T(8,128)(2,1)}, bf16[1024,1024]{1,0:T(8,128)(2,1)S(1)}, u32[]{:S(2)}, u32[]{:S(2)}) collective-permute-start(bf16[1024,1024]{1,0:T(8,128)(2,1)} %shard_map.67), channel_id=1, source_target_pairs={{12,2},{28,18}} | collective-permute-start | bytes 6291464 | tf_op jit(solution)/shard_map/ppermute | solution.py:299
  117.6 72.6 %collective-permute-start.12 = (bf16[1024,1024]{1,0:T(8,128)(2,1)}, bf16[1024,1024]{1,0:T(8,128)(2,1)S(1)}, u32[]{:S(2)}, u32[]{:S(2)}) collective-permute-start(bf16[1024,1024]{1,0:T(8,128)(2,1)} %collective-permute-done.7.refs_0_.x1), channel_id=1, source_target_pairs={{7,6},{8,9},{23,22},{24,25}} | collective-permute-start | bytes 6291464 | tf_op jit(solution)/shard_map/ppermute | solution.py:299
  118.4 53.9 %collective-permute-start.10 = (bf16[512,1024]{1,0:T(8,128)(2,1)}, bf16[512,1024]{1,0:T(8,128)(2,1)S(1)}, u32[]{:S(2)}, u32[]{:S(2)}) collective-permute-start(bf16[512,1024]{1,0:T(8,128)(2,1)} %copy-done.25), channel_id=1, source_target_pairs={{4,0},{5,1},{6,2},{7,3},{8,4},{9,5},{10,6},{11,7},{12,8},{13,9},{1... | collective-permute-start | bytes 3145736 | tf_op jit(solution)/shard_map/ppermute | solution.py:299
  119.7 70.5 %collective-permute-start.11 = (bf16[512,1024]{1,0:T(8,128)(2,1)}, bf16[512,1024]{1,0:T(8,128)(2,1)S(1)}, u32[]{:S(2)}, u32[]{:S(2)}) collective-permute-start(bf16[512,1024]{1,0:T(8,128)(2,1)} %copy-done.11), channel_id=1, source_target_pairs={{4,0},{5,1},{6,2},{7,3},{20,16},{21,17},{22,18},{23,19}} | collective-permute-start | bytes 3145736 | tf_op jit(solution)/shard_map/ppermute | solution.py:299
  121.0 70.5 %copy-start.12 = (bf16[512,1024]{1,0:T(8,128)(2,1)S(1)}, bf16[512,1024]{1,0:T(8,128)(2,1)}, u32[]{:S(2)}) copy-start(bf16[512,1024]{1,0:T(8,128)(2,1)} %copy-done.11) | copy-start | bytes 3145732
  122.6 1.4 copy-start.1
  124.0 66.2 %copy-start.3 = (bf16[1024,1024]{1,0:T(8,128)(2,1)}, bf16[1024,1024]{1,0:T(8,128)(2,1)S(1)}, u32[]{:S(2)}) copy-start(bf16[1024,1024]{1,0:T(8,128)(2,1)S(1)} %collective-permute-done.13.refs_3_.refs_4_) | copy-start | bytes 6291460
  190.2 2.3 copy-start.7
  190.2 1.3 copy-start.26
  194.7 33.6 %collective-permute-start.18 = (bf16[1024,1024]{1,0:T(8,128)(2,1)}, bf16[1024,1024]{1,0:T(8,128)(2,1)}, u32[]{:S(2)}, u32[]{:S(2)}) collective-permute-start(bf16[1024,1024]{1,0:T(8,128)(2,1)} %constant_dynamic-update-slice_fusion.h2), channel_id=1, source_target_pairs={{0,2},{5,7},{16,18},{21,23}} | collective-permute-start | bytes 6291464 | tf_op jit(solution)/shard_map/ppermute | solution.py:299
  197.4 31.0 %collective-permute-start.17 = (bf16[1024,1024]{1,0:T(8,128)(2,1)}, bf16[1024,1024]{1,0:T(8,128)(2,1)}, u32[]{:S(2)}, u32[]{:S(2)}) collective-permute-start(bf16[1024,1024]{1,0:T(8,128)(2,1)} %constant_dynamic-update-slice_fusion.h2), channel_id=1, source_target_pairs={{0,1},{5,4},{16,17},{21,20}} | collective-permute-start | bytes 6291464 | tf_op jit(solution)/shard_map/ppermute | solution.py:299
  200.0 28.3 %collective-permute-start.14 = (bf16[512,1024]{1,0:T(8,128)(2,1)}, bf16[512,1024]{1,0:T(8,128)(2,1)}, u32[]{:S(2)}, u32[]{:S(2)}) collective-permute-start(bf16[512,1024]{1,0:T(8,128)(2,1)} %get-tuple-element.22._dep), channel_id=1, source_target_pairs={{4,0},{5,1},{6,2},{7,3},{8,4},{9,5},{10,6},{11,7},{12,8},{13,9},{1... | collective-permute-start | bytes 3145736 | tf_op jit(solution)/shard_map/ppermute | solution.py:299
  201.3 2.2 copy-start.18
  203.5 1.6 copy-start.19
  205.1 1.0 copy-start.20
  206.2 41.9 %copy-start.4 = (bf16[1024,1024]{1,0:T(8,128)(2,1)S(1)}, bf16[1024,1024]{1,0:T(8,128)(2,1)}, u32[]{:S(2)}) copy-start(bf16[1024,1024]{1,0:T(8,128)(2,1)} %copy-done.3) | copy-start | bytes 6291460
  206.2 41.9 %copy-start.8 = (bf16[512,1024]{1,0:T(8,128)(2,1)S(1)}, bf16[512,1024]{1,0:T(8,128)(2,1)}, u32[]{:S(2)}) copy-start(bf16[512,1024]{1,0:T(8,128)(2,1)} %copy-done.7) | copy-start | bytes 3145732
  211.0 39.3 %copy-start.22 = (bf16[512,512]{1,0:T(8,128)(2,1)}, bf16[512,512]{1,0:T(8,128)(2,1)S(1)}, u32[]{:S(2)}) copy-start(bf16[512,512]{1,0:T(8,128)(2,1)S(1)} %get-tuple-element.23._dep) | copy-start | bytes 1572868
  211.0 28.4 %collective-permute-start.16 = (bf16[512,512]{1,0:T(8,128)(2,1)S(1)}, bf16[512,512]{1,0:T(8,128)(2,1)S(1)}, u32[]{:S(2)}, u32[]{:S(2)}) collective-permute-start(bf16[512,512]{1,0:T(8,128)(2,1)S(1)} %get-tuple-element.26), channel_id=1, source_target_pairs={{0,4},{1,5},{2,6},{3,7},{4,0},{5,1},{6,2},{7,3},{8,12},{9,13},{10,... | collective-permute-start | bytes 1572872 | tf_op jit(solution)/shard_map/ppermute | solution.py:299
  213.7 34.4 %collective-permute-start.15 = (bf16[512,512]{1,0:T(8,128)(2,1)S(1)}, bf16[512,512]{1,0:T(8,128)(2,1)S(1)}, u32[]{:S(2)}, u32[]{:S(2)}) collective-permute-start(bf16[512,512]{1,0:T(8,128)(2,1)S(1)} %get-tuple-element.23._dep), channel_id=1, source_target_pairs={{0,4},{1,5},{2,6},{3,7},{4,0},{5,1},{6,2},{7,3},{8,12},{9,13},{10,... | collective-permute-start | bytes 1572872 | tf_op jit(solution)/shard_map/ppermute | solution.py:299
  250.3 15.8 %copy-start.5 = (bf16[1024,1024]{1,0:T(8,128)(2,1)}, bf16[1024,1024]{1,0:T(8,128)(2,1)S(1)}, u32[]{:S(2)}) copy-start(bf16[1024,1024]{1,0:T(8,128)(2,1)S(1)} %get-tuple-element.29.x3) | copy-start | bytes 6291460
  252.4 10.4 %copy-start.23 = (bf16[512,512]{1,0:T(8,128)(2,1)S(1)}, bf16[512,512]{1,0:T(8,128)(2,1)}, u32[]{:S(2)}) copy-start(bf16[512,512]{1,0:T(8,128)(2,1)} %copy-done.22) | copy-start | bytes 1572868
  252.4 32.6 %collective-permute-start.19 = (bf16[1024,1024]{1,0:T(8,128)(2,1)S(1)}, bf16[1024,1024]{1,0:T(8,128)(2,1)S(1)}, u32[]{:S(2)}, u32[]{:S(2)}) collective-permute-start(bf16[1024,1024]{1,0:T(8,128)(2,1)S(1)} %constant_dynamic-update-slice_fusion.2.h3), channel_id=1, source_target_pairs={{0,1},{16,17}} | collective-permute-start | bytes 6291464 | tf_op jit(solution)/shard_map/ppermute | solution.py:299
  254.0 31.1 %collective-permute-start.20 = (bf16[1024,1024]{1,0:T(8,128)(2,1)}, bf16[1024,1024]{1,0:T(8,128)(2,1)}, u32[]{:S(2)}, u32[]{:S(2)}) collective-permute-start(bf16[1024,1024]{1,0:T(8,128)(2,1)} %get-tuple-element.28.x2), channel_id=1, source_target_pairs={{2,3},{7,6},{18,19},{23,22}} | collective-permute-start | bytes 6291464 | tf_op jit(solution)/shard_map/ppermute | solution.py:299
  255.9 29.1 %collective-permute-start.21 = (bf16[1024,1024]{1,0:T(8,128)(2,1)S(1)}, bf16[1024,1024]{1,0:T(8,128)(2,1)}, u32[]{:S(2)}, u32[]{:S(2)}) collective-permute-start(bf16[1024,1024]{1,0:T(8,128)(2,1)S(1)} %get-tuple-element.29.x3), channel_id=1, source_target_pairs={{2,3},{18,19}} | collective-permute-start | bytes 6291464 | tf_op jit(solution)/shard_map/ppermute | solution.py:299
  258.0 24.9 %collective-permute-start.22 = (bf16[512,1024]{1,0:T(8,128)(2,1)}, bf16[512,1024]{1,0:T(8,128)(2,1)S(1)}, u32[]{:S(2)}, u32[]{:S(2)}) collective-permute-start(bf16[512,1024]{1,0:T(8,128)(2,1)} %get-tuple-element.30._dep), channel_id=1, source_target_pairs={{4,0},{5,1},{6,2},{7,3},{8,4},{9,5},{10,6},{11,7},{12,8},{13,9},{1... | collective-permute-start | bytes 3145736 | tf_op jit(solution)/shard_map/ppermute | solution.py:299
  260.2 22.7 %copy-start.2 = (f32[512,1024]{1,0:T(8,128)S(1)}, f32[512,1024]{1,0:T(8,128)}, u32[]{:S(2)}) copy-start(f32[512,1024]{1,0:T(8,128)} %copy-done.1) | copy-start | bytes 6291460
  260.2 22.7 %copy-start.24 = (s32[8]{0:T(128)S(1)}, s32[8]{0:T(128)}, u32[]{:S(2)}) copy-start(s32[8]{0:T(128)} %structure.1) | copy-start | bytes 100
  260.2 46.4 %collective-permute-start.23 = (bf16[512,512]{1,0:T(8,128)(2,1)}, bf16[512,512]{1,0:T(8,128)(2,1)S(1)}, u32[]{:S(2)}, u32[]{:S(2)}) collective-permute-start(bf16[512,512]{1,0:T(8,128)(2,1)} %shard_map.77), channel_id=1, source_target_pairs={{0,8},{1,9},{2,10},{3,11},{4,12},{5,13},{6,14},{7,15},{8,0},{9,1},... | collective-permute-start | bytes 1572872 | tf_op jit(solution)/shard_map/ppermute | solution.py:299
  266.1 18.9 %copy-start.6 = (f32[1024,1024]{1,0:T(8,128)}, f32[1024,1024]{1,0:T(8,128)S(1)}, u32[]{:S(2)}) copy-start(f32[1024,1024]{1,0:T(8,128)S(1)} %shard_map.73.acc_ref) | copy-start | bytes 12582916
  306.6 1.6 copy-start.13
Sparse Core Ops, SparseCore 0:
  40.6 24.1 all-gather.4
  116.9 64.8 all-gather.2

commit v7 on v6

--- a/solution.py
+++ b/solution.py
@@ -137,7 +137,7 @@
         wait(half, sent_ref, sem)
 
 
-def own_kernel(l0, l1, l2, l3, tt_ref, own_ref, block, sem):
+def own_kernel(l0, l1, l2, l3, tt_ref, _in, own_ref, _out, block, sem):
     r, c = position()
     start_picked((l0, l1, l2, l3), r ^ c, block, sem)
     wait(l0, block, sem)
@@ -317,18 +317,19 @@
         t_block, child_block = shape((w, h), BF16), shape((w, w), BF16)
 
         _, panel_kept = mask_panel(panel, structure)
-        child_row = lax.all_gather(child_inverse, "col", axis=1, tiled=True)
         panel_1 = up(panel_kept, 1)
         root_across = move(root_inverse, lambda r, c: (r, c ^ 2) if lower(r, c) else None)
         below_1 = down(root_inverse, 1)
         (root_late,) = together(root_inverse, earlier=(panel_1,))
         root_beside = move(root_late, lambda r, c: (r, c ^ 1) if lower(r, c) else None)
-        across_3 = move(root_late, lambda r, c: (0, 2) if (r, c) == (3, 0) else None)
         panel_2 = up(panel_1, 2)
         (panel_2,) = together(panel_2, earlier=(below_1, root_across, root_beside))
+        (child_late,) = together(child_inverse, earlier=(root_across,))
+        child_row = lax.all_gather(child_late, "col", axis=1, tiled=True)
         panel_3 = up(panel_2, 3)
         root_both = move(root_across, lambda r, c: (r, c ^ 1) if lower(r, c ^ 2) else None)
         below_2a = down(below_1[:half], 2)
+        across_3 = move(root_across, lambda r, c: (0, 2) if (r, c) == (3, 2) else None)
 
         def to_across(x, rows):
             return move(x, lambda r, c: (r, c ^ 2) if r == c and r in rows else None)
@@ -340,7 +341,6 @@
             return move(x, lambda r, c: (r, c ^ 1) if r == c ^ 2 and r in rows else None)
 
         across_1 = to_across(below_1, (1, 2))
-        beside_1 = to_beside(below_1, (0, 1, 2))
 
         root_row = (root_inverse, root_beside, root_across, root_both)
         panels = (panel_kept, panel_1, panel_2, panel_3)
@@ -359,7 +359,7 @@
             *root_row,
             *panels,
             across_1,
-            beside_1,
+            across_3,
             below_1,
             below_2a,
             gated=2,
@@ -367,19 +367,22 @@
         t_row = lax.all_gather(t, "col", axis=1, tiled=True)
         step = lambda x: move(x, lambda r, c: (r - 1, c))
         chain = [ANY] * 4 + [VMEM] * 2
-        below_2b = came = step(sent)
-        below_3a = down(below_2a, 3)
+        below_2b = came = move(sent, lambda r, c: (r - 1, c) if (r, c) != (1, 3) else None)
+        beside_1 = to_beside(below_1, (0, 1, 2))
         far_1 = on_beside(across_1, (1, 2))
-        (own,) = local_call(
+        own, below_2a = local_call(
             own_kernel,
             [ANY] * 4 + [VMEM],
             [shape((w, h), F32)],
             [pltpu.VMEM((h, h), BF16), dma],
             *root_row,
             t_t,
-        )
-        sent, below_2a = local_call(
-            functools.partial(chain_kernel, step=1, deps=4, gated=1),
+            below_2a,
+            gated=1,
+        )
+        below_3a = down(below_2a, 3)
+        (sent,) = local_call(
+            functools.partial(chain_kernel, step=1, deps=3, gated=0),
             chain,
             [t_block],
             [pltpu.VMEM((h, h), BF16), dma],
@@ -387,11 +390,8 @@
             t_t,
             came,
             own,
-            below_3a,
             far_1,
-            across_3,
-            below_2a,
-            gated=1,
+            beside_1,
         )
         below_2 = jnp.concatenate((below_2a, below_2b), 0)
         below_3b = came = step(sent)

time: 320 us -> 304 us (0.950)
  the two profiles are of different devices: /device:TPU:0 before, /device:TPU:13 now
where the time goes in v7:
time: 304 us; the launch traced here: 303 us
  waiting for transfers between devices  149 us (49%)
  starting transfers between devices  57.7 us (19%)
  Pallas kernels  42.9 us (14%)
  local copies, waits for them, and re-layouts  36.4 us (12%)
  between operations  14.5 us (5%)
    ppermute x24, waiting for transfers between devices, move(): return lax.ppermute(x, AXES, pairs)  149 us
    ppermute x24, starting transfers between devices, move(): return lax.ppermute(x, AXES, pairs)  57.6 us
    pallas_call x10, Pallas kernels, local_call(): pl.pallas_call(kernel, out_shape=outs, in_specs=in_specs + [ANY] * (len(a...  42.9 us
    unnamed x60, local copies, waits for them, and re-layouts  31.6 us
  transfers between devices with their start and end apart: 26, of which 11 were waited for; matrix products, arithmetic and copies ran while one was open for 4% of the time, Pallas kernels for 12%

profile of v7, /device:TPU:13, one launch (start us, length us, event | category | flops | bytes accessed | tf_op | source)
XLA Modules:
  0.0 303.0 jit_solution(1727740072855258097)
XLA Ops:
  7.2 3.3 %collective-permute-start.2 = (bf16[1024,1024]{1,0:T(8,128)(2,1)}, bf16[1024,1024]{1,0:T(8,128)(2,1)S(1)}, u32[]{:S(2)}, u32[]{:S(2)}) collective-permute-start(bf16[1024,1024]{1,0:T(8,128)(2,1)} %l0.9), channel_id=1, source_target_pairs={{0,2},{4,6},{5,7},{8,10},{9,11},{10,8},{12,14},{13,15},{14,12},{15... | collective-permute-start | bytes 6291464 | tf_op jit(solution)/shard_map/ppermute | solution.py:299
  11.2 1.4 broadcast_select_fusion.p0
  12.7 3.2 %collective-permute-start = (bf16[1024,512]{1,0:T(8,128)(2,1)S(1)}, bf16[1024,512]{1,0:T(8,128)(2,1)S(1)}, u32[]{:S(2)}, u32[]{:S(2)}) collective-permute-start(bf16[1024,512]{1,0:T(8,128)(2,1)S(1)} %broadcast_select_fusion.p0), channel_id=1, source_target_pairs={{0,4},{1,5},{2,6},{3,7},{4,8},{5,9},{6,10},{7,11},{8,12},{9,13},{1... | collective-permute-start | bytes 3145736 | tf_op jit(solution)/shard_map/ppermute | solution.py:299
  15.9 2.1 collective-permute-start.5
  18.0 3.1 %copy.16.refs_0_ = bf16[1024,1024]{1,0:T(8,128)(2,1)} copy(bf16[1024,1024]{1,0:T(8,128)(2,1)} %l0.9) | data formatting | bytes 4194304
  21.1 17.2 %collective-permute-done.refs_1_.p1 = bf16[1024,512]{1,0:T(8,128)(2,1)S(1)} collective-permute-done((bf16[1024,512]{1,0:T(8,128)(2,1)S(1)}, bf16[1024,512]{1,0:T(8,128)(2,1)S(1)}, u32[]{:S(2)}, u32[]{:S(2)}) %collective-permute-start) | collective-permute-done | bytes 1048608 | tf_op jit(solution)/shard_map/ppermute | solution.py:299
  38.4 1.0 copy-done.12
  39.3 3.7 %collective-permute-start.1 = (bf16[1024,1024]{1,0:T(8,128)(2,1)}, bf16[1024,1024]{1,0:T(8,128)(2,1)}, u32[]{:S(2)}, u32[]{:S(2)}) collective-permute-start(bf16[1024,1024]{1,0:T(8,128)(2,1)} %shard_map.67), channel_id=1, source_target_pairs={{0,1},{4,5},{5,4},{8,9},{9,8},{10,11},{12,13},{13,12},{14,15},{15,... | collective-permute-start | bytes 6291464 | tf_op jit(solution)/shard_map/ppermute | solution.py:299
  43.0 1.9 copy.20.refs_0_
  44.9 10.1 %collective-permute-done.2.refs_2_.l2.refs_1_ = bf16[1024,1024]{1,0:T(8,128)(2,1)S(1)} collective-permute-done((bf16[1024,1024]{1,0:T(8,128)(2,1)}, bf16[1024,1024]{1,0:T(8,128)(2,1)S(1)}, u32[]{:S(2)}, u32[]{:S(2)}) %collective-permute-start.2) | collective-permute-done | bytes 2097184 | tf_op jit(solution)/shard_map/ppermute | solution.py:299
  54.9 1.4 copy-done
  56.4 3.3 %collective-permute-start.4 = (bf16[1024,512]{1,0:T(8,128)(2,1)S(1)}, bf16[1024,512]{1,0:T(8,128)(2,1)S(1)}, u32[]{:S(2)}, u32[]{:S(2)}) collective-permute-start(bf16[1024,512]{1,0:T(8,128)(2,1)S(1)} %copy-done.13), channel_id=1, source_target_pairs={{4,8},{5,9},{6,10},{7,11},{8,12},{9,13},{10,14},{11,15},{20,24},{2... | collective-permute-start | bytes 3145736 | tf_op jit(solution)/shard_map/ppermute | solution.py:299
  59.7 4.4 %collective-permute-done.5.refs_1_.refs_2_ = bf16[1024,1024]{1,0:T(8,128)(2,1)} collective-permute-done((bf16[1024,1024]{1,0:T(8,128)(2,1)}, bf16[1024,1024]{1,0:T(8,128)(2,1)}, u32[]{:S(2)}, u32[]{:S(2)}) %collective-permute-start.5) | collective-permute-done | bytes 2097184 | tf_op jit(solution)/shard_map/ppermute | solution.py:299
  64.1 2.6 collective-permute-start.7
  67.5 2.0 collective-permute-start.3
  69.5 2.3 slice.4
  71.8 8.7 %collective-permute-done.4.refs_0_ = bf16[1024,512]{1,0:T(8,128)(2,1)S(1)} collective-permute-done((bf16[1024,512]{1,0:T(8,128)(2,1)S(1)}, bf16[1024,512]{1,0:T(8,128)(2,1)S(1)}, u32[]{:S(2)}, u32[]{:S(2)}) %collective-permute-start.4) | collective-permute-done | bytes 1048608 | tf_op jit(solution)/shard_map/ppermute | solution.py:299
  80.5 1.0 copy-done.18
  81.5 1.9 collective-permute-start.9
  84.1 22.2 %collective-permute-done.9.refs_3_ = bf16[512,1024]{1,0:T(8,128)(2,1)} collective-permute-done((bf16[512,1024]{1,0:T(8,128)(2,1)}, bf16[512,1024]{1,0:T(8,128)(2,1)}, u32[]{:S(2)}, u32[]{:S(2)}) %collective-permute-start.9) | collective-permute-done | bytes 1048608 | tf_op jit(solution)/shard_map/ppermute | solution.py:299
  106.3 1.3 copy-done.3
  107.6 1.2 copy-done.14
  108.9 1.2 copy-done.16
  110.1 1.2 copy-done.19
  111.3 5.9 %shard_map.69 = (bf16[1024,512]{1,0:T(8,128)(2,1)S(1)}, bf16[512,1024]{1,0:T(8,128)(2,1)S(1)}, bf16[512,1024]{1,0:T(8,128)(2,1)S(1)}, bf16[1024,1024]{1,0:T(8,128)(2,1)}, bf16[512,1024]{1,0:T(8,128)(2,1)}) custom-call(bf16[1024,1024]{1,0:T(8,128)(2,1)} %l0.9, ...), custom_call_target="tpu_custom_call", output_to_operand_aliasing={{3}: (10, {}), {4}: (11, {})} | custom-call | flops 1 | bytes 1 | tf_op jit(solution)/shard_map/pallas_call | solution.py:265
  117.2 1.0 copy-done.22
  118.2 1.0 copy-done.26
  119.2 1.9 collective-permute-start.10
  121.9 5.8 %collective-permute-start.12 = (bf16[1024,1024]{1,0:T(8,128)(2,1)}, bf16[1024,1024]{1,0:T(8,128)(2,1)S(1)}, u32[]{:S(2)}, u32[]{:S(2)}) collective-permute-start(bf16[1024,1024]{1,0:T(8,128)(2,1)} %get-tuple-element.23.h1), channel_id=1, source_target_pairs={{0,1},{5,4},{10,11},{16,17},{21,20},{26,27}} | collective-permute-start | bytes 6291464 | tf_op jit(solution)/shard_map/ppermute | solution.py:299
  127.8 3.0 %shard_map.71 = (f32[512,1024]{1,0:T(8,128)S(1)}, bf16[512,1024]{1,0:T(8,128)(2,1)}) custom-call(bf16[1024,1024]{1,0:T(8,128)(2,1)} %l0.9, bf16[1024,1024]{1,0:T(8,128)(2,1)} %collective-permute-done.1.refs_3_.l1, bf16[1024,1024]{1,0:T(8,128)(2,1)S(1)} %copy-done.1, bf16[1024,1024]{1,0:T(8,128)(2,1)} %collective-permute-done.3.l3, ...), custom_call_target="tpu_custom_call", output_to_operand_aliasing={{1}: (5, {})} | custom-call | flops 1 | bytes 1 | tf_op jit(solution)/shard_map/pallas_call | solution.py:265
  130.8 3.0 %constant_dynamic-update-slice_fusion.1 = bf16[1024,1024]{1,0:T(8,128)(2,1)} fusion(bf16[512,1024]{1,0:T(8,128)(2,1)} %get-tuple-element.25), kind=kLoop, calls=%fused_computation.2 | loop fusion | bytes 2097152
  133.9 14.7 %collective-permute-done.10.came_ref = bf16[512,1024]{1,0:T(8,128)(2,1)S(1)} collective-permute-done((bf16[512,1024]{1,0:T(8,128)(2,1)}, bf16[512,1024]{1,0:T(8,128)(2,1)S(1)}, u32[]{:S(2)}, u32[]{:S(2)}) %collective-permute-start.10) | collective-permute-done | bytes 1048608 | tf_op jit(solution)/shard_map/ppermute | solution.py:299
  148.6 1.1 constant_dynamic-update-slice_fusion.h2
  149.7 9.5 %collective-permute-start.17 = (bf16[1024,1024]{1,0:T(8,128)(2,1)}, bf16[1024,1024]{1,0:T(8,128)(2,1)}, u32[]{:S(2)}, u32[]{:S(2)}) collective-permute-start(bf16[1024,1024]{1,0:T(8,128)(2,1)} %constant_dynamic-update-slice_fusion.h2), channel_id=1, source_target_pairs={{0,2},{5,7},{16,18},{21,23}} | collective-permute-start | bytes 6291464 | tf_op jit(solution)/shard_map/ppermute | solution.py:299
  159.2 2.6 collective-permute-start.16
  161.8 2.3 collective-permute-start.18
  164.1 1.3 copy-done.27
  166.1 1.0 shard_map.72._dep
  167.2 2.1 collective-permute-start.13
  169.3 2.2 copy-done.17
  171.5 1.6 copy-done.20
  173.1 1.0 copy-done.21
  174.1 4.8 %shard_map.73 = (bf16[512,512]{1,0:T(8,128)(2,1)S(1)}, bf16[512,512]{1,0:T(8,128)(2,1)S(1)}, f32[512,512]{1,0:T(8,128)S(1)}, f32[512,512]{1,0:T(8,128)S(1)}) custom-call(bf16[512,1024]{1,0:T(8,128)(2,1)S(1)} %get-tuple-element.18.tt_ref, bf16[1024,2048]{1,0:T(8,128)(2,1)S(1)} %copy-done.17, bf16[512,512]{1,0:T(8,128)(2,1)S(1)} %copy-done.21, ...), custom_call_target="tpu_custom_call" | custom-call | flops 1 | bytes 1 | tf_op jit(solution)/shard_map/pallas_call | solution.py:265
  179.0 7.4 %collective-permute-done.18.refs_5_ = bf16[512,1024]{1,0:T(8,128)(2,1)} collective-permute-done((bf16[512,1024]{1,0:T(8,128)(2,1)}, bf16[512,1024]{1,0:T(8,128)(2,1)}, u32[]{:S(2)}, u32[]{:S(2)}) %collective-permute-start.18) | collective-permute-done | bytes 1048608 | tf_op jit(solution)/shard_map/ppermute | solution.py:299
  186.4 2.2 collective-permute-start.14
  188.6 0.8 copy-done.23
  189.4 19.5 %collective-permute-done.13.came_ref = bf16[512,1024]{1,0:T(8,128)(2,1)} collective-permute-done((bf16[512,1024]{1,0:T(8,128)(2,1)}, bf16[512,1024]{1,0:T(8,128)(2,1)}, u32[]{:S(2)}, u32[]{:S(2)}) %collective-permute-start.13) | collective-permute-done | bytes 1048608 | tf_op jit(solution)/shard_map/ppermute | solution.py:299
  208.9 11.1 %collective-permute-done.15.refs_1_.near_ref = bf16[512,512]{1,0:T(8,128)(2,1)S(1)} collective-permute-done((bf16[512,512]{1,0:T(8,128)(2,1)S(1)}, bf16[512,512]{1,0:T(8,128)(2,1)S(1)}, u32[]{:S(2)}, u32[]{:S(2)}) %collective-permute-start.15) | collective-permute-done | bytes 524320 | tf_op jit(solution)/shard_map/ppermute | solution.py:299
  220.0 6.1 %collective-permute-done.14.refs_0_.far_ref = bf16[512,512]{1,0:T(8,128)(2,1)S(1)} collective-permute-done((bf16[512,512]{1,0:T(8,128)(2,1)S(1)}, bf16[512,512]{1,0:T(8,128)(2,1)S(1)}, u32[]{:S(2)}, u32[]{:S(2)}) %collective-permute-start.14) | collective-permute-done | bytes 524320 | tf_op jit(solution)/shard_map/ppermute | solution.py:299
  226.1 5.2 %shard_map.75 = (bf16[512,1024]{1,0:T(8,128)(2,1)}, bf16[1024,1024]{1,0:T(8,128)(2,1)}, bf16[1024,1024]{1,0:T(8,128)(2,1)S(1)}, bf16[512,1024]{1,0:T(8,128)(2,1)}) custom-call(bf16[1024,1024]{1,0:T(8,128)(2,1)} %l0.9, bf16[1024,1024]{1,0:T(8,128)(2,1)} %collective-permute-done.1.refs_3_.l1, ...), custom_call_target="tpu_custom_call", output_to_operand_aliasing={{1}: (9, {}), {2}: (10, {}), {3}: (11, {})} | custom-call | flops 1 | bytes 1 | tf_op jit(solution)/shard_map/pallas_call | solution.py:265
  231.4 2.1 constant_dynamic-update-slice_fusion.3
  233.4 1.3 constant_dynamic-update-slice_fusion.2.h3
  234.7 0.9 collective-permute-start.19
  235.7 2.0 collective-permute-start.20
  237.7 2.0 collective-permute-start.21
  239.7 1.9 collective-permute-start.22
  241.6 0.9 shard_map.78
  242.5 5.4 %shard_map.74.acc_ref = f32[1024,1024]{1,0:T(8,128)S(1)} custom-call(bf16[1024,1024]{1,0:T(8,128)(2,1)} %l0.9, bf16[1024,1024]{1,0:T(8,128)(2,1)} %collective-permute-done.1.refs_3_.l1, bf16[1024,1024]{1,0:T(8,128)(2,1)S(1)} %copy-done.2, bf16[1024,1024]{1,0:T(8,128)(2,1)} %collective-permute-done.3.l3, bf16[512,512]{1,0:T(8,128)(2,1)S(1)} %copy-done.24), custom_call_target="tpu_custom_call" | custom-call | flops 1 | bytes 1 | tf_op jit(solution)/shard_map/pallas_call | solution.py:265
  247.9 2.1 copy-done.6
  250.0 27.9 %collective-permute-done.22.came_ref = bf16[512,1024]{1,0:T(8,128)(2,1)S(1)} collective-permute-done((bf16[512,1024]{1,0:T(8,128)(2,1)}, bf16[512,1024]{1,0:T(8,128)(2,1)S(1)}, u32[]{:S(2)}, u32[]{:S(2)}) %collective-permute-start.22) | collective-permute-done | bytes 1048608 | tf_op jit(solution)/shard_map/ppermute | solution.py:299
  277.9 2.1 shard_map.77
  280.1 13.2 %shard_map.76._dep = bf16[1024,1024]{1,0:T(8,128)(2,1)} custom-call(f32[1024,1024]{1,0:T(8,128)} %copy-done.6, bf16[1024,1024]{1,0:T(8,128)(2,1)} %get-tuple-element.23.h1, bf16[1024,1024]{1,0:T(8,128)(2,1)} %constant_dynamic-update-slice_fusion.h2, bf16[1024,1024]{1,0:T(8,128)(2,1)S(1)} %constant_dynamic-update-slice_fusion.2.h3, ...), custom_call_target="tpu_custom_call" | custom-call | flops 1 | bytes 1 | tf_op jit(solution)/shard_map/pallas_call | solution.py:265
  293.3 1.6 copy-done.11
  294.8 1.3 shard_map.79
  (69 shorter events, 4.1 us)
Async XLA Ops:
  7.2 162.1 %all-gather.5.cloned.1.call-start = ((), (), s32[]{:S(2)}) async-start(), calls=%async_computation.1 | async-start | bytes 2621440 | tf_op jit(solution)/shard_map/all_gather | solution.py:328
  7.2 47.7 %collective-permute-start.2 = (bf16[1024,1024]{1,0:T(8,128)(2,1)}, bf16[1024,1024]{1,0:T(8,128)(2,1)S(1)}, u32[]{:S(2)}, u32[]{:S(2)}) collective-permute-start(bf16[1024,1024]{1,0:T(8,128)(2,1)} %l0.9), channel_id=1, source_target_pairs={{0,2},{4,6},{5,7},{8,10},{9,11},{10,8},{12,14},{13,15},{14,12},{15... | collective-permute-start | bytes 6291464 | tf_op jit(solution)/shard_map/ppermute | solution.py:299
  12.6 8.5 %copy-start.15 = (bf16[1024,512]{1,0:T(8,128)(2,1)}, bf16[1024,512]{1,0:T(8,128)(2,1)S(1)}, u32[]{:S(2)}) copy-start(bf16[1024,512]{1,0:T(8,128)(2,1)S(1)} %broadcast_select_fusion.p0) | copy-start | bytes 3145732
  12.7 25.7 %collective-permute-start = (bf16[1024,512]{1,0:T(8,128)(2,1)S(1)}, bf16[1024,512]{1,0:T(8,128)(2,1)S(1)}, u32[]{:S(2)}, u32[]{:S(2)}) collective-permute-start(bf16[1024,512]{1,0:T(8,128)(2,1)S(1)} %broadcast_select_fusion.p0), channel_id=1, source_target_pairs={{0,4},{1,5},{2,6},{3,7},{4,8},{5,9},{6,10},{7,11},{8,12},{9,13},{1... | collective-permute-start | bytes 3145736 | tf_op jit(solution)/shard_map/ppermute | solution.py:299
  15.9 48.2 %collective-permute-start.5 = (bf16[1024,1024]{1,0:T(8,128)(2,1)}, bf16[1024,1024]{1,0:T(8,128)(2,1)}, u32[]{:S(2)}, u32[]{:S(2)}) collective-permute-start(bf16[1024,1024]{1,0:T(8,128)(2,1)} %l0.9), channel_id=1, source_target_pairs={{4,0},{5,1},{8,4},{9,5},{10,6},{12,8},{13,9},{14,10},{15,11},{20,1... | collective-permute-start | bytes 6291464 | tf_op jit(solution)/shard_map/ppermute | solution.py:299
  38.4 1.0 copy-start.12
  39.3 44.1 %collective-permute-start.1 = (bf16[1024,1024]{1,0:T(8,128)(2,1)}, bf16[1024,1024]{1,0:T(8,128)(2,1)}, u32[]{:S(2)}, u32[]{:S(2)}) collective-permute-start(bf16[1024,1024]{1,0:T(8,128)(2,1)} %shard_map.67), channel_id=1, source_target_pairs={{0,1},{4,5},{5,4},{8,9},{9,8},{10,11},{12,13},{13,12},{14,15},{15,... | collective-permute-start | bytes 6291464 | tf_op jit(solution)/shard_map/ppermute | solution.py:299
  44.9 11.5 %copy-start.13 = (bf16[1024,512]{1,0:T(8,128)(2,1)S(1)}, bf16[1024,512]{1,0:T(8,128)(2,1)}, u32[]{:S(2)}) copy-start(bf16[1024,512]{1,0:T(8,128)(2,1)} %copy-done.12) | copy-start | bytes 3145732
  54.9 1.4 copy-start
  56.3 113.0 %all-gather.3.cloned.1.call-start = ((), (), s32[]{:S(2)}) async-start(), calls=%async_computation | async-start | bytes 5242880 | tf_op jit(solution)/shard_map/all_gather | solution.py:367
  56.4 24.1 %collective-permute-start.4 = (bf16[1024,512]{1,0:T(8,128)(2,1)S(1)}, bf16[1024,512]{1,0:T(8,128)(2,1)S(1)}, u32[]{:S(2)}, u32[]{:S(2)}) collective-permute-start(bf16[1024,512]{1,0:T(8,128)(2,1)S(1)} %copy-done.13), channel_id=1, source_target_pairs={{4,8},{5,9},{6,10},{7,11},{8,12},{9,13},{10,14},{11,15},{20,24},{2... | collective-permute-start | bytes 3145736 | tf_op jit(solution)/shard_map/ppermute | solution.py:299
  64.1 42.2 %collective-permute-start.7 = (bf16[1024,1024]{1,0:T(8,128)(2,1)}, bf16[1024,1024]{1,0:T(8,128)(2,1)}, u32[]{:S(2)}, u32[]{:S(2)}) collective-permute-start(bf16[1024,1024]{1,0:T(8,128)(2,1)} %collective-permute-done.5.refs_1_.refs_2_), channel_id=1, source_target_pairs={{5,7},{10,8},{21,23},{26,24}} | collective-permute-start | bytes 6291464 | tf_op jit(solution)/shard_map/ppermute | solution.py:299
  66.7 39.6 %collective-permute-start.8 = (bf16[1024,1024]{1,0:T(8,128)(2,1)}, bf16[1024,1024]{1,0:T(8,128)(2,1)S(1)}, u32[]{:S(2)}, u32[]{:S(2)}) collective-permute-start(bf16[1024,1024]{1,0:T(8,128)(2,1)} %copy-done), channel_id=1, source_target_pairs={{14,2},{30,18}} | collective-permute-start | bytes 6291464 | tf_op jit(solution)/shard_map/ppermute | solution.py:299
  67.5 40.1 %collective-permute-start.3 = (bf16[1024,1024]{1,0:T(8,128)(2,1)}, bf16[1024,1024]{1,0:T(8,128)(2,1)}, u32[]{:S(2)}, u32[]{:S(2)}) collective-permute-start(bf16[1024,1024]{1,0:T(8,128)(2,1)} %copy-done), channel_id=1, source_target_pairs={{2,3},{6,7},{7,6},{8,9},{10,11},{11,10},{12,13},{13,12},{14,15},{1... | collective-permute-start | bytes 6291464 | tf_op jit(solution)/shard_map/ppermute | solution.py:299
  80.5 1.0 copy-start.18
  81.5 24.8 %collective-permute-start.9 = (bf16[512,1024]{1,0:T(8,128)(2,1)}, bf16[512,1024]{1,0:T(8,128)(2,1)}, u32[]{:S(2)}, u32[]{:S(2)}) collective-permute-start(bf16[512,1024]{1,0:T(8,128)(2,1)} %slice.4), channel_id=1, source_target_pairs={{4,0},{5,1},{6,2},{8,4},{9,5},{10,6},{11,7},{20,16},{21,17},{22,18... | collective-permute-start | bytes 3145736 | tf_op jit(solution)/shard_map/ppermute | solution.py:299
  83.4 22.9 %collective-permute-start.6 = (bf16[1024,512]{1,0:T(8,128)(2,1)}, bf16[1024,512]{1,0:T(8,128)(2,1)S(1)}, u32[]{:S(2)}, u32[]{:S(2)}) collective-permute-start(bf16[1024,512]{1,0:T(8,128)(2,1)} %shard_map.68.p2), channel_id=1, source_target_pairs={{8,12},{9,13},{10,14},{11,15},{24,28},{25,29},{26,30},{27,31}} | collective-permute-start | bytes 3145736 | tf_op jit(solution)/shard_map/ppermute | solution.py:299
  106.3 1.3 copy-start.3
  107.6 1.2 copy-start.14
  108.9 1.2 copy-start.16
  110.1 1.2 copy-start.19
  111.3 16.4 %copy-start.1 = (bf16[1024,1024]{1,0:T(8,128)(2,1)S(1)}, bf16[1024,1024]{1,0:T(8,128)(2,1)}, u32[]{:S(2)}) copy-start(bf16[1024,1024]{1,0:T(8,128)(2,1)} %copy-done) | copy-start | bytes 6291460
  117.2 1.0 copy-start.22
  118.2 1.0 copy-start.26
  119.2 29.4 %collective-permute-start.10 = (bf16[512,1024]{1,0:T(8,128)(2,1)}, bf16[512,1024]{1,0:T(8,128)(2,1)S(1)}, u32[]{:S(2)}, u32[]{:S(2)}) collective-permute-start(bf16[512,1024]{1,0:T(8,128)(2,1)} %copy-done.26), channel_id=1, source_target_pairs={{4,0},{5,1},{6,2},{8,4},{9,5},{10,6},{11,7},{12,8},{13,9},{14,10},... | collective-permute-start | bytes 3145736 | tf_op jit(solution)/shard_map/ppermute | solution.py:299
  121.1 43.0 %collective-permute-start.11 = (bf16[1024,1024]{1,0:T(8,128)(2,1)}, bf16[1024,1024]{1,0:T(8,128)(2,1)S(1)}, u32[]{:S(2)}, u32[]{:S(2)}) collective-permute-start(bf16[1024,1024]{1,0:T(8,128)(2,1)} %collective-permute-done.7.refs_0_.x1), channel_id=1, source_target_pairs={{7,6},{8,9},{23,22},{24,25}} | collective-permute-start | bytes 6291464 | tf_op jit(solution)/shard_map/ppermute | solution.py:299
  121.9 42.2 %collective-permute-start.12 = (bf16[1024,1024]{1,0:T(8,128)(2,1)}, bf16[1024,1024]{1,0:T(8,128)(2,1)S(1)}, u32[]{:S(2)}, u32[]{:S(2)}) collective-permute-start(bf16[1024,1024]{1,0:T(8,128)(2,1)} %get-tuple-element.23.h1), channel_id=1, source_target_pairs={{0,1},{5,4},{10,11},{16,17},{21,20},{26,27}} | collective-permute-start | bytes 6291464 | tf_op jit(solution)/shard_map/ppermute | solution.py:299
  130.8 33.3 %copy-start.7 = (f32[512,1024]{1,0:T(8,128)}, f32[512,1024]{1,0:T(8,128)S(1)}, u32[]{:S(2)}) copy-start(f32[512,1024]{1,0:T(8,128)S(1)} %get-tuple-element.22.refs_0_.own_ref) | copy-start | bytes 6291460
  149.7 59.2 %collective-permute-start.17 = (bf16[1024,1024]{1,0:T(8,128)(2,1)}, bf16[1024,1024]{1,0:T(8,128)(2,1)}, u32[]{:S(2)}, u32[]{:S(2)}) collective-permute-start(bf16[1024,1024]{1,0:T(8,128)(2,1)} %constant_dynamic-update-slice_fusion.h2), channel_id=1, source_target_pairs={{0,2},{5,7},{16,18},{21,23}} | collective-permute-start | bytes 6291464 | tf_op jit(solution)/shard_map/ppermute | solution.py:299
  159.2 49.7 %collective-permute-start.16 = (bf16[1024,1024]{1,0:T(8,128)(2,1)}, bf16[1024,1024]{1,0:T(8,128)(2,1)}, u32[]{:S(2)}, u32[]{:S(2)}) collective-permute-start(bf16[1024,1024]{1,0:T(8,128)(2,1)} %constant_dynamic-update-slice_fusion.h2), channel_id=1, source_target_pairs={{0,1},{5,4},{16,17},{21,20}} | collective-permute-start | bytes 6291464 | tf_op jit(solution)/shard_map/ppermute | solution.py:299
  161.8 24.6 %collective-permute-start.18 = (bf16[512,1024]{1,0:T(8,128)(2,1)}, bf16[512,1024]{1,0:T(8,128)(2,1)}, u32[]{:S(2)}, u32[]{:S(2)}) collective-permute-start(bf16[512,1024]{1,0:T(8,128)(2,1)} %get-tuple-element.25), channel_id=1, source_target_pairs={{4,0},{5,1},{6,2},{7,3},{20,16},{21,17},{22,18},{23,19}} | collective-permute-start | bytes 3145736 | tf_op jit(solution)/shard_map/ppermute | solution.py:299
  164.1 1.3 copy-start.27
  164.1 2.0 copy-start.9
  167.2 58.9 %copy-start.4 = (bf16[1024,1024]{1,0:T(8,128)(2,1)S(1)}, bf16[1024,1024]{1,0:T(8,128)(2,1)}, u32[]{:S(2)}) copy-start(bf16[1024,1024]{1,0:T(8,128)(2,1)} %copy-done.3) | copy-start | bytes 6291460
  167.2 41.7 %collective-permute-start.13 = (bf16[512,1024]{1,0:T(8,128)(2,1)}, bf16[512,1024]{1,0:T(8,128)(2,1)}, u32[]{:S(2)}, u32[]{:S(2)}) collective-permute-start(bf16[512,1024]{1,0:T(8,128)(2,1)} %shard_map.72._dep), channel_id=1, source_target_pairs={{4,0},{5,1},{6,2},{7,3},{8,4},{9,5},{10,6},{11,7},{12,8},{13,9},{1... | collective-permute-start | bytes 3145736 | tf_op jit(solution)/shard_map/ppermute | solution.py:299
  169.3 2.2 copy-start.17
  171.5 1.6 copy-start.20
  173.1 1.0 copy-start.21
  179.0 41.1 %collective-permute-start.15 = (bf16[512,512]{1,0:T(8,128)(2,1)S(1)}, bf16[512,512]{1,0:T(8,128)(2,1)S(1)}, u32[]{:S(2)}, u32[]{:S(2)}) collective-permute-start(bf16[512,512]{1,0:T(8,128)(2,1)S(1)} %get-tuple-element.26), channel_id=1, source_target_pairs={{0,4},{1,5},{2,6},{3,7},{4,0},{5,1},{6,2},{7,3},{8,12},{9,13},{10,... | collective-permute-start | bytes 1572872 | tf_op jit(solution)/shard_map/ppermute | solution.py:299
  186.4 39.7 %collective-permute-start.14 = (bf16[512,512]{1,0:T(8,128)(2,1)S(1)}, bf16[512,512]{1,0:T(8,128)(2,1)S(1)}, u32[]{:S(2)}, u32[]{:S(2)}) collective-permute-start(bf16[512,512]{1,0:T(8,128)(2,1)S(1)} %get-tuple-element.24._dep), channel_id=1, source_target_pairs={{0,4},{1,5},{2,6},{3,7},{4,0},{5,1},{6,2},{7,3},{8,12},{9,13},{10,... | collective-permute-start | bytes 1572872 | tf_op jit(solution)/shard_map/ppermute | solution.py:299
  188.6 0.8 copy-start.23
  231.4 16.5 %copy-start.5 = (bf16[1024,1024]{1,0:T(8,128)(2,1)}, bf16[1024,1024]{1,0:T(8,128)(2,1)S(1)}, u32[]{:S(2)}) copy-start(bf16[1024,1024]{1,0:T(8,128)(2,1)S(1)} %get-tuple-element.29.x3) | copy-start | bytes 6291460
  234.7 7.7 %copy-start.2 = (bf16[1024,1024]{1,0:T(8,128)(2,1)S(1)}, bf16[1024,1024]{1,0:T(8,128)(2,1)}, u32[]{:S(2)}) copy-start(bf16[1024,1024]{1,0:T(8,128)(2,1)} %copy-done) | copy-start | bytes 6291460
  234.7 7.7 %copy-start.24 = (bf16[512,512]{1,0:T(8,128)(2,1)S(1)}, bf16[512,512]{1,0:T(8,128)(2,1)}, u32[]{:S(2)}) copy-start(bf16[512,512]{1,0:T(8,128)(2,1)} %copy-done.23) | copy-start | bytes 1572868
  234.7 45.3 %collective-permute-start.19 = (bf16[1024,1024]{1,0:T(8,128)(2,1)S(1)}, bf16[1024,1024]{1,0:T(8,128)(2,1)S(1)}, u32[]{:S(2)}, u32[]{:S(2)}) collective-permute-start(bf16[1024,1024]{1,0:T(8,128)(2,1)S(1)} %constant_dynamic-update-slice_fusion.2.h3), channel_id=1, source_target_pairs={{0,1},{16,17}} | collective-permute-start | bytes 6291464 | tf_op jit(solution)/shard_map/ppermute | solution.py:299
  235.7 44.4 %collective-permute-start.20 = (bf16[1024,1024]{1,0:T(8,128)(2,1)}, bf16[1024,1024]{1,0:T(8,128)(2,1)}, u32[]{:S(2)}, u32[]{:S(2)}) collective-permute-start(bf16[1024,1024]{1,0:T(8,128)(2,1)} %get-tuple-element.28.x2), channel_id=1, source_target_pairs={{2,3},{7,6},{18,19},{23,22}} | collective-permute-start | bytes 6291464 | tf_op jit(solution)/shard_map/ppermute | solution.py:299
  237.7 42.4 %collective-permute-start.21 = (bf16[1024,1024]{1,0:T(8,128)(2,1)S(1)}, bf16[1024,1024]{1,0:T(8,128)(2,1)}, u32[]{:S(2)}, u32[]{:S(2)}) collective-permute-start(bf16[1024,1024]{1,0:T(8,128)(2,1)S(1)} %get-tuple-element.29.x3), channel_id=1, source_target_pairs={{2,3},{18,19}} | collective-permute-start | bytes 6291464 | tf_op jit(solution)/shard_map/ppermute | solution.py:299
  239.7 38.3 %collective-permute-start.22 = (bf16[512,1024]{1,0:T(8,128)(2,1)}, bf16[512,1024]{1,0:T(8,128)(2,1)S(1)}, u32[]{:S(2)}, u32[]{:S(2)}) collective-permute-start(bf16[512,1024]{1,0:T(8,128)(2,1)} %get-tuple-element.30._dep), channel_id=1, source_target_pairs={{4,0},{5,1},{6,2},{7,3},{8,4},{9,5},{10,6},{11,7},{12,8},{13,9},{1... | collective-permute-start | bytes 3145736 | tf_op jit(solution)/shard_map/ppermute | solution.py:299
  242.4 35.5 %copy-start.8 = (f32[512,1024]{1,0:T(8,128)S(1)}, f32[512,1024]{1,0:T(8,128)}, u32[]{:S(2)}) copy-start(f32[512,1024]{1,0:T(8,128)} %copy-done.7) | copy-start | bytes 6291460
  242.5 35.5 %copy-start.25 = (s32[8]{0:T(128)S(1)}, s32[8]{0:T(128)}, u32[]{:S(2)}) copy-start(s32[8]{0:T(128)} %structure.1) | copy-start | bytes 100
  242.5 50.8 %collective-permute-start.23 = (bf16[512,512]{1,0:T(8,128)(2,1)}, bf16[512,512]{1,0:T(8,128)(2,1)S(1)}, u32[]{:S(2)}, u32[]{:S(2)}) collective-permute-start(bf16[512,512]{1,0:T(8,128)(2,1)} %shard_map.78), channel_id=1, source_target_pairs={{0,8},{1,9},{2,10},{3,11},{4,12},{5,13},{6,14},{7,15},{8,0},{9,1},... | collective-permute-start | bytes 1572872 | tf_op jit(solution)/shard_map/ppermute | solution.py:299
  247.9 2.1 copy-start.6
  250.0 30.1 %copy-start.10 = (bf16[1024,1024]{1,0:T(8,128)(2,1)S(1)}, bf16[1024,1024]{1,0:T(8,128)(2,1)}, u32[]{:S(2)}) copy-start(bf16[1024,1024]{1,0:T(8,128)(2,1)} %copy-done.9) | copy-start | bytes 6291460
  293.2 1.6 copy-start.11
Sparse Core Ops, SparseCore 0:
  56.5 28.0 all-gather.4
  119.3 47.5 all-gather.2

commit v8 on v7

--- a/solution.py
+++ b/solution.py
@@ -83,7 +83,7 @@
 
 
 def product_kernel(l0, l1, l2, l3, p0, p1, p2, p3, *refs, deps, gated):
-    below = refs[deps]
+    below = refs[0]
     t_ref, tt_ref, sent_ref = refs[deps + gated : deps + gated + 3]
     rows, panels, acc, row_sems, panel_sems, sem = refs[deps + 2 * gated + 3 :]
     r, c = position()
@@ -137,7 +137,7 @@
         wait(half, sent_ref, sem)
 
 
-def own_kernel(l0, l1, l2, l3, tt_ref, _in, own_ref, _out, block, sem):
+def own_kernel(l0, l1, l2, l3, tt_ref, _in0, _in1, _in2, own_ref, _out0, _out1, _out2, block, sem):
     r, c = position()
     start_picked((l0, l1, l2, l3), r ^ c, block, sem)
     wait(l0, block, sem)
@@ -241,7 +241,7 @@
     out_ref[...] = acc[...].astype(BF16)
 
 
-def cross_end_kernel(structure, own_ref, came_ref, out_ref):
+def cross_end_kernel(structure, own_ref, came_ref, _dep, out_ref):
     for b in range(own_ref.shape[1] // BLOCK):
         rows = slice(b * BLOCK, (b + 1) * BLOCK)
         total = own_ref[:, rows] + came_ref[:, rows].astype(F32)
@@ -323,8 +323,9 @@
         (root_late,) = together(root_inverse, earlier=(panel_1,))
         root_beside = move(root_late, lambda r, c: (r, c ^ 1) if lower(r, c) else None)
         panel_2 = up(panel_1, 2)
-        (panel_2,) = together(panel_2, earlier=(below_1, root_across, root_beside))
-        (child_late,) = together(child_inverse, earlier=(root_across,))
+        panel_2, child_late = together(
+            panel_2, child_inverse, earlier=(below_1, root_across, root_beside)
+        )
         child_row = lax.all_gather(child_late, "col", axis=1, tiled=True)
         panel_3 = up(panel_2, 3)
         root_both = move(root_across, lambda r, c: (r, c ^ 1) if lower(r, c ^ 2) else None)
@@ -344,8 +345,8 @@
 
         root_row = (root_inverse, root_beside, root_across, root_both)
         panels = (panel_kept, panel_1, panel_2, panel_3)
-        t, t_t, sent, below_1, below_2a = local_call(
-            functools.partial(product_kernel, deps=2, gated=2),
+        t, t_t, sent = local_call(
+            functools.partial(product_kernel, deps=4, gated=0),
             [ANY] * 8,
             [shape((h, w), BF16), t_block, t_block],
             [
@@ -358,29 +359,31 @@
             ],
             *root_row,
             *panels,
+            below_1,
             across_1,
             across_3,
-            below_1,
             below_2a,
-            gated=2,
         )
         t_row = lax.all_gather(t, "col", axis=1, tiled=True)
         step = lambda x: move(x, lambda r, c: (r - 1, c))
         chain = [ANY] * 4 + [VMEM] * 2
         below_2b = came = move(sent, lambda r, c: (r - 1, c) if (r, c) != (1, 3) else None)
-        beside_1 = to_beside(below_1, (0, 1, 2))
         far_1 = on_beside(across_1, (1, 2))
-        own, below_2a = local_call(
+        own, below_1, below_2a, across_3 = local_call(
             own_kernel,
             [ANY] * 4 + [VMEM],
             [shape((w, h), F32)],
             [pltpu.VMEM((h, h), BF16), dma],
             *root_row,
             t_t,
+            below_1,
             below_2a,
-            gated=1,
-        )
+            across_3,
+            gated=3,
+        )
+        far_3 = on_beside(across_3, (0,))
         below_3a = down(below_2a, 3)
+        beside_1 = to_beside(below_1, (0, 1, 2))
         (sent,) = local_call(
             functools.partial(chain_kernel, step=1, deps=3, gated=0),
             chain,
@@ -389,7 +392,7 @@
             *root_row,
             t_t,
             came,
-            own,
+            far_3,
             far_1,
             beside_1,
         )
@@ -410,7 +413,6 @@
             sent,
         )
         child_far = move(far_part, lambda r, c: (r ^ 1, c))
-        child_near = move(near_part, lambda r, c: (r ^ 1, c))
         (root_sum,) = local_call(
             diagonal_kernel,
             [],
@@ -419,8 +421,8 @@
             *root_row,
             far_part,
         )
-        sent, across_2, across_3, below_3a = local_call(
-            functools.partial(chain_kernel, step=2, deps=3, gated=3),
+        sent, across_2, below_3a = local_call(
+            functools.partial(chain_kernel, step=2, deps=2, gated=2),
             chain,
             [t_block],
             [pltpu.VMEM((h, h), BF16), dma],
@@ -428,31 +430,20 @@
             t_t,
             came,
             child_far,
-            child_near,
             beside_2,
             across_2,
-            across_3,
             below_3a,
-            gated=3,
+            gated=2,
         )
         came = step(sent)
         (child_onward,) = local_call(
             child_onward_kernel, [VMEM] * 2, [child_block], [], child_on, child_far, sent
         )
+        child_near = move(near_part, lambda r, c: (r ^ 1, c))
         child_last = move(child_onward, lambda r, c: (r ^ 2, c))
         below_3 = jnp.concatenate((below_3a, below_3b), 0)
         beside_3 = to_beside(below_3, (0,))
         far_2 = on_beside(across_2, (0, 1))
-        far_3 = on_beside(across_3, (0,))
-        (sigma_cross,) = local_call(
-            cross_end_kernel,
-            [SMEM] + [VMEM] * 2,
-            [shape((h, w), BF16)],
-            [],
-            structure,
-            own,
-            came,
-        )
         (sigma_root,) = local_call(
             root_kernel,
             [VMEM],
@@ -478,6 +469,16 @@
             far_2,
             far_3,
         )
+        (sigma_cross,) = local_call(
+            cross_end_kernel,
+            [SMEM] + [VMEM] * 2,
+            [shape((h, w), BF16)],
+            [],
+            structure,
+            own,
+            came,
+            sigma_root,
+        )
         (sigma_child,) = local_call(
             child_end_kernel,
             [VMEM] * 3,
@@ -486,7 +487,7 @@
             child_own,
             child_near,
             child_last,
-            sigma_root,
+            sigma_cross,
         )
         return (sigma_root, sigma_cross, sigma_child)
 

time: 304 us -> 293 us (0.964)
  the two profiles are of different devices: /device:TPU:13 before, /device:TPU:0 now
where the time goes in v8:
time: 293 us; the launch traced here: 289 us
  waiting for transfers between devices  138 us (47%)
  starting transfers between devices  66.9 us (23%)
  Pallas kernels  35.9 us (12%)
  local copies, waits for them, and re-layouts  31.9 us (11%)
  between operations  14.5 us (5%)
    ppermute x24, waiting for transfers between devices, move(): return lax.ppermute(x, AXES, pairs)  134 us
    ppermute x24, starting transfers between devices, move(): return lax.ppermute(x, AXES, pairs)  66.8 us
    pallas_call x10, Pallas kernels, local_call(): pl.pallas_call(kernel, out_shape=outs, in_specs=in_specs + [ANY] * (len(a...  35.9 us
    unnamed x62, local copies, waits for them, and re-layouts  28.2 us
  transfers between devices with their start and end apart: 26, of which 9 were waited for; matrix products, arithmetic and copies ran while one was open for 3% of the time, Pallas kernels for 11%

profile of v8, /device:TPU:0, one launch (start us, length us, event | category | flops | bytes accessed | tf_op | source)
XLA Modules:
  0.0 289.5 jit_solution(15949493213371863975)
XLA Ops:
  7.2 0.8 broadcast_compare_fusion
  8.1 1.4 broadcast_select_fusion.p0
  9.5 5.0 %collective-permute-start = (bf16[1024,512]{1,0:T(8,128)(2,1)S(1)}, bf16[1024,512]{1,0:T(8,128)(2,1)S(1)}, u32[]{:S(2)}, u32[]{:S(2)}) collective-permute-start(bf16[1024,512]{1,0:T(8,128)(2,1)S(1)} %broadcast_select_fusion.p0), channel_id=1, source_target_pairs={{0,4},{1,5},{2,6},{3,7},{4,8},{5,9},{6,10},{7,11},{8,12},{9,13},{1... | collective-permute-start | bytes 3145736 | tf_op jit(solution)/shard_map/ppermute | solution.py:299
  14.6 1.3 collective-permute-start.5
  15.9 5.5 %collective-permute-start.2 = (bf16[1024,1024]{1,0:T(8,128)(2,1)S(1)}, bf16[1024,1024]{1,0:T(8,128)(2,1)}, u32[]{:S(2)}, u32[]{:S(2)}) collective-permute-start(bf16[1024,1024]{1,0:T(8,128)(2,1)S(1)} %copy-done), channel_id=1, source_target_pairs={{0,2},{4,6},{5,7},{8,10},{9,11},{10,8},{12,14},{13,15},{14,12},{15... | collective-permute-start | bytes 6291464 | tf_op jit(solution)/shard_map/ppermute | solution.py:299
  21.4 1.3 copy.15.refs_0_
  22.7 14.2 %collective-permute-done.refs_1_.p1 = bf16[1024,512]{1,0:T(8,128)(2,1)S(1)} collective-permute-done((bf16[1024,512]{1,0:T(8,128)(2,1)S(1)}, bf16[1024,512]{1,0:T(8,128)(2,1)S(1)}, u32[]{:S(2)}, u32[]{:S(2)}) %collective-permute-start) | collective-permute-done | bytes 1048608 | tf_op jit(solution)/shard_map/ppermute | solution.py:299
  36.9 1.0 copy-done.9
  37.8 2.7 collective-permute-start.1
  41.2 1.9 copy.17.refs_1_
  43.1 20.5 %collective-permute-done.5.refs_2_.refs_0_._in0 = bf16[1024,1024]{1,0:T(8,128)(2,1)} collective-permute-done((bf16[1024,1024]{1,0:T(8,128)(2,1)S(1)}, bf16[1024,1024]{1,0:T(8,128)(2,1)}, u32[]{:S(2)}, u32[]{:S(2)}) %collective-permute-start.5) | collective-permute-done | bytes 2097184 | tf_op jit(solution)/shard_map/ppermute | solution.py:299
  63.8 0.9 collective-permute-start.7
  64.7 2.1 collective-permute-start.8
  66.8 0.8 collective-permute-start.3
  67.6 1.3 slice.4
  68.9 1.3 collective-permute-start.9
  70.9 30.0 %collective-permute-done.9.refs_3_._in1 = bf16[512,1024]{1,0:T(8,128)(2,1)} collective-permute-done((bf16[512,1024]{1,0:T(8,128)(2,1)S(1)}, bf16[512,1024]{1,0:T(8,128)(2,1)}, u32[]{:S(2)}, u32[]{:S(2)}) %collective-permute-start.9) | collective-permute-done | bytes 1048608 | tf_op jit(solution)/shard_map/ppermute | solution.py:299
  101.0 1.4 copy-done.27
  102.4 1.3 copy-done.1
  103.7 1.2 copy-done.10
  104.9 1.2 copy-done.15
  106.2 2.6 shard_map.69
  108.8 1.0 copy-done.22
  109.8 1.0 copy-done.26
  110.8 1.3 collective-permute-start.10
  112.1 0.8 collective-permute-start.12
  112.9 1.6 shard_map.70
  114.5 1.3 copy-done.18
  115.8 0.8 collective-permute-start.11
  116.6 4.7 %collective-permute-start.13 = (bf16[1024,1024]{1,0:T(8,128)(2,1)}, bf16[1024,1024]{1,0:T(8,128)(2,1)S(1)}, u32[]{:S(2)}, u32[]{:S(2)}) collective-permute-start(bf16[1024,1024]{1,0:T(8,128)(2,1)} %get-tuple-element.25.h1), channel_id=1, source_target_pairs={{0,1},{5,4},{10,11},{16,17},{21,20},{26,27}} | collective-permute-start | bytes 6291464 | tf_op jit(solution)/shard_map/ppermute | solution.py:299
  121.3 2.4 constant_dynamic-update-slice_fusion.1
  123.7 17.6 %collective-permute-done.10.came_ref = bf16[512,1024]{1,0:T(8,128)(2,1)S(1)} collective-permute-done((bf16[512,1024]{1,0:T(8,128)(2,1)}, bf16[512,1024]{1,0:T(8,128)(2,1)S(1)}, u32[]{:S(2)}, u32[]{:S(2)}) %collective-permute-start.10) | collective-permute-done | bytes 1048608 | tf_op jit(solution)/shard_map/ppermute | solution.py:299
  141.3 1.0 constant_dynamic-update-slice_fusion.h2
  142.4 14.7 %collective-permute-start.17 = (bf16[1024,1024]{1,0:T(8,128)(2,1)}, bf16[1024,1024]{1,0:T(8,128)(2,1)}, u32[]{:S(2)}, u32[]{:S(2)}) collective-permute-start(bf16[1024,1024]{1,0:T(8,128)(2,1)} %constant_dynamic-update-slice_fusion.h2), channel_id=1, source_target_pairs={{0,2},{5,7},{16,18},{21,23}} | collective-permute-start | bytes 6291464 | tf_op jit(solution)/shard_map/ppermute | solution.py:299
  157.1 2.6 collective-permute-start.16
  159.7 1.3 collective-permute-start.18
  161.1 1.4 copy-done.6
  162.5 1.0 shard_map.71._dep
  163.5 1.3 collective-permute-start.14
  164.8 4.3 %all-gather.3.cloned.1.call-done.t_row_ref = bf16[1024,2048]{1,0:T(8,128)(2,1)} async-done(((bf16[1024,512]{1,0:T(8,128)(2,1)}), bf16[1024,2048]{1,0:T(8,128)(2,1)}) %all-gather.3.cloned.1.call-update) | async-done | bytes 4194320 | tf_op jit(solution)/shard_map/all_gather | solution.py:367
  169.1 2.2 copy-done.16
  171.3 1.6 copy-done.20
  172.9 1.0 copy-done.21
  174.0 5.1 %shard_map.72 = (bf16[512,512]{1,0:T(8,128)(2,1)S(1)}, bf16[512,512]{1,0:T(8,128)(2,1)}, f32[512,512]{1,0:T(8,128)S(1)}, f32[512,512]{1,0:T(8,128)S(1)}) custom-call(bf16[512,1024]{1,0:T(8,128)(2,1)S(1)} %get-tuple-element.20.tt_ref, bf16[1024,2048]{1,0:T(8,128)(2,1)S(1)} %copy-done.16, bf16[512,512]{1,0:T(8,128)(2,1)S(1)} %copy-done.21, ...), custom_call_target="tpu_custom_call" | custom-call | flops 1 | bytes 1 | tf_op jit(solution)/shard_map/pallas_call | solution.py:265
  179.0 3.4 %collective-permute-start.15 = (bf16[512,512]{1,0:T(8,128)(2,1)S(1)}, bf16[512,512]{1,0:T(8,128)(2,1)S(1)}, u32[]{:S(2)}, u32[]{:S(2)}) collective-permute-start(bf16[512,512]{1,0:T(8,128)(2,1)S(1)} %get-tuple-element.26._dep), channel_id=1, source_target_pairs={{0,4},{1,5},{2,6},{3,7},{4,0},{5,1},{6,2},{7,3},{8,12},{9,13},{10,... | collective-permute-start | bytes 1572872 | tf_op jit(solution)/shard_map/ppermute | solution.py:299
  182.4 0.8 copy-done.23
  183.2 20.4 %collective-permute-done.14.came_ref = bf16[512,1024]{1,0:T(8,128)(2,1)} collective-permute-done((bf16[512,1024]{1,0:T(8,128)(2,1)}, bf16[512,1024]{1,0:T(8,128)(2,1)}, u32[]{:S(2)}, u32[]{:S(2)}) %collective-permute-start.14) | collective-permute-done | bytes 1048608 | tf_op jit(solution)/shard_map/ppermute | solution.py:299
  203.6 11.1 %collective-permute-done.15.refs_0_.far_ref = bf16[512,512]{1,0:T(8,128)(2,1)S(1)} collective-permute-done((bf16[512,512]{1,0:T(8,128)(2,1)S(1)}, bf16[512,512]{1,0:T(8,128)(2,1)S(1)}, u32[]{:S(2)}, u32[]{:S(2)}) %collective-permute-start.15) | collective-permute-done | bytes 524320 | tf_op jit(solution)/shard_map/ppermute | solution.py:299
  214.7 1.2 shard_map.74
  216.0 1.3 constant_dynamic-update-slice_fusion.3
  217.3 1.3 constant_dynamic-update-slice_fusion.2.h3
  218.6 8.8 %collective-permute-start.19 = (bf16[1024,1024]{1,0:T(8,128)(2,1)S(1)}, bf16[1024,1024]{1,0:T(8,128)(2,1)S(1)}, u32[]{:S(2)}, u32[]{:S(2)}) collective-permute-start(bf16[1024,1024]{1,0:T(8,128)(2,1)S(1)} %constant_dynamic-update-slice_fusion.2.h3), channel_id=1, source_target_pairs={{0,1},{16,17}} | collective-permute-start | bytes 6291464 | tf_op jit(solution)/shard_map/ppermute | solution.py:299
  227.4 2.0 collective-permute-start.20
  229.5 1.3 collective-permute-start.21
  230.8 2.7 collective-permute-start.22
  233.7 3.4 %shard_map.73.acc_ref = f32[1024,1024]{1,0:T(8,128)S(1)} custom-call(bf16[1024,1024]{1,0:T(8,128)(2,1)S(1)} %copy-done, bf16[1024,1024]{1,0:T(8,128)(2,1)} %collective-permute-done.1.refs_4_.l1, bf16[1024,1024]{1,0:T(8,128)(2,1)} %collective-permute-done.2.refs_3_.l2, bf16[1024,1024]{1,0:T(8,128)(2,1)S(1)} %copy-done.3, bf16[512,512]{1,0:T(8,128)(2,1)S(1)} %copy-done.24), custom_call_target="tpu_custom_call" | custom-call | flops 1 | bytes 1 | tf_op jit(solution)/shard_map/pallas_call | solution.py:265
  237.1 2.0 copy-done.4
  239.1 16.3 %shard_map.75._dep = bf16[1024,1024]{1,0:T(8,128)(2,1)} custom-call(f32[1024,1024]{1,0:T(8,128)} %copy-done.4, bf16[1024,1024]{1,0:T(8,128)(2,1)} %get-tuple-element.25.h1, bf16[1024,1024]{1,0:T(8,128)(2,1)} %constant_dynamic-update-slice_fusion.h2, bf16[1024,1024]{1,0:T(8,128)(2,1)S(1)} %constant_dynamic-update-slice_fusion.2.h3, ...), custom_call_target="tpu_custom_call" | custom-call | flops 1 | bytes 1 | tf_op jit(solution)/shard_map/pallas_call | solution.py:265
  255.4 5.6 %collective-permute-done.21.came_ref = bf16[512,1024]{1,0:T(8,128)(2,1)S(1)} collective-permute-done((bf16[512,1024]{1,0:T(8,128)(2,1)S(1)}, bf16[512,1024]{1,0:T(8,128)(2,1)S(1)}, u32[]{:S(2)}, u32[]{:S(2)}) %collective-permute-start.21) | collective-permute-done | bytes 1048608 | tf_op jit(solution)/shard_map/ppermute | solution.py:299
  261.0 1.6 copy-done.8
  262.6 2.1 shard_map.76._dep
  264.8 14.1 %collective-permute-done.22.near_ref = bf16[512,512]{1,0:T(8,128)(2,1)} collective-permute-done((bf16[512,512]{1,0:T(8,128)(2,1)}, bf16[512,512]{1,0:T(8,128)(2,1)}, u32[]{:S(2)}, u32[]{:S(2)}) %collective-permute-start.22) | collective-permute-done | bytes 524320 | tf_op jit(solution)/shard_map/ppermute | solution.py:299
  278.9 1.2 copy-done.17
  280.1 2.5 shard_map.78
  (70 shorter events, 1.9 us)
Async XLA Ops:
  7.2 7.4 %copy-start = (bf16[1024,1024]{1,0:T(8,128)(2,1)S(1)}, bf16[1024,1024]{1,0:T(8,128)(2,1)}, u32[]{:S(2)}) copy-start(bf16[1024,1024]{1,0:T(8,128)(2,1)} %l0.9) | copy-start | bytes 6291460
  7.2 157.6 %all-gather.5.cloned.1.call-start = ((), (), s32[]{:S(2)}) async-start(), calls=%async_computation.1 | async-start | bytes 2621440 | tf_op jit(solution)/shard_map/all_gather | solution.py:329
  9.5 13.2 %copy-start.14 = (bf16[1024,512]{1,0:T(8,128)(2,1)}, bf16[1024,512]{1,0:T(8,128)(2,1)S(1)}, u32[]{:S(2)}) copy-start(bf16[1024,512]{1,0:T(8,128)(2,1)S(1)} %broadcast_select_fusion.p0) | copy-start | bytes 3145732
  9.5 27.3 %collective-permute-start = (bf16[1024,512]{1,0:T(8,128)(2,1)S(1)}, bf16[1024,512]{1,0:T(8,128)(2,1)S(1)}, u32[]{:S(2)}, u32[]{:S(2)}) collective-permute-start(bf16[1024,512]{1,0:T(8,128)(2,1)S(1)} %broadcast_select_fusion.p0), channel_id=1, source_target_pairs={{0,4},{1,5},{2,6},{3,7},{4,8},{5,9},{6,10},{7,11},{8,12},{9,13},{1... | collective-permute-start | bytes 3145736 | tf_op jit(solution)/shard_map/ppermute | solution.py:299
  14.6 49.1 %collective-permute-start.5 = (bf16[1024,1024]{1,0:T(8,128)(2,1)S(1)}, bf16[1024,1024]{1,0:T(8,128)(2,1)}, u32[]{:S(2)}, u32[]{:S(2)}) collective-permute-start(bf16[1024,1024]{1,0:T(8,128)(2,1)S(1)} %copy-done), channel_id=1, source_target_pairs={{4,0},{5,1},{8,4},{9,5},{10,6},{12,8},{13,9},{14,10},{15,11},{20,1... | collective-permute-start | bytes 6291464 | tf_op jit(solution)/shard_map/ppermute | solution.py:299
  15.9 47.8 %collective-permute-start.2 = (bf16[1024,1024]{1,0:T(8,128)(2,1)S(1)}, bf16[1024,1024]{1,0:T(8,128)(2,1)}, u32[]{:S(2)}, u32[]{:S(2)}) collective-permute-start(bf16[1024,1024]{1,0:T(8,128)(2,1)S(1)} %copy-done), channel_id=1, source_target_pairs={{0,2},{4,6},{5,7},{8,10},{9,11},{10,8},{12,14},{13,15},{14,12},{15... | collective-permute-start | bytes 6291464 | tf_op jit(solution)/shard_map/ppermute | solution.py:299
  36.9 1.0 copy-start.9
  37.8 25.8 %collective-permute-start.1 = (bf16[1024,1024]{1,0:T(8,128)(2,1)}, bf16[1024,1024]{1,0:T(8,128)(2,1)}, u32[]{:S(2)}, u32[]{:S(2)}) collective-permute-start(bf16[1024,1024]{1,0:T(8,128)(2,1)} %shard_map.67), channel_id=1, source_target_pairs={{0,1},{4,5},{5,4},{8,9},{9,8},{10,11},{12,13},{13,12},{14,15},{15,... | collective-permute-start | bytes 6291464 | tf_op jit(solution)/shard_map/ppermute | solution.py:299
  40.5 2.6 collective-permute-start.4
  43.1 20.5 %copy-start.11 = (bf16[1024,512]{1,0:T(8,128)(2,1)}, bf16[1024,512]{1,0:T(8,128)(2,1)S(1)}, u32[]{:S(2)}) copy-start(bf16[1024,512]{1,0:T(8,128)(2,1)S(1)} %collective-permute-done.4.refs_0_) | copy-start | bytes 3145732
  63.7 6.5 %copy-start.12 = (bf16[1024,512]{1,0:T(8,128)(2,1)S(1)}, bf16[1024,512]{1,0:T(8,128)(2,1)}, u32[]{:S(2)}) copy-start(bf16[1024,512]{1,0:T(8,128)(2,1)} %get-tuple-element.19.p2) | copy-start | bytes 3145732
  63.7 105.4 %all-gather.3.cloned.1.call-start = ((), (), s32[]{:S(2)}) async-start(), calls=%async_computation | async-start | bytes 5242880 | tf_op jit(solution)/shard_map/all_gather | solution.py:367
  63.8 40.0 %copy-start.13 = (bf16[1024,512]{1,0:T(8,128)(2,1)S(1)}, bf16[1024,512]{1,0:T(8,128)(2,1)}, u32[]{:S(2)}) copy-start(bf16[1024,512]{1,0:T(8,128)(2,1)} %get-tuple-element.19.p2) | copy-start | bytes 3145732
  63.8 37.2 %collective-permute-start.7 = (bf16[1024,1024]{1,0:T(8,128)(2,1)}, bf16[1024,1024]{1,0:T(8,128)(2,1)S(1)}, u32[]{:S(2)}, u32[]{:S(2)}) collective-permute-start(bf16[1024,1024]{1,0:T(8,128)(2,1)} %collective-permute-done.5.refs_2_.refs_0_._in0), channel_id=1, source_target_pairs={{5,7},{10,8},{21,23},{26,24}} | collective-permute-start | bytes 6291464 | tf_op jit(solution)/shard_map/ppermute | solution.py:299
  64.7 36.3 %collective-permute-start.8 = (bf16[1024,1024]{1,0:T(8,128)(2,1)}, bf16[1024,1024]{1,0:T(8,128)(2,1)}, u32[]{:S(2)}, u32[]{:S(2)}) collective-permute-start(bf16[1024,1024]{1,0:T(8,128)(2,1)} %collective-permute-done.2.refs_3_.l2), channel_id=1, source_target_pairs={{14,2},{30,18}} | collective-permute-start | bytes 6291464 | tf_op jit(solution)/shard_map/ppermute | solution.py:299
  66.8 34.2 %collective-permute-start.3 = (bf16[1024,1024]{1,0:T(8,128)(2,1)}, bf16[1024,1024]{1,0:T(8,128)(2,1)S(1)}, u32[]{:S(2)}, u32[]{:S(2)}) collective-permute-start(bf16[1024,1024]{1,0:T(8,128)(2,1)} %collective-permute-done.2.refs_3_.l2), channel_id=1, source_target_pairs={{2,3},{6,7},{7,6},{8,9},{10,11},{11,10},{12,13},{13,12},{14,15},{1... | collective-permute-start | bytes 6291464 | tf_op jit(solution)/shard_map/ppermute | solution.py:299
  68.9 32.1 %collective-permute-start.9 = (bf16[512,1024]{1,0:T(8,128)(2,1)S(1)}, bf16[512,1024]{1,0:T(8,128)(2,1)}, u32[]{:S(2)}, u32[]{:S(2)}) collective-permute-start(bf16[512,1024]{1,0:T(8,128)(2,1)S(1)} %slice.4), channel_id=1, source_target_pairs={{4,0},{5,1},{6,2},{8,4},{9,5},{10,6},{11,7},{20,16},{21,17},{22,18... | collective-permute-start | bytes 3145736 | tf_op jit(solution)/shard_map/ppermute | solution.py:299
  70.2 30.8 %collective-permute-start.6 = (bf16[1024,512]{1,0:T(8,128)(2,1)S(1)}, bf16[1024,512]{1,0:T(8,128)(2,1)S(1)}, u32[]{:S(2)}, u32[]{:S(2)}) collective-permute-start(bf16[1024,512]{1,0:T(8,128)(2,1)S(1)} %copy-done.12), channel_id=1, source_target_pairs={{8,12},{9,13},{10,14},{11,15},{24,28},{25,29},{26,30},{27,31}} | collective-permute-start | bytes 3145736 | tf_op jit(solution)/shard_map/ppermute | solution.py:299
  101.0 1.4 copy-start.27
  102.4 1.3 copy-start.1
  103.7 1.2 copy-start.10
  104.9 1.2 copy-start.15
  108.8 1.0 copy-start.22
  109.8 1.0 copy-start.26
  110.8 30.6 %collective-permute-start.10 = (bf16[512,1024]{1,0:T(8,128)(2,1)}, bf16[512,1024]{1,0:T(8,128)(2,1)S(1)}, u32[]{:S(2)}, u32[]{:S(2)}) collective-permute-start(bf16[512,1024]{1,0:T(8,128)(2,1)} %copy-done.26), channel_id=1, source_target_pairs={{4,0},{5,1},{6,2},{8,4},{9,5},{10,6},{11,7},{12,8},{13,9},{14,10},... | collective-permute-start | bytes 3145736 | tf_op jit(solution)/shard_map/ppermute | solution.py:299
  112.1 47.7 %collective-permute-start.12 = (bf16[1024,1024]{1,0:T(8,128)(2,1)}, bf16[1024,1024]{1,0:T(8,128)(2,1)S(1)}, u32[]{:S(2)}, u32[]{:S(2)}) collective-permute-start(bf16[1024,1024]{1,0:T(8,128)(2,1)} %copy-done.27), channel_id=1, source_target_pairs={{7,6},{8,9},{23,22},{24,25}} | collective-permute-start | bytes 6291464 | tf_op jit(solution)/shard_map/ppermute | solution.py:299
  114.5 1.3 copy-start.18
  115.8 45.2 %collective-permute-start.11 = (bf16[1024,1024]{1,0:T(8,128)(2,1)}, bf16[1024,1024]{1,0:T(8,128)(2,1)S(1)}, u32[]{:S(2)}, u32[]{:S(2)}) collective-permute-start(bf16[1024,1024]{1,0:T(8,128)(2,1)} %get-tuple-element.24.x3), channel_id=1, source_target_pairs={{2,3},{18,19}} | collective-permute-start | bytes 6291464 | tf_op jit(solution)/shard_map/ppermute | solution.py:299
  116.6 44.5 %collective-permute-start.13 = (bf16[1024,1024]{1,0:T(8,128)(2,1)}, bf16[1024,1024]{1,0:T(8,128)(2,1)S(1)}, u32[]{:S(2)}, u32[]{:S(2)}) collective-permute-start(bf16[1024,1024]{1,0:T(8,128)(2,1)} %get-tuple-element.25.h1), channel_id=1, source_target_pairs={{0,1},{5,4},{10,11},{16,17},{21,20},{26,27}} | collective-permute-start | bytes 6291464 | tf_op jit(solution)/shard_map/ppermute | solution.py:299
  121.3 41.2 %copy-start.2 = (bf16[1024,1024]{1,0:T(8,128)(2,1)S(1)}, bf16[1024,1024]{1,0:T(8,128)(2,1)}, u32[]{:S(2)}) copy-start(bf16[1024,1024]{1,0:T(8,128)(2,1)} %copy-done.1) | copy-start | bytes 6291460
  142.4 61.2 %collective-permute-start.17 = (bf16[1024,1024]{1,0:T(8,128)(2,1)}, bf16[1024,1024]{1,0:T(8,128)(2,1)}, u32[]{:S(2)}, u32[]{:S(2)}) collective-permute-start(bf16[1024,1024]{1,0:T(8,128)(2,1)} %constant_dynamic-update-slice_fusion.h2), channel_id=1, source_target_pairs={{0,2},{5,7},{16,18},{21,23}} | collective-permute-start | bytes 6291464 | tf_op jit(solution)/shard_map/ppermute | solution.py:299
  157.1 46.5 %collective-permute-start.16 = (bf16[1024,1024]{1,0:T(8,128)(2,1)}, bf16[1024,1024]{1,0:T(8,128)(2,1)}, u32[]{:S(2)}, u32[]{:S(2)}) collective-permute-start(bf16[1024,1024]{1,0:T(8,128)(2,1)} %constant_dynamic-update-slice_fusion.h2), channel_id=1, source_target_pairs={{0,1},{5,4},{16,17},{21,20}} | collective-permute-start | bytes 6291464 | tf_op jit(solution)/shard_map/ppermute | solution.py:299
  159.7 1.3 copy-start.28
  159.7 23.4 %collective-permute-start.18 = (bf16[512,1024]{1,0:T(8,128)(2,1)}, bf16[512,1024]{1,0:T(8,128)(2,1)}, u32[]{:S(2)}, u32[]{:S(2)}) collective-permute-start(bf16[512,1024]{1,0:T(8,128)(2,1)} %get-tuple-element.27), channel_id=1, source_target_pairs={{4,0},{5,1},{6,2},{7,3},{20,16},{21,17},{22,18},{23,19}} | collective-permute-start | bytes 3145736 | tf_op jit(solution)/shard_map/ppermute | solution.py:299
  161.0 2.4 copy-start.5
  161.1 1.4 copy-start.6
  163.5 40.1 %collective-permute-start.14 = (bf16[512,1024]{1,0:T(8,128)(2,1)}, bf16[512,1024]{1,0:T(8,128)(2,1)}, u32[]{:S(2)}, u32[]{:S(2)}) collective-permute-start(bf16[512,1024]{1,0:T(8,128)(2,1)} %shard_map.71._dep), channel_id=1, source_target_pairs={{4,0},{5,1},{6,2},{7,3},{8,4},{9,5},{10,6},{11,7},{12,8},{13,9},{1... | collective-permute-start | bytes 3145736 | tf_op jit(solution)/shard_map/ppermute | solution.py:299
  169.1 2.2 copy-start.16
  171.3 1.6 copy-start.20
  172.9 1.0 copy-start.21
  179.0 35.7 %collective-permute-start.15 = (bf16[512,512]{1,0:T(8,128)(2,1)S(1)}, bf16[512,512]{1,0:T(8,128)(2,1)S(1)}, u32[]{:S(2)}, u32[]{:S(2)}) collective-permute-start(bf16[512,512]{1,0:T(8,128)(2,1)S(1)} %get-tuple-element.26._dep), channel_id=1, source_target_pairs={{0,4},{1,5},{2,6},{3,7},{4,0},{5,1},{6,2},{7,3},{8,12},{9,13},{10,... | collective-permute-start | bytes 1572872 | tf_op jit(solution)/shard_map/ppermute | solution.py:299
  182.4 0.8 copy-start.23
  218.6 15.1 %copy-start.3 = (bf16[1024,1024]{1,0:T(8,128)(2,1)S(1)}, bf16[1024,1024]{1,0:T(8,128)(2,1)}, u32[]{:S(2)}) copy-start(bf16[1024,1024]{1,0:T(8,128)(2,1)} %copy-done.1) | copy-start | bytes 6291460
  218.6 15.1 %copy-start.24 = (bf16[512,512]{1,0:T(8,128)(2,1)S(1)}, bf16[512,512]{1,0:T(8,128)(2,1)}, u32[]{:S(2)}) copy-start(bf16[512,512]{1,0:T(8,128)(2,1)} %copy-done.23) | copy-start | bytes 1572868
  218.6 20.5 %collective-permute-start.19 = (bf16[1024,1024]{1,0:T(8,128)(2,1)S(1)}, bf16[1024,1024]{1,0:T(8,128)(2,1)S(1)}, u32[]{:S(2)}, u32[]{:S(2)}) collective-permute-start(bf16[1024,1024]{1,0:T(8,128)(2,1)S(1)} %constant_dynamic-update-slice_fusion.2.h3), channel_id=1, source_target_pairs={{0,1},{16,17}} | collective-permute-start | bytes 6291464 | tf_op jit(solution)/shard_map/ppermute | solution.py:299
  227.4 11.6 %collective-permute-start.20 = (bf16[1024,1024]{1,0:T(8,128)(2,1)}, bf16[1024,1024]{1,0:T(8,128)(2,1)}, u32[]{:S(2)}, u32[]{:S(2)}) collective-permute-start(bf16[1024,1024]{1,0:T(8,128)(2,1)} %get-tuple-element.29.x2), channel_id=1, source_target_pairs={{2,3},{7,6},{18,19},{23,22}} | collective-permute-start | bytes 6291464 | tf_op jit(solution)/shard_map/ppermute | solution.py:299
  229.5 31.6 %collective-permute-start.21 = (bf16[512,1024]{1,0:T(8,128)(2,1)S(1)}, bf16[512,1024]{1,0:T(8,128)(2,1)S(1)}, u32[]{:S(2)}, u32[]{:S(2)}) collective-permute-start(bf16[512,1024]{1,0:T(8,128)(2,1)S(1)} %get-tuple-element.31._dep), channel_id=1, source_target_pairs={{4,0},{5,1},{6,2},{7,3},{8,4},{9,5},{10,6},{11,7},{12,8},{13,9},{1... | collective-permute-start | bytes 3145736 | tf_op jit(solution)/shard_map/ppermute | solution.py:299
  230.8 48.1 %collective-permute-start.22 = (bf16[512,512]{1,0:T(8,128)(2,1)}, bf16[512,512]{1,0:T(8,128)(2,1)}, u32[]{:S(2)}, u32[]{:S(2)}) collective-permute-start(bf16[512,512]{1,0:T(8,128)(2,1)} %get-tuple-element.33), channel_id=1, source_target_pairs={{0,4},{1,5},{2,6},{3,7},{4,0},{5,1},{6,2},{7,3},{8,12},{9,13},{10,... | collective-permute-start | bytes 1572872 | tf_op jit(solution)/shard_map/ppermute | solution.py:299
  233.6 5.5 %copy-start.7 = (bf16[1024,1024]{1,0:T(8,128)(2,1)S(1)}, bf16[1024,1024]{1,0:T(8,128)(2,1)}, u32[]{:S(2)}) copy-start(bf16[1024,1024]{1,0:T(8,128)(2,1)} %copy-done.6) | copy-start | bytes 6291460
  233.6 45.3 %collective-permute-start.23 = (bf16[512,512]{1,0:T(8,128)(2,1)S(1)}, bf16[512,512]{1,0:T(8,128)(2,1)}, u32[]{:S(2)}, u32[]{:S(2)}) collective-permute-start(bf16[512,512]{1,0:T(8,128)(2,1)S(1)} %shard_map.77), channel_id=1, source_target_pairs={{0,8},{1,9},{2,10},{3,11},{4,12},{5,13},{6,14},{7,15},{8,0},{9,1},... | collective-permute-start | bytes 1572872 | tf_op jit(solution)/shard_map/ppermute | solution.py:299
  237.0 2.0 copy-start.4
  239.0 22.0 %copy-start.19 = (f32[512,1024]{1,0:T(8,128)S(1)}, f32[512,1024]{1,0:T(8,128)}, u32[]{:S(2)}) copy-start(f32[512,1024]{1,0:T(8,128)} %copy-done.18) | copy-start | bytes 6291460
  239.0 22.0 %copy-start.25 = (s32[8]{0:T(128)S(1)}, s32[8]{0:T(128)}, u32[]{:S(2)}) copy-start(s32[8]{0:T(128)} %structure.1) | copy-start | bytes 100
  261.0 1.6 copy-start.8
  278.9 1.2 copy-start.17
Sparse Core Ops, SparseCore 0:
  63.8 29.4 all-gather.4
  110.9 58.1 all-gather.2

commit v9 on v8

--- a/solution.py
+++ b/solution.py
@@ -82,55 +82,69 @@
     return pl.ds(pl.multiple_of(i * TILE, TILE), TILE)
 
 
-def product_kernel(l0, l1, l2, l3, p0, p1, p2, p3, *refs, deps, gated):
-    below = refs[0]
-    t_ref, tt_ref, sent_ref = refs[deps + gated : deps + gated + 3]
-    rows, panels, acc, row_sems, panel_sems, sem = refs[deps + 2 * gated + 3 :]
+def product_kernel(l0, l1, l2, l3, p0, p1, p2, acc_ref, rows, panels, row_sems, panel_sems):
     r, c = position()
-    half = below.at[sent_ref.shape[0] :]
-
-    @pl.when((r == 1) | (r == 2))
-    def _():
-        start(half, sent_ref, sem)
-
     for m, ref in enumerate((l0, l1, l2, l3)):
         j = c ^ m
 
-        @pl.when(j <= r)
+        @pl.when((j <= r) & (r - j < 3))
         def _():
             start(ref, rows.at[r - j], row_sems.at[r - j])
 
-    for s, ref in enumerate((p0, p1, p2, p3)):
+    for s, ref in enumerate((p0, p1, p2)):
 
         @pl.when(s <= r)
         def _():
             start(ref, panels.at[s], panel_sems.at[s])
 
-    for s in range(N):
+    for s in range(3):
 
         @pl.when(s <= r)
         def _():
             wait(l0, rows.at[s], row_sems.at[s])
             wait(p0, panels.at[s], panel_sems.at[s])
 
-            @pl.loop(0, acc.shape[0] // TILE)
+            @pl.loop(0, acc_ref.shape[0] // TILE)
             def _(i):
                 term = dot(rows[s, tile(i), :], panels[s])
                 if s > 0:
-                    term = term + acc[tile(i), :]
-                acc[tile(i), :] = term
-
-    @pl.loop(0, acc.shape[0] // TILE)
-    def _(i):
-        value = acc[tile(i), :]
+                    term = term + acc_ref[tile(i), :]
+                acc_ref[tile(i), :] = term
+
+
+def product_end_kernel(l0, l1, l2, l3, acc_ref, p3_ref, *refs, deps, gated):
+    below = refs[0]
+    t_ref, tt_ref, sent_ref = refs[deps + gated : deps + gated + 3]
+    block, block_sem, sem = refs[deps + 2 * gated + 3 :]
+    r, c = position()
+    half = below.at[sent_ref.shape[0] :]
+
+    @pl.when((r == 1) | (r == 2))
+    def _():
+        start(half, sent_ref, sem)
+
+    def finish(i, value):
         t_ref[tile(i), :] = value.astype(BF16)
         tt_ref[:, tile(i)] = value.T.astype(BF16)
 
+    @pl.when(r < 3)
+    def _():
+        @pl.loop(0, acc_ref.shape[0] // TILE)
+        def _(i):
+            finish(i, acc_ref[tile(i), :])
+
     @pl.when(r == 3)
     def _():
+        start_picked((l0, l1, l2, l3), c, block, block_sem)
+        wait(l0, block, block_sem)
+
+        @pl.loop(0, acc_ref.shape[0] // TILE)
+        def _(i):
+            finish(i, dot(block[tile(i), :], p3_ref[...]) + acc_ref[tile(i), :])
+
         @pl.loop(0, tt_ref.shape[0] // TILE)
         def _(i):
-            sent_ref[tile(i), :] = dot(tt_ref[tile(i), :], rows[3]).astype(BF16)
+            sent_ref[tile(i), :] = dot(tt_ref[tile(i), :], block[...]).astype(BF16)
 
     @pl.when((r == 1) | (r == 2))
     def _():
@@ -345,20 +359,22 @@
 
         root_row = (root_inverse, root_beside, root_across, root_both)
         panels = (panel_kept, panel_1, panel_2, panel_3)
+        (t_sum,) = local_call(
+            product_kernel,
+            [ANY] * 7,
+            [shape((h, w), F32)],
+            [pltpu.VMEM((3, h, h), BF16), pltpu.VMEM((3, h, w), BF16), dma((3,)), dma((3,))],
+            *root_row,
+            *panels[:3],
+        )
         t, t_t, sent = local_call(
-            functools.partial(product_kernel, deps=4, gated=0),
-            [ANY] * 8,
+            functools.partial(product_end_kernel, deps=4, gated=0),
+            [ANY] * 4 + [VMEM] * 2,
             [shape((h, w), BF16), t_block, t_block],
-            [
-                pltpu.VMEM((n, h, h), BF16),
-                pltpu.VMEM((n, h, w), BF16),
-                pltpu.VMEM((h, w), F32),
-                dma((n,)),
-                dma((n,)),
-                dma,
-            ],
+            [pltpu.VMEM((h, h), BF16), dma, dma],
             *root_row,
-            *panels,
+            t_sum,
+            panel_3,
             below_1,
             across_1,
             across_3,
@@ -385,7 +401,7 @@
         below_3a = down(below_2a, 3)
         beside_1 = to_beside(below_1, (0, 1, 2))
         (sent,) = local_call(
-            functools.partial(chain_kernel, step=1, deps=3, gated=0),
+            functools.partial(chain_kernel, step=1, deps=4, gated=0),
             chain,
             [t_block],
             [pltpu.VMEM((h, h), BF16), dma],
@@ -395,6 +411,7 @@
             far_3,
             far_1,
             beside_1,
+            below_3a,
         )
         below_2 = jnp.concatenate((below_2a, below_2b), 0)
         below_3b = came = step(sent)
@@ -413,6 +430,7 @@
             sent,
         )
         child_far = move(far_part, lambda r, c: (r ^ 1, c))
+        child_near = move(near_part, lambda r, c: (r ^ 1, c))
         (root_sum,) = local_call(
             diagonal_kernel,
             [],
@@ -422,7 +440,7 @@
             far_part,
         )
         sent, across_2, below_3a = local_call(
-            functools.partial(chain_kernel, step=2, deps=2, gated=2),
+            functools.partial(chain_kernel, step=2, deps=3, gated=2),
             chain,
             [t_block],
             [pltpu.VMEM((h, h), BF16), dma],
@@ -430,6 +448,7 @@
             t_t,
             came,
             child_far,
+            child_near,
             beside_2,
             across_2,
             below_3a,
@@ -439,7 +458,6 @@
         (child_onward,) = local_call(
             child_onward_kernel, [VMEM] * 2, [child_block], [], child_on, child_far, sent
         )
-        child_near = move(near_part, lambda r, c: (r ^ 1, c))
         child_last = move(child_onward, lambda r, c: (r ^ 2, c))
         below_3 = jnp.concatenate((below_3a, below_3b), 0)
         beside_3 = to_beside(below_3, (0,))

time: 293 us -> 290 us (0.990)
  the two profiles are of different devices: /device:TPU:0 before, /device:TPU:3 now
where the time goes in v9:
time: 290 us; the launch traced here: 289 us
  waiting for transfers between devices  173 us (60%)
  starting transfers between devices  39.9 us (14%)
  local copies, waits for them, and re-layouts  32.3 us (11%)
  Pallas kernels  26.8 us (9%)
  between operations  14.5 us (5%)
    ppermute x24, waiting for transfers between devices, move(): return lax.ppermute(x, AXES, pairs)  173 us
    ppermute x24, starting transfers between devices, move(): return lax.ppermute(x, AXES, pairs)  39.8 us
    unnamed x72, local copies, waits for them, and re-layouts  28.6 us
    pallas_call x11, Pallas kernels, local_call(): pl.pallas_call(kernel, out_shape=outs, in_specs=in_specs + [ANY] * (len(a...  26.8 us
  transfers between devices with their start and end apart: 26, of which 8 were waited for; matrix products, arithmetic and copies ran while one was open for 2% of the time, Pallas kernels for 8%

profile of v9, /device:TPU:3, one launch (start us, length us, event | category | flops | bytes accessed | tf_op | source)
XLA Modules:
  0.0 288.8 jit_solution(10985638510303504004)
XLA Ops:
  7.2 0.8 broadcast_compare_fusion
  8.1 1.4 broadcast_select_fusion.p0
  9.5 3.3 %collective-permute-start = (bf16[1024,512]{1,0:T(8,128)(2,1)S(1)}, bf16[1024,512]{1,0:T(8,128)(2,1)S(1)}, u32[]{:S(2)}, u32[]{:S(2)}) collective-permute-start(bf16[1024,512]{1,0:T(8,128)(2,1)S(1)} %broadcast_select_fusion.p0), channel_id=1, source_target_pairs={{0,4},{1,5},{2,6},{3,7},{4,8},{5,9},{6,10},{7,11},{8,12},{9,13},{1... | collective-permute-start | bytes 3145736 | tf_op jit(solution)/shard_map/ppermute | solution.py:313
  12.8 2.0 collective-permute-start.5
  14.9 2.0 collective-permute-start.2
  16.9 1.3 copy.15.refs_0_
  18.2 16.3 %collective-permute-done.refs_1_.p1 = bf16[1024,512]{1,0:T(8,128)(2,1)S(1)} collective-permute-done((bf16[1024,512]{1,0:T(8,128)(2,1)S(1)}, bf16[1024,512]{1,0:T(8,128)(2,1)S(1)}, u32[]{:S(2)}, u32[]{:S(2)}) %collective-permute-start) | collective-permute-done | bytes 1048608 | tf_op jit(solution)/shard_map/ppermute | solution.py:313
  34.6 1.0 copy-done.15
  35.5 2.0 collective-permute-start.1
  38.3 1.9 copy.17.refs_1_
  40.2 1.0 copy-done.17
  41.3 1.4 collective-permute-start.3
  42.7 0.8 collective-permute-start.7
  43.5 2.1 collective-permute-start.8
  45.6 1.3 slice.4
  47.6 0.7 collective-permute-start.6
  48.4 0.9 collective-permute-done.3.l3
  49.2 1.2 copy-done.20
  50.4 2.0 shard_map.69.acc_ref
  52.5 1.3 copy-done.9
  53.8 1.4 copy-done.30
  55.2 2.2 shard_map.70
  57.4 1.0 copy-done.25
  58.4 1.0 copy-done.29
  59.4 0.7 collective-permute-start.10
  60.1 1.2 copy-done.6
  61.4 3.2 %shard_map.71 = (f32[512,1024]{1,0:T(8,128)S(1)}, bf16[1024,1024]{1,0:T(8,128)(2,1)}, bf16[512,1024]{1,0:T(8,128)(2,1)S(1)}, bf16[1024,1024]{1,0:T(8,128)(2,1)}) custom-call(bf16[1024,1024]{1,0:T(8,128)(2,1)S(1)} %copy-done, bf16[1024,1024]{1,0:T(8,128)(2,1)} %collective-permute-done.1.refs_4_.l1, ...), custom_call_target="tpu_custom_call", output_to_operand_aliasing={{1}: (5, {}), {2}: (6, {}), {3}: (7, {})} | custom-call | flops 1 | bytes 1 | tf_op jit(solution)/shard_map/pallas_call | solution.py:279
  64.5 1.3 copy-done.21
  65.8 1.3 collective-permute-start.11
  67.1 0.8 collective-permute-start.12
  67.9 0.8 collective-permute-start.13
  68.8 1.4 collective-permute-start.14
  70.2 1.0 constant_dynamic-update-slice_fusion.1
  71.2 1.1 constant_dynamic-update-slice_fusion.h2
  72.3 2.0 collective-permute-start.19
  74.3 92.0 %collective-permute-done.14.refs_3_.refs_4_ = bf16[512,1024]{1,0:T(8,128)(2,1)S(1)} collective-permute-done((bf16[512,1024]{1,0:T(8,128)(2,1)S(1)}, bf16[512,1024]{1,0:T(8,128)(2,1)S(1)}, u32[]{:S(2)}, u32[]{:S(2)}) %collective-permute-start.14) | collective-permute-done | bytes 1048608 | tf_op jit(solution)/shard_map/ppermute | solution.py:313
  166.3 2.0 collective-permute-start.18
  168.3 1.3 copy-done.33
  170.3 1.4 copy-done.10
  171.6 1.0 shard_map.72._dep
  172.6 1.3 collective-permute-start.15
  174.0 2.2 copy-done.13
  176.2 1.6 copy-done.23
  177.8 1.0 copy-done.24
  178.8 4.8 %shard_map.73 = (bf16[512,512]{1,0:T(8,128)(2,1)S(1)}, bf16[512,512]{1,0:T(8,128)(2,1)S(1)}, f32[512,512]{1,0:T(8,128)S(1)}, f32[512,512]{1,0:T(8,128)S(1)}) custom-call(bf16[512,1024]{1,0:T(8,128)(2,1)S(1)} %get-tuple-element.20.tt_ref, bf16[1024,2048]{1,0:T(8,128)(2,1)S(1)} %copy-done.13, bf16[512,512]{1,0:T(8,128)(2,1)S(1)} %copy-done.24, ...), custom_call_target="tpu_custom_call" | custom-call | flops 1 | bytes 1 | tf_op jit(solution)/shard_map/pallas_call | solution.py:279
  183.6 1.0 copy-done.26
  184.6 2.1 collective-permute-start.17
  186.7 11.7 %collective-permute-done.15.came_ref = bf16[512,1024]{1,0:T(8,128)(2,1)} collective-permute-done((bf16[512,1024]{1,0:T(8,128)(2,1)}, bf16[512,1024]{1,0:T(8,128)(2,1)}, u32[]{:S(2)}, u32[]{:S(2)}) %collective-permute-start.15) | collective-permute-done | bytes 1048608 | tf_op jit(solution)/shard_map/ppermute | solution.py:313
  198.5 11.1 %collective-permute-done.17.refs_1_.near_ref = bf16[512,512]{1,0:T(8,128)(2,1)S(1)} collective-permute-done((bf16[512,512]{1,0:T(8,128)(2,1)S(1)}, bf16[512,512]{1,0:T(8,128)(2,1)S(1)}, u32[]{:S(2)}, u32[]{:S(2)}) %collective-permute-start.17) | collective-permute-done | bytes 524320 | tf_op jit(solution)/shard_map/ppermute | solution.py:313
  209.6 11.2 %collective-permute-done.16.refs_0_.far_ref = bf16[512,512]{1,0:T(8,128)(2,1)S(1)} collective-permute-done((bf16[512,512]{1,0:T(8,128)(2,1)S(1)}, bf16[512,512]{1,0:T(8,128)(2,1)S(1)}, u32[]{:S(2)}, u32[]{:S(2)}) %collective-permute-start.16) | collective-permute-done | bytes 524320 | tf_op jit(solution)/shard_map/ppermute | solution.py:313
  220.8 1.2 shard_map.75
  222.1 1.3 constant_dynamic-update-slice_fusion.2.h3
  223.5 0.9 collective-permute-start.20
  224.4 1.3 collective-permute-start.21
  225.7 1.3 collective-permute-start.22
  227.1 8.0 %collective-permute-start.23 = (bf16[512,512]{1,0:T(8,128)(2,1)S(1)}, bf16[512,512]{1,0:T(8,128)(2,1)S(1)}, u32[]{:S(2)}, u32[]{:S(2)}) collective-permute-start(bf16[512,512]{1,0:T(8,128)(2,1)S(1)} %shard_map.78), channel_id=1, source_target_pairs={{0,8},{1,9},{2,10},{3,11},{4,12},{5,13},{6,14},{7,15},{8,0},{9,1},... | collective-permute-start | bytes 1572872 | tf_op jit(solution)/shard_map/ppermute | solution.py:313
  235.4 2.0 copy-done.4
  237.4 8.5 %shard_map.76._dep = bf16[1024,1024]{1,0:T(8,128)(2,1)} custom-call(f32[1024,1024]{1,0:T(8,128)} %copy-done.4, bf16[1024,1024]{1,0:T(8,128)(2,1)} %get-tuple-element.25.h1, bf16[1024,1024]{1,0:T(8,128)(2,1)} %constant_dynamic-update-slice_fusion.h2, bf16[1024,1024]{1,0:T(8,128)(2,1)S(1)} %constant_dynamic-update-slice_fusion.2.h3, ...), custom_call_target="tpu_custom_call" | custom-call | flops 1 | bytes 1 | tf_op jit(solution)/shard_map/pallas_call | solution.py:279
  246.0 10.2 %collective-permute-done.22.came_ref = bf16[512,1024]{1,0:T(8,128)(2,1)S(1)} collective-permute-done((bf16[512,1024]{1,0:T(8,128)(2,1)S(1)}, bf16[512,1024]{1,0:T(8,128)(2,1)S(1)}, u32[]{:S(2)}, u32[]{:S(2)}) %collective-permute-start.22) | collective-permute-done | bytes 1048608 | tf_op jit(solution)/shard_map/ppermute | solution.py:313
  256.2 1.6 copy-done.12
  257.8 2.1 shard_map.77._dep
  259.9 19.4 %collective-permute-done.23.last_ref = bf16[512,512]{1,0:T(8,128)(2,1)S(1)} collective-permute-done((bf16[512,512]{1,0:T(8,128)(2,1)S(1)}, bf16[512,512]{1,0:T(8,128)(2,1)S(1)}, u32[]{:S(2)}, u32[]{:S(2)}) %collective-permute-start.23) | collective-permute-done | bytes 524320 | tf_op jit(solution)/shard_map/ppermute | solution.py:313
  279.4 1.2 copy-done.14
  280.6 1.3 shard_map.79
  (81 shorter events, 2.9 us)
Async XLA Ops:
  7.2 5.7 %copy-start = (bf16[1024,1024]{1,0:T(8,128)(2,1)S(1)}, bf16[1024,1024]{1,0:T(8,128)(2,1)}, u32[]{:S(2)}) copy-start(bf16[1024,1024]{1,0:T(8,128)(2,1)} %l0.11) | copy-start | bytes 6291460
  7.2 166.8 %all-gather.5.cloned.1.call-start = ((), (), s32[]{:S(2)}) async-start(), calls=%async_computation.1 | async-start | bytes 2621440 | tf_op jit(solution)/shard_map/all_gather | solution.py:343
  9.5 8.7 %copy-start.19 = (bf16[1024,512]{1,0:T(8,128)(2,1)}, bf16[1024,512]{1,0:T(8,128)(2,1)S(1)}, u32[]{:S(2)}) copy-start(bf16[1024,512]{1,0:T(8,128)(2,1)S(1)} %broadcast_select_fusion.p0) | copy-start | bytes 3145732
  9.5 25.0 %collective-permute-start = (bf16[1024,512]{1,0:T(8,128)(2,1)S(1)}, bf16[1024,512]{1,0:T(8,128)(2,1)S(1)}, u32[]{:S(2)}, u32[]{:S(2)}) collective-permute-start(bf16[1024,512]{1,0:T(8,128)(2,1)S(1)} %broadcast_select_fusion.p0), channel_id=1, source_target_pairs={{0,4},{1,5},{2,6},{3,7},{4,8},{5,9},{6,10},{7,11},{8,12},{9,13},{1... | collective-permute-start | bytes 3145736 | tf_op jit(solution)/shard_map/ppermute | solution.py:313
  12.8 27.3 %collective-permute-start.5 = (bf16[1024,1024]{1,0:T(8,128)(2,1)S(1)}, bf16[1024,1024]{1,0:T(8,128)(2,1)}, u32[]{:S(2)}, u32[]{:S(2)}) collective-permute-start(bf16[1024,1024]{1,0:T(8,128)(2,1)S(1)} %copy-done), channel_id=1, source_target_pairs={{4,0},{5,1},{8,4},{9,5},{10,6},{12,8},{13,9},{14,10},{15,11},{20,1... | collective-permute-start | bytes 6291464 | tf_op jit(solution)/shard_map/ppermute | solution.py:313
  14.9 25.3 %collective-permute-start.2 = (bf16[1024,1024]{1,0:T(8,128)(2,1)S(1)}, bf16[1024,1024]{1,0:T(8,128)(2,1)}, u32[]{:S(2)}, u32[]{:S(2)}) collective-permute-start(bf16[1024,1024]{1,0:T(8,128)(2,1)S(1)} %copy-done), channel_id=1, source_target_pairs={{0,2},{4,6},{5,7},{8,10},{9,11},{10,8},{12,14},{13,15},{14,12},{15... | collective-permute-start | bytes 6291464 | tf_op jit(solution)/shard_map/ppermute | solution.py:313
  34.6 1.0 copy-start.15
  35.5 4.7 %collective-permute-start.1 = (bf16[1024,1024]{1,0:T(8,128)(2,1)}, bf16[1024,1024]{1,0:T(8,128)(2,1)}, u32[]{:S(2)}, u32[]{:S(2)}) collective-permute-start(bf16[1024,1024]{1,0:T(8,128)(2,1)} %shard_map.67), channel_id=1, source_target_pairs={{0,1},{4,5},{5,4},{8,9},{9,8},{10,11},{12,13},{13,12},{14,15},{15,... | collective-permute-start | bytes 6291464 | tf_op jit(solution)/shard_map/ppermute | solution.py:313
  37.6 2.6 collective-permute-start.4
  40.2 1.0 copy-start.17
  41.2 8.0 %copy-start.16 = (bf16[1024,512]{1,0:T(8,128)(2,1)S(1)}, bf16[1024,512]{1,0:T(8,128)(2,1)}, u32[]{:S(2)}) copy-start(bf16[1024,512]{1,0:T(8,128)(2,1)} %copy-done.15) | copy-start | bytes 3145732
  41.2 132.8 %all-gather.3.cloned.1.call-start = ((), (), s32[]{:S(2)}) async-start(), calls=%async_computation | async-start | bytes 5242880 | tf_op jit(solution)/shard_map/all_gather | solution.py:383
  41.2 6.4 %copy-start.18 = (bf16[1024,512]{1,0:T(8,128)(2,1)S(1)}, bf16[1024,512]{1,0:T(8,128)(2,1)}, u32[]{:S(2)}) copy-start(bf16[1024,512]{1,0:T(8,128)(2,1)} %get-tuple-element.19.p2) | copy-start | bytes 3145732
  41.3 8.0 %collective-permute-start.3 = (bf16[1024,1024]{1,0:T(8,128)(2,1)}, bf16[1024,1024]{1,0:T(8,128)(2,1)S(1)}, u32[]{:S(2)}, u32[]{:S(2)}) collective-permute-start(bf16[1024,1024]{1,0:T(8,128)(2,1)} %collective-permute-done.2.refs_3_.l2), channel_id=1, source_target_pairs={{2,3},{6,7},{7,6},{8,9},{10,11},{11,10},{12,13},{13,12},{14,15},{1... | collective-permute-start | bytes 6291464 | tf_op jit(solution)/shard_map/ppermute | solution.py:313
  42.7 11.1 %collective-permute-start.7 = (bf16[1024,1024]{1,0:T(8,128)(2,1)}, bf16[1024,1024]{1,0:T(8,128)(2,1)S(1)}, u32[]{:S(2)}, u32[]{:S(2)}) collective-permute-start(bf16[1024,1024]{1,0:T(8,128)(2,1)} %collective-permute-done.5.refs_2_.refs_0_._in0), channel_id=1, source_target_pairs={{5,7},{10,8},{21,23},{26,24}} | collective-permute-start | bytes 6291464 | tf_op jit(solution)/shard_map/ppermute | solution.py:313
  43.5 10.3 %collective-permute-start.8 = (bf16[1024,1024]{1,0:T(8,128)(2,1)}, bf16[1024,1024]{1,0:T(8,128)(2,1)}, u32[]{:S(2)}, u32[]{:S(2)}) collective-permute-start(bf16[1024,1024]{1,0:T(8,128)(2,1)} %collective-permute-done.2.refs_3_.l2), channel_id=1, source_target_pairs={{14,2},{30,18}} | collective-permute-start | bytes 6291464 | tf_op jit(solution)/shard_map/ppermute | solution.py:313
  46.9 6.9 %collective-permute-start.9 = (bf16[512,1024]{1,0:T(8,128)(2,1)S(1)}, bf16[512,1024]{1,0:T(8,128)(2,1)S(1)}, u32[]{:S(2)}, u32[]{:S(2)}) collective-permute-start(bf16[512,1024]{1,0:T(8,128)(2,1)S(1)} %slice.4), channel_id=1, source_target_pairs={{4,0},{5,1},{6,2},{8,4},{9,5},{10,6},{11,7},{20,16},{21,17},{22,18... | collective-permute-start | bytes 3145736 | tf_op jit(solution)/shard_map/ppermute | solution.py:313
  47.6 6.2 %collective-permute-start.6 = (bf16[1024,512]{1,0:T(8,128)(2,1)S(1)}, bf16[1024,512]{1,0:T(8,128)(2,1)S(1)}, u32[]{:S(2)}, u32[]{:S(2)}) collective-permute-start(bf16[1024,512]{1,0:T(8,128)(2,1)S(1)} %copy-done.18), channel_id=1, source_target_pairs={{8,12},{9,13},{10,14},{11,15},{24,28},{25,29},{26,30},{27,31}} | collective-permute-start | bytes 3145736 | tf_op jit(solution)/shard_map/ppermute | solution.py:313
  49.2 1.2 copy-start.20
  50.4 3.4 %copy-start.1 = (bf16[1024,1024]{1,0:T(8,128)(2,1)}, bf16[1024,1024]{1,0:T(8,128)(2,1)S(1)}, u32[]{:S(2)}) copy-start(bf16[1024,1024]{1,0:T(8,128)(2,1)S(1)} %collective-permute-done.3.l3) | copy-start | bytes 6291460
  52.5 1.3 copy-start.9
  53.8 3.6 %copy-start.5 = (bf16[512,1024]{1,0:T(8,128)(2,1)}, bf16[512,1024]{1,0:T(8,128)(2,1)S(1)}, u32[]{:S(2)}) copy-start(bf16[512,1024]{1,0:T(8,128)(2,1)S(1)} %collective-permute-done.9.refs_3_._in1) | copy-start | bytes 3145732
  53.8 1.4 copy-start.30
  57.4 1.0 copy-start.25
  58.4 1.0 copy-start.29
  59.4 11.8 %collective-permute-start.10 = (bf16[512,1024]{1,0:T(8,128)(2,1)}, bf16[512,1024]{1,0:T(8,128)(2,1)S(1)}, u32[]{:S(2)}, u32[]{:S(2)}) collective-permute-start(bf16[512,1024]{1,0:T(8,128)(2,1)} %copy-done.29), channel_id=1, source_target_pairs={{4,0},{5,1},{6,2},{8,4},{9,5},{10,6},{11,7},{12,8},{13,9},{14,10},... | collective-permute-start | bytes 3145736 | tf_op jit(solution)/shard_map/ppermute | solution.py:313
  60.1 1.2 copy-start.6
  61.4 5.8 %copy-start.31 = (bf16[1024,1024]{1,0:T(8,128)(2,1)S(1)}, bf16[1024,1024]{1,0:T(8,128)(2,1)}, u32[]{:S(2)}) copy-start(bf16[1024,1024]{1,0:T(8,128)(2,1)} %copy-done.30) | copy-start | bytes 6291460
  64.5 1.3 copy-start.21
  65.8 102.5 %collective-permute-start.11 = (bf16[1024,1024]{1,0:T(8,128)(2,1)}, bf16[1024,1024]{1,0:T(8,128)(2,1)S(1)}, u32[]{:S(2)}, u32[]{:S(2)}) collective-permute-start(bf16[1024,1024]{1,0:T(8,128)(2,1)} %get-tuple-element.24.x3), channel_id=1, source_target_pairs={{2,3},{18,19}} | collective-permute-start | bytes 6291464 | tf_op jit(solution)/shard_map/ppermute | solution.py:313
  67.1 101.2 %collective-permute-start.12 = (bf16[1024,1024]{1,0:T(8,128)(2,1)S(1)}, bf16[1024,1024]{1,0:T(8,128)(2,1)S(1)}, u32[]{:S(2)}, u32[]{:S(2)}) collective-permute-start(bf16[1024,1024]{1,0:T(8,128)(2,1)S(1)} %copy-done.31), channel_id=1, source_target_pairs={{7,6},{8,9},{23,22},{24,25}} | collective-permute-start | bytes 6291464 | tf_op jit(solution)/shard_map/ppermute | solution.py:313
  67.9 100.4 %collective-permute-start.13 = (bf16[1024,1024]{1,0:T(8,128)(2,1)}, bf16[1024,1024]{1,0:T(8,128)(2,1)S(1)}, u32[]{:S(2)}, u32[]{:S(2)}) collective-permute-start(bf16[1024,1024]{1,0:T(8,128)(2,1)} %get-tuple-element.25.h1), channel_id=1, source_target_pairs={{0,1},{5,4},{10,11},{16,17},{21,20},{26,27}} | collective-permute-start | bytes 6291464 | tf_op jit(solution)/shard_map/ppermute | solution.py:313
  68.7 102.9 %copy-start.2 = (bf16[1024,1024]{1,0:T(8,128)(2,1)S(1)}, bf16[1024,1024]{1,0:T(8,128)(2,1)}, u32[]{:S(2)}) copy-start(bf16[1024,1024]{1,0:T(8,128)(2,1)} %copy-done.1) | copy-start | bytes 6291460
  68.8 97.5 %collective-permute-start.14 = (bf16[512,1024]{1,0:T(8,128)(2,1)S(1)}, bf16[512,1024]{1,0:T(8,128)(2,1)S(1)}, u32[]{:S(2)}, u32[]{:S(2)}) collective-permute-start(bf16[512,1024]{1,0:T(8,128)(2,1)S(1)} %get-tuple-element.26), channel_id=1, source_target_pairs={{4,0},{5,1},{6,2},{7,3},{20,16},{21,17},{22,18},{23,19}} | collective-permute-start | bytes 3145736 | tf_op jit(solution)/shard_map/ppermute | solution.py:313
  72.3 126.2 %collective-permute-start.19 = (bf16[1024,1024]{1,0:T(8,128)(2,1)}, bf16[1024,1024]{1,0:T(8,128)(2,1)}, u32[]{:S(2)}, u32[]{:S(2)}) collective-permute-start(bf16[1024,1024]{1,0:T(8,128)(2,1)} %constant_dynamic-update-slice_fusion.h2), channel_id=1, source_target_pairs={{0,2},{5,7},{16,18},{21,23}} | collective-permute-start | bytes 6291464 | tf_op jit(solution)/shard_map/ppermute | solution.py:313
  166.3 6.4 %copy-start.7 = (bf16[512,1024]{1,0:T(8,128)(2,1)}, bf16[512,1024]{1,0:T(8,128)(2,1)S(1)}, u32[]{:S(2)}) copy-start(bf16[512,1024]{1,0:T(8,128)(2,1)S(1)} %collective-permute-done.14.refs_3_.refs_4_) | copy-start | bytes 3145732
  166.3 32.2 %collective-permute-start.18 = (bf16[1024,1024]{1,0:T(8,128)(2,1)}, bf16[1024,1024]{1,0:T(8,128)(2,1)}, u32[]{:S(2)}, u32[]{:S(2)}) collective-permute-start(bf16[1024,1024]{1,0:T(8,128)(2,1)} %constant_dynamic-update-slice_fusion.h2), channel_id=1, source_target_pairs={{0,1},{5,4},{16,17},{21,20}} | collective-permute-start | bytes 6291464 | tf_op jit(solution)/shard_map/ppermute | solution.py:313
  168.3 1.3 copy-start.33
  168.3 2.0 copy-start.32
  170.3 1.4 copy-start.10
  172.6 25.8 %collective-permute-start.15 = (bf16[512,1024]{1,0:T(8,128)(2,1)}, bf16[512,1024]{1,0:T(8,128)(2,1)}, u32[]{:S(2)}, u32[]{:S(2)}) collective-permute-start(bf16[512,1024]{1,0:T(8,128)(2,1)} %shard_map.72._dep), channel_id=1, source_target_pairs={{4,0},{5,1},{6,2},{7,3},{8,4},{9,5},{10,6},{11,7},{12,8},{13,9},{1... | collective-permute-start | bytes 3145736 | tf_op jit(solution)/shard_map/ppermute | solution.py:313
  174.0 2.2 copy-start.13
  176.2 1.6 copy-start.23
  177.8 1.0 copy-start.24
  178.8 42.0 %copy-start.8 = (bf16[512,1024]{1,0:T(8,128)(2,1)S(1)}, bf16[512,1024]{1,0:T(8,128)(2,1)}, u32[]{:S(2)}) copy-start(bf16[512,1024]{1,0:T(8,128)(2,1)} %copy-done.7) | copy-start | bytes 3145732
  183.6 1.0 copy-start.26
  184.6 25.0 %collective-permute-start.17 = (bf16[512,512]{1,0:T(8,128)(2,1)S(1)}, bf16[512,512]{1,0:T(8,128)(2,1)S(1)}, u32[]{:S(2)}, u32[]{:S(2)}) collective-permute-start(bf16[512,512]{1,0:T(8,128)(2,1)S(1)} %get-tuple-element.28), channel_id=1, source_target_pairs={{0,4},{1,5},{2,6},{3,7},{4,0},{5,1},{6,2},{7,3},{8,12},{9,13},{10,... | collective-permute-start | bytes 1572872 | tf_op jit(solution)/shard_map/ppermute | solution.py:313
  186.7 34.1 %collective-permute-start.16 = (bf16[512,512]{1,0:T(8,128)(2,1)S(1)}, bf16[512,512]{1,0:T(8,128)(2,1)S(1)}, u32[]{:S(2)}, u32[]{:S(2)}) collective-permute-start(bf16[512,512]{1,0:T(8,128)(2,1)S(1)} %get-tuple-element.27._dep), channel_id=1, source_target_pairs={{0,4},{1,5},{2,6},{3,7},{4,0},{5,1},{6,2},{7,3},{8,12},{9,13},{10,... | collective-permute-start | bytes 1572872 | tf_op jit(solution)/shard_map/ppermute | solution.py:313
  223.4 11.7 %copy-start.3 = (bf16[1024,1024]{1,0:T(8,128)(2,1)S(1)}, bf16[1024,1024]{1,0:T(8,128)(2,1)}, u32[]{:S(2)}) copy-start(bf16[1024,1024]{1,0:T(8,128)(2,1)} %copy-done.1) | copy-start | bytes 6291460
  223.5 14.0 %collective-permute-start.20 = (bf16[1024,1024]{1,0:T(8,128)(2,1)S(1)}, bf16[1024,1024]{1,0:T(8,128)(2,1)S(1)}, u32[]{:S(2)}, u32[]{:S(2)}) collective-permute-start(bf16[1024,1024]{1,0:T(8,128)(2,1)S(1)} %constant_dynamic-update-slice_fusion.2.h3), channel_id=1, source_target_pairs={{0,1},{16,17}} | collective-permute-start | bytes 6291464 | tf_op jit(solution)/shard_map/ppermute | solution.py:313
  224.4 13.0 %collective-permute-start.21 = (bf16[1024,1024]{1,0:T(8,128)(2,1)}, bf16[1024,1024]{1,0:T(8,128)(2,1)}, u32[]{:S(2)}, u32[]{:S(2)}) collective-permute-start(bf16[1024,1024]{1,0:T(8,128)(2,1)} %get-tuple-element.30.x2), channel_id=1, source_target_pairs={{2,3},{7,6},{18,19},{23,22}} | collective-permute-start | bytes 6291464 | tf_op jit(solution)/shard_map/ppermute | solution.py:313
  225.7 30.5 %collective-permute-start.22 = (bf16[512,1024]{1,0:T(8,128)(2,1)S(1)}, bf16[512,1024]{1,0:T(8,128)(2,1)S(1)}, u32[]{:S(2)}, u32[]{:S(2)}) collective-permute-start(bf16[512,1024]{1,0:T(8,128)(2,1)S(1)} %get-tuple-element.32._dep), channel_id=1, source_target_pairs={{4,0},{5,1},{6,2},{7,3},{8,4},{9,5},{10,6},{11,7},{12,8},{13,9},{1... | collective-permute-start | bytes 3145736 | tf_op jit(solution)/shard_map/ppermute | solution.py:313
  227.1 10.3 %copy-start.11 = (bf16[1024,1024]{1,0:T(8,128)(2,1)S(1)}, bf16[1024,1024]{1,0:T(8,128)(2,1)}, u32[]{:S(2)}) copy-start(bf16[1024,1024]{1,0:T(8,128)(2,1)} %copy-done.10) | copy-start | bytes 6291460
  227.1 52.3 %collective-permute-start.23 = (bf16[512,512]{1,0:T(8,128)(2,1)S(1)}, bf16[512,512]{1,0:T(8,128)(2,1)S(1)}, u32[]{:S(2)}, u32[]{:S(2)}) collective-permute-start(bf16[512,512]{1,0:T(8,128)(2,1)S(1)} %shard_map.78), channel_id=1, source_target_pairs={{0,8},{1,9},{2,10},{3,11},{4,12},{5,13},{6,14},{7,15},{8,0},{9,1},... | collective-permute-start | bytes 1572872 | tf_op jit(solution)/shard_map/ppermute | solution.py:313
  235.4 2.0 copy-start.4
  237.4 18.8 %copy-start.22 = (f32[512,1024]{1,0:T(8,128)S(1)}, f32[512,1024]{1,0:T(8,128)}, u32[]{:S(2)}) copy-start(f32[512,1024]{1,0:T(8,128)} %copy-done.21) | copy-start | bytes 6291460
  237.4 18.8 %copy-start.28 = (s32[8]{0:T(128)S(1)}, s32[8]{0:T(128)}, u32[]{:S(2)}) copy-start(s32[8]{0:T(128)} %structure.1) | copy-start | bytes 100
  256.2 1.6 copy-start.12
  257.8 21.6 %copy-start.27 = (f32[512,512]{1,0:T(8,128)S(1)}, f32[512,512]{1,0:T(8,128)}, u32[]{:S(2)}) copy-start(f32[512,512]{1,0:T(8,128)} %copy-done.26) | copy-start | bytes 3145732
  279.4 1.2 copy-start.14
Sparse Core Ops, SparseCore 0:
  41.3 49.7 all-gather.4
  93.3 71.1 all-gather.2

commit v10 on v9

--- a/solution.py
+++ b/solution.py
@@ -368,7 +368,7 @@
             *panels[:3],
         )
         t, t_t, sent = local_call(
-            functools.partial(product_end_kernel, deps=4, gated=0),
+            functools.partial(product_end_kernel, deps=2, gated=0),
             [ANY] * 4 + [VMEM] * 2,
             [shape((h, w), BF16), t_block, t_block],
             [pltpu.VMEM((h, h), BF16), dma, dma],
@@ -377,8 +377,6 @@
             panel_3,
             below_1,
             across_1,
-            across_3,
-            below_2a,
         )
         t_row = lax.all_gather(t, "col", axis=1, tiled=True)
         step = lambda x: move(x, lambda r, c: (r - 1, c))

time: 290 us -> 316 us (1.090)
  the two profiles are of different devices: /device:TPU:3 before, /device:TPU:7 now
where the time goes in v10:
time: 316 us; the launch traced here: 315 us
  waiting for transfers between devices  201 us (64%)
  starting transfers between devices  37.7 us (12%)
  local copies, waits for them, and re-layouts  32.3 us (10%)
  Pallas kernels  26.8 us (8%)
  between operations  14.5 us (5%)
    ppermute x24, waiting for transfers between devices, move(): return lax.ppermute(x, AXES, pairs)  201 us
    ppermute x24, starting transfers between devices, move(): return lax.ppermute(x, AXES, pairs)  37.6 us
    unnamed x72, local copies, waits for them, and re-layouts  28.6 us
    pallas_call x11, Pallas kernels, local_call(): pl.pallas_call(kernel, out_shape=outs, in_specs=in_specs + [ANY] * (len(a...  26.8 us
  transfers between devices with their start and end apart: 26, of which 8 were waited for; matrix products, arithmetic and copies ran while one was open for 2% of the time, Pallas kernels for 8%

profile of v10, /device:TPU:7, one launch (start us, length us, event | category | flops | bytes accessed | tf_op | source)
XLA Modules:
  0.0 314.7 jit_solution(7404175762464185983)
XLA Ops:
  7.2 0.8 broadcast_compare_fusion
  8.1 1.4 broadcast_select_fusion.p0
  9.5 3.3 %collective-permute-start = (bf16[1024,512]{1,0:T(8,128)(2,1)S(1)}, bf16[1024,512]{1,0:T(8,128)(2,1)S(1)}, u32[]{:S(2)}, u32[]{:S(2)}) collective-permute-start(bf16[1024,512]{1,0:T(8,128)(2,1)S(1)} %broadcast_select_fusion.p0), channel_id=1, source_target_pairs={{0,4},{1,5},{2,6},{3,7},{4,8},{5,9},{6,10},{7,11},{8,12},{9,13},{1... | collective-permute-start | bytes 3145736 | tf_op jit(solution)/shard_map/ppermute | solution.py:313
  12.8 2.0 collective-permute-start.5
  14.9 2.0 collective-permute-start.2
  16.9 1.3 copy.15.refs_0_
  18.2 16.3 %collective-permute-done.refs_1_.p1 = bf16[1024,512]{1,0:T(8,128)(2,1)S(1)} collective-permute-done((bf16[1024,512]{1,0:T(8,128)(2,1)S(1)}, bf16[1024,512]{1,0:T(8,128)(2,1)S(1)}, u32[]{:S(2)}, u32[]{:S(2)}) %collective-permute-start) | collective-permute-done | bytes 1048608 | tf_op jit(solution)/shard_map/ppermute | solution.py:313
  34.6 1.0 copy-done.14
  35.5 2.0 collective-permute-start.1
  38.3 1.9 copy.17.refs_1_
  40.2 1.0 copy-done.16
  41.2 1.3 collective-permute-start.3
  42.5 0.8 collective-permute-start.7
  43.3 0.7 collective-permute-start.6
  44.1 5.0 %collective-permute-done.3.l3 = bf16[1024,1024]{1,0:T(8,128)(2,1)S(1)} collective-permute-done((bf16[1024,1024]{1,0:T(8,128)(2,1)}, bf16[1024,1024]{1,0:T(8,128)(2,1)S(1)}, u32[]{:S(2)}, u32[]{:S(2)}) %collective-permute-start.3) | collective-permute-done | bytes 2097184 | tf_op jit(solution)/shard_map/ppermute | solution.py:313
  49.1 1.2 copy-done.17
  50.3 1.2 copy-done.19
  51.5 2.0 shard_map.69.acc_ref
  53.6 1.3 copy-done.7
  54.9 1.4 copy-done.30
  56.3 2.2 shard_map.70
  58.5 1.0 copy-done.24
  59.5 1.0 copy-done.28
  60.5 0.9 collective-permute-start.10
  61.4 1.3 slice.4
  62.7 0.7 collective-permute-start.9
  64.2 3.2 %shard_map.71 = (f32[512,1024]{1,0:T(8,128)S(1)}, bf16[1024,1024]{1,0:T(8,128)(2,1)}, bf16[512,1024]{1,0:T(8,128)(2,1)S(1)}, bf16[1024,1024]{1,0:T(8,128)(2,1)S(1)}) custom-call(bf16[1024,1024]{1,0:T(8,128)(2,1)S(1)} %copy-done, bf16[1024,1024]{1,0:T(8,128)(2,1)} %collective-permute-done.1.refs_4_.l1, ...), custom_call_target="tpu_custom_call", output_to_operand_aliasing={{1}: (5, {}), {2}: (6, {}), {3}: (7, {})} | custom-call | flops 1 | bytes 1 | tf_op jit(solution)/shard_map/pallas_call | solution.py:279
  67.4 1.3 copy-done.20
  68.7 1.3 collective-permute-start.11
  70.0 0.8 collective-permute-start.12
  70.8 0.8 collective-permute-start.13
  71.6 1.4 collective-permute-start.14
  73.0 1.0 constant_dynamic-update-slice_fusion.1
  74.1 1.1 constant_dynamic-update-slice_fusion.h2
  75.1 2.1 collective-permute-start.19
  77.2 115.0 %collective-permute-done.14.refs_3_.refs_4_ = bf16[512,1024]{1,0:T(8,128)(2,1)S(1)} collective-permute-done((bf16[512,1024]{1,0:T(8,128)(2,1)S(1)}, bf16[512,1024]{1,0:T(8,128)(2,1)S(1)}, u32[]{:S(2)}, u32[]{:S(2)}) %collective-permute-start.14) | collective-permute-done | bytes 1048608 | tf_op jit(solution)/shard_map/ppermute | solution.py:313
  192.2 2.0 collective-permute-start.18
  194.3 1.3 copy-done.33
  196.3 1.3 copy-done.8
  197.6 1.0 shard_map.72._dep
  198.6 1.3 collective-permute-start.15
  200.0 2.2 copy-done.12
  202.2 1.6 copy-done.22
  203.8 1.0 copy-done.23
  204.8 4.8 %shard_map.73 = (bf16[512,512]{1,0:T(8,128)(2,1)S(1)}, bf16[512,512]{1,0:T(8,128)(2,1)S(1)}, f32[512,512]{1,0:T(8,128)S(1)}, f32[512,512]{1,0:T(8,128)S(1)}) custom-call(bf16[512,1024]{1,0:T(8,128)(2,1)S(1)} %get-tuple-element.20.tt_ref, bf16[1024,2048]{1,0:T(8,128)(2,1)S(1)} %copy-done.12, bf16[512,512]{1,0:T(8,128)(2,1)S(1)} %copy-done.23, ...), custom_call_target="tpu_custom_call" | custom-call | flops 1 | bytes 1 | tf_op jit(solution)/shard_map/pallas_call | solution.py:279
  209.6 1.0 copy-done.25
  210.6 2.1 collective-permute-start.17
  212.7 12.7 %collective-permute-done.15.came_ref = bf16[512,1024]{1,0:T(8,128)(2,1)} collective-permute-done((bf16[512,1024]{1,0:T(8,128)(2,1)}, bf16[512,1024]{1,0:T(8,128)(2,1)}, u32[]{:S(2)}, u32[]{:S(2)}) %collective-permute-start.15) | collective-permute-done | bytes 1048608 | tf_op jit(solution)/shard_map/ppermute | solution.py:313
  225.4 11.1 %collective-permute-done.17.refs_1_.near_ref = bf16[512,512]{1,0:T(8,128)(2,1)S(1)} collective-permute-done((bf16[512,512]{1,0:T(8,128)(2,1)S(1)}, bf16[512,512]{1,0:T(8,128)(2,1)S(1)}, u32[]{:S(2)}, u32[]{:S(2)}) %collective-permute-start.17) | collective-permute-done | bytes 524320 | tf_op jit(solution)/shard_map/ppermute | solution.py:313
  236.5 11.2 %collective-permute-done.16.refs_0_.far_ref = bf16[512,512]{1,0:T(8,128)(2,1)S(1)} collective-permute-done((bf16[512,512]{1,0:T(8,128)(2,1)S(1)}, bf16[512,512]{1,0:T(8,128)(2,1)S(1)}, u32[]{:S(2)}, u32[]{:S(2)}) %collective-permute-start.16) | collective-permute-done | bytes 524320 | tf_op jit(solution)/shard_map/ppermute | solution.py:313
  247.8 1.2 shard_map.75
  249.1 1.3 constant_dynamic-update-slice_fusion.2.h3
  250.4 0.9 collective-permute-start.20
  251.4 1.3 collective-permute-start.21
  252.7 1.3 collective-permute-start.22
  254.1 7.0 %collective-permute-start.23 = (bf16[512,512]{1,0:T(8,128)(2,1)S(1)}, bf16[512,512]{1,0:T(8,128)(2,1)S(1)}, u32[]{:S(2)}, u32[]{:S(2)}) collective-permute-start(bf16[512,512]{1,0:T(8,128)(2,1)S(1)} %shard_map.78), channel_id=1, source_target_pairs={{0,8},{1,9},{2,10},{3,11},{4,12},{5,13},{6,14},{7,15},{8,0},{9,1},... | collective-permute-start | bytes 1572872 | tf_op jit(solution)/shard_map/ppermute | solution.py:313
  261.4 2.0 copy-done.4
  263.4 8.6 %shard_map.76._dep = bf16[1024,1024]{1,0:T(8,128)(2,1)} custom-call(f32[1024,1024]{1,0:T(8,128)} %copy-done.4, bf16[1024,1024]{1,0:T(8,128)(2,1)} %get-tuple-element.25.h1, bf16[1024,1024]{1,0:T(8,128)(2,1)} %constant_dynamic-update-slice_fusion.h2, bf16[1024,1024]{1,0:T(8,128)(2,1)S(1)} %constant_dynamic-update-slice_fusion.2.h3, ...), custom_call_target="tpu_custom_call" | custom-call | flops 1 | bytes 1 | tf_op jit(solution)/shard_map/pallas_call | solution.py:279
  271.9 10.3 %collective-permute-done.22.came_ref = bf16[512,1024]{1,0:T(8,128)(2,1)S(1)} collective-permute-done((bf16[512,1024]{1,0:T(8,128)(2,1)S(1)}, bf16[512,1024]{1,0:T(8,128)(2,1)S(1)}, u32[]{:S(2)}, u32[]{:S(2)}) %collective-permute-start.22) | collective-permute-done | bytes 1048608 | tf_op jit(solution)/shard_map/ppermute | solution.py:313
  282.3 1.6 copy-done.10
  283.9 2.1 shard_map.77._dep
  286.0 19.3 %collective-permute-done.23.last_ref = bf16[512,512]{1,0:T(8,128)(2,1)S(1)} collective-permute-done((bf16[512,512]{1,0:T(8,128)(2,1)S(1)}, bf16[512,512]{1,0:T(8,128)(2,1)S(1)}, u32[]{:S(2)}, u32[]{:S(2)}) %collective-permute-start.23) | collective-permute-done | bytes 524320 | tf_op jit(solution)/shard_map/ppermute | solution.py:313
  305.3 1.2 copy-done.13
  306.6 1.3 shard_map.79
  (81 shorter events, 3.0 us)
Async XLA Ops:
  7.2 5.7 %copy-start = (bf16[1024,1024]{1,0:T(8,128)(2,1)S(1)}, bf16[1024,1024]{1,0:T(8,128)(2,1)}, u32[]{:S(2)}) copy-start(bf16[1024,1024]{1,0:T(8,128)(2,1)} %l0.11) | copy-start | bytes 6291460
  7.2 192.8 %all-gather.5.cloned.1.call-start = ((), (), s32[]{:S(2)}) async-start(), calls=%async_computation.1 | async-start | bytes 2621440 | tf_op jit(solution)/shard_map/all_gather | solution.py:343
  9.5 8.7 %copy-start.18 = (bf16[1024,512]{1,0:T(8,128)(2,1)}, bf16[1024,512]{1,0:T(8,128)(2,1)S(1)}, u32[]{:S(2)}) copy-start(bf16[1024,512]{1,0:T(8,128)(2,1)S(1)} %broadcast_select_fusion.p0) | copy-start | bytes 3145732
  9.5 25.0 %collective-permute-start = (bf16[1024,512]{1,0:T(8,128)(2,1)S(1)}, bf16[1024,512]{1,0:T(8,128)(2,1)S(1)}, u32[]{:S(2)}, u32[]{:S(2)}) collective-permute-start(bf16[1024,512]{1,0:T(8,128)(2,1)S(1)} %broadcast_select_fusion.p0), channel_id=1, source_target_pairs={{0,4},{1,5},{2,6},{3,7},{4,8},{5,9},{6,10},{7,11},{8,12},{9,13},{1... | collective-permute-start | bytes 3145736 | tf_op jit(solution)/shard_map/ppermute | solution.py:313
  12.8 27.3 %collective-permute-start.5 = (bf16[1024,1024]{1,0:T(8,128)(2,1)S(1)}, bf16[1024,1024]{1,0:T(8,128)(2,1)}, u32[]{:S(2)}, u32[]{:S(2)}) collective-permute-start(bf16[1024,1024]{1,0:T(8,128)(2,1)S(1)} %copy-done), channel_id=1, source_target_pairs={{4,0},{5,1},{8,4},{9,5},{10,6},{12,8},{13,9},{14,10},{15,11},{20,1... | collective-permute-start | bytes 6291464 | tf_op jit(solution)/shard_map/ppermute | solution.py:313
  14.9 25.3 %collective-permute-start.2 = (bf16[1024,1024]{1,0:T(8,128)(2,1)S(1)}, bf16[1024,1024]{1,0:T(8,128)(2,1)}, u32[]{:S(2)}, u32[]{:S(2)}) collective-permute-start(bf16[1024,1024]{1,0:T(8,128)(2,1)S(1)} %copy-done), channel_id=1, source_target_pairs={{0,2},{4,6},{5,7},{8,10},{9,11},{10,8},{12,14},{13,15},{14,12},{15... | collective-permute-start | bytes 6291464 | tf_op jit(solution)/shard_map/ppermute | solution.py:313
  34.6 1.0 copy-start.14
  35.5 5.6 %collective-permute-start.1 = (bf16[1024,1024]{1,0:T(8,128)(2,1)}, bf16[1024,1024]{1,0:T(8,128)(2,1)}, u32[]{:S(2)}, u32[]{:S(2)}) collective-permute-start(bf16[1024,1024]{1,0:T(8,128)(2,1)} %shard_map.67), channel_id=1, source_target_pairs={{0,1},{4,5},{5,4},{8,9},{9,8},{10,11},{12,13},{13,12},{14,15},{15,... | collective-permute-start | bytes 6291464 | tf_op jit(solution)/shard_map/ppermute | solution.py:313
  37.6 2.6 collective-permute-start.4
  40.2 8.9 %copy-start.15 = (bf16[1024,512]{1,0:T(8,128)(2,1)S(1)}, bf16[1024,512]{1,0:T(8,128)(2,1)}, u32[]{:S(2)}) copy-start(bf16[1024,512]{1,0:T(8,128)(2,1)} %copy-done.14) | copy-start | bytes 3145732
  40.2 1.0 copy-start.16
  41.2 158.8 %all-gather.3.cloned.1.call-start = ((), (), s32[]{:S(2)}) async-start(), calls=%async_computation | async-start | bytes 5242880 | tf_op jit(solution)/shard_map/all_gather | solution.py:381
  41.2 7.9 %collective-permute-start.3 = (bf16[1024,1024]{1,0:T(8,128)(2,1)}, bf16[1024,1024]{1,0:T(8,128)(2,1)S(1)}, u32[]{:S(2)}, u32[]{:S(2)}) collective-permute-start(bf16[1024,1024]{1,0:T(8,128)(2,1)} %collective-permute-done.2.refs_3_.l2), channel_id=1, source_target_pairs={{2,3},{6,7},{7,6},{8,9},{10,11},{11,10},{12,13},{13,12},{14,15},{1... | collective-permute-start | bytes 6291464 | tf_op jit(solution)/shard_map/ppermute | solution.py:313
  42.5 12.4 %collective-permute-start.7 = (bf16[1024,1024]{1,0:T(8,128)(2,1)}, bf16[1024,1024]{1,0:T(8,128)(2,1)S(1)}, u32[]{:S(2)}, u32[]{:S(2)}) collective-permute-start(bf16[1024,1024]{1,0:T(8,128)(2,1)} %collective-permute-done.5.refs_2_.refs_0_._in0), channel_id=1, source_target_pairs={{5,7},{10,8},{21,23},{26,24}} | collective-permute-start | bytes 6291464 | tf_op jit(solution)/shard_map/ppermute | solution.py:313
  43.3 11.6 %collective-permute-start.6 = (bf16[1024,512]{1,0:T(8,128)(2,1)}, bf16[1024,512]{1,0:T(8,128)(2,1)S(1)}, u32[]{:S(2)}, u32[]{:S(2)}) collective-permute-start(bf16[1024,512]{1,0:T(8,128)(2,1)} %get-tuple-element.19.p2), channel_id=1, source_target_pairs={{8,12},{9,13},{10,14},{11,15},{24,28},{25,29},{26,30},{27,31}} | collective-permute-start | bytes 3145736 | tf_op jit(solution)/shard_map/ppermute | solution.py:313
  49.1 1.2 copy-start.17
  50.3 1.2 copy-start.19
  51.5 3.4 %copy-start.1 = (bf16[1024,1024]{1,0:T(8,128)(2,1)}, bf16[1024,1024]{1,0:T(8,128)(2,1)S(1)}, u32[]{:S(2)}) copy-start(bf16[1024,1024]{1,0:T(8,128)(2,1)S(1)} %collective-permute-done.3.l3) | copy-start | bytes 6291460
  53.6 1.3 copy-start.7
  54.9 1.4 copy-start.30
  58.5 1.0 copy-start.24
  59.4 1.0 copy-start.28
  60.4 3.0 copy-start.29
  60.5 3.7 %collective-permute-start.10 = (bf16[1024,1024]{1,0:T(8,128)(2,1)}, bf16[1024,1024]{1,0:T(8,128)(2,1)S(1)}, u32[]{:S(2)}, u32[]{:S(2)}) collective-permute-start(bf16[1024,1024]{1,0:T(8,128)(2,1)} %collective-permute-done.2.refs_3_.l2), channel_id=1, source_target_pairs={{14,2},{30,18}} | collective-permute-start | bytes 6291464 | tf_op jit(solution)/shard_map/ppermute | solution.py:313
  62.7 1.5 collective-permute-start.9
  63.4 10.7 %collective-permute-start.8 = (bf16[512,1024]{1,0:T(8,128)(2,1)S(1)}, bf16[512,1024]{1,0:T(8,128)(2,1)S(1)}, u32[]{:S(2)}, u32[]{:S(2)}) collective-permute-start(bf16[512,1024]{1,0:T(8,128)(2,1)S(1)} %copy-done.29), channel_id=1, source_target_pairs={{4,0},{5,1},{6,2},{8,4},{9,5},{10,6},{11,7},{12,8},{13,9},{14,10},... | collective-permute-start | bytes 3145736 | tf_op jit(solution)/shard_map/ppermute | solution.py:313
  64.2 5.8 %copy-start.31 = (bf16[1024,1024]{1,0:T(8,128)(2,1)S(1)}, bf16[1024,1024]{1,0:T(8,128)(2,1)}, u32[]{:S(2)}) copy-start(bf16[1024,1024]{1,0:T(8,128)(2,1)} %copy-done.30) | copy-start | bytes 6291460
  67.4 1.3 copy-start.20
  68.7 6.5 %copy-start.11 = (bf16[1024,1024]{1,0:T(8,128)(2,1)}, bf16[1024,1024]{1,0:T(8,128)(2,1)S(1)}, u32[]{:S(2)}) copy-start(bf16[1024,1024]{1,0:T(8,128)(2,1)S(1)} %get-tuple-element.24.x3) | copy-start | bytes 6291460
  68.7 125.6 %collective-permute-start.11 = (bf16[1024,1024]{1,0:T(8,128)(2,1)S(1)}, bf16[1024,1024]{1,0:T(8,128)(2,1)S(1)}, u32[]{:S(2)}, u32[]{:S(2)}) collective-permute-start(bf16[1024,1024]{1,0:T(8,128)(2,1)S(1)} %get-tuple-element.24.x3), channel_id=1, source_target_pairs={{2,3},{18,19}} | collective-permute-start | bytes 6291464 | tf_op jit(solution)/shard_map/ppermute | solution.py:313
  70.0 124.3 %collective-permute-start.12 = (bf16[1024,1024]{1,0:T(8,128)(2,1)S(1)}, bf16[1024,1024]{1,0:T(8,128)(2,1)S(1)}, u32[]{:S(2)}, u32[]{:S(2)}) collective-permute-start(bf16[1024,1024]{1,0:T(8,128)(2,1)S(1)} %copy-done.31), channel_id=1, source_target_pairs={{7,6},{8,9},{23,22},{24,25}} | collective-permute-start | bytes 6291464 | tf_op jit(solution)/shard_map/ppermute | solution.py:313
  70.8 123.5 %collective-permute-start.13 = (bf16[1024,1024]{1,0:T(8,128)(2,1)}, bf16[1024,1024]{1,0:T(8,128)(2,1)S(1)}, u32[]{:S(2)}, u32[]{:S(2)}) collective-permute-start(bf16[1024,1024]{1,0:T(8,128)(2,1)} %get-tuple-element.25.h1), channel_id=1, source_target_pairs={{0,1},{5,4},{10,11},{16,17},{21,20},{26,27}} | collective-permute-start | bytes 6291464 | tf_op jit(solution)/shard_map/ppermute | solution.py:313
  71.6 126.0 %copy-start.2 = (bf16[1024,1024]{1,0:T(8,128)(2,1)S(1)}, bf16[1024,1024]{1,0:T(8,128)(2,1)}, u32[]{:S(2)}) copy-start(bf16[1024,1024]{1,0:T(8,128)(2,1)} %copy-done.1) | copy-start | bytes 6291460
  71.6 120.6 %collective-permute-start.14 = (bf16[512,1024]{1,0:T(8,128)(2,1)S(1)}, bf16[512,1024]{1,0:T(8,128)(2,1)S(1)}, u32[]{:S(2)}, u32[]{:S(2)}) collective-permute-start(bf16[512,1024]{1,0:T(8,128)(2,1)S(1)} %get-tuple-element.26), channel_id=1, source_target_pairs={{4,0},{5,1},{6,2},{7,3},{20,16},{21,17},{22,18},{23,19}} | collective-permute-start | bytes 3145736 | tf_op jit(solution)/shard_map/ppermute | solution.py:313
  75.1 150.3 %collective-permute-start.19 = (bf16[1024,1024]{1,0:T(8,128)(2,1)}, bf16[1024,1024]{1,0:T(8,128)(2,1)}, u32[]{:S(2)}, u32[]{:S(2)}) collective-permute-start(bf16[1024,1024]{1,0:T(8,128)(2,1)} %constant_dynamic-update-slice_fusion.h2), channel_id=1, source_target_pairs={{0,2},{5,7},{16,18},{21,23}} | collective-permute-start | bytes 6291464 | tf_op jit(solution)/shard_map/ppermute | solution.py:313
  192.2 6.4 %copy-start.5 = (bf16[512,1024]{1,0:T(8,128)(2,1)}, bf16[512,1024]{1,0:T(8,128)(2,1)S(1)}, u32[]{:S(2)}) copy-start(bf16[512,1024]{1,0:T(8,128)(2,1)S(1)} %collective-permute-done.14.refs_3_.refs_4_) | copy-start | bytes 3145732
  192.2 33.2 %collective-permute-start.18 = (bf16[1024,1024]{1,0:T(8,128)(2,1)}, bf16[1024,1024]{1,0:T(8,128)(2,1)}, u32[]{:S(2)}, u32[]{:S(2)}) collective-permute-start(bf16[1024,1024]{1,0:T(8,128)(2,1)} %constant_dynamic-update-slice_fusion.h2), channel_id=1, source_target_pairs={{0,1},{5,4},{16,17},{21,20}} | collective-permute-start | bytes 6291464 | tf_op jit(solution)/shard_map/ppermute | solution.py:313
  194.3 1.3 copy-start.33
  194.3 2.0 copy-start.32
  196.3 1.3 copy-start.8
  198.6 26.8 %collective-permute-start.15 = (bf16[512,1024]{1,0:T(8,128)(2,1)}, bf16[512,1024]{1,0:T(8,128)(2,1)}, u32[]{:S(2)}, u32[]{:S(2)}) collective-permute-start(bf16[512,1024]{1,0:T(8,128)(2,1)} %shard_map.72._dep), channel_id=1, source_target_pairs={{4,0},{5,1},{6,2},{7,3},{8,4},{9,5},{10,6},{11,7},{12,8},{13,9},{1... | collective-permute-start | bytes 3145736 | tf_op jit(solution)/shard_map/ppermute | solution.py:313
  200.0 2.2 copy-start.12
  202.2 1.6 copy-start.22
  203.7 1.0 copy-start.23
  204.8 43.0 %copy-start.6 = (bf16[512,1024]{1,0:T(8,128)(2,1)S(1)}, bf16[512,1024]{1,0:T(8,128)(2,1)}, u32[]{:S(2)}) copy-start(bf16[512,1024]{1,0:T(8,128)(2,1)} %copy-done.5) | copy-start | bytes 3145732
  209.6 1.0 copy-start.25
  210.6 26.0 %collective-permute-start.17 = (bf16[512,512]{1,0:T(8,128)(2,1)S(1)}, bf16[512,512]{1,0:T(8,128)(2,1)S(1)}, u32[]{:S(2)}, u32[]{:S(2)}) collective-permute-start(bf16[512,512]{1,0:T(8,128)(2,1)S(1)} %get-tuple-element.28), channel_id=1, source_target_pairs={{0,4},{1,5},{2,6},{3,7},{4,0},{5,1},{6,2},{7,3},{8,12},{9,13},{10,... | collective-permute-start | bytes 1572872 | tf_op jit(solution)/shard_map/ppermute | solution.py:313
  212.7 35.1 %collective-permute-start.16 = (bf16[512,512]{1,0:T(8,128)(2,1)S(1)}, bf16[512,512]{1,0:T(8,128)(2,1)S(1)}, u32[]{:S(2)}, u32[]{:S(2)}) collective-permute-start(bf16[512,512]{1,0:T(8,128)(2,1)S(1)} %get-tuple-element.27._dep), channel_id=1, source_target_pairs={{0,4},{1,5},{2,6},{3,7},{4,0},{5,1},{6,2},{7,3},{8,12},{9,13},{10,... | collective-permute-start | bytes 1572872 | tf_op jit(solution)/shard_map/ppermute | solution.py:313
  250.4 10.7 %copy-start.3 = (bf16[1024,1024]{1,0:T(8,128)(2,1)S(1)}, bf16[1024,1024]{1,0:T(8,128)(2,1)}, u32[]{:S(2)}) copy-start(bf16[1024,1024]{1,0:T(8,128)(2,1)} %copy-done.1) | copy-start | bytes 6291460
  250.4 12.9 %collective-permute-start.20 = (bf16[1024,1024]{1,0:T(8,128)(2,1)S(1)}, bf16[1024,1024]{1,0:T(8,128)(2,1)S(1)}, u32[]{:S(2)}, u32[]{:S(2)}) collective-permute-start(bf16[1024,1024]{1,0:T(8,128)(2,1)S(1)} %constant_dynamic-update-slice_fusion.2.h3), channel_id=1, source_target_pairs={{0,1},{16,17}} | collective-permute-start | bytes 6291464 | tf_op jit(solution)/shard_map/ppermute | solution.py:313
  251.4 12.0 %collective-permute-start.21 = (bf16[1024,1024]{1,0:T(8,128)(2,1)}, bf16[1024,1024]{1,0:T(8,128)(2,1)}, u32[]{:S(2)}, u32[]{:S(2)}) collective-permute-start(bf16[1024,1024]{1,0:T(8,128)(2,1)} %get-tuple-element.30.x2), channel_id=1, source_target_pairs={{2,3},{7,6},{18,19},{23,22}} | collective-permute-start | bytes 6291464 | tf_op jit(solution)/shard_map/ppermute | solution.py:313
  252.7 29.6 %collective-permute-start.22 = (bf16[512,1024]{1,0:T(8,128)(2,1)S(1)}, bf16[512,1024]{1,0:T(8,128)(2,1)S(1)}, u32[]{:S(2)}, u32[]{:S(2)}) collective-permute-start(bf16[512,1024]{1,0:T(8,128)(2,1)S(1)} %get-tuple-element.32._dep), channel_id=1, source_target_pairs={{4,0},{5,1},{6,2},{7,3},{8,4},{9,5},{10,6},{11,7},{12,8},{13,9},{1... | collective-permute-start | bytes 3145736 | tf_op jit(solution)/shard_map/ppermute | solution.py:313
  254.0 9.3 %copy-start.9 = (bf16[1024,1024]{1,0:T(8,128)(2,1)S(1)}, bf16[1024,1024]{1,0:T(8,128)(2,1)}, u32[]{:S(2)}) copy-start(bf16[1024,1024]{1,0:T(8,128)(2,1)} %copy-done.8) | copy-start | bytes 6291460
  254.1 51.3 %collective-permute-start.23 = (bf16[512,512]{1,0:T(8,128)(2,1)S(1)}, bf16[512,512]{1,0:T(8,128)(2,1)S(1)}, u32[]{:S(2)}, u32[]{:S(2)}) collective-permute-start(bf16[512,512]{1,0:T(8,128)(2,1)S(1)} %shard_map.78), channel_id=1, source_target_pairs={{0,8},{1,9},{2,10},{3,11},{4,12},{5,13},{6,14},{7,15},{8,0},{9,1},... | collective-permute-start | bytes 1572872 | tf_op jit(solution)/shard_map/ppermute | solution.py:313
  261.4 2.0 copy-start.4
  263.4 18.9 %copy-start.21 = (f32[512,1024]{1,0:T(8,128)S(1)}, f32[512,1024]{1,0:T(8,128)}, u32[]{:S(2)}) copy-start(f32[512,1024]{1,0:T(8,128)} %copy-done.20) | copy-start | bytes 6291460
  263.4 18.9 %copy-start.27 = (s32[8]{0:T(128)S(1)}, s32[8]{0:T(128)}, u32[]{:S(2)}) copy-start(s32[8]{0:T(128)} %structure.1) | copy-start | bytes 100
  282.3 1.6 copy-start.10
  283.9 21.5 %copy-start.26 = (f32[512,512]{1,0:T(8,128)S(1)}, f32[512,512]{1,0:T(8,128)}, u32[]{:S(2)}) copy-start(f32[512,512]{1,0:T(8,128)} %copy-done.25) | copy-start | bytes 3145732
  305.3 1.2 copy-start.13
Sparse Core Ops, SparseCore 0:
  41.3 49.9 all-gather.4
  93.5 55.1 all-gather.2
